TPU v7x, 32 devices: a whole 2x2x4 slice. The times are simulated.
32 devices in a mesh: groups: 2 (over x), leaf: 8 (over z, y), rhs: 2 (over core).
Axes of the slice: x: 2, y: 2, z: 4, core: 2. Of those that a mesh axis runs over, the one named last changes fastest.
Arguments:
- vectors: bfloat16 [64, 65536], P('rhs', ('groups', 'leaf')), parts along dimension 1, may hold values from -6 to 6
- tree_order: int32 [65536], P(('groups', 'leaf')), parts along dimension 0, may hold values from 0 to 32767, as said below
- leaf_basis: bfloat16 [32, 65536], P(None, ('groups', 'leaf')), parts along dimension 1, may hold values from -0.75 to 0.75
- near_blocks: bfloat16 [1024, 64, 256], P(('groups', 'leaf')), parts along dimension 0, may hold values from -0.375 to 0.375
- near_lists: int32 [1024, 4], P(('groups', 'leaf')), parts along dimension 0, may hold values from 0 to 511, as said below
- transfers: bfloat16 [32, 32, 2016], P(None, None, ('groups', 'leaf')), parts along dimension 2, may hold values from -0.8984375 to 0.8984375
- couplings: bfloat16 [6, 32, 32, 2016], P(None, None, None, ('groups', 'leaf')), parts along dimension 3, may hold values from -0.4375 to 0.4375
- coupling_lists: int32 [2016, 6], P(('groups', 'leaf')), parts along dimension 0, may hold values from -1 to 511, as said below
- top_transfers: bfloat16 [32, 32, 28], P(None, None, 'groups'), parts along dimension 2, may hold values from -0.8984375 to 0.8984375
- top_couplings: bfloat16 [6, 32, 32, 30], P(None, None, None, 'groups'), parts along dimension 3, may hold values from -0.4375 to 0.4375
- top_lists: int32 [30, 6], P('groups'), parts along dimension 0, may hold values from -1 to 7, as said below
Outputs:
- applied: float32 [64, 65536], P('rhs', ('groups', 'leaf')), parts along dimension 1
There are 2 independent parts, one for each index of `groups`. A program takes and returns all parts, laid end to end along the dimension named above; each array names one. Nothing has to cross between parts.
Inputs may be any that keep to these rules, and one draw needn't show every extreme that they name: tree_order is a permutation of the part's points; tree_order[j] lies in the same block of 32768 positions as j (the points of 8 neighbouring devices along `leaf`). near_lists[i, 0] = i; every entry lies within 8 leaves of i, and that distance is reached. `coupling_lists`: the row of node g of level k (m = 64 >> k) holds used slots first, then -1; a used entry is a node of level k other than g and at most m away from it, and that distance is reached; some node of every level uses all 6 slots. `top_lists`: the row of node j of top level t holds used slots first, then -1; a used entry is a node of that level other than j; a level of one node has none.
All inputs are finite; a program needn't handle non-finite values.
Results may differ from a plain program's by a relative error of at most 0.011.
Values may be sent and summed in bfloat16 or wider, within the bound.
No kernel may reach another device: no remote copies, remote signals or barrier semaphores. Data moves between devices by JAX's collectives and lax.ppermute only.
A program may use at most 128 MiB of HBM per device.

v0:
```python
import jax
import jax.numpy as jnp
from jax import lax
from jax.sharding import PartitionSpec as P

LEVELS = 6
TOPDEV = 1
REACH = 8


def padded_2(shard, sides, width):
    for axis, dim in sides:
        count, length = (lax.axis_size(axis), shard.shape[dim])
        up = [(i, (i + 1) % count) for i in range(count - 1)]
        down = [(j, i) for i, j in up]
        last = lax.slice_in_dim(shard, length - width, length, axis=dim)
        initial = lax.slice_in_dim(shard, 0, width, axis=dim)
        before = lax.ppermute(last, axis, up)
        after = lax.ppermute(initial, axis, down)
        shard = jnp.concatenate([before, shard, after], axis=dim)
    return shard


def couple_nodes(extended, matrices, partners):
    node_count = partners.shape[0]
    slots_used = partners.shape[1]
    flat_ids = jnp.transpose(partners).reshape(-1)
    picked = jnp.take(extended, flat_ids, axis=2)
    picked = picked.reshape(extended.shape[0], extended.shape[1], slots_used, node_count)
    return jnp.einsum("sabi,hbsi->hai", matrices, picked, preferred_element_type=jnp.float32)


def lift_level(coeffs, matrices):
    lifted = jnp.einsum("abc,hac->hbc", matrices, coeffs, preferred_element_type=jnp.float32)
    return lifted.reshape(lifted.shape[0], lifted.shape[1], -1, 2).sum(axis=3).astype(jnp.bfloat16)


def lower_level(field_sum, matrices, downward):
    parents = jnp.repeat(downward, 2, axis=2)
    return (
        field_sum
        + jnp.einsum("abc,hbc->hac", matrices, parents, preferred_element_type=jnp.float32)
    ).astype(jnp.bfloat16)


def local(
    vectors,
    tree_order,
    leaf_basis,
    near_blocks,
    near_lists,
    transfers,
    couplings,
    coupling_lists,
    top_transfers,
    top_couplings,
    top_lists,
):
    columns = vectors.shape[0]
    rank_size = leaf_basis.shape[0]
    leaves_here = near_blocks.shape[0]
    leaf_size = near_blocks.shape[1]
    points_here = leaves_here * leaf_size
    device = lax.axis_index("leaf")
    local_order = tree_order % points_here
    ordered = jnp.take(vectors, local_order, axis=1)
    padded = padded_2(ordered, (("leaf", 1),), REACH * leaf_size)
    by_leaf = padded.reshape(columns, leaves_here + 2 * REACH, leaf_size)
    near_local = (near_lists - device * leaves_here + REACH).reshape(-1)
    gathered = jnp.take(by_leaf, near_local, axis=1).reshape(columns, leaves_here, -1)
    near_part = jnp.einsum(
        "lqc,hlc->hlq", near_blocks, gathered, preferred_element_type=jnp.float32
    )
    basis_leaves = leaf_basis.reshape(rank_size, leaves_here, leaf_size)
    coeffs = jnp.einsum(
        "alp,hlp->hal",
        basis_leaves,
        ordered.reshape(columns, leaves_here, leaf_size),
        preferred_element_type=jnp.float32,
    ).astype(jnp.bfloat16)
    level_list = []
    offset = 0
    node_count = leaves_here
    for tree_depth in range(LEVELS):
        level_list.append((coeffs, offset, node_count))
        coeffs = lift_level(coeffs, transfers[:, :, offset : offset + node_count])
        offset = offset + node_count
        node_count = node_count // 2
    zero_column = jnp.zeros((columns, rank_size, 1), jnp.bfloat16)
    extended_list = [
        jnp.concatenate([padded_2(level_coeffs, (("leaf", 2),), count), zero_column], axis=2)
        for level_coeffs, start, count in level_list
    ]
    field_list = []
    for extended, level_entry in zip(extended_list, level_list):
        start = level_entry[1]
        count = level_entry[2]
        lists_here = coupling_lists[start : start + count]
        local_ids = jnp.where(lists_here >= 0, lists_here - device * count + count, 3 * count)
        field_list.append(
            couple_nodes(extended, couplings[:, :, :, start : start + count], local_ids)
        )
    top_coeffs = lax.all_gather(coeffs, "leaf", axis=2, tiled=True)
    top_list = []
    node_count = top_coeffs.shape[2]
    offset = 0
    while node_count > 1:
        top_list.append((top_coeffs, offset, node_count))
        top_coeffs = lift_level(top_coeffs, top_transfers[:, :, offset : offset + node_count])
        offset = offset + node_count
        node_count = node_count // 2
    top_list.append((top_coeffs, offset, 1))
    downward = None
    for level_coeffs, start, count in reversed(top_list):
        extended = jnp.concatenate([level_coeffs, zero_column], axis=2)
        lists_here = top_lists[start : start + count]
        local_ids = jnp.where(lists_here >= 0, lists_here, count)
        field_sum = couple_nodes(extended, top_couplings[:, :, :, start : start + count], local_ids)
        if downward is None:
            downward = field_sum.astype(jnp.bfloat16)
        else:
            downward = lower_level(field_sum, top_transfers[:, :, start : start + count], downward)
    downward = lax.dynamic_slice_in_dim(downward, device * TOPDEV, TOPDEV, 2)
    for level_entry, field_sum in reversed(list(zip(level_list, field_list))):
        start = level_entry[1]
        count = level_entry[2]
        downward = lower_level(field_sum, transfers[:, :, start : start + count], downward)
    far_part = jnp.einsum(
        "alp,hal->hlp", basis_leaves, downward, preferred_element_type=jnp.float32
    )
    summed = (near_part + far_part).reshape(columns, points_here)
    return jnp.zeros((columns, points_here), jnp.float32).at[:, local_order].set(summed)


def solution(mesh):
    placed = (
        P("rhs", ("groups", "leaf")),
        P(("groups", "leaf")),
        P(None, ("groups", "leaf")),
        P(("groups", "leaf"), None, None),
        P(("groups", "leaf"), None),
        P(None, None, ("groups", "leaf")),
        P(None, None, None, ("groups", "leaf")),
        P(("groups", "leaf"), None),
        P(None, None, "groups"),
        P(None, None, None, "groups"),
        P("groups", None),
    )
    return jax.shard_map(
        local, mesh=mesh, in_specs=placed, out_specs=P("rhs", ("groups", "leaf")), check_vma=False
    )
```

profile of v0, /device:TPU:0, one launch (start us, length us, event | category | flops | bytes accessed | tf_op | source)
XLA Modules:
  0.0 266.5 jit_solution(1364845944833577865)
XLA Ops:
  2.3 15.0 %gather_fusion = bf16[4096,32]{1,0:T(8,128)(2,1)} fusion(bf16[32,4096]{0,1:T(8,128)(2,1)S(1)} %copy.255, s32[4096]{0:T(1024)S(1)} %broadcast_clamp_fusion), kind=kCustom, calls=%fused_computation | custom fusion | bytes 540672 | tf_op jit(solution)/shard_map/jit(_take)/gather | solution.py:66
  17.3 1.6 copy.263
  19.1 1.5 reshape.530
  23.2 6.3 %collective-permute-start.2 = (bf16[32,32,64]{1,0,2:T(8,128)(2,1)}, bf16[32,32,64]{1,0,2:T(8,128)(2,1)}, u32[]{:S(2)}, u32[]{:S(2)}) collective-permute-start(bf16[32,32,64]{1,0,2:T(8,128)(2,1)} %fusion.3), channel_id=1, source_target_pairs={{0,2},{2,4},{4,6},{6,8},{8,10},{10,12},{12,14},{1,3},{3,5},{5,7},{... | collective-permute-start | bytes 393224 | tf_op jit(solution)/shard_map/ppermute | solution.py:18
  30.3 2.3 bitcast_reduce_fusion
  37.9 1.9 bitcast_reduce_fusion.1
  46.0 5.9 %collective-permute-start.12 = (bf16[32,32,2]{1,0,2:T(8,128)(2,1)}, bf16[32,32,2]{1,0,2:T(8,128)(2,1)}, u32[]{:S(2)}, u32[]{:S(2)}) collective-permute-start(bf16[32,32,2]{1,0,2:T(8,128)(2,1)} %bitcast_reduce_fusion.6), channel_id=1, source_target_pairs={{0,2},{2,4},{4,6},{6,8},{8,10},{10,12},{12,14},{1,3},{3,5},{5,7},{... | collective-permute-start | bytes 12296 | tf_op jit(solution)/shard_map/ppermute | solution.py:18
  51.9 3.4 %bitcast_select_fusion = bf16[32,4096]{0,1:T(8,128)(2,1)S(1)} fusion(bf16[4096,32]{1,0:T(8,128)(2,1)} %gather_fusion, pred[4096]{0:T(1024)(128)(4,1)S(1)} %get-tuple-element.17), kind=kLoop, calls=%fused_computation.62 | loop fusion | flops 131072 | bytes 528384 | tf_op jit(solution)/shard_map/jit(_take)/select_n | solution.py:66
  60.3 32.9 %all_gather.3 = bf16[32,32,8]{1,0,2:T(8,128)(2,1)S(1)} all-gather(bf16[32,32,1]{1,0,2:T(8,128)(2,1)S(1)} %fusion.22), channel_id=1, replica_groups=mesh['groups'=2,'leaf'=8,'rhs'=2] {'leaf'}, dimensions={2}, use_global_device_ids=true | all-gather | bytes 18432 | tf_op jit(solution)/shard_map/all_gather | solution.py:103
  107.8 1.9 convolution_bitcast_fusion.5
  109.7 1.7 convolution_bitcast_fusion.7
  115.0 1.6 fusion.49
  122.8 3.2 %slice.108 = bf16[6,32,32,32]{3,2,1,0:T(8,128)(2,1)} slice(bf16[6,32,32,126]{3,2,1,0:T(8,128)(2,1)} %param.17), slice={[0:6], [0:32], [0:32], [64:96]} | slice | bytes 786432 | tf_op jit(solution)/shard_map/slice | solution.py:101
  126.0 1.6 slice.111
  127.7 1.7 slice.114
  129.3 1.7 slice.117
  131.0 1.7 slice.120
  133.7 6.3 %copy.300 = bf16[6,32,32,64]{2,1,0,3:T(8,128)(2,1)} copy(bf16[6,32,32,64]{3,2,1,0:T(8,128)(2,1)} %bitcast.232) | data formatting | bytes 1572864
  140.0 4.2 %copy.302 = bf16[6,32,32,32]{2,1,0,3:T(8,128)(2,1)} copy(bf16[6,32,32,32]{3,2,1,0:T(8,128)(2,1)} %slice.108) | data formatting | bytes 786432
  144.2 3.1 %copy.304 = bf16[6,32,32,16]{2,1,0,3:T(8,128)(2,1)} copy(bf16[6,32,32,16]{3,2,1,0:T(8,128)(2,1)} %slice.111) | data formatting | bytes 393216
  147.9 2.0 copy.306
  149.9 2.7 %copy.308 = bf16[6,32,32,4]{2,1,3,0:T(8,128)(2,1)S(1)} copy(bf16[6,32,32,4]{3,2,1,0:T(8,128)(2,1)} %slice.117) | data formatting | bytes 98304
  152.6 2.5 copy.310
  156.5 4.5 %collective-permute-start.10 = (bf16[32,32,4]{1,0,2:T(8,128)(2,1)S(1)}, bf16[32,32,4]{1,0,2:T(8,128)(2,1)S(1)}, u32[]{:S(2)}, u32[]{:S(2)}) collective-permute-start(bf16[32,32,4]{1,0,2:T(8,128)(2,1)S(1)} %copy-done.18), channel_id=1, source_target_pairs={{0,2},{2,4},{4,6},{6,8},{8,10},{10,12},{12,14},{1,3},{3,5},{5,7},{... | collective-permute-start | bytes 24584 | tf_op jit(solution)/shard_map/ppermute | solution.py:18
  164.2 5.2 %collective-permute-start.8 = (bf16[32,32,8]{1,0,2:T(8,128)(2,1)S(1)}, bf16[32,32,8]{1,0,2:T(8,128)(2,1)}, u32[]{:S(2)}, u32[]{:S(2)}) collective-permute-start(bf16[32,32,8]{1,0,2:T(8,128)(2,1)S(1)} %copy-done.14), channel_id=1, source_target_pairs={{0,2},{2,4},{4,6},{6,8},{8,10},{10,12},{12,14},{1,3},{3,5},{5,7},{... | collective-permute-start | bytes 49160 | tf_op jit(solution)/shard_map/ppermute | solution.py:18
  172.6 5.2 %collective-permute-start = (bf16[32,512]{0,1:T(8,128)(2,1)}, bf16[32,512]{0,1:T(8,128)(2,1)}, u32[]{:S(2)}, u32[]{:S(2)}) collective-permute-start(bf16[32,512]{0,1:T(8,128)(2,1)} %get-tuple-element.19), channel_id=1, source_target_pairs={{0,2},{2,4},{4,6},{6,8},{8,10},{10,12},{12,14},{1,3},{3,5},{5,7},{... | collective-permute-start | bytes 98312 | tf_op jit(solution)/shard_map/ppermute | solution.py:18
  180.6 1.6 fusion.9
  184.5 5.2 %collective-permute-start.6 = (bf16[32,32,16]{1,0,2:T(8,128)(2,1)}, bf16[32,32,16]{1,0,2:T(8,128)(2,1)}, u32[]{:S(2)}, u32[]{:S(2)}) collective-permute-start(bf16[32,32,16]{1,0,2:T(8,128)(2,1)} %bitcast_reduce_fusion.1), channel_id=1, source_target_pairs={{0,2},{2,4},{4,6},{6,8},{8,10},{10,12},{12,14},{1,3},{3,5},{5,7},{... | collective-permute-start | bytes 98312 | tf_op jit(solution)/shard_map/ppermute | solution.py:18
  191.3 2.4 gather_fusion.1
  193.7 3.7 %copy.261 = bf16[32,256,64]{2,1,0:T(8,128)(2,1)} copy(bf16[32,256,64]{2,0,1:T(8,128)(2,1)} %bitcast.234) | data formatting | bytes 2097152 | tf_op jit(solution)/shard_map/jit(_take)/gather | solution.py:70
  197.4 3.3 %gather.72 = bf16[32,64,256]{2,1,0:T(8,128)(2,1)S(1)} reshape(bf16[32,256,64]{2,1,0:T(8,128)(2,1)} %copy.261) | data formatting | bytes 2097152 | tf_op jit(solution)/shard_map/jit(_take)/gather | solution.py:70
  200.8 1.8 fusion.23
  202.7 3.3 %collective-permute-start.4 = (bf16[32,32,32]{1,0,2:T(8,128)(2,1)}, bf16[32,32,32]{1,0,2:T(8,128)(2,1)S(1)}, u32[]{:S(2)}, u32[]{:S(2)}) collective-permute-start(bf16[32,32,32]{1,0,2:T(8,128)(2,1)} %bitcast_reduce_fusion), channel_id=1, source_target_pairs={{0,2},{2,4},{4,6},{6,8},{8,10},{10,12},{12,14},{1,3},{3,5},{5,7},{... | collective-permute-start | bytes 196616 | tf_op jit(solution)/shard_map/ppermute | solution.py:18
  211.2 2.2 gather_fusion.3
  213.4 3.5 %copy.299 = bf16[32,32,6,32]{3,2,1,0:T(8,128)(2,1)S(1)} copy(bf16[32,32,6,32]{1,0,3,2:T(8,128)(2,1)} %bitcast.237) | data formatting | bytes 786432 | tf_op jit(solution)/shard_map/jit(_take)/gather | solution.py:28
  216.8 1.6 broadcast_select_fusion
  218.5 3.7 %copy.271 = bf16[32,32,6,32]{1,0,2,3:T(8,128)(2,1)S(1)} copy(bf16[32,32,6,32]{3,2,1,0:T(8,128)(2,1)} %broadcast_select_fusion) | data formatting | bytes 786432 | tf_op jit(solution)/shard_map/jit(_take)/select_n | solution.py:28
  222.2 2.0 convolution_bitcast_fusion.1
  224.6 1.8 pad_maximum_fusion
  226.3 3.2 %gather_fusion.2 = bf16[384,32,32]{2,1,0:T(8,128)(2,1)} fusion(bf16[32,32,193]{1,0,2:T(8,128)(2,1)S(1)} %pad_maximum_fusion, s32[1024]{0:T(1024)S(1)} %copy-done.26), kind=kCustom, calls=%fused_computation.2 | custom fusion | bytes 1574400 | tf_op jit(solution)/shard_map/jit(_take)/gather | solution.py:28
  229.5 4.6 %copy.298 = bf16[32,32,6,64]{3,2,1,0:T(8,128)(2,1)S(1)} copy(bf16[32,32,6,64]{1,0,3,2:T(8,128)(2,1)} %bitcast.236) | data formatting | bytes 1572864 | tf_op jit(solution)/shard_map/jit(_take)/gather | solution.py:28
  234.2 1.7 broadcast_select_fusion.1
  235.8 5.5 %copy.267 = bf16[32,32,6,64]{1,0,2,3:T(8,128)(2,1)} copy(bf16[32,32,6,64]{3,2,1,0:T(8,128)(2,1)} %broadcast_select_fusion.1) | data formatting | bytes 1572864 | tf_op jit(solution)/shard_map/jit(_take)/select_n | solution.py:28
  241.4 3.9 %convolution_bitcast_fusion = f32[64,32,32]{2,1,0:T(8,128)S(1)} fusion(bf16[32,32,6,64]{1,0,2,3:T(8,128)(2,1)} %copy.267, bf16[6,32,32,64]{2,1,0,3:T(8,128)(2,1)} %copy.300), kind=kOutput, calls=%fused_computation.19 | convolution fusion | flops 25165824 | bytes 1835008 | tf_op jit(solution)/shard_map/sabi,hbsi->hai/dot_general | solution.py:30
  246.2 2.2 fusion
  249.3 2.0 copy.291
  251.3 12.3 %scatter_custom_fusion = f32[32,4096]{0,1:T(8,128)} fusion(s32[4096]{0:T(1024)} %copy-done.25, f32[4096,32]{1,0:T(8,128)} %copy.291, f32[]{:T(128)} %constant.128.clone.1), kind=kCustom, calls=%fused_computation.65 | custom fusion | bytes 524800 | tf_op jit(solution)/shard_map/scatter | solution.py:132
  263.5 3.0 %copy.292 = f32[32,4096]{1,0:T(8,128)} copy(f32[32,4096]{0,1:T(8,128)} %scatter_custom_fusion) | data formatting | bytes 1048576 | tf_op jit(solution)/shard_map/scatter | solution.py:132
  (217 shorter events, 69.6 us)
Async XLA Ops:
  0.0 200.8 %copy-start = (bf16[64,64,256]{2,1,0:T(8,128)(2,1)S(1)}, bf16[64,64,256]{2,1,0:T(8,128)(2,1)}, u32[]{:S(2)}) copy-start(bf16[64,64,256]{2,1,0:T(8,128)(2,1)} %param.14) | copy-start | bytes 6291460
  0.9 16.5 %copy-start.25 = (s32[4096]{0:T(1024)}, s32[4096]{0:T(1024)S(1)}, u32[]{:S(2)}) copy-start(s32[4096]{0:T(1024)S(1)} %get-tuple-element.18) | copy-start | bytes 49156
  17.3 12.1 %copy-start.3 = (bf16[32,32,126]{2,1,0:T(8,128)(2,1)S(1)}, bf16[32,32,126]{2,1,0:T(8,128)(2,1)}, u32[]{:S(2)}) copy-start(bf16[32,32,126]{2,1,0:T(8,128)(2,1)} %param.16) | copy-start | bytes 774148
  20.5 8.9 %copy-start.8 = (bf16[32,64,64]{2,1,0:T(8,128)(2,1)}, bf16[32,64,64]{2,1,0:T(8,128)(2,1)S(1)}, u32[]{:S(2)}) copy-start(bf16[32,64,64]{2,1,0:T(8,128)(2,1)S(1)} %reshape.530) | copy-start | bytes 786436
  21.9 202.7 %collective-permute-start.3 = (bf16[32,32,64]{1,0,2:T(8,128)(2,1)}, bf16[32,32,64]{1,0,2:T(8,128)(2,1)}, u32[]{:S(2)}, u32[]{:S(2)}) collective-permute-start(bf16[32,32,64]{1,0,2:T(8,128)(2,1)} %fusion.3), channel_id=1, source_target_pairs={{2,0},{4,2},{6,4},{8,6},{10,8},{12,10},{14,12},{3,1},{5,3},{7,5},{... | collective-permute-start | bytes 393224 | tf_op jit(solution)/shard_map/ppermute | solution.py:19
  23.2 201.4 %collective-permute-start.2 = (bf16[32,32,64]{1,0,2:T(8,128)(2,1)}, bf16[32,32,64]{1,0,2:T(8,128)(2,1)}, u32[]{:S(2)}, u32[]{:S(2)}) collective-permute-start(bf16[32,32,64]{1,0,2:T(8,128)(2,1)} %fusion.3), channel_id=1, source_target_pairs={{0,2},{2,4},{4,6},{6,8},{8,10},{10,12},{12,14},{1,3},{3,5},{5,7},{... | collective-permute-start | bytes 393224 | tf_op jit(solution)/shard_map/ppermute | solution.py:18
  30.2 9.6 %copy-start.4 = (bf16[32,32,64]{1,0,2:T(8,128)(2,1)}, bf16[32,32,64]{1,0,2:T(8,128)(2,1)S(1)}, u32[]{:S(2)}) copy-start(bf16[32,32,64]{1,0,2:T(8,128)(2,1)S(1)} %copy.301) | copy-start | bytes 393220
  32.5 176.2 %collective-permute-start.5 = (bf16[32,32,32]{1,0,2:T(8,128)(2,1)}, bf16[32,32,32]{1,0,2:T(8,128)(2,1)}, u32[]{:S(2)}, u32[]{:S(2)}) collective-permute-start(bf16[32,32,32]{1,0,2:T(8,128)(2,1)} %bitcast_reduce_fusion), channel_id=1, source_target_pairs={{2,0},{4,2},{6,4},{8,6},{10,8},{12,10},{14,12},{3,1},{5,3},{7,5},{... | collective-permute-start | bytes 196616 | tf_op jit(solution)/shard_map/ppermute | solution.py:19
  37.9 8.0 %copy-start.6 = (bf16[32,32,32]{1,0,2:T(8,128)(2,1)}, bf16[32,32,32]{1,0,2:T(8,128)(2,1)S(1)}, u32[]{:S(2)}) copy-start(bf16[32,32,32]{1,0,2:T(8,128)(2,1)S(1)} %copy.303) | copy-start | bytes 196612
  37.9 17.4 %copy-start.27 = (s32[64,4]{0,1:T(4,128)S(1)}, s32[64,4]{0,1:T(4,128)}, u32[]{:S(2)}) copy-start(s32[64,4]{0,1:T(4,128)} %param.15) | copy-start | bytes 3076
  39.9 16.9 %copy-start.20 = (s32[15,6]{0,1:T(8,128)S(1)}, s32[15,6]{0,1:T(8,128)}, u32[]{:S(2)}) copy-start(s32[15,6]{0,1:T(8,128)} %param.21) | copy-start | bytes 1084
  41.3 4.7 %copy-start.12 = (bf16[32,32,8]{1,0,2:T(8,128)(2,1)}, bf16[32,32,8]{1,0,2:T(8,128)(2,1)S(1)}, u32[]{:S(2)}) copy-start(bf16[32,32,8]{1,0,2:T(8,128)(2,1)S(1)} %copy.307) | copy-start | bytes 49156
  42.5 3.4 %copy-start.15 = (bf16[32,32,4]{1,0,2:T(8,128)(2,1)}, bf16[32,32,4]{1,0,2:T(8,128)(2,1)S(1)}, u32[]{:S(2)}) copy-start(bf16[32,32,4]{1,0,2:T(8,128)(2,1)S(1)} %copy.309) | copy-start | bytes 24580
  43.6 2.3 copy-start.13
  43.8 2.2 copy-start.17
  44.5 53.9 %copy-start.21 = (s32[126,6]{0,1:T(8,128)S(1)}, s32[126,6]{0,1:T(8,128)}, u32[]{:S(2)}) copy-start(s32[126,6]{0,1:T(8,128)} %param.18) | copy-start | bytes 9076
  44.5 110.6 %collective-permute-start.13 = (bf16[32,32,2]{1,0,2:T(8,128)(2,1)}, bf16[32,32,2]{1,0,2:T(8,128)(2,1)}, u32[]{:S(2)}, u32[]{:S(2)}) collective-permute-start(bf16[32,32,2]{1,0,2:T(8,128)(2,1)} %bitcast_reduce_fusion.6), channel_id=1, source_target_pairs={{2,0},{4,2},{6,4},{8,6},{10,8},{12,10},{14,12},{3,1},{5,3},{7,5},{... | collective-permute-start | bytes 12296 | tf_op jit(solution)/shard_map/ppermute | solution.py:19
  46.0 110.5 %collective-permute-start.12 = (bf16[32,32,2]{1,0,2:T(8,128)(2,1)}, bf16[32,32,2]{1,0,2:T(8,128)(2,1)}, u32[]{:S(2)}, u32[]{:S(2)}) collective-permute-start(bf16[32,32,2]{1,0,2:T(8,128)(2,1)} %bitcast_reduce_fusion.6), channel_id=1, source_target_pairs={{0,2},{2,4},{4,6},{6,8},{8,10},{10,12},{12,14},{1,3},{3,5},{5,7},{... | collective-permute-start | bytes 12296 | tf_op jit(solution)/shard_map/ppermute | solution.py:18
  59.4 46.5 %copy-start.22 = (bf16[32,32,2]{1,0,2:T(8,128)(2,1)}, bf16[32,32,2]{1,0,2:T(8,128)(2,1)S(1)}, u32[]{:S(2)}) copy-start(bf16[32,32,2]{1,0,2:T(8,128)(2,1)S(1)} %copy.311) | copy-start | bytes 12292
  97.7 14.3 %copy-start.34 = (pred[6]{0:T(512)(128)(4,1)S(1)}, pred[6]{0:T(512)(128)(4,1)}, u32[]{:S(2)}) copy-start(pred[6]{0:T(512)(128)(4,1)} %compare_and_fusion.10) | copy-start | bytes 22
  122.8 3.2 %copy-start.2 = (bf16[6,32,32,126]{3,2,1,0:T(8,128)(2,1)S(1)}, bf16[6,32,32,126]{3,2,1,0:T(8,128)(2,1)}, u32[]{:S(2)}) copy-start(bf16[6,32,32,126]{3,2,1,0:T(8,128)(2,1)} %param.17) | copy-start | bytes 4644868
  140.0 7.3 %copy-start.30 = (pred[6,16]{1,0:T(8,128)(4,1)S(1)}, pred[6,16]{1,0:T(8,128)(4,1)}, u32[]{:S(2)}) copy-start(pred[6,16]{1,0:T(8,128)(4,1)} %get-tuple-element.11) | copy-start | bytes 292
  149.9 5.3 %copy-start.18 = (bf16[32,32,4]{1,0,2:T(8,128)(2,1)S(1)}, bf16[32,32,4]{1,0,2:T(8,128)(2,1)}, u32[]{:S(2)}) copy-start(bf16[32,32,4]{1,0,2:T(8,128)(2,1)} %copy-done.17) | copy-start | bytes 24580
  149.9 12.6 %copy-start.33 = (pred[6,2]{1,0:T(8,128)(4,1)S(1)}, pred[6,2]{1,0:T(8,128)(4,1)}, u32[]{:S(2)}) copy-start(pred[6,2]{1,0:T(8,128)(4,1)} %get-tuple-element.5) | copy-start | bytes 40
  149.9 12.8 %copy-start.23 = (bf16[32,32,2]{1,0,2:T(8,128)(2,1)S(1)}, bf16[32,32,2]{1,0,2:T(8,128)(2,1)}, u32[]{:S(2)}) copy-start(bf16[32,32,2]{1,0,2:T(8,128)(2,1)} %copy-done.22) | copy-start | bytes 12292
  149.9 13.0 %copy-start.14 = (bf16[32,32,8]{1,0,2:T(8,128)(2,1)S(1)}, bf16[32,32,8]{1,0,2:T(8,128)(2,1)}, u32[]{:S(2)}) copy-start(bf16[32,32,8]{1,0,2:T(8,128)(2,1)} %copy-done.13) | copy-start | bytes 49156
  152.6 18.5 %copy-start.16 = (bf16[32,32,4]{1,0,2:T(8,128)(2,1)S(1)}, bf16[32,32,4]{1,0,2:T(8,128)(2,1)}, u32[]{:S(2)}) copy-start(bf16[32,32,4]{1,0,2:T(8,128)(2,1)} %copy-done.15) | copy-start | bytes 24580
  155.2 7.7 %collective-permute-start.11 = (bf16[32,32,4]{1,0,2:T(8,128)(2,1)S(1)}, bf16[32,32,4]{1,0,2:T(8,128)(2,1)S(1)}, u32[]{:S(2)}, u32[]{:S(2)}) collective-permute-start(bf16[32,32,4]{1,0,2:T(8,128)(2,1)S(1)} %copy-done.18), channel_id=1, source_target_pairs={{2,0},{4,2},{6,4},{8,6},{10,8},{12,10},{14,12},{3,1},{5,3},{7,5},{... | collective-permute-start | bytes 24584 | tf_op jit(solution)/shard_map/ppermute | solution.py:19
  156.5 7.7 %collective-permute-start.10 = (bf16[32,32,4]{1,0,2:T(8,128)(2,1)S(1)}, bf16[32,32,4]{1,0,2:T(8,128)(2,1)S(1)}, u32[]{:S(2)}, u32[]{:S(2)}) collective-permute-start(bf16[32,32,4]{1,0,2:T(8,128)(2,1)S(1)} %copy-done.18), channel_id=1, source_target_pairs={{0,2},{2,4},{4,6},{6,8},{8,10},{10,12},{12,14},{1,3},{3,5},{5,7},{... | collective-permute-start | bytes 24584 | tf_op jit(solution)/shard_map/ppermute | solution.py:18
  162.9 8.4 %collective-permute-start.9 = (bf16[32,32,8]{1,0,2:T(8,128)(2,1)S(1)}, bf16[32,32,8]{1,0,2:T(8,128)(2,1)}, u32[]{:S(2)}, u32[]{:S(2)}) collective-permute-start(bf16[32,32,8]{1,0,2:T(8,128)(2,1)S(1)} %copy-done.14), channel_id=1, source_target_pairs={{2,0},{4,2},{6,4},{8,6},{10,8},{12,10},{14,12},{3,1},{5,3},{7,5},{... | collective-permute-start | bytes 49160 | tf_op jit(solution)/shard_map/ppermute | solution.py:19
  164.2 8.4 %collective-permute-start.8 = (bf16[32,32,8]{1,0,2:T(8,128)(2,1)S(1)}, bf16[32,32,8]{1,0,2:T(8,128)(2,1)}, u32[]{:S(2)}, u32[]{:S(2)}) collective-permute-start(bf16[32,32,8]{1,0,2:T(8,128)(2,1)S(1)} %copy-done.14), channel_id=1, source_target_pairs={{0,2},{2,4},{4,6},{6,8},{8,10},{10,12},{12,14},{1,3},{3,5},{5,7},{... | collective-permute-start | bytes 49160 | tf_op jit(solution)/shard_map/ppermute | solution.py:18
  170.2 20.5 %copy-start.10 = (bf16[32,4096]{1,0:T(8,128)(2,1)S(1)}, bf16[32,4096]{1,0:T(8,128)(2,1)}, u32[]{:S(2)}) copy-start(bf16[32,4096]{1,0:T(8,128)(2,1)} %copy.257) | copy-start | bytes 786436
  171.3 10.9 %collective-permute-start.1 = (bf16[32,512]{0,1:T(8,128)(2,1)}, bf16[32,512]{0,1:T(8,128)(2,1)}, u32[]{:S(2)}, u32[]{:S(2)}) collective-permute-start(bf16[32,512]{0,1:T(8,128)(2,1)} %get-tuple-element.20), channel_id=1, source_target_pairs={{2,0},{4,2},{6,4},{8,6},{10,8},{12,10},{14,12},{3,1},{5,3},{7,5},{... | collective-permute-start | bytes 98312 | tf_op jit(solution)/shard_map/ppermute | solution.py:19
  172.6 11.9 %collective-permute-start = (bf16[32,512]{0,1:T(8,128)(2,1)}, bf16[32,512]{0,1:T(8,128)(2,1)}, u32[]{:S(2)}, u32[]{:S(2)}) collective-permute-start(bf16[32,512]{0,1:T(8,128)(2,1)} %get-tuple-element.19), channel_id=1, source_target_pairs={{0,2},{2,4},{4,6},{6,8},{8,10},{10,12},{12,14},{1,3},{3,5},{5,7},{... | collective-permute-start | bytes 98312 | tf_op jit(solution)/shard_map/ppermute | solution.py:18
  182.2 20.5 %collective-permute-start.7 = (bf16[32,32,16]{1,0,2:T(8,128)(2,1)}, bf16[32,32,16]{1,0,2:T(8,128)(2,1)}, u32[]{:S(2)}, u32[]{:S(2)}) collective-permute-start(bf16[32,32,16]{1,0,2:T(8,128)(2,1)} %bitcast_reduce_fusion.1), channel_id=1, source_target_pairs={{2,0},{4,2},{6,4},{8,6},{10,8},{12,10},{14,12},{3,1},{5,3},{7,5},{... | collective-permute-start | bytes 98312 | tf_op jit(solution)/shard_map/ppermute | solution.py:19
  184.5 21.5 %collective-permute-start.6 = (bf16[32,32,16]{1,0,2:T(8,128)(2,1)}, bf16[32,32,16]{1,0,2:T(8,128)(2,1)}, u32[]{:S(2)}, u32[]{:S(2)}) collective-permute-start(bf16[32,32,16]{1,0,2:T(8,128)(2,1)} %bitcast_reduce_fusion.1), channel_id=1, source_target_pairs={{0,2},{2,4},{4,6},{6,8},{8,10},{10,12},{12,14},{1,3},{3,5},{5,7},{... | collective-permute-start | bytes 98312 | tf_op jit(solution)/shard_map/ppermute | solution.py:18
  197.4 3.3 %copy-start.24 = (pred[64,256]{1,0:T(8,128)(4,1)S(1)}, pred[64,256]{1,0:T(8,128)(4,1)}, u32[]{:S(2)}) copy-start(pred[64,256]{1,0:T(8,128)(4,1)} %broadcast_in_dim.190) | copy-start | bytes 49156
  200.8 7.2 %copy-start.11 = (bf16[6,32,32,16]{2,1,0,3:T(8,128)(2,1)S(1)}, bf16[6,32,32,16]{2,1,0,3:T(8,128)(2,1)}, u32[]{:S(2)}) copy-start(bf16[6,32,32,16]{2,1,0,3:T(8,128)(2,1)} %copy.304) | copy-start | bytes 589828
  200.8 7.2 %copy-start.31 = (pred[6,16]{0,1:T(8,128)(4,1)S(1)}, pred[6,16]{0,1:T(8,128)(4,1)}, u32[]{:S(2)}) copy-start(pred[6,16]{0,1:T(8,128)(4,1)} %copy.272) | copy-start | bytes 292
  202.7 5.8 %copy-start.19 = (bf16[32,32,8]{1,0,2:T(8,128)(2,1)S(1)}, bf16[32,32,8]{1,0,2:T(8,128)(2,1)}, u32[]{:S(2)}) copy-start(bf16[32,32,8]{1,0,2:T(8,128)(2,1)} %fusion.9) | copy-start | bytes 49156
  202.7 7.3 %collective-permute-start.4 = (bf16[32,32,32]{1,0,2:T(8,128)(2,1)}, bf16[32,32,32]{1,0,2:T(8,128)(2,1)S(1)}, u32[]{:S(2)}, u32[]{:S(2)}) collective-permute-start(bf16[32,32,32]{1,0,2:T(8,128)(2,1)} %bitcast_reduce_fusion), channel_id=1, source_target_pairs={{0,2},{2,4},{4,6},{6,8},{8,10},{10,12},{12,14},{1,3},{3,5},{5,7},{... | collective-permute-start | bytes 196616 | tf_op jit(solution)/shard_map/ppermute | solution.py:18
  213.4 3.5 %copy-start.29 = (pred[6,32]{1,0:T(8,128)(4,1)S(1)}, pred[6,32]{1,0:T(8,128)(4,1)}, u32[]{:S(2)}) copy-start(pred[6,32]{1,0:T(8,128)(4,1)} %get-tuple-element.13) | copy-start | bytes 580
  222.2 2.1 copy-start.7
  224.3 2.1 copy-start.26
  229.5 4.7 %copy-start.28 = (pred[6,64]{1,0:T(8,128)(4,1)S(1)}, pred[6,64]{1,0:T(8,128)(4,1)}, u32[]{:S(2)}) copy-start(pred[6,64]{1,0:T(8,128)(4,1)} %get-tuple-element.15) | copy-start | bytes 1156
  241.4 4.8 %copy-start.5 = (bf16[32,32,64]{1,0,2:T(8,128)(2,1)S(1)}, bf16[32,32,64]{1,0,2:T(8,128)(2,1)}, u32[]{:S(2)}) copy-start(bf16[32,32,64]{1,0,2:T(8,128)(2,1)} %copy-done.4) | copy-start | bytes 393220
  241.4 4.8 %copy-start.9 = (bf16[32,64,64]{2,1,0:T(8,128)(2,1)S(1)}, bf16[32,64,64]{2,1,0:T(8,128)(2,1)}, u32[]{:S(2)}) copy-start(bf16[32,64,64]{2,1,0:T(8,128)(2,1)} %copy-done.8) | copy-start | bytes 786436
  249.3 17.2 %copy-start.1 = (bf16[64,64,256]{2,1,0:T(8,128)(2,1)S(1)}, bf16[64,64,256]{2,1,0:T(8,128)(2,1)}, u32[]{:S(2)}) copy-start(bf16[64,64,256]{2,1,0:T(8,128)(2,1)} %param.14) | copy-start | bytes 6291460
  (1 other events, 1.7 us)
where the time goes:
time: 269 us; the launch traced here: 267 us
  local copies, waits for them, and re-layouts  125 us (46%)
  starting transfers between devices  44.8 us (17%)
  matrix products  34.6 us (13%)
  blocking collectives  32.9 us (12%)
  other arithmetic  27.1 us (10%)
    ppermute x7, starting transfers between devices, padded_2(): before = lax.ppermute(last, axis, up)  35.7 us
    all_gather x1, blocking collectives, local(): top_coeffs = lax.all_gather(coeffs, 'leaf', axis=2, tiled=True)  32.9 us
    unnamed x83, local copies, waits for them, and re-layouts  28.3 us
    gather x12, local copies, waits for them, and re-layouts, couple_nodes(): picked = jnp.take(extended, flat_ids, axis=2)  20.2 us
    gather x2, local copies, waits for them, and re-layouts, local(): ordered = jnp.take(vectors, local_order, axis=1)  16.6 us
    scatter x2, local copies, waits for them, and re-layouts, local(): jnp.zeros((columns, points_here), jnp.float32).at[:, local_order]  15.3 us
    dot_general x10, matrix products, couple_nodes(): jnp.einsum('sabi,hbsi->hai', matrices, picked, preferred_element_type=jnp...  13.6 us
    slice x5, local copies, waits for them, and re-layouts, local(): couplings[:, :, :, start:start + count]  9.89 us
  transfers between devices with their start and end apart: 14, of which 1 were waited for; matrix products, arithmetic and copies ran while one was open for 46% of the time, Pallas kernels for 0%

commit v1 on v0

v1 whole, which is shorter than its diff:
```python
import functools

import jax
import jax.numpy as jnp
from jax import lax
from jax.experimental import pallas as pl
from jax.experimental.pallas import tpu as pltpu
from jax.sharding import PartitionSpec as P

LEVELS = 6
REACH = 8
BF = jnp.bfloat16
F32 = jnp.float32
NT = (((1,), (1,)), ((), ()))
NN = (((1,), (0,)), ((), ()))


def iota(shape, axis):
    return lax.broadcasted_iota(jnp.int32, shape, axis)


def dot(a, b, dims):
    return lax.dot_general(a, b, dims, preferred_element_type=F32)


def gather_lanes(src_ref, lo, hi):
    rows, points = src_ref.shape
    lo = jnp.broadcast_to(lo, (8, 128))
    hi = jnp.broadcast_to(hi, (8, 128))
    picked = [jnp.zeros((8, 128), F32) for _ in range(rows // 8)]
    for chunk in range(points // 128):
        here = hi == chunk
        for r in range(rows // 8):
            values = src_ref[pl.ds(r * 8, 8), pl.ds(chunk * 128, 128)]
            moved = jnp.take_along_axis(values, lo, axis=1, mode="promise_in_bounds")
            picked[r] = jnp.where(here, moved, picked[r])
    return jnp.concatenate(picked, axis=0)


def pad_lanes(x):
    short = 128 - x.shape[1]
    return jnp.concatenate([x, jnp.zeros((x.shape[0], short), x.dtype)], axis=1)


def up_kernel(
    vec_ref, order_ref, basis_ref, transfer_ref,
    ordered_ref, left_ref, right_ref, top_ref, weights_ref, masked_ref,
    vec32, rows32,
):
    columns, points = vec_ref.shape
    rank = basis_ref.shape[0]
    halo = left_ref.shape[1] - 4096
    vec32[...] = vec_ref[...].astype(F32)

    def permute(j, carry):
        ids = lax.rem(order_ref[pl.ds(j, 1), :], points)
        picked = gather_lanes(vec32, ids & 127, ids >> 7)
        ordered_ref[:, pl.ds(pl.multiple_of(j * 128, 128), 128)] = picked.astype(BF)
        return carry

    lax.fori_loop(0, points // 128, permute, 0)

    def relayout(a, carry):
        one = transfer_ref[pl.ds(pl.multiple_of(a * rank, rank), rank), :].astype(F32)
        four = pad_lanes(jnp.concatenate([one] * 4, axis=0))
        rows32[pl.ds(a, 128, stride=rank), :] = four.T
        return carry

    lax.fori_loop(0, rank, relayout, 0)
    mine = (iota((256, 128), 0) >> 6) == (iota((256, 128), 1) >> 5)
    mine_leaf = (iota((128, 256), 0) >> 5) == (iota((128, 256), 1) >> 6)
    coeffs = [None] * 32
    for g in range(16):
        weights_ref[g] = jnp.where(mine, rows32[pl.ds(g * 256, 256), :], 0.0).astype(BF)
        one = basis_ref[:, pl.ds(g * 256, 256)].astype(F32)
        masked = jnp.where(mine_leaf, jnp.concatenate([one] * 4, axis=0), 0.0).astype(BF)
        masked_ref[g] = masked
        coeffs[g] = dot(ordered_ref[:, pl.ds(g * 256, 256)], masked, NT).astype(BF)
    for k in range(15):
        pair = jnp.concatenate([coeffs[2 * k], coeffs[2 * k + 1]], axis=1)
        coeffs[16 + k] = dot(pair, weights_ref[k], NN).astype(BF)
    coeffs[31] = dot(coeffs[30], weights_ref[15, :128, :], NN).astype(BF)
    top_ref[0] = dot(coeffs[31], weights_ref[15, 128:, :], NN).astype(BF)
    for g in range(32):
        left_ref[:, pl.ds(halo + g * 128, 128)] = coeffs[g]
        right_ref[:, pl.ds(halo + g * 128, 128)] = coeffs[g]
    left_ref[:, :halo] = ordered_ref[:, :halo]
    right_ref[:, :halo] = ordered_ref[:, points - halo :]


def near_group(leaves_ref, lists_ref, blocks, first, base, columns):
    lane_left = iota((columns, 128), 1) < 64
    picked = []
    for i in range(4):
        spots = [lists_ref[s, first + i] - base for s in range(4)]
        halves = []
        for s in (0, 2):
            even = leaves_ref[spots[s]].astype(F32)
            odd = leaves_ref[spots[s + 1] ^ 1].astype(F32)
            halves.append(jnp.where(lane_left, even, odd))
        picked.append(jnp.concatenate(halves, axis=1))
    moving = jnp.concatenate(picked, axis=0).astype(BF)
    out = dot(moving, blocks, NT)
    leaf_of_lane = iota((columns, 256), 1) >> 6
    total = jnp.where(leaf_of_lane == 0, out[:columns], 0.0)
    for i in range(1, 4):
        total = jnp.where(leaf_of_lane == i, out[i * columns : (i + 1) * columns], total)
    return total


def place_leaves(leaves_ref, first, chunk):
    leaves_ref[first] = chunk
    leaves_ref[first + 1] = pltpu.roll(chunk.astype(F32), 64, 1).astype(BF)


def inner_kernel(
    ordered_ref, blocks_ref, near_ref, order_ref, coupling_ref, lists_ref, weights_ref, masked_ref,
    near_out, matrices_ref, spots_ref, inverse_ref, reach_ref,
    leaves, rows32, wide,
):
    columns, points = ordered_ref.shape
    rank = 32
    count = blocks_ref.shape[0]
    device = lax.axis_index("leaf")

    def invert(j, total):
        ids = lax.rem(order_ref[pl.ds(j, 1), :], points)
        high, low = ids >> 7, ids & 127
        lane = iota((32, 128), 1).astype(F32)
        hit = iota((32, 128), 0) == jnp.broadcast_to(high, (32, 128))
        block = jnp.where(hit, j.astype(F32), 0.0)
        within = jnp.where(hit, lane, 0.0)
        left = jnp.concatenate([block, within], axis=0).astype(BF)
        right = jnp.where(iota((128, 128), 0) == jnp.broadcast_to(low, (128, 128)), 1.0, 0.0).astype(BF)
        return total + dot(left, right, NT)

    inverse_ref[...] = lax.fori_loop(
        0, points // 128, invert, jnp.zeros((64, 128), F32)
    ).astype(jnp.int32)

    node = iota((1, 128), 1)
    size = jnp.full((1, 128), count, jnp.int32)
    start = jnp.zeros((1, 128), jnp.int32)
    offset = 0
    for level in range(LEVELS):
        size = jnp.where(node >= offset, count >> level, size)
        start = jnp.where(node >= offset, offset, start)
        offset += count >> level
    entries = pad_lanes(lists_ref[...])
    for s in range(6):
        entry = entries[s : s + 1]
        place = entry - device * size + size
        side = jnp.where(place >= size, 1, 0) + jnp.where(place >= 2 * size, 1, 0)
        spot = side * 128 + start + place - side * size
        spot = (spot & ~3) | ((spot - s) & 3)
        used = (entry >= 0) & (node < offset)
        spots_ref[pl.ds(s, 1), :] = jnp.where(used, spot, 3 * 128)
    spots_ref[pl.ds(6, 2), :] = jnp.zeros((2, 128), jnp.int32)

    def relayout(a, carry):
        at = pl.multiple_of(a * rank, rank)
        one = [coupling_ref[s, pl.ds(at, rank), :].astype(F32) for s in range(6)]
        full = jnp.concatenate(one + [jnp.zeros_like(one[0])] * 2, axis=0)
        turned = pad_lanes(full).T
        rows32[pl.ds(a, 128, stride=rank), :] = turned[:, :128]
        wide[pl.ds(a, 128, stride=rank), :] = turned[:, 128:]
        return carry

    lax.fori_loop(0, rank, relayout, 0)

    def narrow(g, carry):
        at = pl.multiple_of(g * 128, 128)
        both = jnp.concatenate([rows32[pl.ds(at, 128), :], wide[pl.ds(at, 128), :]], axis=1)
        matrices_ref[g] = both.astype(BF)
        return carry

    lax.fori_loop(0, 32, narrow, 0)

    def place(c, carry):
        chunk = ordered_ref[:, pl.ds(pl.multiple_of(c * 128, 128), 128)]
        place_leaves(leaves, c * 2, chunk)
        return carry

    lax.fori_loop(0, count // 2, place, 0)
    edge = REACH // 4
    near_out[:, : edge * 256] = jnp.zeros((columns, edge * 256), F32)
    near_out[:, points - edge * 256 :] = jnp.zeros((columns, edge * 256), F32)

    def near(g, carry):
        blocks = blocks_ref[pl.ds(g * 4, 4)].reshape(256, 256)
        at = pl.multiple_of(g * 256, 256)
        near_out[:, pl.ds(at, 256)] = near_group(
            leaves, near_ref, blocks, g * 4, device * count, columns
        )
        return carry

    lax.fori_loop(edge, count // 4 - edge, near, 0)

    unit = jnp.where(iota((rank, 128), 1) == iota((rank, 128), 0) + 64, 1.0, 0.0).astype(BF)
    down = [None] * 32
    down[31] = dot(unit, weights_ref[15, 128:, :], NT).astype(BF)
    down[30] = dot(down[31], weights_ref[15, :128, :], NT).astype(BF)
    for k in reversed(range(15)):
        pair = dot(down[16 + k], weights_ref[k], NT).astype(BF)
        down[2 * k], down[2 * k + 1] = pair[:, :128], pair[:, 128:]
    for g in range(16):
        at_points = dot(down[g], masked_ref[g], NN)
        reach_ref[:, pl.ds(g * 256, 256)] = at_points.astype(BF)


def outer_kernel(
    ordered_ref, own_ref, before_ref, after_ref, near_in, blocks_ref, near_ref, matrices_ref,
    spots_ref, inverse_ref, weights_ref, masked_ref, reach_ref,
    partial_ref, reach_out,
    leaves, nodes, far, summed, edges, sems,
):
    columns, points = ordered_ref.shape
    halo = before_ref.shape[1] - 4096
    device = lax.axis_index("leaf")
    count = points // 64
    copies = [
        pltpu.make_async_copy(blocks_ref.at[pl.ds(at, REACH)], edges.at[i], sems.at[i])
        for i, at in enumerate((0, count - REACH))
    ]
    for copy in copies:
        copy.start()

    for c in range(halo // 128):
        place_leaves(leaves, c * 2, before_ref[:, pl.ds(c * 128, 128)])
        place_leaves(leaves, REACH + count + c * 2, after_ref[:, pl.ds(c * 128, 128)])

    def place(c, carry):
        chunk = ordered_ref[:, pl.ds(pl.multiple_of(c * 128, 128), 128)]
        place_leaves(leaves, REACH + c * 2, chunk)
        return carry

    lax.fori_loop(0, count // 2, place, 0)

    nodes[pl.ds(384, 4)] = jnp.zeros((4, columns, 128), BF)
    for side, ref in enumerate((before_ref, own_ref, after_ref)):

        def turn(g, carry, side=side, ref=ref):
            chunk = ref[:, pl.ds(pl.multiple_of(halo + g * 128, 128), 128)].astype(F32)
            for r in range(4):
                turned = chunk if r == 0 else pltpu.roll(chunk, 128 - 32 * r, 1)
                nodes[side * 128 + g * 4 + r] = turned.astype(BF)
            return carry

        lax.fori_loop(0, 32, turn, 0)

    lane_group = iota((columns, 128), 1) >> 5

    def couple(g, carry):
        picked = []
        for i in range(4):
            parts = [nodes[spots_ref[s, g * 4 + i]].astype(F32) for s in range(6)]
            front = parts[0]
            for s in range(1, 4):
                front = jnp.where(lane_group == s, parts[s], front)
            back = jnp.where(lane_group == 1, parts[5], parts[4])
            back = jnp.where(lane_group < 2, back, 0.0)
            picked.append(jnp.concatenate([front, back], axis=1))
        out = dot(jnp.concatenate(picked, axis=0).astype(BF), matrices_ref[g], NT)
        total = out[:columns]
        for i in range(1, 4):
            total = jnp.where(lane_group == i, out[i * columns : (i + 1) * columns], total)
        far[:, pl.ds(pl.multiple_of(g * 128, 128), 128)] = total
        return carry

    lax.fori_loop(0, 32, couple, 0)

    for copy in copies:
        copy.wait()
    down = [None] * 32
    down[31] = far[:, pl.ds(31 * 128, 128)].astype(BF)
    down[30] = (far[:, pl.ds(30 * 128, 128)] + dot(down[31], weights_ref[15, :128, :], NT)).astype(BF)
    for k in reversed(range(15)):
        pair = far[:, pl.ds(k * 256, 256)] + dot(down[16 + k], weights_ref[k], NT)
        pair = pair.astype(BF)
        down[2 * k], down[2 * k + 1] = pair[:, :128], pair[:, 128:]
    groups = count // 4
    for g in range(groups):
        total = dot(down[g], masked_ref[g], NN)
        if g < REACH // 4 or g >= groups - REACH // 4:
            if g < REACH // 4:
                blocks = edges[0, pl.ds(g * 4, 4)].reshape(256, 256)
            else:
                blocks = edges[1, pl.ds((g - groups) * 4 + REACH, 4)].reshape(256, 256)
            total = total + near_group(leaves, near_ref, blocks, g * 4, device * count - REACH, columns)
        else:
            total = total + near_in[:, pl.ds(g * 256, 256)]
        summed[:columns, pl.ds(g * 256, 256)] = total
        summed[columns:, pl.ds(g * 256, 256)] = reach_ref[:, pl.ds(g * 256, 256)].astype(F32)

    def restore(j, carry):
        high = inverse_ref[pl.ds(j, 1), :]
        low = inverse_ref[pl.ds(j + 32, 1), :]
        picked = gather_lanes(summed, low, high)
        at = pl.ds(pl.multiple_of(j * 128, 128), 128)
        partial_ref[:, at] = picked[:columns]
        reach_out[:, at] = picked[columns:].astype(BF)
        return carry

    lax.fori_loop(0, points // 128, restore, 0)


def top_kernel(
    gathered_ref, transfer_ref, coupling_ref, lists_ref, partial_ref, reach_ref, out_ref, coeffs,
):
    node_count = gathered_ref.shape[0]
    columns = gathered_ref.shape[1]
    device = lax.axis_index("leaf")
    total = 2 * node_count - 1
    for q in range(node_count):
        coeffs[q ^ device] = gathered_ref[q][:, 64:96].astype(F32)
    start, count = 0, node_count
    while count > 1:
        for j in range(count // 2):
            lifted = dot(coeffs[start + 2 * j].astype(BF), transfer_ref[start + 2 * j], NN)
            lifted += dot(coeffs[start + 2 * j + 1].astype(BF), transfer_ref[start + 2 * j + 1], NN)
            coeffs[start + count + j] = lifted.astype(BF).astype(F32)
        start, count = start + count, count // 2
    coeffs[total] = jnp.zeros((columns, 32), F32)
    starts, start, count = [], 0, node_count
    while count >= 1:
        starts.append((start, count))
        start, count = start + count, count // 2
    down = None
    for level, (start, count) in reversed(list(enumerate(starts))):
        node = start + (device >> level)
        field = None
        for s in range(6):
            entry = lists_ref[s, node]
            spot = jnp.where(entry >= 0, start + entry, total)
            term = dot(coeffs[spot].astype(BF), coupling_ref[s, node], NT)
            field = term if field is None else field + term
        if down is not None:
            field = field + dot(down, transfer_ref[node], NT)
        down = field.astype(BF)

    points = out_ref.shape[1]
    for c in range(points // 512):
        at = pl.ds(c * 512, 512)
        out_ref[:, at] = partial_ref[:, at] + dot(down, reach_ref[:, at], NN)


VMEM = pl.BlockSpec(memory_space=pltpu.VMEM)
SMEM = pl.BlockSpec(memory_space=pltpu.SMEM)


def call(kernel, outs, scratch, specs, flops, name, args, out_specs=None):
    size = sum(a.size * a.dtype.itemsize for a in args)
    return pl.pallas_call(
        kernel,
        out_shape=[jax.ShapeDtypeStruct(s, t) for s, t in outs],
        in_specs=specs,
        out_specs=[VMEM] * len(outs) if out_specs is None else out_specs,
        scratch_shapes=scratch,
        compiler_params=pltpu.CompilerParams(vmem_limit_bytes=36 * 2**20),
        cost_estimate=pl.CostEstimate(flops=flops, bytes_accessed=size, transcendentals=0),
        name=name,
    )(*args)


def local(
    vectors, tree_order, leaf_basis, near_blocks, near_lists, transfers, couplings, coupling_lists,
    top_transfers, top_couplings, top_lists,
):
    columns, points = vectors.shape
    rank = leaf_basis.shape[0]
    devices = lax.axis_size("leaf")
    halo = REACH * near_blocks.shape[1]
    packed = halo + 128 * rank
    order = tree_order.reshape(points // 128, 128)
    near_t = jnp.transpose(near_lists)
    lists_t = jnp.transpose(coupling_lists)
    moves = transfers.reshape(rank * rank, -1)
    matrices = couplings.reshape(6, rank * rank, -1)

    ordered, to_left, to_right, top, weights, masked = call(
        up_kernel,
        [
            ((columns, points), BF), ((columns, packed), BF), ((columns, packed), BF),
            ((1, columns, 128), BF), ((16, 256, 128), BF), ((16, 128, 256), BF),
        ],
        [pltpu.VMEM((columns, points), F32), pltpu.VMEM((128 * rank, 128), F32)],
        [VMEM] * 4, 10**9, "up", (vectors, order, leaf_basis, moves),
    )
    reached = 1
    gathered = top
    while reached < devices:
        swap = [(i, i ^ reached) for i in range(devices)]
        gathered = jnp.concatenate([gathered, lax.ppermute(gathered, "leaf", swap)], axis=0)
        reached *= 2
    upward = [(i, i + 1) for i in range(devices - 1)]
    before = lax.ppermute(to_right, "leaf", upward)
    after = lax.ppermute(to_left, "leaf", [(j, i) for i, j in upward])

    near_part, coupling_rows, spots, inverse, reach = call(
        inner_kernel,
        [
            ((columns, points), F32), ((32, 128, 256), BF), ((8, 128), jnp.int32),
            ((64, 128), jnp.int32), ((rank, points), BF),
        ],
        [
            pltpu.VMEM((points // 64, columns, 128), BF), pltpu.VMEM((128 * rank, 128), F32),
            pltpu.VMEM((128 * rank, 128), F32),
        ],
        [VMEM, VMEM, SMEM, VMEM, VMEM, VMEM, VMEM, VMEM], 6 * 10**9, "inner",
        (ordered, near_blocks, near_t, order, matrices, lists_t, weights, masked),
    )
    partial, reach_back = call(
        outer_kernel,
        [((columns, points), F32), ((rank, points), BF)],
        [
            pltpu.VMEM((points // 64 + 2 * REACH, columns, 128), BF),
            pltpu.VMEM((388, columns, 128), BF), pltpu.VMEM((columns, 4096), F32),
            pltpu.VMEM((columns + rank, points), F32),
            pltpu.VMEM((2, REACH) + near_blocks.shape[1:], BF), pltpu.SemaphoreType.DMA((2,)),
        ],
        [
            VMEM, VMEM, VMEM, VMEM, VMEM,
            pl.BlockSpec(memory_space=pl.ANY), SMEM, VMEM, SMEM, VMEM, VMEM, VMEM, VMEM,
        ], 4 * 10**9, "outer",
        (
            ordered, to_left, before, after, near_part, near_blocks, near_t, coupling_rows,
            spots, inverse, weights, masked, reach,
        ),
    )
    (applied,) = call(
        top_kernel,
        [((columns, points), F32)],
        [pltpu.VMEM((2 * devices, columns, 32), F32)],
        [VMEM, VMEM, VMEM, SMEM, VMEM, VMEM], 10**9, "top",
        (
            gathered, jnp.transpose(top_transfers, (2, 0, 1)), jnp.transpose(top_couplings, (0, 3, 1, 2)),
            jnp.transpose(top_lists), partial, reach_back,
        ),
    )
    return applied


def solution(mesh):
    placed = (
        P("rhs", ("groups", "leaf")),
        P(("groups", "leaf")),
        P(None, ("groups", "leaf")),
        P(("groups", "leaf"), None, None),
        P(("groups", "leaf"), None),
        P(None, None, ("groups", "leaf")),
        P(None, None, None, ("groups", "leaf")),
        P(("groups", "leaf"), None),
        P(None, None, "groups"),
        P(None, None, None, "groups"),
        P("groups", None),
    )
    return jax.shard_map(
        local, mesh=mesh, in_specs=placed, out_specs=P("rhs", ("groups", "leaf")), check_vma=False
    )
```

time: 269 us -> 76.9 us (0.29)
  local copies, waits for them, and re-layouts: 125 us -> 3.83 us
  Pallas kernels: 0 us -> 57.4 us
  matrix products: 34.6 us -> 0 us
  blocking collectives: 32.9 us -> 0 us
  starting transfers between devices: 44.8 us -> 13.5 us
  other arithmetic: 27.1 us -> 0.02 us
    pallas_call x0 -> x4, Pallas kernels: none -> 57.4 us  [call(): pl.pallas_call(kernel, out_shape=[jax.ShapeDtypeStruct(s, t) for s, t in...]
    gather x17 -> x0, local copies, waits for them, and re-layouts: 46.2 us -> none  [the longest x12 20.2 us: couple_nodes(): picked = jnp.take(extended, flat_ids, axis=2)]
    dot_general x30 -> x0, matrix products: 34.6 us -> none  [the longest x10 13.6 us: couple_nodes(): jnp.einsum('sabi,hbsi->hai', matrices, picked, preferred_element_type=jnp...]
    all_gather x1 -> x0, blocking collectives: 32.9 us -> none  [local(): top_coeffs = lax.all_gather(coeffs, 'leaf', axis=2, tiled=True)]
    ppermute x14 -> x5, starting transfers between devices: 44.8 us -> 13.5 us  [the longest x3 7.7 us: local(): lax.ppermute(gathered, 'leaf', swap)]
    unnamed x83 -> x24, local copies, waits for them, and re-layouts: 28.3 us -> 3.83 us
    scatter x2 -> x0, local copies, waits for them, and re-layouts: 15.3 us -> none  [local(): jnp.zeros((columns, points_here), jnp.float32).at[:, local_order]]
    slice x11 -> x0, local copies, waits for them, and re-layouts: 14.2 us -> none  [the longest x5 9.89 us: local(): couplings[:, :, :, start:start + count]]
  transfers between devices with their start and end apart: 14 -> 5, of which waited for: 1 -> 1; matrix products, arithmetic and copies ran while one was open for 46% -> 0% of each run, Pallas kernels for 0% -> 24%
where the time goes in v1:
time: 76.9 us; the launch traced here: 76.6 us
  Pallas kernels  57.4 us (75%)
  starting transfers between devices  13.5 us (18%)
  local copies, waits for them, and re-layouts  3.83 us (5%)
  waiting for transfers between devices  1.64 us (2%)
    pallas_call x4, Pallas kernels, call(): pl.pallas_call(kernel, out_shape=[jax.ShapeDtypeStruct(s, t) for s, t in...  57.4 us
    ppermute x3, starting transfers between devices, local(): lax.ppermute(gathered, 'leaf', swap)  7.7 us
    ppermute x1, starting transfers between devices, local(): before = lax.ppermute(to_right, 'leaf', upward)  4.56 us
    unnamed x24, local copies, waits for them, and re-layouts  3.83 us
    ppermute x3, waiting for transfers between devices, local(): lax.ppermute(gathered, 'leaf', swap)  1.63 us
  transfers between devices with their start and end apart: 5, of which 1 were waited for; matrix products, arithmetic and copies ran while one was open for 0% of the time, Pallas kernels for 24%

profile of v1, /device:TPU:0, one launch (start us, length us, event | category | flops | bytes accessed | tf_op | source)
XLA Modules:
  0.0 76.6 jit_solution(1401135592627630113)
XLA Ops:
  0.0 0.0 copy-start.1
  0.0 0.0 copy-start
  0.0 0.0 copy-start.3
  0.0 1.1 %copy-done.3 = bf16[32,4096]{1,0:T(8,128)(2,1)S(1)} copy-done((bf16[32,4096]{1,0:T(8,128)(2,1)S(1)}, bf16[32,4096]{1,0:T(8,128)(2,1)}, u32[]{:S(2)}) %copy-start.3) | copy-done | bytes 262168
  1.1 0.0 copy-start.4
  1.1 1.0 %copy-done.4 = bf16[32,4096]{1,0:T(8,128)(2,1)S(1)} copy-done((bf16[32,4096]{1,0:T(8,128)(2,1)S(1)}, bf16[32,4096]{1,0:T(8,128)(2,1)}, u32[]{:S(2)}) %copy-start.4) | copy-done | bytes 262168
  2.1 0.0 copy-start.5
  2.1 0.9 %copy-done.5 = bf16[32,32,126]{2,1,0:T(8,128)(2,1)S(1)} copy-done((bf16[32,32,126]{2,1,0:T(8,128)(2,1)S(1)}, bf16[32,32,126]{2,1,0:T(8,128)(2,1)}, u32[]{:S(2)}) %copy-start.5) | copy-done | bytes 258072
  3.1 0.0 copy-start.7
  3.1 0.7 copy-done.7
  3.8 0.0 copy-start.8
  3.8 0.0 copy-start.9
  3.8 0.0 copy-start.11
  3.8 10.3 %up.1 = (bf16[32,4096]{1,0:T(8,128)(2,1)S(1)}, bf16[32,4608]{1,0:T(8,128)(2,1)S(1)}, bf16[32,4608]{1,0:T(8,128)(2,1)S(1)}, bf16[1,32,128]{2,1,0:T(8,128)(2,1)S(1...) custom-call(bf16[32,4096]{1,0:T(8,128)(2,1)S(1)} %copy-done.3, s32[32,128]{1,0:T(8,128)S(1)} %bitcast.12, ...), custom_call_target="tpu_custom_call" | custom-call | flops 1000000000 | bytes 798720 | tf_op jit(solution)/shard_map/up/pallas_call | solution.py:353
  14.2 3.0 %collective-permute-start = (bf16[1,32,128]{2,1,0:T(8,128)(2,1)S(1)}, bf16[1,32,128]{2,1,0:T(8,128)(2,1)S(1)}, u32[]{:S(2)}, u32[]{:S(2)}) collective-permute-start(bf16[1,32,128]{2,1,0:T(8,128)(2,1)S(1)} %get-tuple-element.18), channel_id=1, source_target_pairs={{0,2},{2,0},{4,6},{6,4},{8,10},{10,8},{12,14},{14,12},{1,3},{3,1},... | collective-permute-start | bytes 24584 | tf_op jit(solution)/shard_map/ppermute | solution.py:393
  17.1 1.6 %collective-permute-done = bf16[1,32,128]{2,1,0:T(8,128)(2,1)S(1)} collective-permute-done((bf16[1,32,128]{2,1,0:T(8,128)(2,1)S(1)}, bf16[1,32,128]{2,1,0:T(8,128)(2,1)S(1)}, u32[]{:S(2)}, u32[]{:S(2)}) %collective-permute-start) | collective-permute-done | bytes 8224 | tf_op jit(solution)/shard_map/ppermute | solution.py:393
  18.8 2.1 %collective-permute-start.1 = (bf16[2,32,128]{2,1,0:T(8,128)(2,1)S(1)}, bf16[2,32,128]{2,1,0:T(8,128)(2,1)S(1)}, u32[]{:S(2)}, u32[]{:S(2)}) collective-permute-start(bf16[2,32,128]{2,1,0:T(8,128)(2,1)S(1)} %pad_maximum_fusion.2), channel_id=1, source_target_pairs={{0,4},{2,6},{4,0},{6,2},{8,12},{10,14},{12,8},{14,10},{1,5},{3,7},... | collective-permute-start | bytes 49160 | tf_op jit(solution)/shard_map/ppermute | solution.py:393
  20.8 1.3 %collective-permute-start.4 = (bf16[32,4608]{1,0:T(8,128)(2,1)S(1)}, bf16[32,4608]{1,0:T(8,128)(2,1)S(1)}, u32[]{:S(2)}, u32[]{:S(2)}) collective-permute-start(bf16[32,4608]{1,0:T(8,128)(2,1)S(1)} %get-tuple-element.20.own_ref), channel_id=1, source_target_pairs={{2,0},{4,2},{6,4},{8,6},{10,8},{12,10},{14,12},{3,1},{5,3},{7,5},{... | collective-permute-start | bytes 884744 | tf_op jit(solution)/shard_map/ppermute | solution.py:397
  22.1 4.6 %collective-permute-start.3 = (bf16[32,4608]{1,0:T(8,128)(2,1)S(1)}, bf16[32,4608]{1,0:T(8,128)(2,1)S(1)}, u32[]{:S(2)}, u32[]{:S(2)}) collective-permute-start(bf16[32,4608]{1,0:T(8,128)(2,1)S(1)} %get-tuple-element.21), channel_id=1, source_target_pairs={{0,2},{2,4},{4,6},{6,8},{8,10},{10,12},{12,14},{1,3},{3,5},{5,7},{... | collective-permute-start | bytes 884744 | tf_op jit(solution)/shard_map/ppermute | solution.py:396
  26.7 0.0 collective-permute-done.1
  26.7 2.6 %collective-permute-start.2 = (bf16[4,32,128]{2,1,0:T(8,128)(2,1)S(1)}, bf16[4,32,128]{2,1,0:T(8,128)(2,1)S(1)}, u32[]{:S(2)}, u32[]{:S(2)}) collective-permute-start(bf16[4,32,128]{2,1,0:T(8,128)(2,1)S(1)} %pad_maximum_fusion.1), channel_id=1, source_target_pairs={{0,8},{2,10},{4,12},{6,14},{8,0},{10,2},{12,4},{14,6},{1,9},{3,11}... | collective-permute-start | bytes 98312 | tf_op jit(solution)/shard_map/ppermute | solution.py:393
  29.4 0.0 copy-done.1
  29.4 0.0 copy-done
  29.4 0.0 copy-done.8
  29.4 0.0 copy-done.9
  29.4 0.0 copy-done.11
  29.4 18.4 %inner.1 = (f32[32,4096]{1,0:T(8,128)S(1)}, bf16[32,128,256]{2,1,0:T(8,128)(2,1)S(1)}, s32[8,128]{1,0:T(8,128)S(1)}, s32[64,128]{1,0:T(8,128)S(1)}, bf16[32,4096]{1,0:T(8,128)(2,1)S(1)}) custom-call(bf16[32,4096]{1,0:T(8,128)(2,1)S(1)} %get-tuple-element.19.ordered_ref, bf16[64,64,256]{2,1,0:T(8,128)(2,1)S(1)} %copy-done, s32[4,64]{1,0:T(4,128)S(1)} %bitcast.16, ...), custom_call_target="tpu_custom_call" | custom-call | flops 6000000000 | bytes 6025168 | tf_op jit(solution)/shard_map/inner/pallas_call | solution.py:353
  47.8 0.0 collective-permute-done.2
  47.9 0.0 collective-permute-done.4.after_ref
  47.9 0.0 collective-permute-done.3.before_ref
  47.9 0.0 copy-start.2
  47.9 0.0 copy-start.6
  47.9 0.0 copy-start.10
  47.9 26.0 %outer.1 = (f32[32,4096]{1,0:T(8,128)S(1)}, bf16[32,4096]{1,0:T(8,128)(2,1)S(1)}) custom-call(bf16[32,4096]{1,0:T(8,128)(2,1)S(1)} %get-tuple-element.19.ordered_ref, bf16[32,4608]{1,0:T(8,128)(2,1)S(1)} %get-tuple-element.20.own_ref, bf16[32,4608]{1,0:T(8,128)(2,1)S(1)} %collective-permute-done.3.before_ref, ...), custom_call_target="tpu_custom_call" | custom-call | flops 4000000000 | bytes 8262656 | tf_op jit(solution)/shard_map/outer/pallas_call | solution.py:353
  74.0 0.0 copy-done.2
  74.0 0.0 copy-done.6
  74.0 0.0 copy-done.10
  74.0 2.6 %top.1 = f32[32,4096]{1,0:T(8,128)} custom-call(bf16[8,32,128]{2,1,0:T(8,128)(2,1)S(1)} %pad_maximum_fusion.gathered_ref, bf16[14,32,32]{2,1,0:T(8,128)(2,1)S(1)} %bitcast.11, bf16[6,15,32,32]{3,2,1,0:T(8,128)(2,1)S(1)} %bitcast.9, s32[6,15]{1,0:T(8,128)S(1)} %bitcast.15, f32[32,4096]{1,0:T(8,128)S(1)} %get-tuple-element.29.partial_ref, ...), custom_call_target="tpu_custom_call" | custom-call | flops 1000000000 | bytes 1065320 | tf_op jit(solution)/shard_map/top/pallas_call | solution.py:353
  (3 shorter events, 0.0 us)
Async XLA Ops:
  0.0 29.4 %copy-start.1 = (bf16[6,32,32,126]{3,2,1,0:T(8,128)(2,1)S(1)}, bf16[6,32,32,126]{3,2,1,0:T(8,128)(2,1)}, u32[]{:S(2)}) copy-start(bf16[6,32,32,126]{3,2,1,0:T(8,128)(2,1)} %param.17) | copy-start | bytes 4644868
  0.0 29.4 %copy-start = (bf16[64,64,256]{2,1,0:T(8,128)(2,1)S(1)}, bf16[64,64,256]{2,1,0:T(8,128)(2,1)}, u32[]{:S(2)}) copy-start(bf16[64,64,256]{2,1,0:T(8,128)(2,1)} %blocks_ref.3) | copy-start | bytes 6291460
  0.0 1.1 %copy-start.3 = (bf16[32,4096]{1,0:T(8,128)(2,1)S(1)}, bf16[32,4096]{1,0:T(8,128)(2,1)}, u32[]{:S(2)}) copy-start(bf16[32,4096]{1,0:T(8,128)(2,1)} %vec_ref.1) | copy-start | bytes 786436
  1.1 1.0 %copy-start.4 = (bf16[32,4096]{1,0:T(8,128)(2,1)S(1)}, bf16[32,4096]{1,0:T(8,128)(2,1)}, u32[]{:S(2)}) copy-start(bf16[32,4096]{1,0:T(8,128)(2,1)} %basis_ref.1) | copy-start | bytes 786436
  2.1 0.9 %copy-start.5 = (bf16[32,32,126]{2,1,0:T(8,128)(2,1)S(1)}, bf16[32,32,126]{2,1,0:T(8,128)(2,1)}, u32[]{:S(2)}) copy-start(bf16[32,32,126]{2,1,0:T(8,128)(2,1)} %param.16) | copy-start | bytes 774148
  3.1 0.7 copy-start.7
  3.8 25.6 %copy-start.8 = (s32[4096]{0:T(1024)S(1)}, s32[4096]{0:T(1024)}, u32[]{:S(2)}) copy-start(s32[4096]{0:T(1024)} %param.12) | copy-start | bytes 49156
  3.8 25.6 %copy-start.9 = (s32[126,6]{0,1:T(8,128)S(1)}, s32[126,6]{0,1:T(8,128)}, u32[]{:S(2)}) copy-start(s32[126,6]{0,1:T(8,128)} %param.18) | copy-start | bytes 9076
  3.8 25.6 %copy-start.11 = (s32[64,4]{0,1:T(4,128)S(1)}, s32[64,4]{0,1:T(4,128)}, u32[]{:S(2)}) copy-start(s32[64,4]{0,1:T(4,128)} %param.15) | copy-start | bytes 3076
  14.2 4.6 %collective-permute-start = (bf16[1,32,128]{2,1,0:T(8,128)(2,1)S(1)}, bf16[1,32,128]{2,1,0:T(8,128)(2,1)S(1)}, u32[]{:S(2)}, u32[]{:S(2)}) collective-permute-start(bf16[1,32,128]{2,1,0:T(8,128)(2,1)S(1)} %get-tuple-element.18), channel_id=1, source_target_pairs={{0,2},{2,0},{4,6},{6,4},{8,10},{10,8},{12,14},{14,12},{1,3},{3,1},... | collective-permute-start | bytes 24584 | tf_op jit(solution)/shard_map/ppermute | solution.py:393
  18.8 7.9 %collective-permute-start.1 = (bf16[2,32,128]{2,1,0:T(8,128)(2,1)S(1)}, bf16[2,32,128]{2,1,0:T(8,128)(2,1)S(1)}, u32[]{:S(2)}, u32[]{:S(2)}) collective-permute-start(bf16[2,32,128]{2,1,0:T(8,128)(2,1)S(1)} %pad_maximum_fusion.2), channel_id=1, source_target_pairs={{0,4},{2,6},{4,0},{6,2},{8,12},{10,14},{12,8},{14,10},{1,5},{3,7},... | collective-permute-start | bytes 49160 | tf_op jit(solution)/shard_map/ppermute | solution.py:393
  20.8 27.0 %collective-permute-start.4 = (bf16[32,4608]{1,0:T(8,128)(2,1)S(1)}, bf16[32,4608]{1,0:T(8,128)(2,1)S(1)}, u32[]{:S(2)}, u32[]{:S(2)}) collective-permute-start(bf16[32,4608]{1,0:T(8,128)(2,1)S(1)} %get-tuple-element.20.own_ref), channel_id=1, source_target_pairs={{2,0},{4,2},{6,4},{8,6},{10,8},{12,10},{14,12},{3,1},{5,3},{7,5},{... | collective-permute-start | bytes 884744 | tf_op jit(solution)/shard_map/ppermute | solution.py:397
  22.1 25.7 %collective-permute-start.3 = (bf16[32,4608]{1,0:T(8,128)(2,1)S(1)}, bf16[32,4608]{1,0:T(8,128)(2,1)S(1)}, u32[]{:S(2)}, u32[]{:S(2)}) collective-permute-start(bf16[32,4608]{1,0:T(8,128)(2,1)S(1)} %get-tuple-element.21), channel_id=1, source_target_pairs={{0,2},{2,4},{4,6},{6,8},{8,10},{10,12},{12,14},{1,3},{3,5},{5,7},{... | collective-permute-start | bytes 884744 | tf_op jit(solution)/shard_map/ppermute | solution.py:396
  26.7 21.1 %collective-permute-start.2 = (bf16[4,32,128]{2,1,0:T(8,128)(2,1)S(1)}, bf16[4,32,128]{2,1,0:T(8,128)(2,1)S(1)}, u32[]{:S(2)}, u32[]{:S(2)}) collective-permute-start(bf16[4,32,128]{2,1,0:T(8,128)(2,1)S(1)} %pad_maximum_fusion.1), channel_id=1, source_target_pairs={{0,8},{2,10},{4,12},{6,14},{8,0},{10,2},{12,4},{14,6},{1,9},{3,11}... | collective-permute-start | bytes 98312 | tf_op jit(solution)/shard_map/ppermute | solution.py:393
  47.9 26.1 %copy-start.2 = (bf16[6,32,32,15]{2,1,3,0:T(8,128)(2,1)S(1)}, bf16[6,32,32,15]{2,1,3,0:T(8,128)(2,1)}, u32[]{:S(2)}) copy-start(bf16[6,32,32,15]{2,1,3,0:T(8,128)(2,1)} %param.20) | copy-start | bytes 552964
  47.9 26.1 %copy-start.6 = (bf16[32,32,14]{1,0,2:T(8,128)(2,1)S(1)}, bf16[32,32,14]{1,0,2:T(8,128)(2,1)}, u32[]{:S(2)}) copy-start(bf16[32,32,14]{1,0,2:T(8,128)(2,1)} %param.19) | copy-start | bytes 86020
  47.9 26.1 %copy-start.10 = (s32[15,6]{0,1:T(8,128)S(1)}, s32[15,6]{0,1:T(8,128)}, u32[]{:S(2)}) copy-start(s32[15,6]{0,1:T(8,128)} %param.21) | copy-start | bytes 1084

commit v2 on v1

v2 whole, which is shorter than its diff:
```python
import functools

import jax
import jax.numpy as jnp
from jax import lax
from jax.experimental import pallas as pl
from jax.experimental.pallas import tpu as pltpu
from jax.sharding import PartitionSpec as P

LEVELS = 6
REACH = 8
BF = jnp.bfloat16
F32 = jnp.float32
NT = (((1,), (1,)), ((), ()))
NN = (((1,), (0,)), ((), ()))


def iota(shape, axis):
    return lax.broadcasted_iota(jnp.int32, shape, axis)


def dot(a, b, dims):
    return lax.dot_general(a, b, dims, preferred_element_type=F32)


def pad_lanes(x):
    short = 128 - x.shape[1]
    return jnp.concatenate([x, jnp.zeros((x.shape[0], short), x.dtype)], axis=1)


def one_hot(ids):
    return jnp.where(iota((256, 256), 0) == jnp.broadcast_to(ids, (256, 256)), 1.0, 0.0).astype(BF)


def pick(stacked, hot, high, rows):
    out = dot(stacked, hot, NN)
    high = jnp.broadcast_to(high, (rows, 256))
    total = out[:rows]
    for block in range(1, stacked.shape[0] // rows):
        total = jnp.where(high == block, out[block * rows : (block + 1) * rows], total)
    return total


def up_kernel(
    vec_hbm, order_hbm, basis_hbm, transfer_hbm,
    ordered_ref, left_ref, right_ref, top_ref, weights_ref, masked_ref, inverse_ref,
    vec_ref, order_ref, basis_ref, transfer_ref, stacked, rows32, sems,
):
    columns, points = vec_ref.shape
    rank = basis_ref.shape[0]
    chunks = points // 256
    halo = left_ref.shape[1] - 4096
    pairs = (
        (transfer_hbm, transfer_ref), (order_hbm, order_ref), (vec_hbm, vec_ref), (basis_hbm, basis_ref),
    )
    copies = [pltpu.make_async_copy(src, dst, sems.at[i]) for i, (src, dst) in enumerate(pairs)]
    for copy in copies:
        copy.start()

    copies[0].wait()
    lane, row = iota((128, 256), 1), iota((128, 256), 0)
    family = (lane & 7) == ((row >> 1) & 7)
    spread = [
        jnp.where(iota((128, 256), 0) == (iota((128, 256), 1) >> 3) + 32 * q, 1.0, 0.0).astype(BF)
        for q in range(4)
    ]
    for m in range(rank // 4):
        turned = pad_lanes(transfer_ref[pl.ds(m * 4 * rank, 4 * rank), :].astype(F32)).T.astype(BF)
        for q in range(4):
            rows32[m * 4 + q] = jnp.where(family, dot(turned, spread[q], NN), 0.0)
    for k in range(16):
        weights_ref[k] = rows32[:, k * 8 : k * 8 + 8, :].reshape(256, 256).astype(BF)

    copies[1].wait()
    copies[2].wait()
    for block in range(chunks):
        stacked[block * columns : (block + 1) * columns, :] = vec_ref[:, block * 256 : (block + 1) * 256]
    within = iota((16, 256), 1).astype(F32)
    inverse = jnp.zeros((32, 256), F32)
    for c in range(chunks):
        ids = jnp.concatenate([order_ref[2 * c : 2 * c + 1, :], order_ref[2 * c + 1 : 2 * c + 2, :]], axis=1)
        ids = lax.rem(ids, points)
        high, low = ids >> 8, ids & 255
        hot = one_hot(low)
        ordered_ref[:, c * 256 : (c + 1) * 256] = pick(stacked[...], hot, high, columns).astype(BF)
        hit = iota((16, 256), 0) == jnp.broadcast_to(high, (16, 256))
        marks = jnp.concatenate([jnp.where(hit, float(c), 0.0), jnp.where(hit, within, 0.0)], axis=0)
        inverse = inverse + dot(marks.astype(BF), hot, NT)
    inverse_ref[...] = inverse.astype(jnp.int32)

    copies[3].wait()
    mine = (iota((256, 512), 0) & 7) == (iota((256, 512), 1) >> 6)
    coeffs = [None] * 16
    for g in range(points // 512):
        one = basis_ref[:, g * 512 : (g + 1) * 512].astype(F32)
        eight = jnp.broadcast_to(one[:, None, :], (rank, 8, 512)).reshape(256, 512)
        masked = jnp.where(mine, eight, 0.0).astype(BF)
        masked_ref[g] = masked
        coeffs[g] = dot(ordered_ref[:, g * 512 : (g + 1) * 512], masked, NT).astype(BF)
    for n in range(7):
        lifted = dot(coeffs[2 * n], weights_ref[2 * n], NN) + dot(coeffs[2 * n + 1], weights_ref[2 * n + 1], NN)
        coeffs[8 + n] = lifted.astype(BF)
    four = dot(coeffs[14], weights_ref[14], NN)
    five = dot(four.astype(BF), weights_ref[15], NN)
    six = dot((four + five).astype(BF), weights_ref[15], NN)
    coeffs[15] = (four + six).astype(BF)
    root = jnp.where(iota((256, 128), 0) == iota((256, 128), 1) * 8 + 6, 1.0, 0.0).astype(BF)
    top_ref[0] = dot(coeffs[15], root, NN).astype(BF)
    for g in range(16):
        left_ref[:, halo + g * 256 : halo + (g + 1) * 256] = coeffs[g]
        right_ref[:, halo + g * 256 : halo + (g + 1) * 256] = coeffs[g]
    left_ref[:, :halo] = ordered_ref[:, :halo]
    right_ref[:, :halo] = ordered_ref[:, points - halo :]


def near_group(leaves_ref, lists_ref, blocks, first, base, columns):
    lane_left = iota((columns, 128), 1) < 64
    picked = []
    for i in range(4):
        spots = [lists_ref[s, first + i] - base for s in range(4)]
        halves = []
        for s in (0, 2):
            even = leaves_ref[spots[s]]
            odd = leaves_ref[spots[s + 1] ^ 1]
            halves.append(jnp.where(lane_left, even, odd))
        picked.append(jnp.concatenate(halves, axis=1))
    moving = jnp.concatenate(picked, axis=0).astype(BF)
    out = dot(moving, blocks, NT)
    leaf_of_lane = iota((columns, 256), 1) >> 6
    total = out[:columns]
    for i in range(1, 4):
        total = jnp.where(leaf_of_lane == i, out[i * columns : (i + 1) * columns], total)
    return total


def place_leaves(leaves_ref, first, chunk):
    chunk = chunk.astype(F32)
    leaves_ref[first] = chunk
    leaves_ref[first + 1] = pltpu.roll(chunk, 64, 1)


def inner_kernel(
    ordered_ref, blocks_ref, near_ref, coupling_ref, lists_ref, weights_ref, masked_ref, inverse_ref,
    near_out, matrices_ref, spots_ref, hot_ref, reach_ref,
    leaves, rows32, stacked,
):
    columns, points = ordered_ref.shape
    rank = 32
    count = blocks_ref.shape[0]
    device = lax.axis_index("leaf")

    node = iota((1, 128), 1)
    size = jnp.full((1, 128), count, jnp.int32)
    start = jnp.zeros((1, 128), jnp.int32)
    offset = 0
    for level in range(LEVELS):
        size = jnp.where(node >= offset, count >> level, size)
        start = jnp.where(node >= offset, offset, start)
        offset += count >> level
    entries = pad_lanes(lists_ref[...])
    for s in range(6):
        entry = entries[s : s + 1]
        place = entry - device * size + size
        side = jnp.where(place >= size, 1, 0) + jnp.where(place >= 2 * size, 1, 0)
        spot = side * 128 + start + place - side * size
        used = (entry >= 0) & (node < offset)
        spots_ref[pl.ds(s, 1), :] = jnp.where(used, spot, 3 * 128)
    spots_ref[pl.ds(6, 2), :] = jnp.zeros((2, 128), jnp.int32)

    def relayout(a, carry):
        at = pl.multiple_of(a * rank, rank)
        one = [coupling_ref[s, pl.ds(at, rank), :].astype(F32) for s in range(6)]
        full = jnp.concatenate(one + [jnp.zeros_like(one[0])] * 2, axis=0)
        rows32[a] = pad_lanes(full).T
        return carry

    lax.fori_loop(0, rank, relayout, 0)

    def narrow(g, carry):
        at = pl.multiple_of(g * 8, 8)
        matrices_ref[g] = rows32[:, pl.ds(at, 8), :].reshape(256, 256).astype(BF)
        return carry

    lax.fori_loop(0, 16, narrow, 0)

    def place(c, carry):
        chunk = ordered_ref[:, pl.ds(pl.multiple_of(c * 128, 128), 128)]
        place_leaves(leaves, c * 2, chunk)
        return carry

    lax.fori_loop(0, count // 2, place, 0)
    edge = REACH // 4
    near_out[:, : edge * 256] = jnp.zeros((columns, edge * 256), F32)
    near_out[:, points - edge * 256 :] = jnp.zeros((columns, edge * 256), F32)

    def near(g, carry):
        blocks = blocks_ref[pl.ds(g * 4, 4)].reshape(256, 256)
        at = pl.multiple_of(g * 256, 256)
        near_out[:, pl.ds(at, 256)] = near_group(
            leaves, near_ref, blocks, g * 4, device * count, columns
        )
        return carry

    lax.fori_loop(edge, count // 4 - edge, near, 0)

    unit = jnp.where(iota((rank, 256), 1) == iota((rank, 256), 0) * 8 + 6, 1.0, 0.0)
    five = dot(unit.astype(BF), weights_ref[15], NT)
    down = [None] * 16
    down[15] = dot((unit + five).astype(BF), weights_ref[15], NT).astype(BF)
    for k in reversed(range(15)):
        down[k] = dot(down[8 + k // 2], weights_ref[k], NT).astype(BF)
    for g in range(points // 512):
        at_points = dot(down[g], masked_ref[g], NN).astype(BF)
        stacked[2 * g * rank : (2 * g + 1) * rank, :] = at_points[:, :256]
        stacked[(2 * g + 1) * rank : (2 * g + 2) * rank, :] = at_points[:, 256:]
    for c in range(points // 256):
        hot = one_hot(inverse_ref[16 + c : 17 + c, :])
        hot_ref[c] = hot
        reach_ref[:, c * 256 : (c + 1) * 256] = pick(
            stacked[...], hot, inverse_ref[c : c + 1, :], rank
        ).astype(BF)


def outer_kernel(
    ordered_ref, own_ref, before_ref, after_ref, near_in, blocks_ref, near_ref, matrices_ref,
    spots_ref, inverse_ref, weights_ref, masked_ref, hot_ref,
    partial_ref,
    leaves, nodes, far, stacked, stacked_nodes, edges, sems,
):
    columns, points = ordered_ref.shape
    halo = before_ref.shape[1] - 4096
    device = lax.axis_index("leaf")
    count = points // 64
    copies = [
        pltpu.make_async_copy(blocks_ref.at[pl.ds(at, REACH)], edges.at[i], sems.at[i])
        for i, at in enumerate((0, count - REACH))
    ]
    for copy in copies:
        copy.start()

    for c in range(halo // 128):
        place_leaves(leaves, c * 2, before_ref[:, pl.ds(c * 128, 128)])
        place_leaves(leaves, REACH + count + c * 2, after_ref[:, pl.ds(c * 128, 128)])

    def place(c, carry):
        chunk = ordered_ref[:, pl.ds(pl.multiple_of(c * 128, 128), 128)]
        place_leaves(leaves, REACH + c * 2, chunk)
        return carry

    lax.fori_loop(0, count // 2, place, 0)

    nodes[3 * 128] = jnp.zeros((columns, 128), F32)
    lane, row = iota((256, 1024), 1), iota((256, 1024), 0)
    spread = jnp.where(row == (lane & 31) * 8 + (lane >> 7), 1.0, 0.0).astype(BF)
    for side, ref in enumerate((before_ref, own_ref, after_ref)):
        for n in range(16):
            stacked_nodes[n * columns : (n + 1) * columns, :] = ref[:, halo + n * 256 : halo + (n + 1) * 256]
        for c in range(0, 8, 2):
            out = dot(stacked_nodes[...], spread[:, c * 128 : (c + 2) * 128], NN)
            for n in range(16):
                both = out[n * columns : (n + 1) * columns]
                nodes[side * 128 + n * 8 + c] = both[:, :128]
                nodes[side * 128 + n * 8 + c + 1] = both[:, 128:]

    lane_group = iota((columns, 128), 1) >> 5
    lane_node = iota((columns, 256), 1) & 7

    def couple(g, carry):
        picked = []
        for i in range(8):
            parts = [nodes[spots_ref[s, g * 8 + i]] for s in range(6)]
            front = parts[0]
            for s in range(1, 4):
                front = jnp.where(lane_group == s, parts[s], front)
            back = jnp.where(lane_group == 1, parts[5], parts[4])
            back = jnp.where(lane_group < 2, back, 0.0)
            picked.append(jnp.concatenate([front, back], axis=1))
        out = dot(jnp.concatenate(picked, axis=0).astype(BF), matrices_ref[g], NT)
        total = out[:columns]
        for i in range(1, 8):
            total = jnp.where(lane_node == i, out[i * columns : (i + 1) * columns], total)
        far[:, pl.ds(pl.multiple_of(g * 256, 256), 256)] = total
        return carry

    lax.fori_loop(0, 16, couple, 0)

    for copy in copies:
        copy.wait()
    down = [None] * 16
    last = far[:, 15 * 256 :]
    five = jnp.where(lane_node >= 4, last, 0.0).astype(BF)
    down[15] = (last + dot(five, weights_ref[15], NT)).astype(BF)
    for k in reversed(range(15)):
        down[k] = (far[:, k * 256 : (k + 1) * 256] + dot(down[8 + k // 2], weights_ref[k], NT)).astype(BF)
    groups = count // 4
    edge = REACH // 4
    for g in range(groups):
        if g < edge:
            blocks = edges[0, g * 4 : g * 4 + 4].reshape(256, 256)
        elif g >= groups - edge:
            at = (g - groups + edge) * 4
            blocks = edges[1, at : at + 4].reshape(256, 256)
        else:
            blocks = None
        if blocks is None:
            near = near_in[:, g * 256 : (g + 1) * 256]
        else:
            near = near_group(leaves, near_ref, blocks, g * 4, device * count - REACH, columns)
        if g % 2 == 0:
            at_points = dot(down[g // 2], masked_ref[g // 2], NN)
        half = at_points[:, g % 2 * 256 : (g % 2 + 1) * 256]
        stacked[g * columns : (g + 1) * columns, :] = (near + half).astype(BF)

    for c in range(points // 256):
        partial_ref[:, c * 256 : (c + 1) * 256] = pick(
            stacked[...], hot_ref[c], inverse_ref[c : c + 1, :], columns
        )


def top_kernel(
    gathered_ref, transfer_ref, coupling_ref, lists_ref, partial_ref, reach_ref, out_ref, coeffs,
):
    node_count = gathered_ref.shape[0]
    columns = gathered_ref.shape[1]
    device = lax.axis_index("leaf")
    total = 2 * node_count - 1
    for q in range(node_count):
        coeffs[q ^ device] = gathered_ref[q][:, :32].astype(F32)
    start, count = 0, node_count
    while count > 1:
        for j in range(count // 2):
            lifted = dot(coeffs[start + 2 * j].astype(BF), transfer_ref[start + 2 * j], NN)
            lifted += dot(coeffs[start + 2 * j + 1].astype(BF), transfer_ref[start + 2 * j + 1], NN)
            coeffs[start + count + j] = lifted.astype(BF).astype(F32)
        start, count = start + count, count // 2
    coeffs[total] = jnp.zeros((columns, 32), F32)
    starts, start, count = [], 0, node_count
    while count >= 1:
        starts.append((start, count))
        start, count = start + count, count // 2
    down = None
    for level, (start, count) in reversed(list(enumerate(starts))):
        node = start + (device >> level)
        field = None
        for s in range(6):
            entry = lists_ref[s, node]
            spot = jnp.where(entry >= 0, start + entry, total)
            term = dot(coeffs[spot].astype(BF), coupling_ref[s, node], NT)
            field = term if field is None else field + term
        if down is not None:
            field = field + dot(down, transfer_ref[node], NT)
        down = field.astype(BF)

    points = out_ref.shape[1]
    for c in range(points // 512):
        at = pl.ds(c * 512, 512)
        out_ref[:, at] = partial_ref[:, at] + dot(down, reach_ref[:, at], NN)


VMEM = pl.BlockSpec(memory_space=pltpu.VMEM)
SMEM = pl.BlockSpec(memory_space=pltpu.SMEM)


def call(kernel, outs, scratch, specs, flops, name, args, out_specs=None):
    size = sum(a.size * a.dtype.itemsize for a in args)
    return pl.pallas_call(
        kernel,
        out_shape=[jax.ShapeDtypeStruct(s, t) for s, t in outs],
        in_specs=specs,
        out_specs=[VMEM] * len(outs) if out_specs is None else out_specs,
        scratch_shapes=scratch,
        compiler_params=pltpu.CompilerParams(vmem_limit_bytes=36 * 2**20),
        cost_estimate=pl.CostEstimate(flops=flops, bytes_accessed=size, transcendentals=0),
        name=name,
    )(*args)


def local(
    vectors, tree_order, leaf_basis, near_blocks, near_lists, transfers, couplings, coupling_lists,
    top_transfers, top_couplings, top_lists,
):
    columns, points = vectors.shape
    rank = leaf_basis.shape[0]
    devices = lax.axis_size("leaf")
    halo = REACH * near_blocks.shape[1]
    packed = halo + 128 * rank
    order = tree_order.reshape(points // 128, 128)
    near_t = jnp.transpose(near_lists)
    lists_t = jnp.transpose(coupling_lists)
    moves = transfers.reshape(rank * rank, -1)
    matrices = couplings.reshape(6, rank * rank, -1)

    ordered, to_left, to_right, top, weights, masked, inverse = call(
        up_kernel,
        [
            ((columns, points), BF), ((columns, packed), BF), ((columns, packed), BF), ((1, columns, 128), BF),
            ((16, 256, 256), BF), ((points // 512, 256, 512), BF), ((32, 256), jnp.int32),
        ],
        [
            pltpu.VMEM(vectors.shape, BF), pltpu.VMEM(order.shape, jnp.int32),
            pltpu.VMEM(leaf_basis.shape, BF), pltpu.VMEM(moves.shape, BF),
            pltpu.VMEM((points // 256 * columns, 256), BF), pltpu.VMEM((rank, 128, 256), F32),
            pltpu.SemaphoreType.DMA((4,)),
        ],
        [pl.BlockSpec(memory_space=pl.ANY)] * 4, 10**9, "up", (vectors, order, leaf_basis, moves),
    )
    reached = 1
    gathered = top
    while reached < devices:
        swap = [(i, i ^ reached) for i in range(devices)]
        gathered = jnp.concatenate([gathered, lax.ppermute(gathered, "leaf", swap)], axis=0)
        reached *= 2
    upward = [(i, i + 1) for i in range(devices - 1)]
    before = lax.ppermute(to_right, "leaf", upward)
    after = lax.ppermute(to_left, "leaf", [(j, i) for i, j in upward])

    near_part, coupling_rows, spots, hot, reach = call(
        inner_kernel,
        [
            ((columns, points), F32), ((16, 256, 256), BF), ((8, 128), jnp.int32),
            ((points // 256, 256, 256), BF), ((rank, points), BF),
        ],
        [
            pltpu.VMEM((points // 64, columns, 128), F32), pltpu.VMEM((rank, 128, 256), F32),
            pltpu.VMEM((points // 256 * rank, 256), BF),
        ],
        [VMEM, VMEM, SMEM, VMEM, VMEM, VMEM, VMEM, VMEM], 6 * 10**9, "inner",
        (ordered, near_blocks, near_t, matrices, lists_t, weights, masked, inverse),
    )
    (partial,) = call(
        outer_kernel,
        [((columns, points), F32)],
        [
            pltpu.VMEM((points // 64 + 2 * REACH, columns, 128), F32),
            pltpu.VMEM((385, columns, 128), F32), pltpu.VMEM((columns, 4096), F32),
            pltpu.VMEM((points // 256 * columns, 256), BF), pltpu.VMEM((16 * columns, 256), BF),
            pltpu.VMEM((2, REACH) + near_blocks.shape[1:], BF), pltpu.SemaphoreType.DMA((2,)),
        ],
        [
            VMEM, VMEM, VMEM, VMEM, VMEM, pl.BlockSpec(memory_space=pl.ANY), SMEM, VMEM,
            SMEM, VMEM, VMEM, VMEM, VMEM,
        ], 4 * 10**9, "outer",
        (
            ordered, to_left, before, after, near_part, near_blocks, near_t, coupling_rows,
            spots, inverse, weights, masked, hot,
        ),
    )
    (applied,) = call(
        top_kernel,
        [((columns, points), F32)],
        [pltpu.VMEM((2 * devices, columns, 32), F32)],
        [VMEM, VMEM, VMEM, SMEM, VMEM, VMEM], 10**9, "top",
        (
            gathered, jnp.transpose(top_transfers, (2, 0, 1)), jnp.transpose(top_couplings, (0, 3, 1, 2)),
            jnp.transpose(top_lists), partial, reach,
        ),
    )
    return applied


def solution(mesh):
    placed = (
        P("rhs", ("groups", "leaf")),
        P(("groups", "leaf")),
        P(None, ("groups", "leaf")),
        P(("groups", "leaf"), None, None),
        P(("groups", "leaf"), None),
        P(None, None, ("groups", "leaf")),
        P(None, None, None, ("groups", "leaf")),
        P(("groups", "leaf"), None),
        P(None, None, "groups"),
        P(None, None, None, "groups"),
        P("groups", None),
    )
    return jax.shard_map(
        local, mesh=mesh, in_specs=placed, out_specs=P("rhs", ("groups", "leaf")), check_vma=False
    )
```

time: 76.9 us -> 48.8 us (0.63)
  Pallas kernels: 57.4 us -> 29.3 us
    pallas_call x4, Pallas kernels: 57.4 us -> 29.3 us  [call(): pl.pallas_call(kernel, out_shape=[jax.ShapeDtypeStruct(s, t) for s, t in...]
    unnamed x24 -> x22, local copies, waits for them, and re-layouts: 3.83 us -> 3.83 us
where the time goes in v2:
time: 48.8 us; the launch traced here: 48.6 us
  Pallas kernels  29.3 us (60%)
  starting transfers between devices  13.6 us (28%)
  local copies, waits for them, and re-layouts  3.83 us (8%)
  waiting for transfers between devices  1.64 us (3%)
    pallas_call x4, Pallas kernels, call(): pl.pallas_call(kernel, out_shape=[jax.ShapeDtypeStruct(s, t) for s, t in...  29.3 us
    ppermute x3, starting transfers between devices, local(): lax.ppermute(gathered, 'leaf', swap)  7.74 us
    ppermute x1, starting transfers between devices, local(): before = lax.ppermute(to_right, 'leaf', upward)  4.56 us
    unnamed x22, local copies, waits for them, and re-layouts  3.83 us
    ppermute x3, waiting for transfers between devices, local(): lax.ppermute(gathered, 'leaf', swap)  1.64 us
    ppermute x1, starting transfers between devices, local(): after = lax.ppermute(to_left, 'leaf', [(j, i) for i, j in upward])  1.28 us
  transfers between devices with their start and end apart: 5, of which 1 were waited for; matrix products, arithmetic and copies ran while one was open for 0% of the time, Pallas kernels for 24%

profile of v2, /device:TPU:0, one launch (start us, length us, event | category | flops | bytes accessed | tf_op | source)
XLA Modules:
  0.0 48.6 jit_solution(15748731237797861839)
XLA Ops:
  0.0 0.0 copy-start.1
  0.0 0.0 copy-start
  0.0 0.0 copy-start.3
  0.0 1.1 %copy-done.3 = bf16[32,4096]{1,0:T(8,128)(2,1)S(1)} copy-done((bf16[32,4096]{1,0:T(8,128)(2,1)S(1)}, bf16[32,4096]{1,0:T(8,128)(2,1)}, u32[]{:S(2)}) %copy-start.3) | copy-done | bytes 262168
  1.1 0.0 copy-start.4
  1.1 1.0 %copy-done.4 = bf16[32,4096]{1,0:T(8,128)(2,1)S(1)} copy-done((bf16[32,4096]{1,0:T(8,128)(2,1)S(1)}, bf16[32,4096]{1,0:T(8,128)(2,1)}, u32[]{:S(2)}) %copy-start.4) | copy-done | bytes 262168
  2.1 0.0 copy-start.5
  2.1 0.9 %copy-done.5 = bf16[32,32,126]{2,1,0:T(8,128)(2,1)S(1)} copy-done((bf16[32,32,126]{2,1,0:T(8,128)(2,1)S(1)}, bf16[32,32,126]{2,1,0:T(8,128)(2,1)}, u32[]{:S(2)}) %copy-start.5) | copy-done | bytes 258072
  3.1 0.0 copy-start.7
  3.1 0.7 %copy-done.7 = s32[4096]{0:T(1024)S(1)} copy-done((s32[4096]{0:T(1024)S(1)}, s32[4096]{0:T(1024)}, u32[]{:S(2)}) %copy-start.7) | copy-done | bytes 16408
  3.8 0.0 copy-start.8
  3.8 0.0 copy-start.10
  3.8 4.7 %up.1 = (bf16[32,4096]{1,0:T(8,128)(2,1)S(1)}, bf16[32,4608]{1,0:T(8,128)(2,1)S(1)}, bf16[32,4608]{1,0:T(8,128)(2,1)S(1)}, bf16[1,32,128]{2,1,0:T(8,128)(2,1)S(1...) custom-call(bf16[32,4096]{1,0:T(8,128)(2,1)S(1)} %copy-done.3, ...), custom_call_target="tpu_custom_call" | custom-call | flops 1000000000 | bytes 798720 | tf_op jit(solution)/shard_map/up/pallas_call | solution.py:366
  8.5 3.0 %collective-permute-start = (bf16[1,32,128]{2,1,0:T(8,128)(2,1)S(1)}, bf16[1,32,128]{2,1,0:T(8,128)(2,1)S(1)}, u32[]{:S(2)}, u32[]{:S(2)}) collective-permute-start(bf16[1,32,128]{2,1,0:T(8,128)(2,1)S(1)} %get-tuple-element.17), channel_id=1, source_target_pairs={{0,2},{2,0},{4,6},{6,4},{8,10},{10,8},{12,14},{14,12},{1,3},{3,1},... | collective-permute-start | bytes 24584 | tf_op jit(solution)/shard_map/ppermute | solution.py:411
  11.5 1.6 %collective-permute-done = bf16[1,32,128]{2,1,0:T(8,128)(2,1)S(1)} collective-permute-done((bf16[1,32,128]{2,1,0:T(8,128)(2,1)S(1)}, bf16[1,32,128]{2,1,0:T(8,128)(2,1)S(1)}, u32[]{:S(2)}, u32[]{:S(2)}) %collective-permute-start) | collective-permute-done | bytes 8224 | tf_op jit(solution)/shard_map/ppermute | solution.py:411
  13.2 2.1 %collective-permute-start.1 = (bf16[2,32,128]{2,1,0:T(8,128)(2,1)S(1)}, bf16[2,32,128]{2,1,0:T(8,128)(2,1)S(1)}, u32[]{:S(2)}, u32[]{:S(2)}) collective-permute-start(bf16[2,32,128]{2,1,0:T(8,128)(2,1)S(1)} %pad_maximum_fusion.2), channel_id=1, source_target_pairs={{0,4},{2,6},{4,0},{6,2},{8,12},{10,14},{12,8},{14,10},{1,5},{3,7},... | collective-permute-start | bytes 49160 | tf_op jit(solution)/shard_map/ppermute | solution.py:411
  15.2 1.3 %collective-permute-start.4 = (bf16[32,4608]{1,0:T(8,128)(2,1)S(1)}, bf16[32,4608]{1,0:T(8,128)(2,1)S(1)}, u32[]{:S(2)}, u32[]{:S(2)}) collective-permute-start(bf16[32,4608]{1,0:T(8,128)(2,1)S(1)} %get-tuple-element.19.own_ref), channel_id=1, source_target_pairs={{2,0},{4,2},{6,4},{8,6},{10,8},{12,10},{14,12},{3,1},{5,3},{7,5},{... | collective-permute-start | bytes 884744 | tf_op jit(solution)/shard_map/ppermute | solution.py:415
  16.5 4.6 %collective-permute-start.3 = (bf16[32,4608]{1,0:T(8,128)(2,1)S(1)}, bf16[32,4608]{1,0:T(8,128)(2,1)S(1)}, u32[]{:S(2)}, u32[]{:S(2)}) collective-permute-start(bf16[32,4608]{1,0:T(8,128)(2,1)S(1)} %get-tuple-element.20), channel_id=1, source_target_pairs={{0,2},{2,4},{4,6},{6,8},{8,10},{10,12},{12,14},{1,3},{3,5},{5,7},{... | collective-permute-start | bytes 884744 | tf_op jit(solution)/shard_map/ppermute | solution.py:414
  21.1 0.0 collective-permute-done.1
  21.1 2.6 %collective-permute-start.2 = (bf16[4,32,128]{2,1,0:T(8,128)(2,1)S(1)}, bf16[4,32,128]{2,1,0:T(8,128)(2,1)S(1)}, u32[]{:S(2)}, u32[]{:S(2)}) collective-permute-start(bf16[4,32,128]{2,1,0:T(8,128)(2,1)S(1)} %pad_maximum_fusion.1), channel_id=1, source_target_pairs={{0,8},{2,10},{4,12},{6,14},{8,0},{10,2},{12,4},{14,6},{1,9},{3,11}... | collective-permute-start | bytes 98312 | tf_op jit(solution)/shard_map/ppermute | solution.py:411
  23.8 0.0 copy-done.1
  23.8 0.0 copy-done
  23.8 0.0 copy-done.8
  23.8 0.0 copy-done.10
  23.8 11.7 %inner.1 = (f32[32,4096]{1,0:T(8,128)S(1)}, bf16[16,256,256]{2,1,0:T(8,128)(2,1)S(1)}, s32[8,128]{1,0:T(8,128)S(1)}, bf16[16,256,256]{2,1,0:T(8,128)(2,1)S(1)}, bf16[32,4096]{1,0:T(8,128)(2,1)S(1)}) custom-call(bf16[32,4096]{1,0:T(8,128)(2,1)S(1)} %get-tuple-element.18.ordered_ref, bf16[64,64,256]{2,1,0:T(8,128)(2,1)S(1)} %copy-done, s32[4,64]{1,0:T(4,128)S(1)} %bitcast.15, ...), custom_call_target="tpu_custom_call" | custom-call | flops 6000000000 | bytes 8138704 | tf_op jit(solution)/shard_map/inner/pallas_call | solution.py:366
  35.5 0.0 collective-permute-done.2
  35.5 0.0 collective-permute-done.4.after_ref
  35.5 0.0 collective-permute-done.3.before_ref
  35.5 0.0 copy-start.2
  35.5 0.0 copy-start.6
  35.6 0.0 copy-start.9
  35.6 10.4 %outer.1.partial_ref = f32[32,4096]{1,0:T(8,128)S(1)} custom-call(bf16[32,4096]{1,0:T(8,128)(2,1)S(1)} %get-tuple-element.18.ordered_ref, bf16[32,4608]{1,0:T(8,128)(2,1)S(1)} %get-tuple-element.19.own_ref, bf16[32,4608]{1,0:T(8,128)(2,1)S(1)} %collective-permute-done.3.before_ref, bf16[32,4608]{1,0:T(8,128)(2,1)S(1)} %collective-permute-done.4.after_ref, ...), custom_call_target="tpu_custom_call" | custom-call | flops 4000000000 | bytes 12194816 | tf_op jit(solution)/shard_map/outer/pallas_call | solution.py:366
  46.0 0.0 copy-done.2
  46.0 0.0 copy-done.6
  46.0 0.0 copy-done.9
  46.0 2.6 %top.1 = f32[32,4096]{1,0:T(8,128)} custom-call(bf16[8,32,128]{2,1,0:T(8,128)(2,1)S(1)} %pad_maximum_fusion.gathered_ref, bf16[14,32,32]{2,1,0:T(8,128)(2,1)S(1)} %bitcast.11, bf16[6,15,32,32]{3,2,1,0:T(8,128)(2,1)S(1)} %bitcast.9, s32[6,15]{1,0:T(8,128)S(1)} %bitcast.14, f32[32,4096]{1,0:T(8,128)S(1)} %outer.1.partial_ref, ...), custom_call_target="tpu_custom_call" | custom-call | flops 1000000000 | bytes 1065320 | tf_op jit(solution)/shard_map/top/pallas_call | solution.py:366
  (3 shorter events, 0.0 us)
Async XLA Ops:
  0.0 23.8 %copy-start.1 = (bf16[6,32,32,126]{3,2,1,0:T(8,128)(2,1)S(1)}, bf16[6,32,32,126]{3,2,1,0:T(8,128)(2,1)}, u32[]{:S(2)}) copy-start(bf16[6,32,32,126]{3,2,1,0:T(8,128)(2,1)} %param.17) | copy-start | bytes 4644868
  0.0 23.8 %copy-start = (bf16[64,64,256]{2,1,0:T(8,128)(2,1)S(1)}, bf16[64,64,256]{2,1,0:T(8,128)(2,1)}, u32[]{:S(2)}) copy-start(bf16[64,64,256]{2,1,0:T(8,128)(2,1)} %blocks_ref.3) | copy-start | bytes 6291460
  0.0 1.1 %copy-start.3 = (bf16[32,4096]{1,0:T(8,128)(2,1)S(1)}, bf16[32,4096]{1,0:T(8,128)(2,1)}, u32[]{:S(2)}) copy-start(bf16[32,4096]{1,0:T(8,128)(2,1)} %vec_hbm.1) | copy-start | bytes 786436
  1.1 1.0 %copy-start.4 = (bf16[32,4096]{1,0:T(8,128)(2,1)S(1)}, bf16[32,4096]{1,0:T(8,128)(2,1)}, u32[]{:S(2)}) copy-start(bf16[32,4096]{1,0:T(8,128)(2,1)} %basis_hbm.1) | copy-start | bytes 786436
  2.1 0.9 %copy-start.5 = (bf16[32,32,126]{2,1,0:T(8,128)(2,1)S(1)}, bf16[32,32,126]{2,1,0:T(8,128)(2,1)}, u32[]{:S(2)}) copy-start(bf16[32,32,126]{2,1,0:T(8,128)(2,1)} %param.16) | copy-start | bytes 774148
  3.1 0.7 %copy-start.7 = (s32[4096]{0:T(1024)S(1)}, s32[4096]{0:T(1024)}, u32[]{:S(2)}) copy-start(s32[4096]{0:T(1024)} %param.12) | copy-start | bytes 49156
  3.8 20.0 %copy-start.8 = (s32[126,6]{0,1:T(8,128)S(1)}, s32[126,6]{0,1:T(8,128)}, u32[]{:S(2)}) copy-start(s32[126,6]{0,1:T(8,128)} %param.18) | copy-start | bytes 9076
  3.8 20.0 %copy-start.10 = (s32[64,4]{0,1:T(4,128)S(1)}, s32[64,4]{0,1:T(4,128)}, u32[]{:S(2)}) copy-start(s32[64,4]{0,1:T(4,128)} %param.15) | copy-start | bytes 3076
  8.5 4.7 %collective-permute-start = (bf16[1,32,128]{2,1,0:T(8,128)(2,1)S(1)}, bf16[1,32,128]{2,1,0:T(8,128)(2,1)S(1)}, u32[]{:S(2)}, u32[]{:S(2)}) collective-permute-start(bf16[1,32,128]{2,1,0:T(8,128)(2,1)S(1)} %get-tuple-element.17), channel_id=1, source_target_pairs={{0,2},{2,0},{4,6},{6,4},{8,10},{10,8},{12,14},{14,12},{1,3},{3,1},... | collective-permute-start | bytes 24584 | tf_op jit(solution)/shard_map/ppermute | solution.py:411
  13.2 7.9 %collective-permute-start.1 = (bf16[2,32,128]{2,1,0:T(8,128)(2,1)S(1)}, bf16[2,32,128]{2,1,0:T(8,128)(2,1)S(1)}, u32[]{:S(2)}, u32[]{:S(2)}) collective-permute-start(bf16[2,32,128]{2,1,0:T(8,128)(2,1)S(1)} %pad_maximum_fusion.2), channel_id=1, source_target_pairs={{0,4},{2,6},{4,0},{6,2},{8,12},{10,14},{12,8},{14,10},{1,5},{3,7},... | collective-permute-start | bytes 49160 | tf_op jit(solution)/shard_map/ppermute | solution.py:411
  15.2 20.3 %collective-permute-start.4 = (bf16[32,4608]{1,0:T(8,128)(2,1)S(1)}, bf16[32,4608]{1,0:T(8,128)(2,1)S(1)}, u32[]{:S(2)}, u32[]{:S(2)}) collective-permute-start(bf16[32,4608]{1,0:T(8,128)(2,1)S(1)} %get-tuple-element.19.own_ref), channel_id=1, source_target_pairs={{2,0},{4,2},{6,4},{8,6},{10,8},{12,10},{14,12},{3,1},{5,3},{7,5},{... | collective-permute-start | bytes 884744 | tf_op jit(solution)/shard_map/ppermute | solution.py:415
  16.5 19.0 %collective-permute-start.3 = (bf16[32,4608]{1,0:T(8,128)(2,1)S(1)}, bf16[32,4608]{1,0:T(8,128)(2,1)S(1)}, u32[]{:S(2)}, u32[]{:S(2)}) collective-permute-start(bf16[32,4608]{1,0:T(8,128)(2,1)S(1)} %get-tuple-element.20), channel_id=1, source_target_pairs={{0,2},{2,4},{4,6},{6,8},{8,10},{10,12},{12,14},{1,3},{3,5},{5,7},{... | collective-permute-start | bytes 884744 | tf_op jit(solution)/shard_map/ppermute | solution.py:414
  21.1 14.4 %collective-permute-start.2 = (bf16[4,32,128]{2,1,0:T(8,128)(2,1)S(1)}, bf16[4,32,128]{2,1,0:T(8,128)(2,1)S(1)}, u32[]{:S(2)}, u32[]{:S(2)}) collective-permute-start(bf16[4,32,128]{2,1,0:T(8,128)(2,1)S(1)} %pad_maximum_fusion.1), channel_id=1, source_target_pairs={{0,8},{2,10},{4,12},{6,14},{8,0},{10,2},{12,4},{14,6},{1,9},{3,11}... | collective-permute-start | bytes 98312 | tf_op jit(solution)/shard_map/ppermute | solution.py:411
  35.5 10.4 %copy-start.2 = (bf16[6,32,32,15]{2,1,3,0:T(8,128)(2,1)S(1)}, bf16[6,32,32,15]{2,1,3,0:T(8,128)(2,1)}, u32[]{:S(2)}) copy-start(bf16[6,32,32,15]{2,1,3,0:T(8,128)(2,1)} %param.20) | copy-start | bytes 552964
  35.5 10.4 %copy-start.6 = (bf16[32,32,14]{1,0,2:T(8,128)(2,1)S(1)}, bf16[32,32,14]{1,0,2:T(8,128)(2,1)}, u32[]{:S(2)}) copy-start(bf16[32,32,14]{1,0,2:T(8,128)(2,1)} %param.19) | copy-start | bytes 86020
  35.6 10.4 %copy-start.9 = (s32[15,6]{0,1:T(8,128)S(1)}, s32[15,6]{0,1:T(8,128)}, u32[]{:S(2)}) copy-start(s32[15,6]{0,1:T(8,128)} %param.21) | copy-start | bytes 1084

commit v3 on v2

--- a/solution.py
+++ b/solution.py
@@ -43,13 +43,14 @@
 
 def up_kernel(
     vec_hbm, order_hbm, basis_hbm, transfer_hbm,
-    ordered_ref, left_ref, right_ref, top_ref, weights_ref, masked_ref, inverse_ref,
+    ordered_ref, first_ref, second_ref, top_ref, weights_ref, masked_ref, inverse_ref,
     vec_ref, order_ref, basis_ref, transfer_ref, stacked, rows32, sems,
 ):
     columns, points = vec_ref.shape
     rank = basis_ref.shape[0]
     chunks = points // 256
-    halo = left_ref.shape[1] - 4096
+    halo = first_ref.shape[1] - 4096
+    odd = lax.axis_index("leaf") % 2 == 1
     pairs = (
         (transfer_hbm, transfer_ref), (order_hbm, order_ref), (vec_hbm, vec_ref), (basis_hbm, basis_ref),
     )
@@ -105,12 +106,23 @@
     six = dot((four + five).astype(BF), weights_ref[15], NN)
     coeffs[15] = (four + six).astype(BF)
     root = jnp.where(iota((256, 128), 0) == iota((256, 128), 1) * 8 + 6, 1.0, 0.0).astype(BF)
-    top_ref[0] = dot(coeffs[15], root, NN).astype(BF)
+    tile = dot(coeffs[15], root, NN).astype(BF)
+    for q in range(top_ref.shape[0]):
+        top_ref[q] = tile
     for g in range(16):
-        left_ref[:, halo + g * 256 : halo + (g + 1) * 256] = coeffs[g]
-        right_ref[:, halo + g * 256 : halo + (g + 1) * 256] = coeffs[g]
-    left_ref[:, :halo] = ordered_ref[:, :halo]
-    right_ref[:, :halo] = ordered_ref[:, points - halo :]
+        first_ref[:, halo + g * 256 : halo + (g + 1) * 256] = coeffs[g]
+        second_ref[:, halo + g * 256 : halo + (g + 1) * 256] = coeffs[g]
+    low_edge, high_edge = ordered_ref[:, :halo], ordered_ref[:, points - halo :]
+
+    @pl.when(odd)
+    def _():
+        first_ref[:, :halo] = low_edge
+        second_ref[:, :halo] = high_edge
+
+    @pl.when(jnp.logical_not(odd))
+    def _():
+        first_ref[:, :halo] = high_edge
+        second_ref[:, :halo] = low_edge
 
 
 def near_group(leaves_ref, lists_ref, blocks, first, base, columns):
@@ -139,15 +151,10 @@
     leaves_ref[first + 1] = pltpu.roll(chunk, 64, 1)
 
 
-def inner_kernel(
-    ordered_ref, blocks_ref, near_ref, coupling_ref, lists_ref, weights_ref, masked_ref, inverse_ref,
-    near_out, matrices_ref, spots_ref, hot_ref, reach_ref,
-    leaves, rows32, stacked,
-):
-    columns, points = ordered_ref.shape
+def matrices_kernel(coupling_ref, lists_ref, matrices_ref, spots_ref, rows32):
     rank = 32
-    count = blocks_ref.shape[0]
     device = lax.axis_index("leaf")
+    count = 64
 
     node = iota((1, 128), 1)
     size = jnp.full((1, 128), count, jnp.int32)
@@ -167,28 +174,21 @@
         spots_ref[pl.ds(s, 1), :] = jnp.where(used, spot, 3 * 128)
     spots_ref[pl.ds(6, 2), :] = jnp.zeros((2, 128), jnp.int32)
 
-    def relayout(a, carry):
-        at = pl.multiple_of(a * rank, rank)
-        one = [coupling_ref[s, pl.ds(at, rank), :].astype(F32) for s in range(6)]
-        full = jnp.concatenate(one + [jnp.zeros_like(one[0])] * 2, axis=0)
-        rows32[a] = pad_lanes(full).T
-        return carry
-
-    lax.fori_loop(0, rank, relayout, 0)
-
-    def narrow(g, carry):
-        at = pl.multiple_of(g * 8, 8)
-        matrices_ref[g] = rows32[:, pl.ds(at, 8), :].reshape(256, 256).astype(BF)
-        return carry
-
-    lax.fori_loop(0, 16, narrow, 0)
-
-    def place(c, carry):
-        chunk = ordered_ref[:, pl.ds(pl.multiple_of(c * 128, 128), 128)]
-        place_leaves(leaves, c * 2, chunk)
-        return carry
-
-    lax.fori_loop(0, count // 2, place, 0)
+    for a in range(rank):
+        one = [coupling_ref[s, a * rank : (a + 1) * rank, :].astype(F32) for s in range(6)]
+        full = pad_lanes(jnp.concatenate(one, axis=0))
+        turned = jnp.concatenate([full[:128].T, pad_lanes(full[128:].T)], axis=1)
+        rows32[a] = turned
+    for g in range(16):
+        matrices_ref[g] = rows32[:, g * 8 : g * 8 + 8, :].reshape(256, 256).astype(BF)
+
+
+def near_kernel(ordered_ref, blocks_ref, near_ref, near_out, leaves):
+    columns, points = ordered_ref.shape
+    count = blocks_ref.shape[0]
+    device = lax.axis_index("leaf")
+    for c in range(count // 2):
+        place_leaves(leaves, c * 2, ordered_ref[:, c * 128 : (c + 1) * 128])
     edge = REACH // 4
     near_out[:, : edge * 256] = jnp.zeros((columns, edge * 256), F32)
     near_out[:, points - edge * 256 :] = jnp.zeros((columns, edge * 256), F32)
@@ -201,8 +201,11 @@
         )
         return carry
 
-    lax.fori_loop(edge, count // 4 - edge, near, 0)
-
+    lax.fori_loop(edge, count // 4 - edge, near, 0, unroll=4)
+
+
+def reach_kernel(weights_ref, masked_ref, inverse_ref, hot_ref, reach_ref, stacked):
+    rank, points = reach_ref.shape
     unit = jnp.where(iota((rank, 256), 1) == iota((rank, 256), 0) * 8 + 6, 1.0, 0.0)
     five = dot(unit.astype(BF), weights_ref[15], NT)
     down = [None] * 16
@@ -222,13 +225,13 @@
 
 
 def outer_kernel(
-    ordered_ref, own_ref, before_ref, after_ref, near_in, blocks_ref, near_ref, matrices_ref,
+    ordered_ref, own_ref, first_ref, second_ref, near_in, blocks_ref, near_ref, matrices_ref,
     spots_ref, inverse_ref, weights_ref, masked_ref, hot_ref,
     partial_ref,
     leaves, nodes, far, stacked, stacked_nodes, edges, sems,
 ):
     columns, points = ordered_ref.shape
-    halo = before_ref.shape[1] - 4096
+    halo = first_ref.shape[1] - 4096
     device = lax.axis_index("leaf")
     count = points // 64
     copies = [
@@ -238,21 +241,18 @@
     for copy in copies:
         copy.start()
 
-    for c in range(halo // 128):
-        place_leaves(leaves, c * 2, before_ref[:, pl.ds(c * 128, 128)])
-        place_leaves(leaves, REACH + count + c * 2, after_ref[:, pl.ds(c * 128, 128)])
-
-    def place(c, carry):
-        chunk = ordered_ref[:, pl.ds(pl.multiple_of(c * 128, 128), 128)]
-        place_leaves(leaves, REACH + c * 2, chunk)
-        return carry
-
-    lax.fori_loop(0, count // 2, place, 0)
+    odd = device % 2
+    for ref, right in ((first_ref, 1 - odd), (second_ref, odd)):
+        for c in range(halo // 128):
+            place_leaves(leaves, right * (REACH + count) + c * 2, ref[:, c * 128 : (c + 1) * 128])
+    near_ends = REACH * 64 * 2 // 128
+    for c in list(range(near_ends)) + list(range(count // 2 - near_ends, count // 2)):
+        place_leaves(leaves, REACH + c * 2, ordered_ref[:, c * 128 : (c + 1) * 128])
 
     nodes[3 * 128] = jnp.zeros((columns, 128), F32)
     lane, row = iota((256, 1024), 1), iota((256, 1024), 0)
     spread = jnp.where(row == (lane & 31) * 8 + (lane >> 7), 1.0, 0.0).astype(BF)
-    for side, ref in enumerate((before_ref, own_ref, after_ref)):
+    for side, ref in ((1, own_ref), (2 - 2 * odd, first_ref), (2 * odd, second_ref)):
         for n in range(16):
             stacked_nodes[n * columns : (n + 1) * columns, :] = ref[:, halo + n * 256 : halo + (n + 1) * 256]
         for c in range(0, 8, 2):
@@ -282,7 +282,7 @@
         far[:, pl.ds(pl.multiple_of(g * 256, 256), 256)] = total
         return carry
 
-    lax.fori_loop(0, 16, couple, 0)
+    lax.fori_loop(0, 16, couple, 0, unroll=4)
 
     for copy in copies:
         copy.wait()
@@ -325,7 +325,7 @@
     device = lax.axis_index("leaf")
     total = 2 * node_count - 1
     for q in range(node_count):
-        coeffs[q ^ device] = gathered_ref[q][:, :32].astype(F32)
+        coeffs[q] = gathered_ref[q][:, :32].astype(F32)
     start, count = 0, node_count
     while count > 1:
         for j in range(count // 2):
@@ -361,15 +361,19 @@
 SMEM = pl.BlockSpec(memory_space=pltpu.SMEM)
 
 
-def call(kernel, outs, scratch, specs, flops, name, args, out_specs=None):
+def in_hbm(x):
+    return pltpu.with_memory_space_constraint(x, pltpu.HBM)
+
+
+def call(kernel, outs, scratch, specs, flops, name, args, mib=36):
     size = sum(a.size * a.dtype.itemsize for a in args)
     return pl.pallas_call(
         kernel,
         out_shape=[jax.ShapeDtypeStruct(s, t) for s, t in outs],
         in_specs=specs,
-        out_specs=[VMEM] * len(outs) if out_specs is None else out_specs,
+        out_specs=[VMEM] * len(outs),
         scratch_shapes=scratch,
-        compiler_params=pltpu.CompilerParams(vmem_limit_bytes=36 * 2**20),
+        compiler_params=pltpu.CompilerParams(vmem_limit_bytes=mib * 2**20),
         cost_estimate=pl.CostEstimate(flops=flops, bytes_accessed=size, transcendentals=0),
         name=name,
     )(*args)
@@ -390,10 +394,10 @@
     moves = transfers.reshape(rank * rank, -1)
     matrices = couplings.reshape(6, rank * rank, -1)
 
-    ordered, to_left, to_right, top, weights, masked, inverse = call(
+    ordered, first, second, top, weights, masked, inverse = call(
         up_kernel,
         [
-            ((columns, points), BF), ((columns, packed), BF), ((columns, packed), BF), ((1, columns, 128), BF),
+            ((columns, points), BF), ((columns, packed), BF), ((columns, packed), BF), ((devices, columns, 128), BF),
             ((16, 256, 256), BF), ((points // 512, 256, 512), BF), ((32, 256), jnp.int32),
         ],
         [
@@ -402,30 +406,29 @@
             pltpu.VMEM((points // 256 * columns, 256), BF), pltpu.VMEM((rank, 128, 256), F32),
             pltpu.SemaphoreType.DMA((4,)),
         ],
-        [pl.BlockSpec(memory_space=pl.ANY)] * 4, 10**9, "up", (vectors, order, leaf_basis, moves),
-    )
-    reached = 1
-    gathered = top
-    while reached < devices:
-        swap = [(i, i ^ reached) for i in range(devices)]
-        gathered = jnp.concatenate([gathered, lax.ppermute(gathered, "leaf", swap)], axis=0)
-        reached *= 2
-    upward = [(i, i + 1) for i in range(devices - 1)]
-    before = lax.ppermute(to_right, "leaf", upward)
-    after = lax.ppermute(to_left, "leaf", [(j, i) for i, j in upward])
-
-    near_part, coupling_rows, spots, hot, reach = call(
-        inner_kernel,
-        [
-            ((columns, points), F32), ((16, 256, 256), BF), ((8, 128), jnp.int32),
-            ((points // 256, 256, 256), BF), ((rank, points), BF),
-        ],
-        [
-            pltpu.VMEM((points // 64, columns, 128), F32), pltpu.VMEM((rank, 128, 256), F32),
-            pltpu.VMEM((points // 256 * rank, 256), BF),
-        ],
-        [VMEM, VMEM, SMEM, VMEM, VMEM, VMEM, VMEM, VMEM], 6 * 10**9, "inner",
-        (ordered, near_blocks, near_t, matrices, lists_t, weights, masked, inverse),
+        [pl.BlockSpec(memory_space=pl.ANY)] * 4, 10**9, "up",
+        tuple(in_hbm(x) for x in (vectors, order, leaf_basis, moves)),
+    )
+    gathered = lax.all_to_all(top, "leaf", 0, 0)
+    evens = [(i, i + 1) for i in range(0, devices - 1, 2)]
+    odds = [(i, i + 1) for i in range(1, devices - 1, 2)]
+    from_first = lax.ppermute(first, "leaf", evens + [(j, i) for i, j in evens])
+    from_second = lax.ppermute(second, "leaf", odds + [(j, i) for i, j in odds])
+
+    coupling_rows, spots = call(
+        matrices_kernel, [((16, 256, 256), BF), ((8, 128), jnp.int32)],
+        [pltpu.VMEM((rank, 128, 256), F32)],
+        [VMEM, VMEM], 3 * 10**9, "matrices", (matrices, lists_t),
+    )
+    (near_part,) = call(
+        near_kernel, [((columns, points), F32)],
+        [pltpu.VMEM((points // 64, columns, 128), F32)],
+        [VMEM, VMEM, SMEM], 3 * 10**9, "near", (ordered, near_blocks, near_t),
+    )
+    hot, reach = call(
+        reach_kernel, [((points // 256, 256, 256), BF), ((rank, points), BF)],
+        [pltpu.VMEM((points // 256 * rank, 256), BF)],
+        [VMEM, VMEM, VMEM], 4 * 10**9, "reach", (weights, masked, inverse),
     )
     (partial,) = call(
         outer_kernel,
@@ -441,7 +444,7 @@
             SMEM, VMEM, VMEM, VMEM, VMEM,
         ], 4 * 10**9, "outer",
         (
-            ordered, to_left, before, after, near_part, near_blocks, near_t, coupling_rows,
+            ordered, first, from_first, from_second, near_part, in_hbm(near_blocks), near_t, coupling_rows,
             spots, inverse, weights, masked, hot,
         ),
     )

time: 48.8 us -> 44.2 us (0.906)
  Pallas kernels: 29.3 us -> 19.8 us
  local copies, waits for them, and re-layouts: 3.83 us -> 7.41 us
  waiting for transfers between devices: 1.64 us -> 3.74 us
  starting transfers between devices: 13.6 us -> 12.7 us
    pallas_call x4 -> x6, Pallas kernels: 29.3 us -> 19.8 us  [call(): pl.pallas_call(kernel, out_shape=[jax.ShapeDtypeStruct(s, t) for s, t in...]
    ppermute x5 -> x2, starting transfers between devices: 13.6 us -> 5.45 us  [the longest x1 4.78 us: local(): from_first = lax.ppermute(first, 'leaf', evens + [(j, i) for i, j in evens])]
    all_to_all x0 -> x1, starting transfers between devices: none -> 7.27 us  [local(): gathered = lax.all_to_all(top, 'leaf', 0, 0)]
    unnamed x22 -> x32, local copies, waits for them, and re-layouts: 3.83 us -> 7.41 us
    ppermute x5 -> x2, waiting for transfers between devices: 1.64 us -> 3.74 us  [the longest x1 3.73 us: local(): from_first = lax.ppermute(first, 'leaf', evens + [(j, i) for i, j in evens])]
  transfers between devices with their start and end apart: 5 -> 3, of which waited for: 1 -> 1; matrix products, arithmetic and copies ran while one was open for 0% -> 0% of each run, Pallas kernels for 24% -> 25%
where the time goes in v3:
time: 44.2 us; the launch traced here: 43.8 us
  Pallas kernels  19.8 us (45%)
  starting transfers between devices  12.7 us (29%)
  local copies, waits for them, and re-layouts  7.41 us (17%)
  waiting for transfers between devices  3.74 us (8%)
    pallas_call x6, Pallas kernels, call(): pl.pallas_call(kernel, out_shape=[jax.ShapeDtypeStruct(s, t) for s, t in...  19.8 us
    unnamed x32, local copies, waits for them, and re-layouts  7.41 us
    all_to_all x1, starting transfers between devices, local(): gathered = lax.all_to_all(top, 'leaf', 0, 0)  7.27 us
    ppermute x1, starting transfers between devices, local(): from_first = lax.ppermute(first, 'leaf', evens + [(j, i) for i, j in evens])  4.78 us
    ppermute x1, waiting for transfers between devices, local(): from_first = lax.ppermute(first, 'leaf', evens + [(j, i) for i, j in evens])  3.73 us
  transfers between devices with their start and end apart: 3, of which 1 were waited for; matrix products, arithmetic and copies ran while one was open for 0% of the time, Pallas kernels for 25%

profile of v3, /device:TPU:0, one launch (start us, length us, event | category | flops | bytes accessed | tf_op | source)
XLA Modules:
  0.0 43.8 jit_solution(6752097566312384087)
XLA Ops:
  0.0 6.2 %up.1 = (bf16[32,4096]{1,0:T(8,128)(2,1)S(1)}, bf16[32,4608]{1,0:T(8,128)(2,1)S(1)}, bf16[32,4608]{1,0:T(8,128)(2,1)S(1)}, bf16[8,32,128]{2,1,0:T(8,128)(2,1)}, ...) custom-call(bf16[32,4096]{1,0:T(8,128)(2,1)} %vec_hbm.1, ...), custom_call_target="tpu_custom_call" | custom-call | flops 1000000000 | bytes 798720 | tf_op jit(solution)/shard_map/up/pallas_call | solution.py:370
  6.2 0.0 copy-start.7
  6.2 1.3 %copy-done.7 = bf16[8,256,512]{2,1,0:T(8,128)(2,1)} copy-done((bf16[8,256,512]{2,1,0:T(8,128)(2,1)}, bf16[8,256,512]{2,1,0:T(8,128)(2,1)S(1)}, u32[]{:S(2)}) %copy-start.7) | copy-done | bytes 2097176
  7.5 0.0 copy-start.14
  7.5 0.7 %copy-done.14 = bf16[32,4096]{1,0:T(8,128)(2,1)} copy-done((bf16[32,4096]{1,0:T(8,128)(2,1)}, bf16[32,4096]{1,0:T(8,128)(2,1)S(1)}, u32[]{:S(2)}) %copy-start.14) | copy-done | bytes 262168
  8.2 7.3 %all-to-all-start = ((bf16[8,32,128]{2,1,0:T(8,128)(2,1)}), bf16[8,32,128]{2,1,0:T(8,128)(2,1)S(1)}, u32[]{:S(2)}, u32[]{:S(2)}) async-start(bf16[8,32,128]{2,1,0:T(8,128)(2,1)} %get-tuple-element.16), calls=%async_computation | async-start | bytes 131072 | tf_op jit(solution)/shard_map/all_to_all | solution.py:412
  15.5 0.7 %collective-permute-start.1 = (bf16[32,4608]{1,0:T(8,128)(2,1)S(1)}, bf16[32,4608]{1,0:T(8,128)(2,1)S(1)}, u32[]{:S(2)}, u32[]{:S(2)}) collective-permute-start(bf16[32,4608]{1,0:T(8,128)(2,1)S(1)} %get-tuple-element.19), channel_id=1, source_target_pairs={{2,4},{6,8},{10,12},{4,2},{8,6},{12,10},{3,5},{7,9},{11,13},{5,3},... | collective-permute-start | bytes 884744 | tf_op jit(solution)/shard_map/ppermute | solution.py:416
  16.2 4.8 %collective-permute-start = (bf16[32,4608]{1,0:T(8,128)(2,1)S(1)}, bf16[32,4608]{1,0:T(8,128)(2,1)S(1)}, u32[]{:S(2)}, u32[]{:S(2)}) collective-permute-start(bf16[32,4608]{1,0:T(8,128)(2,1)S(1)} %get-tuple-element.18.own_ref), channel_id=1, source_target_pairs={{0,2},{4,6},{8,10},{12,14},{2,0},{6,4},{10,8},{14,12},{1,3},{5,7},... | collective-permute-start | bytes 884744 | tf_op jit(solution)/shard_map/ppermute | solution.py:415
  20.9 0.0 copy-start.8
  20.9 1.6 %copy-done.8 = bf16[8,256,512]{2,1,0:T(8,128)(2,1)S(1)} copy-done((bf16[8,256,512]{2,1,0:T(8,128)(2,1)S(1)}, bf16[8,256,512]{2,1,0:T(8,128)(2,1)}, u32[]{:S(2)}) %copy-start.8) | copy-done | bytes 2097176
  22.5 0.0 copy-start.1
  22.5 0.0 copy-start.4
  22.5 2.7 %reach.1 = (bf16[16,256,256]{2,1,0:T(8,128)(2,1)S(1)}, bf16[32,4096]{1,0:T(8,128)(2,1)S(1)}) custom-call(bf16[16,256,256]{2,1,0:T(8,128)(2,1)S(1)} %get-tuple-element.23.weights_ref, bf16[8,256,512]{2,1,0:T(8,128)(2,1)S(1)} %copy-done.8, s32[32,256]{1,0:T(8,128)S(1)} %get-tuple-element.22.inverse_ref), custom_call_target="tpu_custom_call" | custom-call | flops 4000000000 | bytes 4227072 | tf_op jit(solution)/shard_map/reach/pallas_call | solution.py:370
  25.3 0.0 copy-start.12
  25.3 0.0 copy-done.1
  25.3 0.0 copy-done.4
  25.3 0.0 copy-start
  25.3 0.0 copy-start.6
  25.3 0.0 copy-start.15
  25.3 0.6 %matrices.1 = (bf16[16,256,256]{2,1,0:T(8,128)(2,1)S(1)}, s32[8,128]{1,0:T(8,128)S(1)}) custom-call(bf16[6,1024,126]{2,1,0:T(8,128)(2,1)S(1)} %bitcast.8, s32[6,126]{1,0:T(8,128)S(1)} %bitcast.11), custom_call_target="tpu_custom_call" | custom-call | flops 3000000000 | bytes 1551312 | tf_op jit(solution)/shard_map/matrices/pallas_call | solution.py:370
  26.0 0.0 copy-done.12
  26.0 1.0 %copy-done = bf16[64,64,256]{2,1,0:T(8,128)(2,1)S(1)} copy-done((bf16[64,64,256]{2,1,0:T(8,128)(2,1)S(1)}, bf16[64,64,256]{2,1,0:T(8,128)(2,1)}, u32[]{:S(2)}) %copy-start) | copy-done | bytes 2097176
  27.0 0.0 copy-done.6
  27.0 0.0 copy-done.15
  27.0 0.0 copy-start.9
  27.0 1.7 %near.1.near_in = f32[32,4096]{1,0:T(8,128)S(1)} custom-call(bf16[32,4096]{1,0:T(8,128)(2,1)S(1)} %copy-done.15, bf16[64,64,256]{2,1,0:T(8,128)(2,1)S(1)} %copy-done, s32[4,64]{1,0:T(4,128)S(1)} %bitcast.13), custom_call_target="tpu_custom_call" | custom-call | flops 3000000000 | bytes 2360320 | tf_op jit(solution)/shard_map/near/pallas_call | solution.py:370
  28.7 0.0 collective-permute-done.1.second_ref
  28.7 3.7 %collective-permute-done.first_ref = bf16[32,4608]{1,0:T(8,128)(2,1)S(1)} collective-permute-done((bf16[32,4608]{1,0:T(8,128)(2,1)S(1)}, bf16[32,4608]{1,0:T(8,128)(2,1)S(1)}, u32[]{:S(2)}, u32[]{:S(2)}) %collective-permute-start) | collective-permute-done | bytes 294944 | tf_op jit(solution)/shard_map/ppermute | solution.py:415
  32.4 0.0 copy-done.9
  32.4 0.0 copy-start.2
  32.4 0.0 copy-start.3
  32.4 0.0 copy-start.5
  32.4 6.0 %outer.1.partial_ref = f32[32,4096]{1,0:T(8,128)S(1)} custom-call(bf16[32,4096]{1,0:T(8,128)(2,1)S(1)} %copy-done.15, bf16[32,4608]{1,0:T(8,128)(2,1)S(1)} %get-tuple-element.18.own_ref, bf16[32,4608]{1,0:T(8,128)(2,1)S(1)} %collective-permute-done.first_ref, bf16[32,4608]{1,0:T(8,128)(2,1)S(1)} %collective-permute-done.1.second_ref, ...), custom_call_target="tpu_custom_call" | custom-call | flops 4000000000 | bytes 12194816 | tf_op jit(solution)/shard_map/outer/pallas_call | solution.py:370
  38.5 0.0 copy-start.10
  38.5 0.8 %copy-done.10 = f32[32,4096]{1,0:T(8,128)} copy-done((f32[32,4096]{1,0:T(8,128)}, f32[32,4096]{1,0:T(8,128)S(1)}, u32[]{:S(2)}) %copy-start.10) | copy-done | bytes 524312
  39.3 0.0 all-to-all-done.gathered_ref
  39.3 0.0 copy-done.2
  39.3 0.0 copy-done.3
  39.3 0.0 copy-done.5
  39.3 0.0 copy-start.11
  39.3 1.0 %copy-done.11 = f32[32,4096]{1,0:T(8,128)S(1)} copy-done((f32[32,4096]{1,0:T(8,128)S(1)}, f32[32,4096]{1,0:T(8,128)}, u32[]{:S(2)}) %copy-start.11) | copy-done | bytes 524312
  40.3 0.0 copy-start.13
  40.3 0.9 %copy-done.13 = bf16[32,4096]{1,0:T(8,128)(2,1)S(1)} copy-done((bf16[32,4096]{1,0:T(8,128)(2,1)S(1)}, bf16[32,4096]{1,0:T(8,128)(2,1)}, u32[]{:S(2)}) %copy-start.13) | copy-done | bytes 262168
  41.3 2.5 %top.1 = f32[32,4096]{1,0:T(8,128)} custom-call(bf16[8,32,128]{2,1,0:T(8,128)(2,1)S(1)} %all-to-all-done.gathered_ref, bf16[14,32,32]{2,1,0:T(8,128)(2,1)S(1)} %bitcast.10, bf16[6,15,32,32]{3,2,1,0:T(8,128)(2,1)S(1)} %bitcast.9, s32[6,15]{1,0:T(8,128)S(1)} %bitcast.12, f32[32,4096]{1,0:T(8,128)S(1)} %copy-done.11, bf16[32,4096]{1,0:T(8,128)(2,1)S(1)} %copy-done.13), custom_call_target="tpu_custom_call" | custom-call | flops 1000000000 | bytes 1065320 | tf_op jit(solution)/shard_map/top/pallas_call | solution.py:370
Async XLA Ops:
  6.2 1.3 %copy-start.7 = (bf16[8,256,512]{2,1,0:T(8,128)(2,1)}, bf16[8,256,512]{2,1,0:T(8,128)(2,1)S(1)}, u32[]{:S(2)}) copy-start(bf16[8,256,512]{2,1,0:T(8,128)(2,1)S(1)} %get-tuple-element.24.masked_ref) | copy-start | bytes 6291460
  7.5 0.7 %copy-start.14 = (bf16[32,4096]{1,0:T(8,128)(2,1)}, bf16[32,4096]{1,0:T(8,128)(2,1)S(1)}, u32[]{:S(2)}) copy-start(bf16[32,4096]{1,0:T(8,128)(2,1)S(1)} %get-tuple-element.17.ordered_ref) | copy-start | bytes 786436
  8.2 31.0 %all-to-all-start = ((bf16[8,32,128]{2,1,0:T(8,128)(2,1)}), bf16[8,32,128]{2,1,0:T(8,128)(2,1)S(1)}, u32[]{:S(2)}, u32[]{:S(2)}) async-start(bf16[8,32,128]{2,1,0:T(8,128)(2,1)} %get-tuple-element.16), calls=%async_computation | async-start | bytes 131072 | tf_op jit(solution)/shard_map/all_to_all | solution.py:412
  15.5 13.2 %collective-permute-start.1 = (bf16[32,4608]{1,0:T(8,128)(2,1)S(1)}, bf16[32,4608]{1,0:T(8,128)(2,1)S(1)}, u32[]{:S(2)}, u32[]{:S(2)}) collective-permute-start(bf16[32,4608]{1,0:T(8,128)(2,1)S(1)} %get-tuple-element.19), channel_id=1, source_target_pairs={{2,4},{6,8},{10,12},{4,2},{8,6},{12,10},{3,5},{7,9},{11,13},{5,3},... | collective-permute-start | bytes 884744 | tf_op jit(solution)/shard_map/ppermute | solution.py:416
  16.2 16.2 %collective-permute-start = (bf16[32,4608]{1,0:T(8,128)(2,1)S(1)}, bf16[32,4608]{1,0:T(8,128)(2,1)S(1)}, u32[]{:S(2)}, u32[]{:S(2)}) collective-permute-start(bf16[32,4608]{1,0:T(8,128)(2,1)S(1)} %get-tuple-element.18.own_ref), channel_id=1, source_target_pairs={{0,2},{4,6},{8,10},{12,14},{2,0},{6,4},{10,8},{14,12},{1,3},{5,7},... | collective-permute-start | bytes 884744 | tf_op jit(solution)/shard_map/ppermute | solution.py:415
  20.9 1.6 %copy-start.8 = (bf16[8,256,512]{2,1,0:T(8,128)(2,1)S(1)}, bf16[8,256,512]{2,1,0:T(8,128)(2,1)}, u32[]{:S(2)}) copy-start(bf16[8,256,512]{2,1,0:T(8,128)(2,1)} %copy-done.7) | copy-start | bytes 6291460
  22.5 2.7 %copy-start.1 = (bf16[6,32,32,126]{3,2,1,0:T(8,128)(2,1)S(1)}, bf16[6,32,32,126]{3,2,1,0:T(8,128)(2,1)}, u32[]{:S(2)}) copy-start(bf16[6,32,32,126]{3,2,1,0:T(8,128)(2,1)} %param.17) | copy-start | bytes 4644868
  22.5 2.7 %copy-start.4 = (s32[126,6]{0,1:T(8,128)S(1)}, s32[126,6]{0,1:T(8,128)}, u32[]{:S(2)}) copy-start(s32[126,6]{0,1:T(8,128)} %param.18) | copy-start | bytes 9076
  25.3 0.7 %copy-start.12 = (bf16[32,4096]{1,0:T(8,128)(2,1)}, bf16[32,4096]{1,0:T(8,128)(2,1)S(1)}, u32[]{:S(2)}) copy-start(bf16[32,4096]{1,0:T(8,128)(2,1)S(1)} %get-tuple-element.26.reach_ref) | copy-start | bytes 786436
  25.3 1.7 %copy-start = (bf16[64,64,256]{2,1,0:T(8,128)(2,1)S(1)}, bf16[64,64,256]{2,1,0:T(8,128)(2,1)}, u32[]{:S(2)}) copy-start(bf16[64,64,256]{2,1,0:T(8,128)(2,1)} %blocks_ref.3) | copy-start | bytes 6291460
  25.3 1.7 %copy-start.6 = (s32[64,4]{0,1:T(4,128)S(1)}, s32[64,4]{0,1:T(4,128)}, u32[]{:S(2)}) copy-start(s32[64,4]{0,1:T(4,128)} %param.15) | copy-start | bytes 3076
  25.3 1.7 %copy-start.15 = (bf16[32,4096]{1,0:T(8,128)(2,1)S(1)}, bf16[32,4096]{1,0:T(8,128)(2,1)}, u32[]{:S(2)}) copy-start(bf16[32,4096]{1,0:T(8,128)(2,1)} %copy-done.14) | copy-start | bytes 786436
  27.0 5.4 %copy-start.9 = (bf16[8,256,512]{2,1,0:T(8,128)(2,1)S(1)}, bf16[8,256,512]{2,1,0:T(8,128)(2,1)}, u32[]{:S(2)}) copy-start(bf16[8,256,512]{2,1,0:T(8,128)(2,1)} %copy-done.7) | copy-start | bytes 6291460
  32.4 6.9 %copy-start.2 = (bf16[6,32,32,15]{2,1,3,0:T(8,128)(2,1)S(1)}, bf16[6,32,32,15]{2,1,3,0:T(8,128)(2,1)}, u32[]{:S(2)}) copy-start(bf16[6,32,32,15]{2,1,3,0:T(8,128)(2,1)} %param.20) | copy-start | bytes 552964
  32.4 6.9 %copy-start.3 = (bf16[32,32,14]{1,0,2:T(8,128)(2,1)S(1)}, bf16[32,32,14]{1,0,2:T(8,128)(2,1)}, u32[]{:S(2)}) copy-start(bf16[32,32,14]{1,0,2:T(8,128)(2,1)} %param.19) | copy-start | bytes 86020
  32.4 6.9 %copy-start.5 = (s32[15,6]{0,1:T(8,128)S(1)}, s32[15,6]{0,1:T(8,128)}, u32[]{:S(2)}) copy-start(s32[15,6]{0,1:T(8,128)} %param.21) | copy-start | bytes 1084
  38.5 0.8 %copy-start.10 = (f32[32,4096]{1,0:T(8,128)}, f32[32,4096]{1,0:T(8,128)S(1)}, u32[]{:S(2)}) copy-start(f32[32,4096]{1,0:T(8,128)S(1)} %outer.1.partial_ref) | copy-start | bytes 1572868
  39.3 1.0 %copy-start.11 = (f32[32,4096]{1,0:T(8,128)S(1)}, f32[32,4096]{1,0:T(8,128)}, u32[]{:S(2)}) copy-start(f32[32,4096]{1,0:T(8,128)} %copy-done.10) | copy-start | bytes 1572868
  40.3 0.9 %copy-start.13 = (bf16[32,4096]{1,0:T(8,128)(2,1)S(1)}, bf16[32,4096]{1,0:T(8,128)(2,1)}, u32[]{:S(2)}) copy-start(bf16[32,4096]{1,0:T(8,128)(2,1)} %copy-done.12) | copy-start | bytes 786436

commit v4 on v3

--- a/solution.py
+++ b/solution.py
@@ -106,9 +106,7 @@
     six = dot((four + five).astype(BF), weights_ref[15], NN)
     coeffs[15] = (four + six).astype(BF)
     root = jnp.where(iota((256, 128), 0) == iota((256, 128), 1) * 8 + 6, 1.0, 0.0).astype(BF)
-    tile = dot(coeffs[15], root, NN).astype(BF)
-    for q in range(top_ref.shape[0]):
-        top_ref[q] = tile
+    top_ref[...] = dot(coeffs[15], root, NN).astype(BF)
     for g in range(16):
         first_ref[:, halo + g * 256 : halo + (g + 1) * 256] = coeffs[g]
         second_ref[:, halo + g * 256 : halo + (g + 1) * 256] = coeffs[g]
@@ -151,10 +149,17 @@
     leaves_ref[first + 1] = pltpu.roll(chunk, 64, 1)
 
 
-def matrices_kernel(coupling_ref, lists_ref, matrices_ref, spots_ref, rows32):
+def matrices_kernel(
+    coupling_ref, lists_ref, inverse_ref, top_ref, matrices_ref, spots_ref, hot_ref, copies_ref, rows32,
+):
     rank = 32
     device = lax.axis_index("leaf")
     count = 64
+
+    for q in range(copies_ref.shape[0]):
+        copies_ref[q] = top_ref[...]
+    for c in range(hot_ref.shape[0]):
+        hot_ref[c] = one_hot(inverse_ref[16 + c : 17 + c, :])
 
     node = iota((1, 128), 1)
     size = jnp.full((1, 128), count, jnp.int32)
@@ -204,31 +209,45 @@
     lax.fori_loop(edge, count // 4 - edge, near, 0, unroll=4)
 
 
-def reach_kernel(weights_ref, masked_ref, inverse_ref, hot_ref, reach_ref, stacked):
-    rank, points = reach_ref.shape
-    unit = jnp.where(iota((rank, 256), 1) == iota((rank, 256), 0) * 8 + 6, 1.0, 0.0)
-    five = dot(unit.astype(BF), weights_ref[15], NT)
-    down = [None] * 16
-    down[15] = dot((unit + five).astype(BF), weights_ref[15], NT).astype(BF)
-    for k in reversed(range(15)):
-        down[k] = dot(down[8 + k // 2], weights_ref[k], NT).astype(BF)
-    for g in range(points // 512):
-        at_points = dot(down[g], masked_ref[g], NN).astype(BF)
-        stacked[2 * g * rank : (2 * g + 1) * rank, :] = at_points[:, :256]
-        stacked[(2 * g + 1) * rank : (2 * g + 2) * rank, :] = at_points[:, 256:]
-    for c in range(points // 256):
-        hot = one_hot(inverse_ref[16 + c : 17 + c, :])
-        hot_ref[c] = hot
-        reach_ref[:, c * 256 : (c + 1) * 256] = pick(
-            stacked[...], hot, inverse_ref[c : c + 1, :], rank
-        ).astype(BF)
+def root_part(gathered_ref, transfer_ref, coupling_ref, lists_ref, coeffs, device):
+    node_count, columns = gathered_ref.shape[:2]
+    total = 2 * node_count - 1
+    coeffs[total] = jnp.zeros((columns, 32), F32)
+    values = [gathered_ref[q][:, :32] for q in range(node_count)]
+    start, count = 0, node_count
+    starts = [(0, node_count)]
+    for j in range(node_count):
+        coeffs[j] = values[j].astype(F32)
+    while count > 1:
+        for j in range(count // 2):
+            left, right = start + 2 * j, start + 2 * j + 1
+            lifted = dot(values[left], transfer_ref[left], NN) + dot(values[right], transfer_ref[right], NN)
+            values.append(lifted.astype(BF))
+            coeffs[start + count + j] = values[-1].astype(F32)
+        start, count = start + count, count // 2
+        starts.append((start, count))
+    fields = []
+    for level, (start, count) in enumerate(starts):
+        node = start + (device >> level)
+        field = None
+        for s in range(6):
+            entry = lists_ref[s, node]
+            spot = jnp.where(entry >= 0, start + entry, total)
+            term = dot(coeffs[spot].astype(BF), coupling_ref[s, node], NT)
+            field = term if field is None else field + term
+        fields.append((node, field))
+    down = fields.pop()[1].astype(BF)
+    for node, field in reversed(fields):
+        down = (field + dot(down, transfer_ref[node], NT)).astype(BF)
+    return down
 
 
 def outer_kernel(
     ordered_ref, own_ref, first_ref, second_ref, near_in, blocks_ref, near_ref, matrices_ref,
     spots_ref, inverse_ref, weights_ref, masked_ref, hot_ref,
-    partial_ref,
-    leaves, nodes, far, stacked, stacked_nodes, edges, sems,
+    gathered_ref, top_transfer_ref, top_coupling_ref, top_lists_ref,
+    applied_ref,
+    leaves, nodes, far, stacked, stacked_nodes, edges, coeffs, sems,
 ):
     columns, points = ordered_ref.shape
     halo = first_ref.shape[1] - 4096
@@ -240,6 +259,10 @@
     ]
     for copy in copies:
         copy.start()
+
+    root = root_part(gathered_ref, top_transfer_ref, top_coupling_ref, top_lists_ref, coeffs, device)
+    sixth = jnp.where(iota((32, 256), 1) == iota((32, 256), 0) * 8 + 6, 1.0, 0.0).astype(BF)
+    six = dot(root, sixth, NN)
 
     odd = device % 2
     for ref, right in ((first_ref, 1 - odd), (second_ref, odd)):
@@ -265,7 +288,7 @@
     lane_group = iota((columns, 128), 1) >> 5
     lane_node = iota((columns, 256), 1) & 7
 
-    def couple(g, carry):
+    for g in range(16):
         picked = []
         for i in range(8):
             parts = [nodes[spots_ref[s, g * 8 + i]] for s in range(6)]
@@ -279,17 +302,15 @@
         total = out[:columns]
         for i in range(1, 8):
             total = jnp.where(lane_node == i, out[i * columns : (i + 1) * columns], total)
-        far[:, pl.ds(pl.multiple_of(g * 256, 256), 256)] = total
-        return carry
-
-    lax.fori_loop(0, 16, couple, 0, unroll=4)
+        far[:, g * 256 : (g + 1) * 256] = total
 
     for copy in copies:
         copy.wait()
     down = [None] * 16
     last = far[:, 15 * 256 :]
-    five = jnp.where(lane_node >= 4, last, 0.0).astype(BF)
-    down[15] = (last + dot(five, weights_ref[15], NT)).astype(BF)
+    five = last + dot(six.astype(BF), weights_ref[15], NT)
+    five = jnp.where(lane_node >= 4, five, 0.0) + six
+    down[15] = (last + dot(five.astype(BF), weights_ref[15], NT)).astype(BF)
     for k in reversed(range(15)):
         down[k] = (far[:, k * 256 : (k + 1) * 256] + dot(down[8 + k // 2], weights_ref[k], NT)).astype(BF)
     groups = count // 4
@@ -312,51 +333,11 @@
         stacked[g * columns : (g + 1) * columns, :] = (near + half).astype(BF)
 
     for c in range(points // 256):
-        partial_ref[:, c * 256 : (c + 1) * 256] = pick(
+        applied_ref[:, c * 256 : (c + 1) * 256] = pick(
             stacked[...], hot_ref[c], inverse_ref[c : c + 1, :], columns
         )
 
 
-def top_kernel(
-    gathered_ref, transfer_ref, coupling_ref, lists_ref, partial_ref, reach_ref, out_ref, coeffs,
-):
-    node_count = gathered_ref.shape[0]
-    columns = gathered_ref.shape[1]
-    device = lax.axis_index("leaf")
-    total = 2 * node_count - 1
-    for q in range(node_count):
-        coeffs[q] = gathered_ref[q][:, :32].astype(F32)
-    start, count = 0, node_count
-    while count > 1:
-        for j in range(count // 2):
-            lifted = dot(coeffs[start + 2 * j].astype(BF), transfer_ref[start + 2 * j], NN)
-            lifted += dot(coeffs[start + 2 * j + 1].astype(BF), transfer_ref[start + 2 * j + 1], NN)
-            coeffs[start + count + j] = lifted.astype(BF).astype(F32)
-        start, count = start + count, count // 2
-    coeffs[total] = jnp.zeros((columns, 32), F32)
-    starts, start, count = [], 0, node_count
-    while count >= 1:
-        starts.append((start, count))
-        start, count = start + count, count // 2
-    down = None
-    for level, (start, count) in reversed(list(enumerate(starts))):
-        node = start + (device >> level)
-        field = None
-        for s in range(6):
-            entry = lists_ref[s, node]
-            spot = jnp.where(entry >= 0, start + entry, total)
-            term = dot(coeffs[spot].astype(BF), coupling_ref[s, node], NT)
-            field = term if field is None else field + term
-        if down is not None:
-            field = field + dot(down, transfer_ref[node], NT)
-        down = field.astype(BF)
-
-    points = out_ref.shape[1]
-    for c in range(points // 512):
-        at = pl.ds(c * 512, 512)
-        out_ref[:, at] = partial_ref[:, at] + dot(down, reach_ref[:, at], NN)
-
-
 VMEM = pl.BlockSpec(memory_space=pltpu.VMEM)
 SMEM = pl.BlockSpec(memory_space=pltpu.SMEM)
 
@@ -365,7 +346,7 @@
     return pltpu.with_memory_space_constraint(x, pltpu.HBM)
 
 
-def call(kernel, outs, scratch, specs, flops, name, args, mib=36):
+def call(kernel, outs, scratch, specs, flops, name, args, mib=16):
     size = sum(a.size * a.dtype.itemsize for a in args)
     return pl.pallas_call(
         kernel,
@@ -397,7 +378,7 @@
     ordered, first, second, top, weights, masked, inverse = call(
         up_kernel,
         [
-            ((columns, points), BF), ((columns, packed), BF), ((columns, packed), BF), ((devices, columns, 128), BF),
+            ((columns, points), BF), ((columns, packed), BF), ((columns, packed), BF), ((columns, 128), BF),
             ((16, 256, 256), BF), ((points // 512, 256, 512), BF), ((32, 256), jnp.int32),
         ],
         [
@@ -409,53 +390,42 @@
         [pl.BlockSpec(memory_space=pl.ANY)] * 4, 10**9, "up",
         tuple(in_hbm(x) for x in (vectors, order, leaf_basis, moves)),
     )
-    gathered = lax.all_to_all(top, "leaf", 0, 0)
     evens = [(i, i + 1) for i in range(0, devices - 1, 2)]
     odds = [(i, i + 1) for i in range(1, devices - 1, 2)]
     from_first = lax.ppermute(first, "leaf", evens + [(j, i) for i, j in evens])
     from_second = lax.ppermute(second, "leaf", odds + [(j, i) for i, j in odds])
 
-    coupling_rows, spots = call(
-        matrices_kernel, [((16, 256, 256), BF), ((8, 128), jnp.int32)],
+    coupling_rows, spots, hot, copies = call(
+        matrices_kernel,
+        [
+            ((16, 256, 256), BF), ((8, 128), jnp.int32), ((points // 256, 256, 256), BF),
+            ((devices, columns, 128), BF),
+        ],
         [pltpu.VMEM((rank, 128, 256), F32)],
-        [VMEM, VMEM], 3 * 10**9, "matrices", (matrices, lists_t),
-    )
+        [VMEM] * 4, 3 * 10**9, "matrices", (matrices, lists_t, inverse, top),
+    )
+    gathered = lax.all_to_all(copies, "leaf", 0, 0)
     (near_part,) = call(
         near_kernel, [((columns, points), F32)],
         [pltpu.VMEM((points // 64, columns, 128), F32)],
         [VMEM, VMEM, SMEM], 3 * 10**9, "near", (ordered, near_blocks, near_t),
     )
-    hot, reach = call(
-        reach_kernel, [((points // 256, 256, 256), BF), ((rank, points), BF)],
-        [pltpu.VMEM((points // 256 * rank, 256), BF)],
-        [VMEM, VMEM, VMEM], 4 * 10**9, "reach", (weights, masked, inverse),
-    )
-    (partial,) = call(
+    (applied,) = call(
         outer_kernel,
         [((columns, points), F32)],
         [
             pltpu.VMEM((points // 64 + 2 * REACH, columns, 128), F32),
             pltpu.VMEM((385, columns, 128), F32), pltpu.VMEM((columns, 4096), F32),
             pltpu.VMEM((points // 256 * columns, 256), BF), pltpu.VMEM((16 * columns, 256), BF),
-            pltpu.VMEM((2, REACH) + near_blocks.shape[1:], BF), pltpu.SemaphoreType.DMA((2,)),
+            pltpu.VMEM((2, REACH) + near_blocks.shape[1:], BF),
+            pltpu.VMEM((2 * devices, columns, 32), F32), pltpu.SemaphoreType.DMA((2,)),
         ],
-        [
-            VMEM, VMEM, VMEM, VMEM, VMEM, pl.BlockSpec(memory_space=pl.ANY), SMEM, VMEM,
-            SMEM, VMEM, VMEM, VMEM, VMEM,
-        ], 4 * 10**9, "outer",
+        [VMEM] * 5 + [pl.BlockSpec(memory_space=pl.ANY), SMEM, VMEM, SMEM] + [VMEM] * 7 + [SMEM],
+        4 * 10**9, "outer",
         (
             ordered, first, from_first, from_second, near_part, in_hbm(near_blocks), near_t, coupling_rows,
-            spots, inverse, weights, masked, hot,
-        ),
-    )
-    (applied,) = call(
-        top_kernel,
-        [((columns, points), F32)],
-        [pltpu.VMEM((2 * devices, columns, 32), F32)],
-        [VMEM, VMEM, VMEM, SMEM, VMEM, VMEM], 10**9, "top",
-        (
-            gathered, jnp.transpose(top_transfers, (2, 0, 1)), jnp.transpose(top_couplings, (0, 3, 1, 2)),
-            jnp.transpose(top_lists), partial, reach,
+            spots, inverse, weights, masked, hot, gathered, jnp.transpose(top_transfers, (2, 0, 1)),
+            jnp.transpose(top_couplings, (0, 3, 1, 2)), jnp.transpose(top_lists),
         ),
     )
     return applied

time: 44.2 us -> 50.1 us (1.13)
  local copies, waits for them, and re-layouts: 7.41 us -> 17.1 us
  Pallas kernels: 19.8 us -> 17.7 us
  starting transfers between devices: 12.7 us -> 11.1 us
    unnamed x32 -> x40, local copies, waits for them, and re-layouts: 7.41 us -> 17.1 us
    ppermute x1, waiting for transfers between devices: 3.73 us -> 0.01 us  [local(): from_first = lax.ppermute(first, 'leaf', evens + [(j, i) for i, j in evens])]
    all_to_all x1, waiting for transfers between devices: 0.01 us -> 3.48 us  [local(): gathered = lax.all_to_all(copies, 'leaf', 0, 0)]
    all_to_all x1, starting transfers between devices: 7.27 us -> 4.7 us  [local(): gathered = lax.all_to_all(copies, 'leaf', 0, 0)]
    pallas_call x6 -> x4, Pallas kernels: 19.8 us -> 17.7 us  [call(): pl.pallas_call(kernel, out_shape=[jax.ShapeDtypeStruct(s, t) for s, t in...]
    ppermute x1, starting transfers between devices: 4.78 us -> 5.77 us  [local(): from_first = lax.ppermute(first, 'leaf', evens + [(j, i) for i, j in evens])]
  transfers between devices with their start and end apart: 3 -> 3, of which waited for: 1 -> 1; matrix products, arithmetic and copies ran while one was open for 0% -> 0% of each run, Pallas kernels for 25% -> 6%
where the time goes in v4:
time: 50.1 us; the launch traced here: 49.6 us
  Pallas kernels  17.7 us (35%)
  local copies, waits for them, and re-layouts  17.1 us (34%)
  starting transfers between devices  11.1 us (22%)
  waiting for transfers between devices  3.49 us (7%)
    pallas_call x4, Pallas kernels, call(): pl.pallas_call(kernel, out_shape=[jax.ShapeDtypeStruct(s, t) for s, t in...  17.7 us
    unnamed x40, local copies, waits for them, and re-layouts  17.1 us
    ppermute x1, starting transfers between devices, local(): from_first = lax.ppermute(first, 'leaf', evens + [(j, i) for i, j in evens])  5.77 us
    all_to_all x1, starting transfers between devices, local(): gathered = lax.all_to_all(copies, 'leaf', 0, 0)  4.7 us
    all_to_all x1, waiting for transfers between devices, local(): gathered = lax.all_to_all(copies, 'leaf', 0, 0)  3.48 us
  transfers between devices with their start and end apart: 3, of which 1 were waited for; matrix products, arithmetic and copies ran while one was open for 0% of the time, Pallas kernels for 6%

profile of v4, /device:TPU:0, one launch (start us, length us, event | category | flops | bytes accessed | tf_op | source)
XLA Modules:
  0.0 49.6 jit_solution(7649509058350685587)
XLA Ops:
  0.0 0.0 copy-start.4
  0.0 0.0 copy-start.1
  0.0 6.4 %up.1 = (bf16[32,4096]{1,0:T(8,128)(2,1)S(1)}, bf16[32,4608]{1,0:T(8,128)(2,1)S(1)}, bf16[32,4608]{1,0:T(8,128)(2,1)}, bf16[32,128]{1,0:T(8,128)(2,1)S(1)}, bf16...) custom-call(bf16[32,4096]{1,0:T(8,128)(2,1)} %vec_hbm.1, ...), custom_call_target="tpu_custom_call" | custom-call | flops 1000000000 | bytes 798720 | tf_op jit(solution)/shard_map/up/pallas_call | solution.py:351
  6.4 0.0 copy-start.7
  6.4 1.3 %copy-done.7 = bf16[16,256,256]{2,1,0:T(8,128)(2,1)} copy-done((bf16[16,256,256]{2,1,0:T(8,128)(2,1)}, bf16[16,256,256]{2,1,0:T(8,128)(2,1)S(1)}, u32[]{:S(2)}) %copy-start.7) | copy-done | bytes 2097176
  7.8 0.0 copy-start.9
  7.8 1.3 %copy-done.9 = bf16[8,256,512]{2,1,0:T(8,128)(2,1)} copy-done((bf16[8,256,512]{2,1,0:T(8,128)(2,1)}, bf16[8,256,512]{2,1,0:T(8,128)(2,1)S(1)}, u32[]{:S(2)}) %copy-start.9) | copy-done | bytes 2097176
  9.1 0.0 copy-start.17
  9.1 0.7 %copy-done.17 = bf16[32,4096]{1,0:T(8,128)(2,1)} copy-done((bf16[32,4096]{1,0:T(8,128)(2,1)}, bf16[32,4096]{1,0:T(8,128)(2,1)S(1)}, u32[]{:S(2)}) %copy-start.17) | copy-done | bytes 262168
  9.8 0.7 %collective-permute-start.1 = (bf16[32,4608]{1,0:T(8,128)(2,1)}, bf16[32,4608]{1,0:T(8,128)(2,1)S(1)}, u32[]{:S(2)}, u32[]{:S(2)}) collective-permute-start(bf16[32,4608]{1,0:T(8,128)(2,1)} %get-tuple-element.18), channel_id=1, source_target_pairs={{2,4},{6,8},{10,12},{4,2},{8,6},{12,10},{3,5},{7,9},{11,13},{5,3},... | collective-permute-start | bytes 884744 | tf_op jit(solution)/shard_map/ppermute | solution.py:396
  10.5 5.8 %collective-permute-start = (bf16[32,4608]{1,0:T(8,128)(2,1)S(1)}, bf16[32,4608]{1,0:T(8,128)(2,1)}, u32[]{:S(2)}, u32[]{:S(2)}) collective-permute-start(bf16[32,4608]{1,0:T(8,128)(2,1)S(1)} %get-tuple-element.17.own_ref), channel_id=1, source_target_pairs={{0,2},{4,6},{8,10},{12,14},{2,0},{6,4},{10,8},{14,12},{1,3},{5,7},... | collective-permute-start | bytes 884744 | tf_op jit(solution)/shard_map/ppermute | solution.py:395
  16.2 0.0 copy-done.4
  16.2 0.0 copy-done.1
  16.2 0.0 copy-start
  16.2 0.0 copy-start.6
  16.3 1.4 %matrices.1 = (bf16[16,256,256]{2,1,0:T(8,128)(2,1)S(1)}, s32[8,128]{1,0:T(8,128)S(1)}, bf16[16,256,256]{2,1,0:T(8,128)(2,1)S(1)}, bf16[8,32,128]{2,1,0:T(8,128)(2,1)}) custom-call(bf16[6,1024,126]{2,1,0:T(8,128)(2,1)S(1)} %bitcast.8, s32[6,126]{1,0:T(8,128)S(1)} %bitcast.11, s32[32,256]{1,0:T(8,128)S(1)} %get-tuple-element.19.inverse_ref, ...), custom_call_target="tpu_custom_call" | custom-call | flops 3000000000 | bytes 1592272 | tf_op jit(solution)/shard_map/matrices/pallas_call | solution.py:351
  17.7 0.0 copy-start.11
  17.7 1.3 %copy-done.11 = bf16[16,256,256]{2,1,0:T(8,128)(2,1)} copy-done((bf16[16,256,256]{2,1,0:T(8,128)(2,1)}, bf16[16,256,256]{2,1,0:T(8,128)(2,1)S(1)}, u32[]{:S(2)}) %copy-start.11) | copy-done | bytes 2097176
  19.0 0.0 copy-start.13
  19.0 1.4 %copy-done.13 = bf16[16,256,256]{2,1,0:T(8,128)(2,1)} copy-done((bf16[16,256,256]{2,1,0:T(8,128)(2,1)}, bf16[16,256,256]{2,1,0:T(8,128)(2,1)S(1)}, u32[]{:S(2)}) %copy-start.13) | copy-done | bytes 2097176
  20.4 4.7 %all-to-all-start = ((bf16[8,32,128]{2,1,0:T(8,128)(2,1)}), bf16[8,32,128]{2,1,0:T(8,128)(2,1)S(1)}, u32[]{:S(2)}, u32[]{:S(2)}) async-start(bf16[8,32,128]{2,1,0:T(8,128)(2,1)} %get-tuple-element.26), calls=%async_computation | async-start | bytes 131072 | tf_op jit(solution)/shard_map/all_to_all | solution.py:407
  25.1 0.0 copy-done
  25.1 0.0 copy-done.6
  25.1 0.0 copy-start.18
  25.1 0.9 %copy-done.18 = bf16[32,4096]{1,0:T(8,128)(2,1)S(1)} copy-done((bf16[32,4096]{1,0:T(8,128)(2,1)S(1)}, bf16[32,4096]{1,0:T(8,128)(2,1)}, u32[]{:S(2)}) %copy-start.18) | copy-done | bytes 262168
  26.1 0.0 copy-start.2
  26.1 0.0 copy-start.5
  26.1 1.6 %near.1.near_in = f32[32,4096]{1,0:T(8,128)S(1)} custom-call(bf16[32,4096]{1,0:T(8,128)(2,1)S(1)} %copy-done.18, bf16[64,64,256]{2,1,0:T(8,128)(2,1)S(1)} %copy-done, s32[4,64]{1,0:T(4,128)S(1)} %bitcast.13), custom_call_target="tpu_custom_call" | custom-call | flops 3000000000 | bytes 2360320 | tf_op jit(solution)/shard_map/near/pallas_call | solution.py:351
  27.7 0.0 copy-start.15
  27.7 0.8 %copy-done.15 = f32[32,4096]{1,0:T(8,128)} copy-done((f32[32,4096]{1,0:T(8,128)}, f32[32,4096]{1,0:T(8,128)S(1)}, u32[]{:S(2)}) %copy-start.15) | copy-done | bytes 524312
  28.5 3.5 %all-to-all-done.gathered_ref = bf16[8,32,128]{2,1,0:T(8,128)(2,1)S(1)} async-done(((bf16[8,32,128]{2,1,0:T(8,128)(2,1)}), bf16[8,32,128]{2,1,0:T(8,128)(2,1)S(1)}, u32[]{:S(2)}, u32[]{:S(2)}) %all-to-all-start) | async-done | bytes 65568 | tf_op jit(solution)/shard_map/all_to_all | solution.py:407
  32.0 0.0 collective-permute-done.1.second_ref
  32.0 0.0 collective-permute-done.first_ref
  32.0 0.0 copy-done.2
  32.0 0.0 copy-done.5
  32.0 0.0 copy-start.3
  32.0 0.9 %copy-done.3 = bf16[32,32,14]{1,0,2:T(8,128)(2,1)S(1)} copy-done((bf16[32,32,14]{1,0,2:T(8,128)(2,1)S(1)}, bf16[32,32,14]{1,0,2:T(8,128)(2,1)}, u32[]{:S(2)}) %copy-start.3) | copy-done | bytes 28696
  32.9 0.0 copy-start.8
  32.9 1.6 %copy-done.8 = bf16[16,256,256]{2,1,0:T(8,128)(2,1)S(1)} copy-done((bf16[16,256,256]{2,1,0:T(8,128)(2,1)S(1)}, bf16[16,256,256]{2,1,0:T(8,128)(2,1)}, u32[]{:S(2)}) %copy-start.8) | copy-done | bytes 2097176
  34.5 0.0 copy-start.10
  34.5 1.6 %copy-done.10 = bf16[8,256,512]{2,1,0:T(8,128)(2,1)S(1)} copy-done((bf16[8,256,512]{2,1,0:T(8,128)(2,1)S(1)}, bf16[8,256,512]{2,1,0:T(8,128)(2,1)}, u32[]{:S(2)}) %copy-start.10) | copy-done | bytes 2097176
  36.1 0.0 copy-start.12
  36.1 1.6 %copy-done.12 = bf16[16,256,256]{2,1,0:T(8,128)(2,1)S(1)} copy-done((bf16[16,256,256]{2,1,0:T(8,128)(2,1)S(1)}, bf16[16,256,256]{2,1,0:T(8,128)(2,1)}, u32[]{:S(2)}) %copy-start.12) | copy-done | bytes 2097176
  37.7 0.0 copy-start.14
  37.7 1.6 %copy-done.14 = bf16[16,256,256]{2,1,0:T(8,128)(2,1)S(1)} copy-done((bf16[16,256,256]{2,1,0:T(8,128)(2,1)S(1)}, bf16[16,256,256]{2,1,0:T(8,128)(2,1)}, u32[]{:S(2)}) %copy-start.14) | copy-done | bytes 2097176
  39.3 1.0 %copy-done.16 = f32[32,4096]{1,0:T(8,128)S(1)} copy-done((f32[32,4096]{1,0:T(8,128)S(1)}, f32[32,4096]{1,0:T(8,128)}, u32[]{:S(2)}) %copy-start.16) | copy-done | bytes 524312
  40.3 0.9 %copy-done.19 = bf16[32,4096]{1,0:T(8,128)(2,1)S(1)} copy-done((bf16[32,4096]{1,0:T(8,128)(2,1)S(1)}, bf16[32,4096]{1,0:T(8,128)(2,1)}, u32[]{:S(2)}) %copy-start.19) | copy-done | bytes 262168
  41.3 8.3 %outer.1 = f32[32,4096]{1,0:T(8,128)} custom-call(bf16[32,4096]{1,0:T(8,128)(2,1)S(1)} %copy-done.19, bf16[32,4608]{1,0:T(8,128)(2,1)S(1)} %get-tuple-element.17.own_ref, bf16[32,4608]{1,0:T(8,128)(2,1)} %collective-permute-done.first_ref, bf16[32,4608]{1,0:T(8,128)(2,1)S(1)} %collective-permute-done.1.second_ref, f32[32,4096]{1,0:T(8,128)S(1)} %copy-done.16, ...), custom_call_target="tpu_custom_call" | custom-call | flops 4000000000 | bytes 12473704 | tf_op jit(solution)/shard_map/outer/pallas_call | solution.py:351
  (2 shorter events, 0.0 us)
Async XLA Ops:
  0.0 16.2 %copy-start.4 = (s32[126,6]{0,1:T(8,128)S(1)}, s32[126,6]{0,1:T(8,128)}, u32[]{:S(2)}) copy-start(s32[126,6]{0,1:T(8,128)} %param.18) | copy-start | bytes 9076
  0.0 16.2 %copy-start.1 = (bf16[6,32,32,126]{3,2,1,0:T(8,128)(2,1)S(1)}, bf16[6,32,32,126]{3,2,1,0:T(8,128)(2,1)}, u32[]{:S(2)}) copy-start(bf16[6,32,32,126]{3,2,1,0:T(8,128)(2,1)} %param.17) | copy-start | bytes 4644868
  6.4 1.3 %copy-start.7 = (bf16[16,256,256]{2,1,0:T(8,128)(2,1)}, bf16[16,256,256]{2,1,0:T(8,128)(2,1)S(1)}, u32[]{:S(2)}) copy-start(bf16[16,256,256]{2,1,0:T(8,128)(2,1)S(1)} %get-tuple-element.23.weights_ref) | copy-start | bytes 6291460
  7.8 1.3 %copy-start.9 = (bf16[8,256,512]{2,1,0:T(8,128)(2,1)}, bf16[8,256,512]{2,1,0:T(8,128)(2,1)S(1)}, u32[]{:S(2)}) copy-start(bf16[8,256,512]{2,1,0:T(8,128)(2,1)S(1)} %get-tuple-element.24.masked_ref) | copy-start | bytes 6291460
  9.1 0.7 %copy-start.17 = (bf16[32,4096]{1,0:T(8,128)(2,1)}, bf16[32,4096]{1,0:T(8,128)(2,1)S(1)}, u32[]{:S(2)}) copy-start(bf16[32,4096]{1,0:T(8,128)(2,1)S(1)} %get-tuple-element.16.ordered_ref) | copy-start | bytes 786436
  9.8 22.2 %collective-permute-start.1 = (bf16[32,4608]{1,0:T(8,128)(2,1)}, bf16[32,4608]{1,0:T(8,128)(2,1)S(1)}, u32[]{:S(2)}, u32[]{:S(2)}) collective-permute-start(bf16[32,4608]{1,0:T(8,128)(2,1)} %get-tuple-element.18), channel_id=1, source_target_pairs={{2,4},{6,8},{10,12},{4,2},{8,6},{12,10},{3,5},{7,9},{11,13},{5,3},... | collective-permute-start | bytes 884744 | tf_op jit(solution)/shard_map/ppermute | solution.py:396
  10.5 21.5 %collective-permute-start = (bf16[32,4608]{1,0:T(8,128)(2,1)S(1)}, bf16[32,4608]{1,0:T(8,128)(2,1)}, u32[]{:S(2)}, u32[]{:S(2)}) collective-permute-start(bf16[32,4608]{1,0:T(8,128)(2,1)S(1)} %get-tuple-element.17.own_ref), channel_id=1, source_target_pairs={{0,2},{4,6},{8,10},{12,14},{2,0},{6,4},{10,8},{14,12},{1,3},{5,7},... | collective-permute-start | bytes 884744 | tf_op jit(solution)/shard_map/ppermute | solution.py:395
  16.2 8.8 %copy-start = (bf16[64,64,256]{2,1,0:T(8,128)(2,1)S(1)}, bf16[64,64,256]{2,1,0:T(8,128)(2,1)}, u32[]{:S(2)}) copy-start(bf16[64,64,256]{2,1,0:T(8,128)(2,1)} %blocks_ref.3) | copy-start | bytes 6291460
  16.2 8.9 %copy-start.6 = (s32[64,4]{0,1:T(4,128)S(1)}, s32[64,4]{0,1:T(4,128)}, u32[]{:S(2)}) copy-start(s32[64,4]{0,1:T(4,128)} %param.15) | copy-start | bytes 3076
  17.7 1.4 %copy-start.11 = (bf16[16,256,256]{2,1,0:T(8,128)(2,1)}, bf16[16,256,256]{2,1,0:T(8,128)(2,1)S(1)}, u32[]{:S(2)}) copy-start(bf16[16,256,256]{2,1,0:T(8,128)(2,1)S(1)} %get-tuple-element.21.matrices_ref) | copy-start | bytes 6291460
  19.0 1.4 %copy-start.13 = (bf16[16,256,256]{2,1,0:T(8,128)(2,1)}, bf16[16,256,256]{2,1,0:T(8,128)(2,1)S(1)}, u32[]{:S(2)}) copy-start(bf16[16,256,256]{2,1,0:T(8,128)(2,1)S(1)} %get-tuple-element.25.hot_ref) | copy-start | bytes 6291460
  20.4 11.6 %all-to-all-start = ((bf16[8,32,128]{2,1,0:T(8,128)(2,1)}), bf16[8,32,128]{2,1,0:T(8,128)(2,1)S(1)}, u32[]{:S(2)}, u32[]{:S(2)}) async-start(bf16[8,32,128]{2,1,0:T(8,128)(2,1)} %get-tuple-element.26), calls=%async_computation | async-start | bytes 131072 | tf_op jit(solution)/shard_map/all_to_all | solution.py:407
  25.1 1.0 %copy-start.18 = (bf16[32,4096]{1,0:T(8,128)(2,1)S(1)}, bf16[32,4096]{1,0:T(8,128)(2,1)}, u32[]{:S(2)}) copy-start(bf16[32,4096]{1,0:T(8,128)(2,1)} %copy-done.17) | copy-start | bytes 786436
  26.1 5.9 %copy-start.2 = (bf16[6,32,32,15]{2,1,3,0:T(8,128)(2,1)S(1)}, bf16[6,32,32,15]{2,1,3,0:T(8,128)(2,1)}, u32[]{:S(2)}) copy-start(bf16[6,32,32,15]{2,1,3,0:T(8,128)(2,1)} %param.20) | copy-start | bytes 552964
  26.1 6.0 %copy-start.5 = (s32[15,6]{0,1:T(8,128)S(1)}, s32[15,6]{0,1:T(8,128)}, u32[]{:S(2)}) copy-start(s32[15,6]{0,1:T(8,128)} %param.21) | copy-start | bytes 1084
  27.7 0.8 %copy-start.15 = (f32[32,4096]{1,0:T(8,128)}, f32[32,4096]{1,0:T(8,128)S(1)}, u32[]{:S(2)}) copy-start(f32[32,4096]{1,0:T(8,128)S(1)} %near.1.near_in) | copy-start | bytes 1572868
  32.0 0.9 %copy-start.3 = (bf16[32,32,14]{1,0,2:T(8,128)(2,1)S(1)}, bf16[32,32,14]{1,0,2:T(8,128)(2,1)}, u32[]{:S(2)}) copy-start(bf16[32,32,14]{1,0,2:T(8,128)(2,1)} %param.19) | copy-start | bytes 86020
  32.9 1.6 %copy-start.8 = (bf16[16,256,256]{2,1,0:T(8,128)(2,1)S(1)}, bf16[16,256,256]{2,1,0:T(8,128)(2,1)}, u32[]{:S(2)}) copy-start(bf16[16,256,256]{2,1,0:T(8,128)(2,1)} %copy-done.7) | copy-start | bytes 6291460
  34.5 1.6 %copy-start.10 = (bf16[8,256,512]{2,1,0:T(8,128)(2,1)S(1)}, bf16[8,256,512]{2,1,0:T(8,128)(2,1)}, u32[]{:S(2)}) copy-start(bf16[8,256,512]{2,1,0:T(8,128)(2,1)} %copy-done.9) | copy-start | bytes 6291460
  36.1 1.6 %copy-start.12 = (bf16[16,256,256]{2,1,0:T(8,128)(2,1)S(1)}, bf16[16,256,256]{2,1,0:T(8,128)(2,1)}, u32[]{:S(2)}) copy-start(bf16[16,256,256]{2,1,0:T(8,128)(2,1)} %copy-done.11) | copy-start | bytes 6291460
  37.7 1.6 %copy-start.14 = (bf16[16,256,256]{2,1,0:T(8,128)(2,1)S(1)}, bf16[16,256,256]{2,1,0:T(8,128)(2,1)}, u32[]{:S(2)}) copy-start(bf16[16,256,256]{2,1,0:T(8,128)(2,1)} %copy-done.13) | copy-start | bytes 6291460
  39.3 1.0 %copy-start.16 = (f32[32,4096]{1,0:T(8,128)S(1)}, f32[32,4096]{1,0:T(8,128)}, u32[]{:S(2)}) copy-start(f32[32,4096]{1,0:T(8,128)} %copy-done.15) | copy-start | bytes 1572868
  40.3 0.9 %copy-start.19 = (bf16[32,4096]{1,0:T(8,128)(2,1)S(1)}, bf16[32,4096]{1,0:T(8,128)(2,1)}, u32[]{:S(2)}) copy-start(bf16[32,4096]{1,0:T(8,128)(2,1)} %copy-done.17) | copy-start | bytes 786436

commit v5 on v4

--- a/solution.py
+++ b/solution.py
@@ -30,6 +30,12 @@
 
 def one_hot(ids):
     return jnp.where(iota((256, 256), 0) == jnp.broadcast_to(ids, (256, 256)), 1.0, 0.0).astype(BF)
+
+
+def split_ids(order_ref, c, points):
+    ids = jnp.concatenate([order_ref[2 * c : 2 * c + 1, :], order_ref[2 * c + 1 : 2 * c + 2, :]], axis=1)
+    ids = lax.rem(ids, points)
+    return ids >> 8, ids & 255
 
 
 def pick(stacked, hot, high, rows):
@@ -41,24 +47,42 @@
     return total
 
 
-def up_kernel(
-    vec_hbm, order_hbm, basis_hbm, transfer_hbm,
-    ordered_ref, first_ref, second_ref, top_ref, weights_ref, masked_ref, inverse_ref,
-    vec_ref, order_ref, basis_ref, transfer_ref, stacked, rows32, sems,
+def leaf_kernel(
+    vec_hbm, order_hbm, basis_hbm, ordered_ref, message_ref, masked_ref,
+    vec_ref, order_ref, basis_ref, stacked, sems,
 ):
     columns, points = vec_ref.shape
     rank = basis_ref.shape[0]
-    chunks = points // 256
-    halo = first_ref.shape[1] - 4096
-    odd = lax.axis_index("leaf") % 2 == 1
-    pairs = (
-        (transfer_hbm, transfer_ref), (order_hbm, order_ref), (vec_hbm, vec_ref), (basis_hbm, basis_ref),
-    )
+    halo = REACH * 64
+    pairs = ((order_hbm, order_ref), (vec_hbm, vec_ref), (basis_hbm, basis_ref))
     copies = [pltpu.make_async_copy(src, dst, sems.at[i]) for i, (src, dst) in enumerate(pairs)]
     for copy in copies:
         copy.start()
-
     copies[0].wait()
+    copies[1].wait()
+    for block in range(points // 256):
+        stacked[block * columns : (block + 1) * columns, :] = vec_ref[:, block * 256 : (block + 1) * 256]
+    for c in range(points // 256):
+        high, low = split_ids(order_ref, c, points)
+        ordered_ref[:, c * 256 : (c + 1) * 256] = pick(stacked[...], one_hot(low), high, columns).astype(BF)
+
+    copies[2].wait()
+    mine = (iota((256, 512), 0) & 7) == (iota((256, 512), 1) >> 6)
+    for g in range(points // 512):
+        one = basis_ref[:, g * 512 : (g + 1) * 512].astype(F32)
+        eight = jnp.broadcast_to(one[:, None, :], (rank, 8, 512)).reshape(256, 512)
+        masked = jnp.where(mine, eight, 0.0).astype(BF)
+        masked_ref[g] = masked
+        coeffs = dot(ordered_ref[:, g * 512 : (g + 1) * 512], masked, NT).astype(BF)
+        message_ref[:, 2 * halo + g * 256 : 2 * halo + (g + 1) * 256] = coeffs
+    message_ref[:, :halo] = ordered_ref[:, :halo]
+    message_ref[:, halo : 2 * halo] = ordered_ref[:, points - halo :]
+
+
+def lift_kernel(message_ref, transfer_ref, lifted_ref, top_ref, weights_ref, rows32):
+    rank = 32
+    base = 2 * REACH * 64
+
     lane, row = iota((128, 256), 1), iota((128, 256), 0)
     family = (lane & 7) == ((row >> 1) & 7)
     spread = [
@@ -66,38 +90,12 @@
         for q in range(4)
     ]
     for m in range(rank // 4):
-        turned = pad_lanes(transfer_ref[pl.ds(m * 4 * rank, 4 * rank), :].astype(F32)).T.astype(BF)
+        turned = pad_lanes(transfer_ref[m * 4 * rank : (m + 1) * 4 * rank, :].astype(F32)).T.astype(BF)
         for q in range(4):
             rows32[m * 4 + q] = jnp.where(family, dot(turned, spread[q], NN), 0.0)
     for k in range(16):
         weights_ref[k] = rows32[:, k * 8 : k * 8 + 8, :].reshape(256, 256).astype(BF)
-
-    copies[1].wait()
-    copies[2].wait()
-    for block in range(chunks):
-        stacked[block * columns : (block + 1) * columns, :] = vec_ref[:, block * 256 : (block + 1) * 256]
-    within = iota((16, 256), 1).astype(F32)
-    inverse = jnp.zeros((32, 256), F32)
-    for c in range(chunks):
-        ids = jnp.concatenate([order_ref[2 * c : 2 * c + 1, :], order_ref[2 * c + 1 : 2 * c + 2, :]], axis=1)
-        ids = lax.rem(ids, points)
-        high, low = ids >> 8, ids & 255
-        hot = one_hot(low)
-        ordered_ref[:, c * 256 : (c + 1) * 256] = pick(stacked[...], hot, high, columns).astype(BF)
-        hit = iota((16, 256), 0) == jnp.broadcast_to(high, (16, 256))
-        marks = jnp.concatenate([jnp.where(hit, float(c), 0.0), jnp.where(hit, within, 0.0)], axis=0)
-        inverse = inverse + dot(marks.astype(BF), hot, NT)
-    inverse_ref[...] = inverse.astype(jnp.int32)
-
-    copies[3].wait()
-    mine = (iota((256, 512), 0) & 7) == (iota((256, 512), 1) >> 6)
-    coeffs = [None] * 16
-    for g in range(points // 512):
-        one = basis_ref[:, g * 512 : (g + 1) * 512].astype(F32)
-        eight = jnp.broadcast_to(one[:, None, :], (rank, 8, 512)).reshape(256, 512)
-        masked = jnp.where(mine, eight, 0.0).astype(BF)
-        masked_ref[g] = masked
-        coeffs[g] = dot(ordered_ref[:, g * 512 : (g + 1) * 512], masked, NT).astype(BF)
+    coeffs = [message_ref[:, base + g * 256 : base + (g + 1) * 256] for g in range(8)] + [None] * 8
     for n in range(7):
         lifted = dot(coeffs[2 * n], weights_ref[2 * n], NN) + dot(coeffs[2 * n + 1], weights_ref[2 * n + 1], NN)
         coeffs[8 + n] = lifted.astype(BF)
@@ -106,21 +104,9 @@
     six = dot((four + five).astype(BF), weights_ref[15], NN)
     coeffs[15] = (four + six).astype(BF)
     root = jnp.where(iota((256, 128), 0) == iota((256, 128), 1) * 8 + 6, 1.0, 0.0).astype(BF)
-    top_ref[...] = dot(coeffs[15], root, NN).astype(BF)
-    for g in range(16):
-        first_ref[:, halo + g * 256 : halo + (g + 1) * 256] = coeffs[g]
-        second_ref[:, halo + g * 256 : halo + (g + 1) * 256] = coeffs[g]
-    low_edge, high_edge = ordered_ref[:, :halo], ordered_ref[:, points - halo :]
-
-    @pl.when(odd)
-    def _():
-        first_ref[:, :halo] = low_edge
-        second_ref[:, :halo] = high_edge
-
-    @pl.when(jnp.logical_not(odd))
-    def _():
-        first_ref[:, :halo] = high_edge
-        second_ref[:, :halo] = low_edge
+    top_ref[0] = dot(coeffs[15], root, NN).astype(BF)
+    for g in range(8):
+        lifted_ref[:, g * 256 : (g + 1) * 256] = coeffs[8 + g]
 
 
 def near_group(leaves_ref, lists_ref, blocks, first, base, columns):
@@ -150,16 +136,24 @@
 
 
 def matrices_kernel(
-    coupling_ref, lists_ref, inverse_ref, top_ref, matrices_ref, spots_ref, hot_ref, copies_ref, rows32,
+    coupling_ref, lists_ref, order_ref, matrices_ref, spots_ref, hot_ref, blocks_ref, rows32,
 ):
     rank = 32
     device = lax.axis_index("leaf")
     count = 64
-
-    for q in range(copies_ref.shape[0]):
-        copies_ref[q] = top_ref[...]
-    for c in range(hot_ref.shape[0]):
-        hot_ref[c] = one_hot(inverse_ref[16 + c : 17 + c, :])
+    chunks = hot_ref.shape[0]
+
+    within = iota((16, 256), 1).astype(F32)
+    inverse = jnp.zeros((32, 256), F32)
+    for c in range(chunks):
+        high, low = split_ids(order_ref, c, chunks * 256)
+        hit = iota((16, 256), 0) == jnp.broadcast_to(high, (16, 256))
+        marks = jnp.concatenate([jnp.where(hit, float(c), 0.0), jnp.where(hit, within, 0.0)], axis=0)
+        inverse = inverse + dot(marks.astype(BF), one_hot(low), NT)
+    inverse = inverse.astype(jnp.int32)
+    blocks_ref[...] = inverse[:16]
+    for c in range(chunks):
+        hot_ref[c] = one_hot(inverse[16 + c : 17 + c, :])
 
     node = iota((1, 128), 1)
     size = jnp.full((1, 128), count, jnp.int32)
@@ -209,15 +203,17 @@
     lax.fori_loop(edge, count // 4 - edge, near, 0, unroll=4)
 
 
-def root_part(gathered_ref, transfer_ref, coupling_ref, lists_ref, coeffs, device):
-    node_count, columns = gathered_ref.shape[:2]
+def root_kernel(near_ref, far_ref, transfer_ref, coupling_ref, lists_ref, six_ref, coeffs):
+    node_count, columns = 2 * near_ref.shape[0], near_ref.shape[1]
+    device = lax.axis_index("leaf")
     total = 2 * node_count - 1
     coeffs[total] = jnp.zeros((columns, 32), F32)
-    values = [gathered_ref[q][:, :32] for q in range(node_count)]
+    for q in range(node_count):
+        ref = near_ref if q < node_count // 2 else far_ref
+        coeffs[q ^ device] = ref[q % (node_count // 2)][:, :32].astype(F32)
+    values = [coeffs[j].astype(BF) for j in range(node_count)]
     start, count = 0, node_count
     starts = [(0, node_count)]
-    for j in range(node_count):
-        coeffs[j] = values[j].astype(F32)
     while count > 1:
         for j in range(count // 2):
             left, right = start + 2 * j, start + 2 * j + 1
@@ -239,18 +235,18 @@
     down = fields.pop()[1].astype(BF)
     for node, field in reversed(fields):
         down = (field + dot(down, transfer_ref[node], NT)).astype(BF)
-    return down
+    sixth = jnp.where(iota((32, 256), 1) == iota((32, 256), 0) * 8 + 6, 1.0, 0.0).astype(BF)
+    six_ref[...] = dot(down, sixth, NN)
 
 
 def outer_kernel(
-    ordered_ref, own_ref, first_ref, second_ref, near_in, blocks_ref, near_ref, matrices_ref,
-    spots_ref, inverse_ref, weights_ref, masked_ref, hot_ref,
-    gathered_ref, top_transfer_ref, top_coupling_ref, top_lists_ref,
+    ordered_ref, own0_ref, own1_ref, first0_ref, first1_ref, second0_ref, second1_ref, near_in, blocks_ref,
+    near_ref, matrices_ref, spots_ref, inverse_ref, weights_ref, masked_ref, hot_ref, six_ref,
     applied_ref,
-    leaves, nodes, far, stacked, stacked_nodes, edges, coeffs, sems,
+    leaves, nodes, far, stacked, stacked_nodes, edges, sems,
 ):
     columns, points = ordered_ref.shape
-    halo = first_ref.shape[1] - 4096
+    halo = REACH * 64
     device = lax.axis_index("leaf")
     count = points // 64
     copies = [
@@ -260,14 +256,11 @@
     for copy in copies:
         copy.start()
 
-    root = root_part(gathered_ref, top_transfer_ref, top_coupling_ref, top_lists_ref, coeffs, device)
-    sixth = jnp.where(iota((32, 256), 1) == iota((32, 256), 0) * 8 + 6, 1.0, 0.0).astype(BF)
-    six = dot(root, sixth, NN)
-
     odd = device % 2
-    for ref, right in ((first_ref, 1 - odd), (second_ref, odd)):
+    for ref, right in ((first0_ref, 1 - odd), (second0_ref, odd)):
         for c in range(halo // 128):
-            place_leaves(leaves, right * (REACH + count) + c * 2, ref[:, c * 128 : (c + 1) * 128])
+            at = pl.multiple_of((1 - right) * halo + c * 128, 128)
+            place_leaves(leaves, right * (REACH + count) + c * 2, ref[:, pl.ds(at, 128)])
     near_ends = REACH * 64 * 2 // 128
     for c in list(range(near_ends)) + list(range(count // 2 - near_ends, count // 2)):
         place_leaves(leaves, REACH + c * 2, ordered_ref[:, c * 128 : (c + 1) * 128])
@@ -275,9 +268,14 @@
     nodes[3 * 128] = jnp.zeros((columns, 128), F32)
     lane, row = iota((256, 1024), 1), iota((256, 1024), 0)
     spread = jnp.where(row == (lane & 31) * 8 + (lane >> 7), 1.0, 0.0).astype(BF)
-    for side, ref in ((1, own_ref), (2 - 2 * odd, first_ref), (2 * odd, second_ref)):
-        for n in range(16):
-            stacked_nodes[n * columns : (n + 1) * columns, :] = ref[:, halo + n * 256 : halo + (n + 1) * 256]
+    sources = (
+        (1, own0_ref, own1_ref), (2 - 2 * odd, first0_ref, first1_ref), (2 * odd, second0_ref, second1_ref),
+    )
+    for side, ref0, ref1 in sources:
+        for n in range(8):
+            at = 2 * halo + n * 256
+            stacked_nodes[n * columns : (n + 1) * columns, :] = ref0[:, at : at + 256]
+            stacked_nodes[(8 + n) * columns : (9 + n) * columns, :] = ref1[:, n * 256 : (n + 1) * 256]
         for c in range(0, 8, 2):
             out = dot(stacked_nodes[...], spread[:, c * 128 : (c + 2) * 128], NN)
             for n in range(16):
@@ -306,6 +304,7 @@
 
     for copy in copies:
         copy.wait()
+    six = six_ref[...]
     down = [None] * 16
     last = far[:, 15 * 256 :]
     five = last + dot(six.astype(BF), weights_ref[15], NT)
@@ -368,47 +367,65 @@
     rank = leaf_basis.shape[0]
     devices = lax.axis_size("leaf")
     halo = REACH * near_blocks.shape[1]
-    packed = halo + 128 * rank
     order = tree_order.reshape(points // 128, 128)
     near_t = jnp.transpose(near_lists)
     lists_t = jnp.transpose(coupling_lists)
     moves = transfers.reshape(rank * rank, -1)
     matrices = couplings.reshape(6, rank * rank, -1)
 
-    ordered, first, second, top, weights, masked, inverse = call(
-        up_kernel,
-        [
-            ((columns, points), BF), ((columns, packed), BF), ((columns, packed), BF), ((columns, 128), BF),
-            ((16, 256, 256), BF), ((points // 512, 256, 512), BF), ((32, 256), jnp.int32),
-        ],
+    any_spec = pl.BlockSpec(memory_space=pl.ANY)
+    ordered, own0, masked = call(
+        leaf_kernel,
+        [((columns, points), BF), ((columns, 2 * halo + 2048), BF), ((points // 512, 256, 512), BF)],
         [
             pltpu.VMEM(vectors.shape, BF), pltpu.VMEM(order.shape, jnp.int32),
-            pltpu.VMEM(leaf_basis.shape, BF), pltpu.VMEM(moves.shape, BF),
-            pltpu.VMEM((points // 256 * columns, 256), BF), pltpu.VMEM((rank, 128, 256), F32),
-            pltpu.SemaphoreType.DMA((4,)),
+            pltpu.VMEM(leaf_basis.shape, BF), pltpu.VMEM((points // 256 * columns, 256), BF),
+            pltpu.SemaphoreType.DMA((3,)),
         ],
-        [pl.BlockSpec(memory_space=pl.ANY)] * 4, 10**9, "up",
-        tuple(in_hbm(x) for x in (vectors, order, leaf_basis, moves)),
-    )
-    evens = [(i, i + 1) for i in range(0, devices - 1, 2)]
-    odds = [(i, i + 1) for i in range(1, devices - 1, 2)]
-    from_first = lax.ppermute(first, "leaf", evens + [(j, i) for i, j in evens])
-    from_second = lax.ppermute(second, "leaf", odds + [(j, i) for i, j in odds])
-
-    coupling_rows, spots, hot, copies = call(
+        [any_spec] * 3, 10**9, "leaf", tuple(in_hbm(x) for x in (vectors, order, leaf_basis)),
+    )
+    pairs = [(i, i ^ 1) for i in range(devices)]
+    onward = [(i, i + 2) for i in range(0, devices - 2, 2)] + [(i, i - 2) for i in range(3, devices, 2)]
+    first0 = lax.ppermute(own0, "leaf", pairs)
+    own1, top, weights = call(
+        lift_kernel,
+        [((columns, 2048), BF), ((1, columns, 128), BF), ((16, 256, 256), BF)],
+        [pltpu.VMEM((rank, 128, 256), F32)], [VMEM, VMEM], 10**9, "lift", (own0, moves),
+    )
+    first1 = lax.ppermute(own1, "leaf", pairs)
+    coupling_rows, spots, hot, blocks = call(
         matrices_kernel,
         [
             ((16, 256, 256), BF), ((8, 128), jnp.int32), ((points // 256, 256, 256), BF),
-            ((devices, columns, 128), BF),
+            ((points // 256, 256), jnp.int32),
         ],
         [pltpu.VMEM((rank, 128, 256), F32)],
-        [VMEM] * 4, 3 * 10**9, "matrices", (matrices, lists_t, inverse, top),
-    )
-    gathered = lax.all_to_all(copies, "leaf", 0, 0)
+        [VMEM] * 3, 3 * 10**9, "matrices", (matrices, lists_t, order),
+    )
+    first0, blocks = lax.optimization_barrier((first0, blocks))
+    second0 = lax.ppermute(first0, "leaf", onward)
+    reached, held = 1, [top]
+    while reached < devices:
+        near_half = held[0] if len(held) == 1 else jnp.concatenate(held, axis=0)
+        far_half = lax.ppermute(near_half, "leaf", [(i, i ^ reached) for i in range(devices)])
+        held = [near_half, far_half]
+        reached *= 2
+
+    first0, ordered_late = lax.optimization_barrier((first0, ordered))
     (near_part,) = call(
         near_kernel, [((columns, points), F32)],
         [pltpu.VMEM((points // 64, columns, 128), F32)],
-        [VMEM, VMEM, SMEM], 3 * 10**9, "near", (ordered, near_blocks, near_t),
+        [VMEM, VMEM, SMEM], 3 * 10**9, "near", (ordered_late, near_blocks, near_t),
+    )
+    first1, near_part = lax.optimization_barrier((first1, near_part))
+    second1 = lax.ppermute(first1, "leaf", onward)
+    (six,) = call(
+        root_kernel, [((columns, 256), F32)], [pltpu.VMEM((2 * devices, columns, 32), F32)],
+        [VMEM] * 4 + [SMEM], 10**9, "root",
+        (
+            *held, jnp.transpose(top_transfers, (2, 0, 1)), jnp.transpose(top_couplings, (0, 3, 1, 2)),
+            jnp.transpose(top_lists),
+        ),
     )
     (applied,) = call(
         outer_kernel,
@@ -417,15 +434,13 @@
             pltpu.VMEM((points // 64 + 2 * REACH, columns, 128), F32),
             pltpu.VMEM((385, columns, 128), F32), pltpu.VMEM((columns, 4096), F32),
             pltpu.VMEM((points // 256 * columns, 256), BF), pltpu.VMEM((16 * columns, 256), BF),
-            pltpu.VMEM((2, REACH) + near_blocks.shape[1:], BF),
-            pltpu.VMEM((2 * devices, columns, 32), F32), pltpu.SemaphoreType.DMA((2,)),
+            pltpu.VMEM((2, REACH) + near_blocks.shape[1:], BF), pltpu.SemaphoreType.DMA((2,)),
         ],
-        [VMEM] * 5 + [pl.BlockSpec(memory_space=pl.ANY), SMEM, VMEM, SMEM] + [VMEM] * 7 + [SMEM],
+        [VMEM] * 8 + [any_spec, SMEM, VMEM, SMEM] + [VMEM] * 5,
         4 * 10**9, "outer",
         (
-            ordered, first, from_first, from_second, near_part, in_hbm(near_blocks), near_t, coupling_rows,
-            spots, inverse, weights, masked, hot, gathered, jnp.transpose(top_transfers, (2, 0, 1)),
-            jnp.transpose(top_couplings, (0, 3, 1, 2)), jnp.transpose(top_lists),
+            ordered, own0, own1, first0, first1, second0, second1, near_part, in_hbm(near_blocks),
+            near_t, coupling_rows, spots, blocks, weights, masked, hot, six,
         ),
     )
     return applied

time: 50.1 us -> 37.2 us (0.74)
  local copies, waits for them, and re-layouts: 17.1 us -> 0.07 us
  starting transfers between devices: 11.1 us -> 14.1 us
  waiting for transfers between devices: 3.49 us -> 5.4 us
    unnamed x40 -> x20, local copies, waits for them, and re-layouts: 17.1 us -> 0.06 us
    ppermute x2 -> x7, starting transfers between devices: 6.44 us -> 14.1 us  [the longest x1 5.04 us: local(): second1 = lax.ppermute(first1, 'leaf', onward)]
    ppermute x2 -> x7, waiting for transfers between devices: 0.01 us -> 5.4 us  [the longest x3 5.36 us: local(): lax.ppermute(near_half, 'leaf', [(i, i ^ reached) for i in range(devices)])]
    all_to_all x1 -> x0, starting transfers between devices: 4.7 us -> none  [local(): gathered = lax.all_to_all(copies, 'leaf', 0, 0)]
    all_to_all x1 -> x0, waiting for transfers between devices: 3.48 us -> none  [local(): gathered = lax.all_to_all(copies, 'leaf', 0, 0)]
    pallas_call x4 -> x6, Pallas kernels: 17.7 us -> 17.2 us  [call(): pl.pallas_call(kernel, out_shape=[jax.ShapeDtypeStruct(s, t) for s, t in...]
  transfers between devices with their start and end apart: 3 -> 7, of which waited for: 1 -> 2; matrix products, arithmetic and copies ran while one was open for 0% -> 0% of each run, Pallas kernels for 6% -> 19%
where the time goes in v5:
time: 37.2 us; the launch traced here: 37 us
  Pallas kernels  17.2 us (46%)
  starting transfers between devices  14.1 us (38%)
  waiting for transfers between devices  5.4 us (15%)
    pallas_call x6, Pallas kernels, call(): pl.pallas_call(kernel, out_shape=[jax.ShapeDtypeStruct(s, t) for s, t in...  17.2 us
    ppermute x3, waiting for transfers between devices, local(): lax.ppermute(near_half, 'leaf', [(i, i ^ reached) for i in range(devices)])  5.36 us
    ppermute x1, starting transfers between devices, local(): second1 = lax.ppermute(first1, 'leaf', onward)  5.04 us
    ppermute x1, starting transfers between devices, local(): first0 = lax.ppermute(own0, 'leaf', pairs)  3.03 us
    ppermute x3, starting transfers between devices, local(): lax.ppermute(near_half, 'leaf', [(i, i ^ reached) for i in range(devices)])  2.15 us
    ppermute x1, starting transfers between devices, local(): first1 = lax.ppermute(own1, 'leaf', pairs)  2 us
    ppermute x1, starting transfers between devices, local(): second0 = lax.ppermute(first0, 'leaf', onward)  1.92 us
  transfers between devices with their start and end apart: 7, of which 2 were waited for; matrix products, arithmetic and copies ran while one was open for 0% of the time, Pallas kernels for 19%

profile of v5, /device:TPU:0, one launch (start us, length us, event | category | flops | bytes accessed | tf_op | source)
XLA Modules:
  0.0 37.0 jit_solution(815753947072955240)
XLA Ops:
  0.0 0.0 copy-start.3
  0.0 3.2 %leaf.1 = (bf16[32,4096]{1,0:T(8,128)(2,1)S(1)}, bf16[32,3072]{1,0:T(8,128)(2,1)S(1)}, bf16[8,256,512]{2,1,0:T(8,128)(2,1)S(1)}) custom-call(bf16[32,4096]{1,0:T(8,128)(2,1)} %vec_hbm.1, s32[32,128]{1,0:T(8,128)} %bitcast.12, bf16[32,4096]{1,0:T(8,128)(2,1)} %basis_hbm.1), custom_call_target="tpu_custom_call" | custom-call | flops 1000000000 | bytes 540672 | tf_op jit(solution)/shard_map/leaf/pallas_call | solution.py:350
  3.2 0.0 copy-start.1
  3.2 0.0 copy-start.5
  3.3 0.0 copy-start.6
  3.3 3.0 %collective-permute-start = (bf16[32,3072]{1,0:T(8,128)(2,1)S(1)}, bf16[32,3072]{1,0:T(8,128)(2,1)S(1)}, u32[]{:S(2)}, u32[]{:S(2)}) collective-permute-start(bf16[32,3072]{1,0:T(8,128)(2,1)S(1)} %get-tuple-element.22.message_ref.own0_ref), channel_id=1, source_target_pairs={{0,2},{2,0},{4,6},{6,4},{8,10},{10,8},{12,14},{14,12},{1,3},{3,1},... | collective-permute-start | bytes 589832 | tf_op jit(solution)/shard_map/ppermute | solution.py:389
  6.3 0.0 copy-done.3
  6.3 1.8 %lift.1 = (bf16[32,2048]{1,0:T(8,128)(2,1)S(1)}, bf16[1,32,128]{2,1,0:T(8,128)(2,1)S(1)}, bf16[16,256,256]{2,1,0:T(8,128)(2,1)S(1)}) custom-call(bf16[32,3072]{1,0:T(8,128)(2,1)S(1)} %get-tuple-element.22.message_ref.own0_ref, bf16[1024,126]{1,0:T(8,128)(2,1)S(1)} %bitcast.10), custom_call_target="tpu_custom_call" | custom-call | flops 1000000000 | bytes 454656 | tf_op jit(solution)/shard_map/lift/pallas_call | solution.py:350
  8.1 0.0 collective-permute-start.4
  8.1 2.0 %collective-permute-start.1 = (bf16[32,2048]{1,0:T(8,128)(2,1)S(1)}, bf16[32,2048]{1,0:T(8,128)(2,1)S(1)}, u32[]{:S(2)}, u32[]{:S(2)}) collective-permute-start(bf16[32,2048]{1,0:T(8,128)(2,1)S(1)} %get-tuple-element.23.own1_ref), channel_id=1, source_target_pairs={{0,2},{2,0},{4,6},{6,4},{8,10},{10,8},{12,14},{14,12},{1,3},{3,1},... | collective-permute-start | bytes 393224 | tf_op jit(solution)/shard_map/ppermute | solution.py:395
  10.1 0.0 copy-done.1
  10.1 0.0 copy-done.5
  10.1 0.0 copy-done.6
  10.1 0.0 copy-start
  10.1 0.0 copy-start.8
  10.1 1.7 %matrices.1 = (bf16[16,256,256]{2,1,0:T(8,128)(2,1)S(1)}, s32[8,128]{1,0:T(8,128)S(1)}, bf16[16,256,256]{2,1,0:T(8,128)(2,1)S(1)}, s32[16,256]{1,0:T(8,128)S(1)}) custom-call(bf16[6,1024,126]{2,1,0:T(8,128)(2,1)S(1)} %bitcast.8, s32[6,126]{1,0:T(8,128)S(1)} %bitcast.14, s32[32,128]{1,0:T(8,128)S(1)} %bitcast.13), custom_call_target="tpu_custom_call" | custom-call | flops 3000000000 | bytes 1567696 | tf_op jit(solution)/shard_map/matrices/pallas_call | solution.py:350
  11.9 0.3 collective-permute-done.4
  12.2 2.0 %collective-permute-start.5 = (bf16[2,32,128]{2,1,0:T(8,128)(2,1)S(1)}, bf16[2,32,128]{2,1,0:T(8,128)(2,1)S(1)}, u32[]{:S(2)}, u32[]{:S(2)}) collective-permute-start(bf16[2,32,128]{2,1,0:T(8,128)(2,1)S(1)} %pad_maximum_fusion), channel_id=1, source_target_pairs={{0,4},{2,6},{4,0},{6,2},{8,12},{10,14},{12,8},{14,10},{1,5},{3,7},... | collective-permute-start | bytes 49160 | tf_op jit(solution)/shard_map/ppermute | solution.py:410
  14.3 0.0 collective-permute-done.first0_ref
  14.3 1.9 %collective-permute-start.2 = (bf16[32,3072]{1,0:T(8,128)(2,1)S(1)}, bf16[32,3072]{1,0:T(8,128)(2,1)S(1)}, u32[]{:S(2)}, u32[]{:S(2)}) collective-permute-start(bf16[32,3072]{1,0:T(8,128)(2,1)S(1)} %collective-permute-done.first0_ref), channel_id=1, source_target_pairs={{0,4},{4,8},{8,12},{6,2},{10,6},{14,10},{1,5},{5,9},{9,13},{7,3},{... | collective-permute-start | bytes 589832 | tf_op jit(solution)/shard_map/ppermute | solution.py:406
  16.2 0.0 copy-done
  16.2 0.0 copy-done.8
  16.2 0.0 copy-start.2
  16.2 0.0 copy-start.4
  16.2 0.0 copy-start.7
  16.3 1.7 %near.1.near_in = f32[32,4096]{1,0:T(8,128)S(1)} custom-call(bf16[32,4096]{1,0:T(8,128)(2,1)S(1)} %get-tuple-element.27.ordered_ref, bf16[64,64,256]{2,1,0:T(8,128)(2,1)S(1)} %copy-done, s32[4,64]{1,0:T(4,128)S(1)} %bitcast.16), custom_call_target="tpu_custom_call" | custom-call | flops 3000000000 | bytes 2360320 | tf_op jit(solution)/shard_map/near/pallas_call | solution.py:350
  17.9 0.0 collective-permute-done.1.first1_ref
  18.0 5.0 %collective-permute-start.3 = (bf16[32,2048]{1,0:T(8,128)(2,1)S(1)}, bf16[32,2048]{1,0:T(8,128)(2,1)S(1)}, u32[]{:S(2)}, u32[]{:S(2)}) collective-permute-start(bf16[32,2048]{1,0:T(8,128)(2,1)S(1)} %collective-permute-done.1.first1_ref), channel_id=1, source_target_pairs={{0,4},{4,8},{8,12},{6,2},{10,6},{14,10},{1,5},{5,9},{9,13},{7,3},{... | collective-permute-start | bytes 393224 | tf_op jit(solution)/shard_map/ppermute | solution.py:421
  23.0 0.0 collective-permute-done.5
  23.0 0.1 collective-permute-start.6
  23.1 5.0 %collective-permute-done.6.far_ref = bf16[4,32,128]{2,1,0:T(8,128)(2,1)S(1)} collective-permute-done((bf16[4,32,128]{2,1,0:T(8,128)(2,1)S(1)}, bf16[4,32,128]{2,1,0:T(8,128)(2,1)S(1)}, u32[]{:S(2)}, u32[]{:S(2)}) %collective-permute-start.6) | collective-permute-done | bytes 32800 | tf_op jit(solution)/shard_map/ppermute | solution.py:410
  28.1 0.0 copy-done.2
  28.1 0.0 copy-done.4
  28.1 0.0 copy-done.7
  28.2 1.7 %root.1.six_ref = f32[32,256]{1,0:T(8,128)S(1)} custom-call(bf16[4,32,128]{2,1,0:T(8,128)(2,1)S(1)} %constant_dynamic-update-slice_fusion.near_ref, bf16[4,32,128]{2,1,0:T(8,128)(2,1)S(1)} %collective-permute-done.6.far_ref, bf16[14,32,32]{2,1,0:T(8,128)(2,1)S(1)} %bitcast.11, bf16[6,15,32,32]{3,2,1,0:T(8,128)(2,1)S(1)} %bitcast.9, s32[6,15]{1,0:T(8,128)S(1)} %bitcast.15), custom_call_target="tpu_custom_call" | custom-call | flops 1000000000 | bytes 278888 | tf_op jit(solution)/shard_map/root/pallas_call | solution.py:350
  29.8 0.0 collective-permute-done.3.second1_ref
  29.8 0.0 collective-permute-done.2.second0_ref
  29.9 7.2 %outer.1 = f32[32,4096]{1,0:T(8,128)} custom-call(bf16[32,4096]{1,0:T(8,128)(2,1)S(1)} %get-tuple-element.27.ordered_ref, bf16[32,3072]{1,0:T(8,128)(2,1)S(1)} %get-tuple-element.22.message_ref.own0_ref, bf16[32,2048]{1,0:T(8,128)(2,1)S(1)} %get-tuple-element.23.own1_ref, bf16[32,3072]{1,0:T(8,128)(2,1)S(1)} %collective-permute-done.first0_ref, ...), custom_call_target="tpu_custom_call" | custom-call | flops 4000000000 | bytes 12309504 | tf_op jit(solution)/shard_map/outer/pallas_call | solution.py:350
  (4 shorter events, 0.0 us)
Async XLA Ops:
  0.0 6.3 %copy-start.3 = (bf16[32,32,126]{2,1,0:T(8,128)(2,1)S(1)}, bf16[32,32,126]{2,1,0:T(8,128)(2,1)}, u32[]{:S(2)}) copy-start(bf16[32,32,126]{2,1,0:T(8,128)(2,1)} %param.16) | copy-start | bytes 774148
  3.2 6.9 %copy-start.1 = (bf16[6,32,32,126]{3,2,1,0:T(8,128)(2,1)S(1)}, bf16[6,32,32,126]{3,2,1,0:T(8,128)(2,1)}, u32[]{:S(2)}) copy-start(bf16[6,32,32,126]{3,2,1,0:T(8,128)(2,1)} %param.17) | copy-start | bytes 4644868
  3.2 6.9 %copy-start.5 = (s32[4096]{0:T(1024)S(1)}, s32[4096]{0:T(1024)}, u32[]{:S(2)}) copy-start(s32[4096]{0:T(1024)} %param.12) | copy-start | bytes 49156
  3.3 6.9 %copy-start.6 = (s32[126,6]{0,1:T(8,128)S(1)}, s32[126,6]{0,1:T(8,128)}, u32[]{:S(2)}) copy-start(s32[126,6]{0,1:T(8,128)} %param.18) | copy-start | bytes 9076
  3.3 11.0 %collective-permute-start = (bf16[32,3072]{1,0:T(8,128)(2,1)S(1)}, bf16[32,3072]{1,0:T(8,128)(2,1)S(1)}, u32[]{:S(2)}, u32[]{:S(2)}) collective-permute-start(bf16[32,3072]{1,0:T(8,128)(2,1)S(1)} %get-tuple-element.22.message_ref.own0_ref), channel_id=1, source_target_pairs={{0,2},{2,0},{4,6},{6,4},{8,10},{10,8},{12,14},{14,12},{1,3},{3,1},... | collective-permute-start | bytes 589832 | tf_op jit(solution)/shard_map/ppermute | solution.py:389
  8.1 4.1 %collective-permute-start.4 = (bf16[1,32,128]{2,1,0:T(8,128)(2,1)S(1)}, bf16[1,32,128]{2,1,0:T(8,128)(2,1)S(1)}, u32[]{:S(2)}, u32[]{:S(2)}) collective-permute-start(bf16[1,32,128]{2,1,0:T(8,128)(2,1)S(1)} %get-tuple-element.36), channel_id=1, source_target_pairs={{0,2},{2,0},{4,6},{6,4},{8,10},{10,8},{12,14},{14,12},{1,3},{3,1},... | collective-permute-start | bytes 24584 | tf_op jit(solution)/shard_map/ppermute | solution.py:410
  8.1 9.8 %collective-permute-start.1 = (bf16[32,2048]{1,0:T(8,128)(2,1)S(1)}, bf16[32,2048]{1,0:T(8,128)(2,1)S(1)}, u32[]{:S(2)}, u32[]{:S(2)}) collective-permute-start(bf16[32,2048]{1,0:T(8,128)(2,1)S(1)} %get-tuple-element.23.own1_ref), channel_id=1, source_target_pairs={{0,2},{2,0},{4,6},{6,4},{8,10},{10,8},{12,14},{14,12},{1,3},{3,1},... | collective-permute-start | bytes 393224 | tf_op jit(solution)/shard_map/ppermute | solution.py:395
  10.1 6.1 %copy-start = (bf16[64,64,256]{2,1,0:T(8,128)(2,1)S(1)}, bf16[64,64,256]{2,1,0:T(8,128)(2,1)}, u32[]{:S(2)}) copy-start(bf16[64,64,256]{2,1,0:T(8,128)(2,1)} %blocks_ref.3) | copy-start | bytes 6291460
  10.1 6.1 %copy-start.8 = (s32[64,4]{0,1:T(4,128)S(1)}, s32[64,4]{0,1:T(4,128)}, u32[]{:S(2)}) copy-start(s32[64,4]{0,1:T(4,128)} %param.15) | copy-start | bytes 3076
  12.2 10.8 %collective-permute-start.5 = (bf16[2,32,128]{2,1,0:T(8,128)(2,1)S(1)}, bf16[2,32,128]{2,1,0:T(8,128)(2,1)S(1)}, u32[]{:S(2)}, u32[]{:S(2)}) collective-permute-start(bf16[2,32,128]{2,1,0:T(8,128)(2,1)S(1)} %pad_maximum_fusion), channel_id=1, source_target_pairs={{0,4},{2,6},{4,0},{6,2},{8,12},{10,14},{12,8},{14,10},{1,5},{3,7},... | collective-permute-start | bytes 49160 | tf_op jit(solution)/shard_map/ppermute | solution.py:410
  14.3 15.6 %collective-permute-start.2 = (bf16[32,3072]{1,0:T(8,128)(2,1)S(1)}, bf16[32,3072]{1,0:T(8,128)(2,1)S(1)}, u32[]{:S(2)}, u32[]{:S(2)}) collective-permute-start(bf16[32,3072]{1,0:T(8,128)(2,1)S(1)} %collective-permute-done.first0_ref), channel_id=1, source_target_pairs={{0,4},{4,8},{8,12},{6,2},{10,6},{14,10},{1,5},{5,9},{9,13},{7,3},{... | collective-permute-start | bytes 589832 | tf_op jit(solution)/shard_map/ppermute | solution.py:406
  16.2 11.9 %copy-start.2 = (bf16[6,32,32,15]{2,1,3,0:T(8,128)(2,1)S(1)}, bf16[6,32,32,15]{2,1,3,0:T(8,128)(2,1)}, u32[]{:S(2)}) copy-start(bf16[6,32,32,15]{2,1,3,0:T(8,128)(2,1)} %param.20) | copy-start | bytes 552964
  16.2 11.9 %copy-start.4 = (bf16[32,32,14]{1,0,2:T(8,128)(2,1)S(1)}, bf16[32,32,14]{1,0,2:T(8,128)(2,1)}, u32[]{:S(2)}) copy-start(bf16[32,32,14]{1,0,2:T(8,128)(2,1)} %param.19) | copy-start | bytes 86020
  16.2 11.9 %copy-start.7 = (s32[15,6]{0,1:T(8,128)S(1)}, s32[15,6]{0,1:T(8,128)}, u32[]{:S(2)}) copy-start(s32[15,6]{0,1:T(8,128)} %param.21) | copy-start | bytes 1084
  18.0 11.9 %collective-permute-start.3 = (bf16[32,2048]{1,0:T(8,128)(2,1)S(1)}, bf16[32,2048]{1,0:T(8,128)(2,1)S(1)}, u32[]{:S(2)}, u32[]{:S(2)}) collective-permute-start(bf16[32,2048]{1,0:T(8,128)(2,1)S(1)} %collective-permute-done.1.first1_ref), channel_id=1, source_target_pairs={{0,4},{4,8},{8,12},{6,2},{10,6},{14,10},{1,5},{5,9},{9,13},{7,3},{... | collective-permute-start | bytes 393224 | tf_op jit(solution)/shard_map/ppermute | solution.py:421
  23.0 5.1 %collective-permute-start.6 = (bf16[4,32,128]{2,1,0:T(8,128)(2,1)S(1)}, bf16[4,32,128]{2,1,0:T(8,128)(2,1)S(1)}, u32[]{:S(2)}, u32[]{:S(2)}) collective-permute-start(bf16[4,32,128]{2,1,0:T(8,128)(2,1)S(1)} %constant_dynamic-update-slice_fusion.near_ref), channel_id=1, source_target_pairs={{0,8},{2,10},{4,12},{6,14},{8,0},{10,2},{12,4},{14,6},{1,9},{3,11}... | collective-permute-start | bytes 98312 | tf_op jit(solution)/shard_map/ppermute | solution.py:410

commit v6 on v5

--- a/solution.py
+++ b/solution.py
@@ -29,7 +29,9 @@
 
 
 def one_hot(ids):
-    return jnp.where(iota((256, 256), 0) == jnp.broadcast_to(ids, (256, 256)), 1.0, 0.0).astype(BF)
+    ids = jnp.broadcast_to(ids.astype(F32), (16, 256)).astype(BF)
+    rows = iota((256, 256), 0).astype(F32).astype(BF)
+    return jnp.where(rows == jnp.concatenate([ids] * 16, axis=0), jnp.ones((), BF), jnp.zeros((), BF))
 
 
 def split_ids(order_ref, c, points):
@@ -103,14 +105,22 @@
     five = dot(four.astype(BF), weights_ref[15], NN)
     six = dot((four + five).astype(BF), weights_ref[15], NN)
     coeffs[15] = (four + six).astype(BF)
-    root = jnp.where(iota((256, 128), 0) == iota((256, 128), 1) * 8 + 6, 1.0, 0.0).astype(BF)
-    top_ref[0] = dot(coeffs[15], root, NN).astype(BF)
+    width = top_ref.shape[1]
+    slot = lax.axis_index("leaf") // 2 * rank
+    row, lane = iota((256, width), 0), iota((256, width), 1) - slot
+    root = jnp.where((row == lane * 8 + 6) & (lane >= 0), 1.0, 0.0).astype(BF)
+    top_ref[...] = dot(coeffs[15], root, NN).astype(BF)
+    lifted_ref[:, 2048:] = jnp.zeros((lifted_ref.shape[0], width), BF)
     for g in range(8):
         lifted_ref[:, g * 256 : (g + 1) * 256] = coeffs[8 + g]
 
 
+def lane_numbers(rows):
+    return iota((rows, 128), 1).astype(F32).astype(BF)
+
+
 def near_group(leaves_ref, lists_ref, blocks, first, base, columns):
-    lane_left = iota((columns, 128), 1) < 64
+    lane_left = lane_numbers(columns) < 64
     picked = []
     for i in range(4):
         spots = [lists_ref[s, first + i] - base for s in range(4)]
@@ -120,8 +130,7 @@
             odd = leaves_ref[spots[s + 1] ^ 1]
             halves.append(jnp.where(lane_left, even, odd))
         picked.append(jnp.concatenate(halves, axis=1))
-    moving = jnp.concatenate(picked, axis=0).astype(BF)
-    out = dot(moving, blocks, NT)
+    out = dot(jnp.concatenate(picked, axis=0), blocks, NT)
     leaf_of_lane = iota((columns, 256), 1) >> 6
     total = out[:columns]
     for i in range(1, 4):
@@ -130,9 +139,8 @@
 
 
 def place_leaves(leaves_ref, first, chunk):
-    chunk = chunk.astype(F32)
     leaves_ref[first] = chunk
-    leaves_ref[first + 1] = pltpu.roll(chunk, 64, 1)
+    leaves_ref[first + 1] = pltpu.roll(chunk.astype(F32), 64, 1).astype(BF)
 
 
 def matrices_kernel(
@@ -203,14 +211,16 @@
     lax.fori_loop(edge, count // 4 - edge, near, 0, unroll=4)
 
 
-def root_kernel(near_ref, far_ref, transfer_ref, coupling_ref, lists_ref, six_ref, coeffs):
-    node_count, columns = 2 * near_ref.shape[0], near_ref.shape[1]
+def root_kernel(own_ref, other_ref, transfer_ref, coupling_ref, lists_ref, six_ref, coeffs):
+    columns, rank = own_ref.shape[0], 32
+    node_count = lists_ref.shape[1] // 2 + 1
     device = lax.axis_index("leaf")
     total = 2 * node_count - 1
-    coeffs[total] = jnp.zeros((columns, 32), F32)
+    coeffs[total] = jnp.zeros((columns, rank), F32)
     for q in range(node_count):
-        ref = near_ref if q < node_count // 2 else far_ref
-        coeffs[q ^ device] = ref[q % (node_count // 2)][:, :32].astype(F32)
+        ref = own_ref if q % 2 == 0 else other_ref
+        at = 2048 + q // 2 * rank
+        coeffs[q ^ (device & 1)] = ref[:, at : at + rank].astype(F32)
     values = [coeffs[j].astype(BF) for j in range(node_count)]
     start, count = 0, node_count
     starts = [(0, node_count)]
@@ -242,8 +252,8 @@
 def outer_kernel(
     ordered_ref, own0_ref, own1_ref, first0_ref, first1_ref, second0_ref, second1_ref, near_in, blocks_ref,
     near_ref, matrices_ref, spots_ref, inverse_ref, weights_ref, masked_ref, hot_ref, six_ref,
-    applied_ref,
-    leaves, nodes, far, stacked, stacked_nodes, edges, sems,
+    applied_hbm,
+    applied_ref, leaves, nodes, far, stacked, stacked_nodes, edges, sems, out_sems,
 ):
     columns, points = ordered_ref.shape
     halo = REACH * 64
@@ -265,7 +275,7 @@
     for c in list(range(near_ends)) + list(range(count // 2 - near_ends, count // 2)):
         place_leaves(leaves, REACH + c * 2, ordered_ref[:, c * 128 : (c + 1) * 128])
 
-    nodes[3 * 128] = jnp.zeros((columns, 128), F32)
+    nodes[3 * 128] = jnp.zeros((columns, 128), BF)
     lane, row = iota((256, 1024), 1), iota((256, 1024), 0)
     spread = jnp.where(row == (lane & 31) * 8 + (lane >> 7), 1.0, 0.0).astype(BF)
     sources = (
@@ -279,24 +289,23 @@
         for c in range(0, 8, 2):
             out = dot(stacked_nodes[...], spread[:, c * 128 : (c + 2) * 128], NN)
             for n in range(16):
-                both = out[n * columns : (n + 1) * columns]
+                both = out[n * columns : (n + 1) * columns].astype(BF)
                 nodes[side * 128 + n * 8 + c] = both[:, :128]
                 nodes[side * 128 + n * 8 + c + 1] = both[:, 128:]
 
-    lane_group = iota((columns, 128), 1) >> 5
+    lane = lane_numbers(columns)
     lane_node = iota((columns, 256), 1) & 7
 
     for g in range(16):
         picked = []
         for i in range(8):
             parts = [nodes[spots_ref[s, g * 8 + i]] for s in range(6)]
-            front = parts[0]
-            for s in range(1, 4):
-                front = jnp.where(lane_group == s, parts[s], front)
-            back = jnp.where(lane_group == 1, parts[5], parts[4])
-            back = jnp.where(lane_group < 2, back, 0.0)
+            front = jnp.where(lane < 32, parts[0], parts[1])
+            front = jnp.where(lane < 64, front, jnp.where(lane < 96, parts[2], parts[3]))
+            back = jnp.where(lane < 32, parts[4], parts[5])
+            back = jnp.where(lane < 64, back, jnp.zeros((), BF))
             picked.append(jnp.concatenate([front, back], axis=1))
-        out = dot(jnp.concatenate(picked, axis=0).astype(BF), matrices_ref[g], NT)
+        out = dot(jnp.concatenate(picked, axis=0), matrices_ref[g], NT)
         total = out[:columns]
         for i in range(1, 8):
             total = jnp.where(lane_node == i, out[i * columns : (i + 1) * columns], total)
@@ -331,10 +340,17 @@
         half = at_points[:, g % 2 * 256 : (g % 2 + 1) * 256]
         stacked[g * columns : (g + 1) * columns, :] = (near + half).astype(BF)
 
+    writes = []
     for c in range(points // 256):
         applied_ref[:, c * 256 : (c + 1) * 256] = pick(
             stacked[...], hot_ref[c], inverse_ref[c : c + 1, :], columns
         )
+        if c % 4 == 3:
+            at = pl.ds((c - 3) * 256, 1024)
+            writes.append(pltpu.make_async_copy(applied_ref.at[:, at], applied_hbm.at[:, at], out_sems.at[c // 4]))
+            writes[-1].start()
+    for write in writes:
+        write.wait()
 
 
 VMEM = pl.BlockSpec(memory_space=pltpu.VMEM)
@@ -345,16 +361,16 @@
     return pltpu.with_memory_space_constraint(x, pltpu.HBM)
 
 
-def call(kernel, outs, scratch, specs, flops, name, args, mib=16):
+def call(kernel, outs, scratch, specs, flops, name, args, mib=16, out_specs=None):
     size = sum(a.size * a.dtype.itemsize for a in args)
     return pl.pallas_call(
         kernel,
         out_shape=[jax.ShapeDtypeStruct(s, t) for s, t in outs],
         in_specs=specs,
-        out_specs=[VMEM] * len(outs),
+        out_specs=out_specs or [VMEM] * len(outs),
         scratch_shapes=scratch,
         compiler_params=pltpu.CompilerParams(vmem_limit_bytes=mib * 2**20),
-        cost_estimate=pl.CostEstimate(flops=flops, bytes_accessed=size, transcendentals=0),
+        cost_estimate=pl.CostEstimate(flops=flops, bytes_accessed=0, transcendentals=0),
         name=name,
     )(*args)
 
@@ -374,6 +390,7 @@
     matrices = couplings.reshape(6, rank * rank, -1)
 
     any_spec = pl.BlockSpec(memory_space=pl.ANY)
+    tile = max(devices // 2 * rank, 128)
     ordered, own0, masked = call(
         leaf_kernel,
         [((columns, points), BF), ((columns, 2 * halo + 2048), BF), ((points // 512, 256, 512), BF)],
@@ -389,10 +406,14 @@
     first0 = lax.ppermute(own0, "leaf", pairs)
     own1, top, weights = call(
         lift_kernel,
-        [((columns, 2048), BF), ((1, columns, 128), BF), ((16, 256, 256), BF)],
+        [((columns, 2048 + tile), BF), ((columns, tile), BF), ((16, 256, 256), BF)],
         [pltpu.VMEM((rank, 128, 256), F32)], [VMEM, VMEM], 10**9, "lift", (own0, moves),
     )
-    first1 = lax.ppermute(own1, "leaf", pairs)
+    steps = [1 << k for k in reversed(range(1, devices.bit_length() - 1))]
+
+    def step(tile_sum, reached):
+        return tile_sum + lax.ppermute(tile_sum, "leaf", [(i, i ^ reached) for i in range(devices)])
+
     coupling_rows, spots, hot, blocks = call(
         matrices_kernel,
         [
@@ -400,30 +421,29 @@
             ((points // 256, 256), jnp.int32),
         ],
         [pltpu.VMEM((rank, 128, 256), F32)],
-        [VMEM] * 3, 3 * 10**9, "matrices", (matrices, lists_t, order),
-    )
-    first0, blocks = lax.optimization_barrier((first0, blocks))
+        [VMEM] * 3, 10**7, "matrices", (matrices, lists_t, order),
+    )
+    for reached in steps[:-1]:
+        top = step(top, reached)
+    first0, top, blocks, ordered_late = lax.optimization_barrier((first0, top, blocks, ordered))
     second0 = lax.ppermute(first0, "leaf", onward)
-    reached, held = 1, [top]
-    while reached < devices:
-        near_half = held[0] if len(held) == 1 else jnp.concatenate(held, axis=0)
-        far_half = lax.ppermute(near_half, "leaf", [(i, i ^ reached) for i in range(devices)])
-        held = [near_half, far_half]
-        reached *= 2
-
-    first0, ordered_late = lax.optimization_barrier((first0, ordered))
+    for reached in steps[-1:]:
+        top = step(top, reached)
     (near_part,) = call(
         near_kernel, [((columns, points), F32)],
-        [pltpu.VMEM((points // 64, columns, 128), F32)],
-        [VMEM, VMEM, SMEM], 3 * 10**9, "near", (ordered_late, near_blocks, near_t),
-    )
-    first1, near_part = lax.optimization_barrier((first1, near_part))
+        [pltpu.VMEM((points // 64, columns, 128), BF)],
+        [VMEM, VMEM, SMEM], 10**7, "near", (ordered_late, near_blocks, near_t),
+    )
+    own1 = lax.dynamic_update_slice(own1, top, (0, 2048))
+    own1, near_part = lax.optimization_barrier((own1, near_part))
+    first1 = lax.ppermute(own1, "leaf", pairs)
+    first1, second0 = lax.optimization_barrier((first1, second0))
     second1 = lax.ppermute(first1, "leaf", onward)
     (six,) = call(
         root_kernel, [((columns, 256), F32)], [pltpu.VMEM((2 * devices, columns, 32), F32)],
-        [VMEM] * 4 + [SMEM], 10**9, "root",
+        [VMEM] * 4 + [SMEM], 10**6, "root",
         (
-            *held, jnp.transpose(top_transfers, (2, 0, 1)), jnp.transpose(top_couplings, (0, 3, 1, 2)),
+            own1, first1, jnp.transpose(top_transfers, (2, 0, 1)), jnp.transpose(top_couplings, (0, 3, 1, 2)),
             jnp.transpose(top_lists),
         ),
     )
@@ -431,10 +451,11 @@
         outer_kernel,
         [((columns, points), F32)],
         [
-            pltpu.VMEM((points // 64 + 2 * REACH, columns, 128), F32),
-            pltpu.VMEM((385, columns, 128), F32), pltpu.VMEM((columns, 4096), F32),
+            pltpu.VMEM((columns, points), F32), pltpu.VMEM((points // 64 + 2 * REACH, columns, 128), BF),
+            pltpu.VMEM((385, columns, 128), BF), pltpu.VMEM((columns, 4096), F32),
             pltpu.VMEM((points // 256 * columns, 256), BF), pltpu.VMEM((16 * columns, 256), BF),
             pltpu.VMEM((2, REACH) + near_blocks.shape[1:], BF), pltpu.SemaphoreType.DMA((2,)),
+            pltpu.SemaphoreType.DMA((points // 1024,)),
         ],
         [VMEM] * 8 + [any_spec, SMEM, VMEM, SMEM] + [VMEM] * 5,
         4 * 10**9, "outer",
@@ -442,6 +463,7 @@
             ordered, own0, own1, first0, first1, second0, second1, near_part, in_hbm(near_blocks),
             near_t, coupling_rows, spots, blocks, weights, masked, hot, six,
         ),
+        out_specs=[any_spec],
     )
     return applied
 

time: 37.2 us -> 37.7 us (1.013)
  waiting for transfers between devices: 5.4 us -> 6.68 us
  Pallas kernels: 17.2 us -> 16.4 us
    ppermute x1, waiting for transfers between devices: 0.01 us -> 5.04 us  [local(): first1 = lax.ppermute(own1, 'leaf', pairs)]
    ppermute x3 -> x2, waiting for transfers between devices: 5.36 us -> 0.83 us  [step(): lax.ppermute(tile_sum, 'leaf', [(i, i ^ reached) for i in range(devices)])]
    ppermute x3 -> x2, starting transfers between devices: 2.15 us -> 4.24 us  [step(): lax.ppermute(tile_sum, 'leaf', [(i, i ^ reached) for i in range(devices)])]
    ppermute x1, starting transfers between devices: 2 us -> 0.07 us  [local(): first1 = lax.ppermute(own1, 'leaf', pairs)]
    pallas_call x6, Pallas kernels: 17.2 us -> 16.4 us  [call(): pl.pallas_call(kernel, out_shape=[jax.ShapeDtypeStruct(s, t) for s, t in...]
    ppermute x1, waiting for transfers between devices: 0.01 us -> 0.8 us  [local(): second1 = lax.ppermute(first1, 'leaf', onward)]
    ppermute x1, starting transfers between devices: 5.04 us -> 4.6 us  [local(): second1 = lax.ppermute(first1, 'leaf', onward)]
    ppermute x1, starting transfers between devices: 1.92 us -> 2.35 us  [local(): second0 = lax.ppermute(first0, 'leaf', onward)]
  transfers between devices with their start and end apart: 7 -> 6, of which waited for: 2 -> 3; matrix products, arithmetic and copies ran while one was open for 0% -> 0% of each run, Pallas kernels for 19% -> 17%
where the time goes in v6:
time: 37.7 us; the launch traced here: 37.6 us
  Pallas kernels  16.4 us (44%)
  starting transfers between devices  14.3 us (38%)
  waiting for transfers between devices  6.68 us (18%)
    pallas_call x6, Pallas kernels, call(): pl.pallas_call(kernel, out_shape=[jax.ShapeDtypeStruct(s, t) for s, t in...  16.4 us
    ppermute x1, waiting for transfers between devices, local(): first1 = lax.ppermute(own1, 'leaf', pairs)  5.04 us
    ppermute x1, starting transfers between devices, local(): second1 = lax.ppermute(first1, 'leaf', onward)  4.6 us
    ppermute x2, starting transfers between devices, step(): lax.ppermute(tile_sum, 'leaf', [(i, i ^ reached) for i in range(devices)])  4.24 us
    ppermute x1, starting transfers between devices, local(): first0 = lax.ppermute(own0, 'leaf', pairs)  3.03 us
    ppermute x1, starting transfers between devices, local(): second0 = lax.ppermute(first0, 'leaf', onward)  2.35 us
    ppermute x2, waiting for transfers between devices, step(): lax.ppermute(tile_sum, 'leaf', [(i, i ^ reached) for i in range(devices)])  0.83 us
    ppermute x1, waiting for transfers between devices, local(): second1 = lax.ppermute(first1, 'leaf', onward)  0.8 us
  transfers between devices with their start and end apart: 6, of which 3 were waited for; matrix products, arithmetic and copies ran while one was open for 0% of the time, Pallas kernels for 17%

profile of v6, /device:TPU:0, one launch (start us, length us, event | category | flops | bytes accessed | tf_op | source)
XLA Modules:
  0.0 37.6 jit_solution(11886879937774986476)
XLA Ops:
  0.0 0.0 copy-start.8
  0.0 3.2 %leaf.1 = (bf16[32,4096]{1,0:T(8,128)(2,1)S(1)}, bf16[32,3072]{1,0:T(8,128)(2,1)S(1)}, bf16[8,256,512]{2,1,0:T(8,128)(2,1)S(1)}) custom-call(bf16[32,4096]{1,0:T(8,128)(2,1)} %vec_hbm.1, s32[32,128]{1,0:T(8,128)} %bitcast.11, bf16[32,4096]{1,0:T(8,128)(2,1)} %basis_hbm.1), custom_call_target="tpu_custom_call" | custom-call | flops 1000000000 | tf_op jit(solution)/shard_map/leaf/pallas_call | solution.py:366
  3.2 0.0 copy-start.1
  3.2 0.0 copy-start.4
  3.2 0.0 copy-start.5
  3.2 3.0 %collective-permute-start = (bf16[32,3072]{1,0:T(8,128)(2,1)S(1)}, bf16[32,3072]{1,0:T(8,128)(2,1)S(1)}, u32[]{:S(2)}, u32[]{:S(2)}) collective-permute-start(bf16[32,3072]{1,0:T(8,128)(2,1)S(1)} %get-tuple-element.24.message_ref.own0_ref), channel_id=1, source_target_pairs={{0,2},{2,0},{4,6},{6,4},{8,10},{10,8},{12,14},{14,12},{1,3},{3,1},... | collective-permute-start | bytes 589832 | tf_op jit(solution)/shard_map/ppermute | solution.py:406
  6.3 0.0 copy-done.8
  6.3 0.0 copy-start
  6.3 0.0 copy-start.7
  6.3 1.8 %lift.1 = (bf16[32,2176]{1,0:T(8,128)(2,1)S(1)}, bf16[32,128]{1,0:T(8,128)(2,1)S(1)}, bf16[16,256,256]{2,1,0:T(8,128)(2,1)S(1)}) custom-call(bf16[32,3072]{1,0:T(8,128)(2,1)S(1)} %get-tuple-element.24.message_ref.own0_ref, bf16[1024,126]{1,0:T(8,128)(2,1)S(1)} %bitcast.17), custom_call_target="tpu_custom_call" | custom-call | flops 1000000000 | tf_op jit(solution)/shard_map/lift/pallas_call | solution.py:366
  8.0 2.6 %collective-permute-start.1 = (bf16[32,128]{1,0:T(8,128)(2,1)S(1)}, bf16[32,128]{1,0:T(8,128)(2,1)S(1)}, u32[]{:S(2)}, u32[]{:S(2)}) collective-permute-start(bf16[32,128]{1,0:T(8,128)(2,1)S(1)} %get-tuple-element.26), channel_id=1, source_target_pairs={{0,8},{2,10},{4,12},{6,14},{8,0},{10,2},{12,4},{14,6},{1,9},{3,11}... | collective-permute-start | bytes 24584 | tf_op jit(solution)/shard_map/ppermute | solution.py:415
  10.6 0.0 copy-done.1
  10.6 0.0 copy-done.4
  10.6 0.0 copy-done.5
  10.6 0.0 copy-start.2
  10.6 0.0 copy-start.3
  10.7 0.0 copy-start.6
  10.7 1.1 %matrices.1 = (bf16[16,256,256]{2,1,0:T(8,128)(2,1)S(1)}, s32[8,128]{1,0:T(8,128)S(1)}, bf16[16,256,256]{2,1,0:T(8,128)(2,1)S(1)}, s32[16,256]{1,0:T(8,128)S(1)}) custom-call(bf16[6,1024,126]{2,1,0:T(8,128)(2,1)S(1)} %bitcast.8, s32[6,126]{1,0:T(8,128)S(1)} %bitcast.13, s32[32,128]{1,0:T(8,128)S(1)} %bitcast.12), custom_call_target="tpu_custom_call" | custom-call | flops 10000000 | tf_op jit(solution)/shard_map/matrices/pallas_call | solution.py:366
  11.8 0.8 %collective-permute-done.1 = bf16[32,128]{1,0:T(8,128)(2,1)S(1)} collective-permute-done((bf16[32,128]{1,0:T(8,128)(2,1)S(1)}, bf16[32,128]{1,0:T(8,128)(2,1)S(1)}, u32[]{:S(2)}, u32[]{:S(2)}) %collective-permute-start.1) | collective-permute-done | bytes 8224 | tf_op jit(solution)/shard_map/ppermute | solution.py:415
  12.6 0.0 collective-permute-done.first0_ref
  12.6 1.6 %collective-permute-start.2 = (bf16[32,128]{1,0:T(8,128)(2,1)S(1)}, bf16[32,128]{1,0:T(8,128)(2,1)S(1)}, u32[]{:S(2)}, u32[]{:S(2)}) collective-permute-start(bf16[32,128]{1,0:T(8,128)(2,1)S(1)} %add.6), channel_id=1, source_target_pairs={{0,4},{2,6},{4,0},{6,2},{8,12},{10,14},{12,8},{14,10},{1,5},{3,7},... | collective-permute-start | bytes 24584 | tf_op jit(solution)/shard_map/ppermute | solution.py:415
  14.2 2.4 %collective-permute-start.4 = (bf16[32,3072]{1,0:T(8,128)(2,1)S(1)}, bf16[32,3072]{1,0:T(8,128)(2,1)S(1)}, u32[]{:S(2)}, u32[]{:S(2)}) collective-permute-start(bf16[32,3072]{1,0:T(8,128)(2,1)S(1)} %collective-permute-done.first0_ref), channel_id=1, source_target_pairs={{0,4},{4,8},{8,12},{6,2},{10,6},{14,10},{1,5},{5,9},{9,13},{7,3},{... | collective-permute-start | bytes 589832 | tf_op jit(solution)/shard_map/ppermute | solution.py:429
  16.6 0.0 copy-done
  16.6 0.0 copy-done.7
  16.6 1.7 %near.1.near_in = f32[32,4096]{1,0:T(8,128)S(1)} custom-call(bf16[32,4096]{1,0:T(8,128)(2,1)S(1)} %get-tuple-element.29.ordered_ref, bf16[64,64,256]{2,1,0:T(8,128)(2,1)S(1)} %copy-done, s32[4,64]{1,0:T(4,128)S(1)} %bitcast.15), custom_call_target="tpu_custom_call" | custom-call | flops 10000000 | tf_op jit(solution)/shard_map/near/pallas_call | solution.py:366
  18.3 0.0 collective-permute-done.2
  18.3 0.1 collective-permute-start.3
  18.4 5.0 %collective-permute-done.3.other_ref.first1_ref = bf16[32,2176]{1,0:T(8,128)(2,1)S(1)} collective-permute-done((bf16[32,2176]{1,0:T(8,128)(2,1)S(1)}, bf16[32,2176]{1,0:T(8,128)(2,1)S(1)}, u32[]{:S(2)}, u32[]{:S(2)}) %collective-permute-start.3) | collective-permute-done | bytes 139296 | tf_op jit(solution)/shard_map/ppermute | solution.py:439
  23.5 0.0 collective-permute-done.4.second0_ref
  23.5 4.6 %collective-permute-start.5 = (bf16[32,2176]{1,0:T(8,128)(2,1)S(1)}, bf16[32,2176]{1,0:T(8,128)(2,1)S(1)}, u32[]{:S(2)}, u32[]{:S(2)}) collective-permute-start(bf16[32,2176]{1,0:T(8,128)(2,1)S(1)} %collective-permute-done.3.other_ref.first1_ref), channel_id=1, source_target_pairs={{0,4},{4,8},{8,12},{6,2},{10,6},{14,10},{1,5},{5,9},{9,13},{7,3},{... | collective-permute-start | bytes 417800 | tf_op jit(solution)/shard_map/ppermute | solution.py:441
  28.1 0.0 copy-done.2
  28.1 0.0 copy-done.3
  28.1 0.0 copy-done.6
  28.1 1.7 %root.1.six_ref = f32[32,256]{1,0:T(8,128)S(1)} custom-call(bf16[32,2176]{1,0:T(8,128)(2,1)S(1)} %add_dynamic-update-slice_fusion.own_ref.own1_ref, bf16[32,2176]{1,0:T(8,128)(2,1)S(1)} %collective-permute-done.3.other_ref.first1_ref, bf16[14,32,32]{2,1,0:T(8,128)(2,1)S(1)} %bitcast.10, bf16[6,15,32,32]{3,2,1,0:T(8,128)(2,1)S(1)} %bitcast.9, ...), custom_call_target="tpu_custom_call" | custom-call | flops 1000000 | tf_op jit(solution)/shard_map/root/pallas_call | solution.py:366
  29.8 0.8 %collective-permute-done.5.second1_ref = bf16[32,2176]{1,0:T(8,128)(2,1)S(1)} collective-permute-done((bf16[32,2176]{1,0:T(8,128)(2,1)S(1)}, bf16[32,2176]{1,0:T(8,128)(2,1)S(1)}, u32[]{:S(2)}, u32[]{:S(2)}) %collective-permute-start.5) | collective-permute-done | bytes 139296 | tf_op jit(solution)/shard_map/ppermute | solution.py:441
  30.6 6.9 %outer.1 = f32[32,4096]{1,0:T(8,128)} custom-call(bf16[32,4096]{1,0:T(8,128)(2,1)S(1)} %get-tuple-element.29.ordered_ref, bf16[32,3072]{1,0:T(8,128)(2,1)S(1)} %get-tuple-element.24.message_ref.own0_ref, bf16[32,2176]{1,0:T(8,128)(2,1)S(1)} %add_dynamic-update-slice_fusion.own_ref.own1_ref, bf16[32,3072]{1,0:T(8,128)(2,1)S(1)} %collective-permute-done.first0_ref, ...), custom_call_target="tpu_custom_call" | custom-call | flops 4000000000 | tf_op jit(solution)/shard_map/outer/pallas_call | solution.py:366
  (2 shorter events, 0.0 us)
Async XLA Ops:
  0.0 6.3 %copy-start.8 = (bf16[32,32,126]{2,1,0:T(8,128)(2,1)S(1)}, bf16[32,32,126]{2,1,0:T(8,128)(2,1)}, u32[]{:S(2)}) copy-start(bf16[32,32,126]{2,1,0:T(8,128)(2,1)} %param.16) | copy-start | bytes 774148
  3.2 7.4 %copy-start.1 = (bf16[6,32,32,126]{3,2,1,0:T(8,128)(2,1)S(1)}, bf16[6,32,32,126]{3,2,1,0:T(8,128)(2,1)}, u32[]{:S(2)}) copy-start(bf16[6,32,32,126]{3,2,1,0:T(8,128)(2,1)} %param.17) | copy-start | bytes 4644868
  3.2 7.4 %copy-start.4 = (s32[4096]{0:T(1024)S(1)}, s32[4096]{0:T(1024)}, u32[]{:S(2)}) copy-start(s32[4096]{0:T(1024)} %param.12) | copy-start | bytes 49156
  3.2 7.4 %copy-start.5 = (s32[126,6]{0,1:T(8,128)S(1)}, s32[126,6]{0,1:T(8,128)}, u32[]{:S(2)}) copy-start(s32[126,6]{0,1:T(8,128)} %param.18) | copy-start | bytes 9076
  3.2 9.4 %collective-permute-start = (bf16[32,3072]{1,0:T(8,128)(2,1)S(1)}, bf16[32,3072]{1,0:T(8,128)(2,1)S(1)}, u32[]{:S(2)}, u32[]{:S(2)}) collective-permute-start(bf16[32,3072]{1,0:T(8,128)(2,1)S(1)} %get-tuple-element.24.message_ref.own0_ref), channel_id=1, source_target_pairs={{0,2},{2,0},{4,6},{6,4},{8,10},{10,8},{12,14},{14,12},{1,3},{3,1},... | collective-permute-start | bytes 589832 | tf_op jit(solution)/shard_map/ppermute | solution.py:406
  6.3 10.3 %copy-start = (bf16[64,64,256]{2,1,0:T(8,128)(2,1)S(1)}, bf16[64,64,256]{2,1,0:T(8,128)(2,1)}, u32[]{:S(2)}) copy-start(bf16[64,64,256]{2,1,0:T(8,128)(2,1)} %blocks_ref.3) | copy-start | bytes 6291460
  6.3 10.4 %copy-start.7 = (s32[64,4]{0,1:T(4,128)S(1)}, s32[64,4]{0,1:T(4,128)}, u32[]{:S(2)}) copy-start(s32[64,4]{0,1:T(4,128)} %param.15) | copy-start | bytes 3076
  8.0 4.6 %collective-permute-start.1 = (bf16[32,128]{1,0:T(8,128)(2,1)S(1)}, bf16[32,128]{1,0:T(8,128)(2,1)S(1)}, u32[]{:S(2)}, u32[]{:S(2)}) collective-permute-start(bf16[32,128]{1,0:T(8,128)(2,1)S(1)} %get-tuple-element.26), channel_id=1, source_target_pairs={{0,8},{2,10},{4,12},{6,14},{8,0},{10,2},{12,4},{14,6},{1,9},{3,11}... | collective-permute-start | bytes 24584 | tf_op jit(solution)/shard_map/ppermute | solution.py:415
  10.6 17.4 %copy-start.2 = (bf16[6,32,32,15]{2,1,3,0:T(8,128)(2,1)S(1)}, bf16[6,32,32,15]{2,1,3,0:T(8,128)(2,1)}, u32[]{:S(2)}) copy-start(bf16[6,32,32,15]{2,1,3,0:T(8,128)(2,1)} %param.20) | copy-start | bytes 552964
  10.6 17.4 %copy-start.3 = (bf16[32,32,14]{1,0,2:T(8,128)(2,1)S(1)}, bf16[32,32,14]{1,0,2:T(8,128)(2,1)}, u32[]{:S(2)}) copy-start(bf16[32,32,14]{1,0,2:T(8,128)(2,1)} %param.19) | copy-start | bytes 86020
  10.7 17.4 %copy-start.6 = (s32[15,6]{0,1:T(8,128)S(1)}, s32[15,6]{0,1:T(8,128)}, u32[]{:S(2)}) copy-start(s32[15,6]{0,1:T(8,128)} %param.21) | copy-start | bytes 1084
  12.6 5.7 %collective-permute-start.2 = (bf16[32,128]{1,0:T(8,128)(2,1)S(1)}, bf16[32,128]{1,0:T(8,128)(2,1)S(1)}, u32[]{:S(2)}, u32[]{:S(2)}) collective-permute-start(bf16[32,128]{1,0:T(8,128)(2,1)S(1)} %add.6), channel_id=1, source_target_pairs={{0,4},{2,6},{4,0},{6,2},{8,12},{10,14},{12,8},{14,10},{1,5},{3,7},... | collective-permute-start | bytes 24584 | tf_op jit(solution)/shard_map/ppermute | solution.py:415
  14.2 9.2 %collective-permute-start.4 = (bf16[32,3072]{1,0:T(8,128)(2,1)S(1)}, bf16[32,3072]{1,0:T(8,128)(2,1)S(1)}, u32[]{:S(2)}, u32[]{:S(2)}) collective-permute-start(bf16[32,3072]{1,0:T(8,128)(2,1)S(1)} %collective-permute-done.first0_ref), channel_id=1, source_target_pairs={{0,4},{4,8},{8,12},{6,2},{10,6},{14,10},{1,5},{5,9},{9,13},{7,3},{... | collective-permute-start | bytes 589832 | tf_op jit(solution)/shard_map/ppermute | solution.py:429
  18.3 5.1 %collective-permute-start.3 = (bf16[32,2176]{1,0:T(8,128)(2,1)S(1)}, bf16[32,2176]{1,0:T(8,128)(2,1)S(1)}, u32[]{:S(2)}, u32[]{:S(2)}) collective-permute-start(bf16[32,2176]{1,0:T(8,128)(2,1)S(1)} %add_dynamic-update-slice_fusion.own_ref.own1_ref), channel_id=1, source_target_pairs={{0,2},{2,0},{4,6},{6,4},{8,10},{10,8},{12,14},{14,12},{1,3},{3,1},... | collective-permute-start | bytes 417800 | tf_op jit(solution)/shard_map/ppermute | solution.py:439
  23.5 7.2 %collective-permute-start.5 = (bf16[32,2176]{1,0:T(8,128)(2,1)S(1)}, bf16[32,2176]{1,0:T(8,128)(2,1)S(1)}, u32[]{:S(2)}, u32[]{:S(2)}) collective-permute-start(bf16[32,2176]{1,0:T(8,128)(2,1)S(1)} %collective-permute-done.3.other_ref.first1_ref), channel_id=1, source_target_pairs={{0,4},{4,8},{8,12},{6,2},{10,6},{14,10},{1,5},{5,9},{9,13},{7,3},{... | collective-permute-start | bytes 417800 | tf_op jit(solution)/shard_map/ppermute | solution.py:441

commit v7 on v6

--- a/solution.py
+++ b/solution.py
@@ -110,7 +110,6 @@
     row, lane = iota((256, width), 0), iota((256, width), 1) - slot
     root = jnp.where((row == lane * 8 + 6) & (lane >= 0), 1.0, 0.0).astype(BF)
     top_ref[...] = dot(coeffs[15], root, NN).astype(BF)
-    lifted_ref[:, 2048:] = jnp.zeros((lifted_ref.shape[0], width), BF)
     for g in range(8):
         lifted_ref[:, g * 256 : (g + 1) * 256] = coeffs[8 + g]
 
@@ -219,7 +218,7 @@
     coeffs[total] = jnp.zeros((columns, rank), F32)
     for q in range(node_count):
         ref = own_ref if q % 2 == 0 else other_ref
-        at = 2048 + q // 2 * rank
+        at = q // 2 * rank
         coeffs[q ^ (device & 1)] = ref[:, at : at + rank].astype(F32)
     values = [coeffs[j].astype(BF) for j in range(node_count)]
     start, count = 0, node_count
@@ -406,14 +405,18 @@
     first0 = lax.ppermute(own0, "leaf", pairs)
     own1, top, weights = call(
         lift_kernel,
-        [((columns, 2048 + tile), BF), ((columns, tile), BF), ((16, 256, 256), BF)],
+        [((columns, 2048), BF), ((columns, tile), BF), ((16, 256, 256), BF)],
         [pltpu.VMEM((rank, 128, 256), F32)], [VMEM, VMEM], 10**9, "lift", (own0, moves),
     )
+    first1 = lax.ppermute(own1, "leaf", pairs)
+
+    def step(tile_sum, reached):
+        return lax.ppermute(tile_sum, "leaf", [(i, i ^ reached) for i in range(devices)])
+
     steps = [1 << k for k in reversed(range(1, devices.bit_length() - 1))]
-
-    def step(tile_sum, reached):
-        return tile_sum + lax.ppermute(tile_sum, "leaf", [(i, i ^ reached) for i in range(devices)])
-
+    for reached in steps[:-2]:
+        top = top + step(top, reached)
+    other = step(top, steps[-2])
     coupling_rows, spots, hot, blocks = call(
         matrices_kernel,
         [
@@ -421,29 +424,28 @@
             ((points // 256, 256), jnp.int32),
         ],
         [pltpu.VMEM((rank, 128, 256), F32)],
-        [VMEM] * 3, 10**7, "matrices", (matrices, lists_t, order),
-    )
-    for reached in steps[:-1]:
-        top = step(top, reached)
-    first0, top, blocks, ordered_late = lax.optimization_barrier((first0, top, blocks, ordered))
+        [VMEM] * 3, 10**6, "matrices", (matrices, lists_t, order),
+    )
+    first0, blocks, other = lax.optimization_barrier((first0, blocks, other))
     second0 = lax.ppermute(first0, "leaf", onward)
-    for reached in steps[-1:]:
-        top = step(top, reached)
+    top = top + other
+    other = step(top, steps[-1])
+    first1, other = lax.optimization_barrier((first1, other))
+    top = top + other
+    second1 = lax.ppermute(first1, "leaf", onward)
+    other = step(top, 1)
+    first1, ordered_late = lax.optimization_barrier((first1, ordered))
     (near_part,) = call(
         near_kernel, [((columns, points), F32)],
         [pltpu.VMEM((points // 64, columns, 128), BF)],
-        [VMEM, VMEM, SMEM], 10**7, "near", (ordered_late, near_blocks, near_t),
-    )
-    own1 = lax.dynamic_update_slice(own1, top, (0, 2048))
-    own1, near_part = lax.optimization_barrier((own1, near_part))
-    first1 = lax.ppermute(own1, "leaf", pairs)
-    first1, second0 = lax.optimization_barrier((first1, second0))
-    second1 = lax.ppermute(first1, "leaf", onward)
+        [VMEM, VMEM, SMEM], 10**6, "near", (ordered_late, near_blocks, near_t),
+    )
+    other, near_part = lax.optimization_barrier((other, near_part))
     (six,) = call(
         root_kernel, [((columns, 256), F32)], [pltpu.VMEM((2 * devices, columns, 32), F32)],
         [VMEM] * 4 + [SMEM], 10**6, "root",
         (
-            own1, first1, jnp.transpose(top_transfers, (2, 0, 1)), jnp.transpose(top_couplings, (0, 3, 1, 2)),
+            top, other, jnp.transpose(top_transfers, (2, 0, 1)), jnp.transpose(top_couplings, (0, 3, 1, 2)),
             jnp.transpose(top_lists),
         ),
     )

time: 37.7 us -> 36.9 us (0.979)
  waiting for transfers between devices: 6.68 us -> 4.53 us
  starting transfers between devices: 14.3 us -> 15.6 us
    ppermute x1, waiting for transfers between devices: 5.04 us -> 0.01 us  [local(): first1 = lax.ppermute(own1, 'leaf', pairs)]
    ppermute x2 -> x3, waiting for transfers between devices: 0.83 us -> 4.5 us  [step(): lax.ppermute(tile_sum, 'leaf', [(i, i ^ reached) for i in range(devices)])]
    ppermute x1, starting transfers between devices: 2.35 us -> 3.82 us  [local(): second0 = lax.ppermute(first0, 'leaf', onward)]
    ppermute x1, waiting for transfers between devices: 0.8 us -> 0.01 us  [local(): second1 = lax.ppermute(first1, 'leaf', onward)]
    ppermute x1, starting transfers between devices: 4.6 us -> 3.9 us  [local(): second1 = lax.ppermute(first1, 'leaf', onward)]
    ppermute x2 -> x3, starting transfers between devices: 4.24 us -> 4.76 us  [step(): lax.ppermute(tile_sum, 'leaf', [(i, i ^ reached) for i in range(devices)])]
  transfers between devices with their start and end apart: 6 -> 7, of which waited for: 3 -> 3; matrix products, arithmetic and copies ran while one was open for 0% -> 0% of each run, Pallas kernels for 17% -> 17%
where the time goes in v7:
time: 36.9 us; the launch traced here: 36.7 us
  Pallas kernels  16.4 us (44%)
  starting transfers between devices  15.6 us (42%)
  waiting for transfers between devices  4.53 us (12%)
    pallas_call x6, Pallas kernels, call(): pl.pallas_call(kernel, out_shape=[jax.ShapeDtypeStruct(s, t) for s, t in...  16.4 us
    ppermute x3, starting transfers between devices, step(): lax.ppermute(tile_sum, 'leaf', [(i, i ^ reached) for i in range(devices)])  4.76 us
    ppermute x3, waiting for transfers between devices, step(): lax.ppermute(tile_sum, 'leaf', [(i, i ^ reached) for i in range(devices)])  4.5 us
    ppermute x1, starting transfers between devices, local(): second1 = lax.ppermute(first1, 'leaf', onward)  3.9 us
    ppermute x1, starting transfers between devices, local(): second0 = lax.ppermute(first0, 'leaf', onward)  3.82 us
    ppermute x1, starting transfers between devices, local(): first0 = lax.ppermute(own0, 'leaf', pairs)  3.03 us
  transfers between devices with their start and end apart: 7, of which 3 were waited for; matrix products, arithmetic and copies ran while one was open for 0% of the time, Pallas kernels for 17%

profile of v7, /device:TPU:0, one launch (start us, length us, event | category | flops | bytes accessed | tf_op | source)
XLA Modules:
  0.0 36.7 jit_solution(1795229365894443534)
XLA Ops:
  0.0 0.0 copy-start.8
  0.0 3.2 %leaf.1 = (bf16[32,4096]{1,0:T(8,128)(2,1)S(1)}, bf16[32,3072]{1,0:T(8,128)(2,1)S(1)}, bf16[8,256,512]{2,1,0:T(8,128)(2,1)S(1)}) custom-call(bf16[32,4096]{1,0:T(8,128)(2,1)} %vec_hbm.1, s32[32,128]{1,0:T(8,128)} %bitcast.11, bf16[32,4096]{1,0:T(8,128)(2,1)} %basis_hbm.1), custom_call_target="tpu_custom_call" | custom-call | flops 1000000000 | tf_op jit(solution)/shard_map/leaf/pallas_call | solution.py:365
  3.2 0.0 copy-start.1
  3.2 0.0 copy-start.4
  3.2 0.0 copy-start.5
  3.2 3.0 %collective-permute-start = (bf16[32,3072]{1,0:T(8,128)(2,1)S(1)}, bf16[32,3072]{1,0:T(8,128)(2,1)S(1)}, u32[]{:S(2)}, u32[]{:S(2)}) collective-permute-start(bf16[32,3072]{1,0:T(8,128)(2,1)S(1)} %get-tuple-element.25.message_ref.own0_ref), channel_id=1, source_target_pairs={{0,2},{2,0},{4,6},{6,4},{8,10},{10,8},{12,14},{14,12},{1,3},{3,1},... | collective-permute-start | bytes 589832 | tf_op jit(solution)/shard_map/ppermute | solution.py:405
  6.3 0.0 copy-done.8
  6.3 0.0 copy-start
  6.3 0.0 copy-start.7
  6.3 1.8 %lift.1 = (bf16[32,2048]{1,0:T(8,128)(2,1)S(1)}, bf16[32,128]{1,0:T(8,128)(2,1)S(1)}, bf16[16,256,256]{2,1,0:T(8,128)(2,1)S(1)}) custom-call(bf16[32,3072]{1,0:T(8,128)(2,1)S(1)} %get-tuple-element.25.message_ref.own0_ref, bf16[1024,126]{1,0:T(8,128)(2,1)S(1)} %bitcast.17), custom_call_target="tpu_custom_call" | custom-call | flops 1000000000 | tf_op jit(solution)/shard_map/lift/pallas_call | solution.py:365
  8.0 0.1 collective-permute-start.2
  8.1 3.1 %collective-permute-start.1 = (bf16[32,128]{1,0:T(8,128)(2,1)S(1)}, bf16[32,128]{1,0:T(8,128)(2,1)S(1)}, u32[]{:S(2)}, u32[]{:S(2)}) collective-permute-start(bf16[32,128]{1,0:T(8,128)(2,1)S(1)} %get-tuple-element.28), channel_id=1, source_target_pairs={{0,8},{2,10},{4,12},{6,14},{8,0},{10,2},{12,4},{14,6},{1,9},{3,11}... | collective-permute-start | bytes 24584 | tf_op jit(solution)/shard_map/ppermute | solution.py:414
  11.1 0.0 copy-done.1
  11.2 0.0 copy-done.4
  11.2 0.0 copy-done.5
  11.2 0.0 copy-start.2
  11.2 0.0 copy-start.3
  11.2 0.0 copy-start.6
  11.2 1.1 %matrices.1 = (bf16[16,256,256]{2,1,0:T(8,128)(2,1)S(1)}, s32[8,128]{1,0:T(8,128)S(1)}, bf16[16,256,256]{2,1,0:T(8,128)(2,1)S(1)}, s32[16,256]{1,0:T(8,128)S(1)}) custom-call(bf16[6,1024,126]{2,1,0:T(8,128)(2,1)S(1)} %bitcast.8, s32[6,126]{1,0:T(8,128)S(1)} %bitcast.13, s32[32,128]{1,0:T(8,128)S(1)} %bitcast.12), custom_call_target="tpu_custom_call" | custom-call | flops 1000000 | tf_op jit(solution)/shard_map/matrices/pallas_call | solution.py:365
  12.3 0.5 %collective-permute-done.1 = bf16[32,128]{1,0:T(8,128)(2,1)S(1)} collective-permute-done((bf16[32,128]{1,0:T(8,128)(2,1)S(1)}, bf16[32,128]{1,0:T(8,128)(2,1)S(1)}, u32[]{:S(2)}, u32[]{:S(2)}) %collective-permute-start.1) | collective-permute-done | bytes 8224 | tf_op jit(solution)/shard_map/ppermute | solution.py:414
  12.8 0.0 collective-permute-done.first0_ref
  12.8 3.8 %collective-permute-start.4 = (bf16[32,3072]{1,0:T(8,128)(2,1)S(1)}, bf16[32,3072]{1,0:T(8,128)(2,1)S(1)}, u32[]{:S(2)}, u32[]{:S(2)}) collective-permute-start(bf16[32,3072]{1,0:T(8,128)(2,1)S(1)} %collective-permute-done.first0_ref), channel_id=1, source_target_pairs={{0,4},{4,8},{8,12},{6,2},{10,6},{14,10},{1,5},{5,9},{9,13},{7,3},{... | collective-permute-start | bytes 589832 | tf_op jit(solution)/shard_map/ppermute | solution.py:430
  16.6 1.6 %collective-permute-start.3 = (bf16[32,128]{1,0:T(8,128)(2,1)S(1)}, bf16[32,128]{1,0:T(8,128)(2,1)S(1)}, u32[]{:S(2)}, u32[]{:S(2)}) collective-permute-start(bf16[32,128]{1,0:T(8,128)(2,1)S(1)} %add.6), channel_id=1, source_target_pairs={{0,4},{2,6},{4,0},{6,2},{8,12},{10,14},{12,8},{14,10},{1,5},{3,7},... | collective-permute-start | bytes 24584 | tf_op jit(solution)/shard_map/ppermute | solution.py:414
  18.2 0.0 collective-permute-done.2.first1_ref
  18.3 2.1 %collective-permute-done.3 = bf16[32,128]{1,0:T(8,128)(2,1)S(1)} collective-permute-done((bf16[32,128]{1,0:T(8,128)(2,1)S(1)}, bf16[32,128]{1,0:T(8,128)(2,1)S(1)}, u32[]{:S(2)}, u32[]{:S(2)}) %collective-permute-start.3) | collective-permute-done | bytes 8224 | tf_op jit(solution)/shard_map/ppermute | solution.py:414
  20.3 3.9 %collective-permute-start.5 = (bf16[32,2048]{1,0:T(8,128)(2,1)S(1)}, bf16[32,2048]{1,0:T(8,128)(2,1)S(1)}, u32[]{:S(2)}, u32[]{:S(2)}) collective-permute-start(bf16[32,2048]{1,0:T(8,128)(2,1)S(1)} %collective-permute-done.2.first1_ref), channel_id=1, source_target_pairs={{0,4},{4,8},{8,12},{6,2},{10,6},{14,10},{1,5},{5,9},{9,13},{7,3},{... | collective-permute-start | bytes 393224 | tf_op jit(solution)/shard_map/ppermute | solution.py:435
  24.3 0.1 collective-permute-start.6
  24.3 0.0 copy-done
  24.3 0.0 copy-done.7
  24.4 1.7 %near.1.near_in = f32[32,4096]{1,0:T(8,128)S(1)} custom-call(bf16[32,4096]{1,0:T(8,128)(2,1)S(1)} %get-tuple-element.34.ordered_ref, bf16[64,64,256]{2,1,0:T(8,128)(2,1)S(1)} %copy-done, s32[4,64]{1,0:T(4,128)S(1)} %bitcast.15), custom_call_target="tpu_custom_call" | custom-call | flops 1000000 | tf_op jit(solution)/shard_map/near/pallas_call | solution.py:365
  26.0 1.9 %collective-permute-done.6.other_ref = bf16[32,128]{1,0:T(8,128)(2,1)S(1)} collective-permute-done((bf16[32,128]{1,0:T(8,128)(2,1)S(1)}, bf16[32,128]{1,0:T(8,128)(2,1)S(1)}, u32[]{:S(2)}, u32[]{:S(2)}) %collective-permute-start.6) | collective-permute-done | bytes 8224 | tf_op jit(solution)/shard_map/ppermute | solution.py:414
  28.0 0.0 copy-done.2
  28.0 0.0 copy-done.3
  28.0 0.0 copy-done.6
  28.0 1.7 %root.1.six_ref = f32[32,256]{1,0:T(8,128)S(1)} custom-call(bf16[32,128]{1,0:T(8,128)(2,1)S(1)} %add.7.own_ref, bf16[32,128]{1,0:T(8,128)(2,1)S(1)} %collective-permute-done.6.other_ref, bf16[14,32,32]{2,1,0:T(8,128)(2,1)S(1)} %bitcast.10, bf16[6,15,32,32]{3,2,1,0:T(8,128)(2,1)S(1)} %bitcast.9, s32[6,15]{1,0:T(8,128)S(1)} %bitcast.14), custom_call_target="tpu_custom_call" | custom-call | flops 1000000 | tf_op jit(solution)/shard_map/root/pallas_call | solution.py:365
  29.7 0.0 collective-permute-done.5.second1_ref
  29.7 0.0 collective-permute-done.4.second0_ref
  29.8 6.9 %outer.1 = f32[32,4096]{1,0:T(8,128)} custom-call(bf16[32,4096]{1,0:T(8,128)(2,1)S(1)} %get-tuple-element.34.ordered_ref, bf16[32,3072]{1,0:T(8,128)(2,1)S(1)} %get-tuple-element.25.message_ref.own0_ref, bf16[32,2048]{1,0:T(8,128)(2,1)S(1)} %get-tuple-element.26.own1_ref, bf16[32,3072]{1,0:T(8,128)(2,1)S(1)} %collective-permute-done.first0_ref, ...), custom_call_target="tpu_custom_call" | custom-call | flops 4000000000 | tf_op jit(solution)/shard_map/outer/pallas_call | solution.py:365
  (2 shorter events, 0.0 us)
Async XLA Ops:
  0.0 6.3 %copy-start.8 = (bf16[32,32,126]{2,1,0:T(8,128)(2,1)S(1)}, bf16[32,32,126]{2,1,0:T(8,128)(2,1)}, u32[]{:S(2)}) copy-start(bf16[32,32,126]{2,1,0:T(8,128)(2,1)} %param.16) | copy-start | bytes 774148
  3.2 7.9 %copy-start.1 = (bf16[6,32,32,126]{3,2,1,0:T(8,128)(2,1)S(1)}, bf16[6,32,32,126]{3,2,1,0:T(8,128)(2,1)}, u32[]{:S(2)}) copy-start(bf16[6,32,32,126]{3,2,1,0:T(8,128)(2,1)} %param.17) | copy-start | bytes 4644868
  3.2 7.9 %copy-start.4 = (s32[4096]{0:T(1024)S(1)}, s32[4096]{0:T(1024)}, u32[]{:S(2)}) copy-start(s32[4096]{0:T(1024)} %param.12) | copy-start | bytes 49156
  3.2 7.9 %copy-start.5 = (s32[126,6]{0,1:T(8,128)S(1)}, s32[126,6]{0,1:T(8,128)}, u32[]{:S(2)}) copy-start(s32[126,6]{0,1:T(8,128)} %param.18) | copy-start | bytes 9076
  3.2 9.5 %collective-permute-start = (bf16[32,3072]{1,0:T(8,128)(2,1)S(1)}, bf16[32,3072]{1,0:T(8,128)(2,1)S(1)}, u32[]{:S(2)}, u32[]{:S(2)}) collective-permute-start(bf16[32,3072]{1,0:T(8,128)(2,1)S(1)} %get-tuple-element.25.message_ref.own0_ref), channel_id=1, source_target_pairs={{0,2},{2,0},{4,6},{6,4},{8,10},{10,8},{12,14},{14,12},{1,3},{3,1},... | collective-permute-start | bytes 589832 | tf_op jit(solution)/shard_map/ppermute | solution.py:405
  6.3 18.1 %copy-start = (bf16[64,64,256]{2,1,0:T(8,128)(2,1)S(1)}, bf16[64,64,256]{2,1,0:T(8,128)(2,1)}, u32[]{:S(2)}) copy-start(bf16[64,64,256]{2,1,0:T(8,128)(2,1)} %blocks_ref.3) | copy-start | bytes 6291460
  6.3 18.1 %copy-start.7 = (s32[64,4]{0,1:T(4,128)S(1)}, s32[64,4]{0,1:T(4,128)}, u32[]{:S(2)}) copy-start(s32[64,4]{0,1:T(4,128)} %param.15) | copy-start | bytes 3076
  8.0 10.2 %collective-permute-start.2 = (bf16[32,2048]{1,0:T(8,128)(2,1)S(1)}, bf16[32,2048]{1,0:T(8,128)(2,1)S(1)}, u32[]{:S(2)}, u32[]{:S(2)}) collective-permute-start(bf16[32,2048]{1,0:T(8,128)(2,1)S(1)} %get-tuple-element.26.own1_ref), channel_id=1, source_target_pairs={{0,2},{2,0},{4,6},{6,4},{8,10},{10,8},{12,14},{14,12},{1,3},{3,1},... | collective-permute-start | bytes 393224 | tf_op jit(solution)/shard_map/ppermute | solution.py:411
  8.1 4.7 %collective-permute-start.1 = (bf16[32,128]{1,0:T(8,128)(2,1)S(1)}, bf16[32,128]{1,0:T(8,128)(2,1)S(1)}, u32[]{:S(2)}, u32[]{:S(2)}) collective-permute-start(bf16[32,128]{1,0:T(8,128)(2,1)S(1)} %get-tuple-element.28), channel_id=1, source_target_pairs={{0,8},{2,10},{4,12},{6,14},{8,0},{10,2},{12,4},{14,6},{1,9},{3,11}... | collective-permute-start | bytes 24584 | tf_op jit(solution)/shard_map/ppermute | solution.py:414
  11.2 16.8 %copy-start.2 = (bf16[6,32,32,15]{2,1,3,0:T(8,128)(2,1)S(1)}, bf16[6,32,32,15]{2,1,3,0:T(8,128)(2,1)}, u32[]{:S(2)}) copy-start(bf16[6,32,32,15]{2,1,3,0:T(8,128)(2,1)} %param.20) | copy-start | bytes 552964
  11.2 16.8 %copy-start.3 = (bf16[32,32,14]{1,0,2:T(8,128)(2,1)S(1)}, bf16[32,32,14]{1,0,2:T(8,128)(2,1)}, u32[]{:S(2)}) copy-start(bf16[32,32,14]{1,0,2:T(8,128)(2,1)} %param.19) | copy-start | bytes 86020
  11.2 16.8 %copy-start.6 = (s32[15,6]{0,1:T(8,128)S(1)}, s32[15,6]{0,1:T(8,128)}, u32[]{:S(2)}) copy-start(s32[15,6]{0,1:T(8,128)} %param.21) | copy-start | bytes 1084
  12.8 17.0 %collective-permute-start.4 = (bf16[32,3072]{1,0:T(8,128)(2,1)S(1)}, bf16[32,3072]{1,0:T(8,128)(2,1)S(1)}, u32[]{:S(2)}, u32[]{:S(2)}) collective-permute-start(bf16[32,3072]{1,0:T(8,128)(2,1)S(1)} %collective-permute-done.first0_ref), channel_id=1, source_target_pairs={{0,4},{4,8},{8,12},{6,2},{10,6},{14,10},{1,5},{5,9},{9,13},{7,3},{... | collective-permute-start | bytes 589832 | tf_op jit(solution)/shard_map/ppermute | solution.py:430
  16.6 3.7 %collective-permute-start.3 = (bf16[32,128]{1,0:T(8,128)(2,1)S(1)}, bf16[32,128]{1,0:T(8,128)(2,1)S(1)}, u32[]{:S(2)}, u32[]{:S(2)}) collective-permute-start(bf16[32,128]{1,0:T(8,128)(2,1)S(1)} %add.6), channel_id=1, source_target_pairs={{0,4},{2,6},{4,0},{6,2},{8,12},{10,14},{12,8},{14,10},{1,5},{3,7},... | collective-permute-start | bytes 24584 | tf_op jit(solution)/shard_map/ppermute | solution.py:414
  20.3 9.4 %collective-permute-start.5 = (bf16[32,2048]{1,0:T(8,128)(2,1)S(1)}, bf16[32,2048]{1,0:T(8,128)(2,1)S(1)}, u32[]{:S(2)}, u32[]{:S(2)}) collective-permute-start(bf16[32,2048]{1,0:T(8,128)(2,1)S(1)} %collective-permute-done.2.first1_ref), channel_id=1, source_target_pairs={{0,4},{4,8},{8,12},{6,2},{10,6},{14,10},{1,5},{5,9},{9,13},{7,3},{... | collective-permute-start | bytes 393224 | tf_op jit(solution)/shard_map/ppermute | solution.py:435
  24.3 3.7 %collective-permute-start.6 = (bf16[32,128]{1,0:T(8,128)(2,1)S(1)}, bf16[32,128]{1,0:T(8,128)(2,1)S(1)}, u32[]{:S(2)}, u32[]{:S(2)}) collective-permute-start(bf16[32,128]{1,0:T(8,128)(2,1)S(1)} %add.7.own_ref), channel_id=1, source_target_pairs={{0,2},{2,0},{4,6},{6,4},{8,10},{10,8},{12,14},{14,12},{1,3},{3,1},... | collective-permute-start | bytes 24584 | tf_op jit(solution)/shard_map/ppermute | solution.py:414

commit v8 on v7

--- a/solution.py
+++ b/solution.py
@@ -50,12 +50,11 @@
 
 
 def leaf_kernel(
-    vec_hbm, order_hbm, basis_hbm, ordered_ref, message_ref, masked_ref,
-    vec_ref, order_ref, basis_ref, stacked, sems,
+    vec_hbm, order_hbm, basis_hbm, ordered_ref, zero_ref, masked_hbm,
+    vec_ref, order_ref, basis_ref, stacked, masked_ref, sems, out_sems,
 ):
     columns, points = vec_ref.shape
     rank = basis_ref.shape[0]
-    halo = REACH * 64
     pairs = ((order_hbm, order_ref), (vec_hbm, vec_ref), (basis_hbm, basis_ref))
     copies = [pltpu.make_async_copy(src, dst, sems.at[i]) for i, (src, dst) in enumerate(pairs)]
     for copy in copies:
@@ -70,20 +69,27 @@
 
     copies[2].wait()
     mine = (iota((256, 512), 0) & 7) == (iota((256, 512), 1) >> 6)
+    writes = []
     for g in range(points // 512):
         one = basis_ref[:, g * 512 : (g + 1) * 512].astype(F32)
         eight = jnp.broadcast_to(one[:, None, :], (rank, 8, 512)).reshape(256, 512)
         masked = jnp.where(mine, eight, 0.0).astype(BF)
         masked_ref[g] = masked
+        writes.append(pltpu.make_async_copy(masked_ref.at[g], masked_hbm.at[g], out_sems.at[g]))
+        writes[-1].start()
         coeffs = dot(ordered_ref[:, g * 512 : (g + 1) * 512], masked, NT).astype(BF)
-        message_ref[:, 2 * halo + g * 256 : 2 * halo + (g + 1) * 256] = coeffs
-    message_ref[:, :halo] = ordered_ref[:, :halo]
-    message_ref[:, halo : 2 * halo] = ordered_ref[:, points - halo :]
-
-
-def lift_kernel(message_ref, transfer_ref, lifted_ref, top_ref, weights_ref, rows32):
+        zero_ref[:, g * 256 : (g + 1) * 256] = coeffs
+    for write in writes:
+        write.wait()
+
+
+def lift_kernel(
+    zero_ref, ordered_ref, transfer_ref, first_ref, second_ref, copies_ref, weights_hbm,
+    rows32, weights_ref, sem,
+):
     rank = 32
-    base = 2 * REACH * 64
+    base = REACH * 64
+    points = ordered_ref.shape[1]
 
     lane, row = iota((128, 256), 1), iota((128, 256), 0)
     family = (lane & 7) == ((row >> 1) & 7)
@@ -97,7 +103,9 @@
             rows32[m * 4 + q] = jnp.where(family, dot(turned, spread[q], NN), 0.0)
     for k in range(16):
         weights_ref[k] = rows32[:, k * 8 : k * 8 + 8, :].reshape(256, 256).astype(BF)
-    coeffs = [message_ref[:, base + g * 256 : base + (g + 1) * 256] for g in range(8)] + [None] * 8
+    write = pltpu.make_async_copy(weights_ref, weights_hbm, sem)
+    write.start()
+    coeffs = [zero_ref[:, g * 256 : (g + 1) * 256] for g in range(8)] + [None] * 8
     for n in range(7):
         lifted = dot(coeffs[2 * n], weights_ref[2 * n], NN) + dot(coeffs[2 * n + 1], weights_ref[2 * n + 1], NN)
         coeffs[8 + n] = lifted.astype(BF)
@@ -105,13 +113,18 @@
     five = dot(four.astype(BF), weights_ref[15], NN)
     six = dot((four + five).astype(BF), weights_ref[15], NN)
     coeffs[15] = (four + six).astype(BF)
-    width = top_ref.shape[1]
-    slot = lax.axis_index("leaf") // 2 * rank
-    row, lane = iota((256, width), 0), iota((256, width), 1) - slot
-    root = jnp.where((row == lane * 8 + 6) & (lane >= 0), 1.0, 0.0).astype(BF)
-    top_ref[...] = dot(coeffs[15], root, NN).astype(BF)
-    for g in range(8):
-        lifted_ref[:, g * 256 : (g + 1) * 256] = coeffs[8 + g]
+    root = jnp.where(iota((256, 128), 0) == iota((256, 128), 1) * 8 + 6, 1.0, 0.0).astype(BF)
+    tile = dot(coeffs[15], root, NN).astype(BF)
+    for q in range(copies_ref.shape[0]):
+        copies_ref[q] = tile
+    odd = lax.axis_index("leaf") % 2 == 1
+    low, high = ordered_ref[:, :base], ordered_ref[:, points - base :]
+    first_ref[:, :base] = jnp.where(odd, low, high)
+    second_ref[:, :base] = jnp.where(odd, high, low)
+    for g in range(16):
+        first_ref[:, base + g * 256 : base + (g + 1) * 256] = coeffs[g]
+        second_ref[:, base + g * 256 : base + (g + 1) * 256] = coeffs[g]
+    write.wait()
 
 
 def lane_numbers(rows):
@@ -210,17 +223,14 @@
     lax.fori_loop(edge, count // 4 - edge, near, 0, unroll=4)
 
 
-def root_kernel(own_ref, other_ref, transfer_ref, coupling_ref, lists_ref, six_ref, coeffs):
-    columns, rank = own_ref.shape[0], 32
-    node_count = lists_ref.shape[1] // 2 + 1
+def root_kernel(gathered_ref, transfer_ref, coupling_ref, lists_ref, six_ref, coeffs):
+    node_count, columns = gathered_ref.shape[:2]
     device = lax.axis_index("leaf")
     total = 2 * node_count - 1
-    coeffs[total] = jnp.zeros((columns, rank), F32)
+    coeffs[total] = jnp.zeros((columns, 32), F32)
+    values = [gathered_ref[q][:, :32] for q in range(node_count)]
     for q in range(node_count):
-        ref = own_ref if q % 2 == 0 else other_ref
-        at = q // 2 * rank
-        coeffs[q ^ (device & 1)] = ref[:, at : at + rank].astype(F32)
-    values = [coeffs[j].astype(BF) for j in range(node_count)]
+        coeffs[q] = values[q].astype(F32)
     start, count = 0, node_count
     starts = [(0, node_count)]
     while count > 1:
@@ -249,10 +259,10 @@
 
 
 def outer_kernel(
-    ordered_ref, own0_ref, own1_ref, first0_ref, first1_ref, second0_ref, second1_ref, near_in, blocks_ref,
-    near_ref, matrices_ref, spots_ref, inverse_ref, weights_ref, masked_ref, hot_ref, six_ref,
+    ordered_ref, own_ref, first_ref, second_ref, near_in, blocks_ref,
+    near_ref, matrices_ref, spots_ref, inverse_ref, weights_hbm, masked_hbm, hot_ref, six_ref,
     applied_hbm,
-    applied_ref, leaves, nodes, far, stacked, stacked_nodes, edges, sems, out_sems,
+    applied_ref, leaves, nodes, far, stacked, stacked_nodes, edges, weights_ref, masked_ref, sems, out_sems,
 ):
     columns, points = ordered_ref.shape
     halo = REACH * 64
@@ -262,14 +272,15 @@
         pltpu.make_async_copy(blocks_ref.at[pl.ds(at, REACH)], edges.at[i], sems.at[i])
         for i, at in enumerate((0, count - REACH))
     ]
+    copies.append(pltpu.make_async_copy(weights_hbm, weights_ref, sems.at[2]))
+    copies.append(pltpu.make_async_copy(masked_hbm, masked_ref, sems.at[3]))
     for copy in copies:
         copy.start()
 
     odd = device % 2
-    for ref, right in ((first0_ref, 1 - odd), (second0_ref, odd)):
+    for ref, right in ((first_ref, 1 - odd), (second_ref, odd)):
         for c in range(halo // 128):
-            at = pl.multiple_of((1 - right) * halo + c * 128, 128)
-            place_leaves(leaves, right * (REACH + count) + c * 2, ref[:, pl.ds(at, 128)])
+            place_leaves(leaves, right * (REACH + count) + c * 2, ref[:, c * 128 : (c + 1) * 128])
     near_ends = REACH * 64 * 2 // 128
     for c in list(range(near_ends)) + list(range(count // 2 - near_ends, count // 2)):
         place_leaves(leaves, REACH + c * 2, ordered_ref[:, c * 128 : (c + 1) * 128])
@@ -277,14 +288,9 @@
     nodes[3 * 128] = jnp.zeros((columns, 128), BF)
     lane, row = iota((256, 1024), 1), iota((256, 1024), 0)
     spread = jnp.where(row == (lane & 31) * 8 + (lane >> 7), 1.0, 0.0).astype(BF)
-    sources = (
-        (1, own0_ref, own1_ref), (2 - 2 * odd, first0_ref, first1_ref), (2 * odd, second0_ref, second1_ref),
-    )
-    for side, ref0, ref1 in sources:
-        for n in range(8):
-            at = 2 * halo + n * 256
-            stacked_nodes[n * columns : (n + 1) * columns, :] = ref0[:, at : at + 256]
-            stacked_nodes[(8 + n) * columns : (9 + n) * columns, :] = ref1[:, n * 256 : (n + 1) * 256]
+    for side, ref in ((1, own_ref), (2 - 2 * odd, first_ref), (2 * odd, second_ref)):
+        for n in range(16):
+            stacked_nodes[n * columns : (n + 1) * columns, :] = ref[:, halo + n * 256 : halo + (n + 1) * 256]
         for c in range(0, 8, 2):
             out = dot(stacked_nodes[...], spread[:, c * 128 : (c + 2) * 128], NN)
             for n in range(16):
@@ -364,7 +370,7 @@
     size = sum(a.size * a.dtype.itemsize for a in args)
     return pl.pallas_call(
         kernel,
-        out_shape=[jax.ShapeDtypeStruct(s, t) for s, t in outs],
+        out_shape=[jax.ShapeDtypeStruct(*o) if isinstance(o, tuple) else o for o in outs],
         in_specs=specs,
         out_specs=out_specs or [VMEM] * len(outs),
         scratch_shapes=scratch,
@@ -389,34 +395,36 @@
     matrices = couplings.reshape(6, rank * rank, -1)
 
     any_spec = pl.BlockSpec(memory_space=pl.ANY)
-    tile = max(devices // 2 * rank, 128)
-    ordered, own0, masked = call(
+    ordered, zero, masked = call(
         leaf_kernel,
-        [((columns, points), BF), ((columns, 2 * halo + 2048), BF), ((points // 512, 256, 512), BF)],
+        [((columns, points), BF), ((columns, 2048), BF), pltpu.HBM((points // 512, 256, 512), BF)],
         [
             pltpu.VMEM(vectors.shape, BF), pltpu.VMEM(order.shape, jnp.int32),
             pltpu.VMEM(leaf_basis.shape, BF), pltpu.VMEM((points // 256 * columns, 256), BF),
-            pltpu.SemaphoreType.DMA((3,)),
+            pltpu.VMEM((points // 512, 256, 512), BF), pltpu.SemaphoreType.DMA((3,)),
+            pltpu.SemaphoreType.DMA((points // 512,)),
         ],
         [any_spec] * 3, 10**9, "leaf", tuple(in_hbm(x) for x in (vectors, order, leaf_basis)),
+        out_specs=[VMEM, VMEM, any_spec],
     )
     pairs = [(i, i ^ 1) for i in range(devices)]
-    onward = [(i, i + 2) for i in range(0, devices - 2, 2)] + [(i, i - 2) for i in range(3, devices, 2)]
-    first0 = lax.ppermute(own0, "leaf", pairs)
-    own1, top, weights = call(
+    odds = [(i, i + 1) for i in range(1, devices - 1, 2)]
+    to_first, to_second, copies, weights = call(
         lift_kernel,
-        [((columns, 2048), BF), ((columns, tile), BF), ((16, 256, 256), BF)],
-        [pltpu.VMEM((rank, 128, 256), F32)], [VMEM, VMEM], 10**9, "lift", (own0, moves),
-    )
-    first1 = lax.ppermute(own1, "leaf", pairs)
-
-    def step(tile_sum, reached):
-        return lax.ppermute(tile_sum, "leaf", [(i, i ^ reached) for i in range(devices)])
-
-    steps = [1 << k for k in reversed(range(1, devices.bit_length() - 1))]
-    for reached in steps[:-2]:
-        top = top + step(top, reached)
-    other = step(top, steps[-2])
+        [
+            ((columns, halo + 4096), BF), ((columns, halo + 4096), BF), ((devices, columns, 128), BF),
+            pltpu.HBM((16, 256, 256), BF),
+        ],
+        [
+            pltpu.VMEM((rank, 128, 256), F32), pltpu.VMEM((16, 256, 256), BF),
+            pltpu.SemaphoreType.DMA(()),
+        ],
+        [VMEM] * 3, 10**6, "lift", (zero, ordered, moves), out_specs=[VMEM] * 3 + [any_spec],
+    )
+    first = lax.ppermute(to_first, "leaf", pairs)
+    second = lax.ppermute(to_second, "leaf", odds + [(j, i) for i, j in odds])
+    gathered = lax.all_to_all(copies, "leaf", 0, 0)
+    gathered, order, ordered_late = lax.optimization_barrier((gathered, order, ordered))
     coupling_rows, spots, hot, blocks = call(
         matrices_kernel,
         [
@@ -426,26 +434,16 @@
         [pltpu.VMEM((rank, 128, 256), F32)],
         [VMEM] * 3, 10**6, "matrices", (matrices, lists_t, order),
     )
-    first0, blocks, other = lax.optimization_barrier((first0, blocks, other))
-    second0 = lax.ppermute(first0, "leaf", onward)
-    top = top + other
-    other = step(top, steps[-1])
-    first1, other = lax.optimization_barrier((first1, other))
-    top = top + other
-    second1 = lax.ppermute(first1, "leaf", onward)
-    other = step(top, 1)
-    first1, ordered_late = lax.optimization_barrier((first1, ordered))
     (near_part,) = call(
         near_kernel, [((columns, points), F32)],
         [pltpu.VMEM((points // 64, columns, 128), BF)],
         [VMEM, VMEM, SMEM], 10**6, "near", (ordered_late, near_blocks, near_t),
     )
-    other, near_part = lax.optimization_barrier((other, near_part))
     (six,) = call(
         root_kernel, [((columns, 256), F32)], [pltpu.VMEM((2 * devices, columns, 32), F32)],
-        [VMEM] * 4 + [SMEM], 10**6, "root",
+        [VMEM] * 3 + [SMEM], 10**6, "root",
         (
-            top, other, jnp.transpose(top_transfers, (2, 0, 1)), jnp.transpose(top_couplings, (0, 3, 1, 2)),
+            gathered, jnp.transpose(top_transfers, (2, 0, 1)), jnp.transpose(top_couplings, (0, 3, 1, 2)),
             jnp.transpose(top_lists),
         ),
     )
@@ -456,14 +454,15 @@
             pltpu.VMEM((columns, points), F32), pltpu.VMEM((points // 64 + 2 * REACH, columns, 128), BF),
             pltpu.VMEM((385, columns, 128), BF), pltpu.VMEM((columns, 4096), F32),
             pltpu.VMEM((points // 256 * columns, 256), BF), pltpu.VMEM((16 * columns, 256), BF),
-            pltpu.VMEM((2, REACH) + near_blocks.shape[1:], BF), pltpu.SemaphoreType.DMA((2,)),
+            pltpu.VMEM((2, REACH) + near_blocks.shape[1:], BF), pltpu.VMEM((16, 256, 256), BF),
+            pltpu.VMEM((points // 512, 256, 512), BF), pltpu.SemaphoreType.DMA((4,)),
             pltpu.SemaphoreType.DMA((points // 1024,)),
         ],
-        [VMEM] * 8 + [any_spec, SMEM, VMEM, SMEM] + [VMEM] * 5,
+        [VMEM] * 5 + [any_spec, SMEM, VMEM, SMEM, VMEM, any_spec, any_spec, VMEM, VMEM],
         4 * 10**9, "outer",
         (
-            ordered, own0, own1, first0, first1, second0, second1, near_part, in_hbm(near_blocks),
-            near_t, coupling_rows, spots, blocks, weights, masked, hot, six,
+            ordered_late, to_first, first, second, near_part, in_hbm(near_blocks),
+            near_t, coupling_rows, spots, blocks, in_hbm(weights), in_hbm(masked), hot, six,
         ),
         out_specs=[any_spec],
     )

time: 36.9 us -> 38.7 us (1.049)
  blocking collectives: 0 us -> 12.6 us
  starting transfers between devices: 15.6 us -> 6.46 us
  waiting for transfers between devices: 4.53 us -> 0.03 us
  Pallas kernels: 16.4 us -> 19.3 us
    all_to_all x0 -> x1, blocking collectives: none -> 12.6 us  [local(): gathered = lax.all_to_all(copies, 'leaf', 0, 0)]
    ppermute x7 -> x2, starting transfers between devices: 15.6 us -> 6.46 us  [the longest x1 5.78 us: local(): first = lax.ppermute(to_first, 'leaf', pairs)]
    ppermute x7 -> x2, waiting for transfers between devices: 4.53 us -> 0.03 us  [the longest x1 0.03 us: local(): first = lax.ppermute(to_first, 'leaf', pairs)]
    pallas_call x6, Pallas kernels: 16.4 us -> 19.3 us  [call(): pl.pallas_call(kernel, out_shape=[jax.ShapeDtypeStruct(*o) if isinstance(...]
  transfers between devices with their start and end apart: 7 -> 2, of which waited for: 3 -> 0; matrix products, arithmetic and copies ran while one was open for 0% -> 0% of each run, Pallas kernels for 17% -> 11%
where the time goes in v8:
time: 38.7 us; the launch traced here: 38.5 us
  Pallas kernels  19.3 us (50%)
  blocking collectives  12.6 us (33%)
  starting transfers between devices  6.46 us (17%)
    pallas_call x6, Pallas kernels, call(): pl.pallas_call(kernel, out_shape=[jax.ShapeDtypeStruct(*o) if isinstance(...  19.3 us
    all_to_all x1, blocking collectives, local(): gathered = lax.all_to_all(copies, 'leaf', 0, 0)  12.6 us
    ppermute x1, starting transfers between devices, local(): first = lax.ppermute(to_first, 'leaf', pairs)  5.78 us
  transfers between devices with their start and end apart: 2, of which 0 were waited for; matrix products, arithmetic and copies ran while one was open for 0% of the time, Pallas kernels for 11%

profile of v8, /device:TPU:0, one launch (start us, length us, event | category | flops | bytes accessed | tf_op | source)
XLA Modules:
  0.0 38.5 jit_solution(4256096721980176581)
XLA Ops:
  0.0 0.0 copy-start.3
  0.0 0.0 copy-start
  0.0 0.0 copy-start.8
  0.0 4.4 %leaf.1 = (bf16[32,4096]{1,0:T(8,128)(2,1)S(1)}, bf16[32,2048]{1,0:T(8,128)(2,1)S(1)}, bf16[8,256,512]{2,1,0:T(8,128)(2,1)}) custom-call(bf16[32,4096]{1,0:T(8,128)(2,1)} %vec_hbm.1, s32[32,128]{1,0:T(8,128)} %bitcast.12, bf16[32,4096]{1,0:T(8,128)(2,1)} %basis_hbm.1), custom_call_target="tpu_custom_call" | custom-call | flops 1000000000 | tf_op jit(solution)/shard_map/leaf/pallas_call | solution.py:371
  4.5 0.0 copy-start.1
  4.5 0.0 copy-start.5
  4.5 0.0 copy-start.6
  4.5 0.0 copy-done.3
  4.5 2.1 %lift.1 = (bf16[32,4608]{1,0:T(8,128)(2,1)S(1)}, bf16[32,4608]{1,0:T(8,128)(2,1)S(1)}, bf16[8,32,128]{2,1,0:T(8,128)(2,1)S(1)}, bf16[16,256,256]{2,1,0:T(8,128)(2,1)}) custom-call(bf16[32,2048]{1,0:T(8,128)(2,1)S(1)} %get-tuple-element.19.zero_ref, bf16[32,4096]{1,0:T(8,128)(2,1)S(1)} %get-tuple-element.22.ordered_ref, bf16[1024,126]{1,0:T(8,128)(2,1)S(1)} %bitcast.10), custom_call_target="tpu_custom_call" | custom-call | flops 1000000 | tf_op jit(solution)/shard_map/lift/pallas_call | solution.py:371
  6.6 0.7 %collective-permute-start.1 = (bf16[32,4608]{1,0:T(8,128)(2,1)S(1)}, bf16[32,4608]{1,0:T(8,128)(2,1)S(1)}, u32[]{:S(2)}, u32[]{:S(2)}) collective-permute-start(bf16[32,4608]{1,0:T(8,128)(2,1)S(1)} %get-tuple-element.24), channel_id=1, source_target_pairs={{2,4},{6,8},{10,12},{4,2},{8,6},{12,10},{3,5},{7,9},{11,13},{5,3},... | collective-permute-start | bytes 884744 | tf_op jit(solution)/shard_map/ppermute | solution.py:425
  7.3 5.8 %collective-permute-start = (bf16[32,4608]{1,0:T(8,128)(2,1)S(1)}, bf16[32,4608]{1,0:T(8,128)(2,1)S(1)}, u32[]{:S(2)}, u32[]{:S(2)}) collective-permute-start(bf16[32,4608]{1,0:T(8,128)(2,1)S(1)} %get-tuple-element.23.own_ref), channel_id=1, source_target_pairs={{0,2},{2,0},{4,6},{6,4},{8,10},{10,8},{12,14},{14,12},{1,3},{3,1},... | collective-permute-start | bytes 884744 | tf_op jit(solution)/shard_map/ppermute | solution.py:424
  13.1 12.6 %all_to_all.5.gathered_ref = bf16[8,32,128]{2,1,0:T(8,128)(2,1)S(1)} all-to-all(bf16[8,32,128]{2,1,0:T(8,128)(2,1)S(1)} %get-tuple-element.21), channel_id=1, replica_groups=mesh['groups'=2,'leaf'=8,'rhs'=2] {'leaf'}, dimensions={0} | all-to-all | bytes 131072 | tf_op jit(solution)/shard_map/all_to_all | solution.py:426
  25.7 0.0 copy-done
  25.7 0.0 copy-done.8
  25.7 0.0 copy-start.2
  25.7 0.0 copy-start.4
  25.7 0.0 copy-start.7
  25.7 1.7 %near.1.near_in = f32[32,4096]{1,0:T(8,128)S(1)} custom-call(bf16[32,4096]{1,0:T(8,128)(2,1)S(1)} %get-tuple-element.22.ordered_ref, bf16[64,64,256]{2,1,0:T(8,128)(2,1)S(1)} %copy-done, s32[4,64]{1,0:T(4,128)S(1)} %bitcast.16), custom_call_target="tpu_custom_call" | custom-call | flops 1000000 | tf_op jit(solution)/shard_map/near/pallas_call | solution.py:371
  27.4 0.0 copy-done.1
  27.4 0.0 copy-done.5
  27.4 0.0 copy-done.6
  27.4 1.1 %matrices.1 = (bf16[16,256,256]{2,1,0:T(8,128)(2,1)S(1)}, s32[8,128]{1,0:T(8,128)S(1)}, bf16[16,256,256]{2,1,0:T(8,128)(2,1)S(1)}, s32[16,256]{1,0:T(8,128)S(1)}) custom-call(bf16[6,1024,126]{2,1,0:T(8,128)(2,1)S(1)} %bitcast.8, s32[6,126]{1,0:T(8,128)S(1)} %bitcast.14, s32[32,128]{1,0:T(8,128)S(1)} %bitcast.13), custom_call_target="tpu_custom_call" | custom-call | flops 1000000 | tf_op jit(solution)/shard_map/matrices/pallas_call | solution.py:371
  28.5 0.0 copy-done.2
  28.5 0.0 copy-done.4
  28.5 0.0 copy-done.7
  28.5 1.7 %root.1.six_ref = f32[32,256]{1,0:T(8,128)S(1)} custom-call(bf16[8,32,128]{2,1,0:T(8,128)(2,1)S(1)} %all_to_all.5.gathered_ref, bf16[14,32,32]{2,1,0:T(8,128)(2,1)S(1)} %bitcast.11, bf16[6,15,32,32]{3,2,1,0:T(8,128)(2,1)S(1)} %bitcast.9, s32[6,15]{1,0:T(8,128)S(1)} %bitcast.15), custom_call_target="tpu_custom_call" | custom-call | flops 1000000 | tf_op jit(solution)/shard_map/root/pallas_call | solution.py:371
  30.2 0.0 collective-permute-done.1.second_ref
  30.2 0.0 collective-permute-done.first_ref
  30.2 8.3 %outer.1 = f32[32,4096]{1,0:T(8,128)} custom-call(bf16[32,4096]{1,0:T(8,128)(2,1)S(1)} %get-tuple-element.22.ordered_ref, bf16[32,4608]{1,0:T(8,128)(2,1)S(1)} %get-tuple-element.23.own_ref, bf16[32,4608]{1,0:T(8,128)(2,1)S(1)} %collective-permute-done.first_ref, bf16[32,4608]{1,0:T(8,128)(2,1)S(1)} %collective-permute-done.1.second_ref, ...), custom_call_target="tpu_custom_call" | custom-call | flops 4000000000 | tf_op jit(solution)/shard_map/outer/pallas_call | solution.py:371
Async XLA Ops:
  0.0 4.5 %copy-start.3 = (bf16[32,32,126]{2,1,0:T(8,128)(2,1)S(1)}, bf16[32,32,126]{2,1,0:T(8,128)(2,1)}, u32[]{:S(2)}) copy-start(bf16[32,32,126]{2,1,0:T(8,128)(2,1)} %param.16) | copy-start | bytes 774148
  0.0 25.7 %copy-start = (bf16[64,64,256]{2,1,0:T(8,128)(2,1)S(1)}, bf16[64,64,256]{2,1,0:T(8,128)(2,1)}, u32[]{:S(2)}) copy-start(bf16[64,64,256]{2,1,0:T(8,128)(2,1)} %blocks_ref.3) | copy-start | bytes 6291460
  0.0 25.7 %copy-start.8 = (s32[64,4]{0,1:T(4,128)S(1)}, s32[64,4]{0,1:T(4,128)}, u32[]{:S(2)}) copy-start(s32[64,4]{0,1:T(4,128)} %param.15) | copy-start | bytes 3076
  4.5 22.9 %copy-start.1 = (bf16[6,32,32,126]{3,2,1,0:T(8,128)(2,1)S(1)}, bf16[6,32,32,126]{3,2,1,0:T(8,128)(2,1)}, u32[]{:S(2)}) copy-start(bf16[6,32,32,126]{3,2,1,0:T(8,128)(2,1)} %param.17) | copy-start | bytes 4644868
  4.5 22.9 %copy-start.5 = (s32[4096]{0:T(1024)S(1)}, s32[4096]{0:T(1024)}, u32[]{:S(2)}) copy-start(s32[4096]{0:T(1024)} %param.12) | copy-start | bytes 49156
  4.5 22.9 %copy-start.6 = (s32[126,6]{0,1:T(8,128)S(1)}, s32[126,6]{0,1:T(8,128)}, u32[]{:S(2)}) copy-start(s32[126,6]{0,1:T(8,128)} %param.18) | copy-start | bytes 9076
  6.6 23.6 %collective-permute-start.1 = (bf16[32,4608]{1,0:T(8,128)(2,1)S(1)}, bf16[32,4608]{1,0:T(8,128)(2,1)S(1)}, u32[]{:S(2)}, u32[]{:S(2)}) collective-permute-start(bf16[32,4608]{1,0:T(8,128)(2,1)S(1)} %get-tuple-element.24), channel_id=1, source_target_pairs={{2,4},{6,8},{10,12},{4,2},{8,6},{12,10},{3,5},{7,9},{11,13},{5,3},... | collective-permute-start | bytes 884744 | tf_op jit(solution)/shard_map/ppermute | solution.py:425
  7.3 22.9 %collective-permute-start = (bf16[32,4608]{1,0:T(8,128)(2,1)S(1)}, bf16[32,4608]{1,0:T(8,128)(2,1)S(1)}, u32[]{:S(2)}, u32[]{:S(2)}) collective-permute-start(bf16[32,4608]{1,0:T(8,128)(2,1)S(1)} %get-tuple-element.23.own_ref), channel_id=1, source_target_pairs={{0,2},{2,0},{4,6},{6,4},{8,10},{10,8},{12,14},{14,12},{1,3},{3,1},... | collective-permute-start | bytes 884744 | tf_op jit(solution)/shard_map/ppermute | solution.py:424
  25.7 2.8 %copy-start.2 = (bf16[6,32,32,15]{2,1,3,0:T(8,128)(2,1)S(1)}, bf16[6,32,32,15]{2,1,3,0:T(8,128)(2,1)}, u32[]{:S(2)}) copy-start(bf16[6,32,32,15]{2,1,3,0:T(8,128)(2,1)} %param.20) | copy-start | bytes 552964
  25.7 2.8 %copy-start.4 = (bf16[32,32,14]{1,0,2:T(8,128)(2,1)S(1)}, bf16[32,32,14]{1,0,2:T(8,128)(2,1)}, u32[]{:S(2)}) copy-start(bf16[32,32,14]{1,0,2:T(8,128)(2,1)} %param.19) | copy-start | bytes 86020
  25.7 2.8 %copy-start.7 = (s32[15,6]{0,1:T(8,128)S(1)}, s32[15,6]{0,1:T(8,128)}, u32[]{:S(2)}) copy-start(s32[15,6]{0,1:T(8,128)} %param.21) | copy-start | bytes 1084

commit v9 on v8

--- a/solution.py
+++ b/solution.py
@@ -50,11 +50,12 @@
 
 
 def leaf_kernel(
-    vec_hbm, order_hbm, basis_hbm, ordered_ref, zero_ref, masked_hbm,
-    vec_ref, order_ref, basis_ref, stacked, masked_ref, sems, out_sems,
+    vec_hbm, order_hbm, basis_hbm, ordered_ref, message_ref, masked_ref,
+    vec_ref, order_ref, basis_ref, stacked, sems,
 ):
     columns, points = vec_ref.shape
     rank = basis_ref.shape[0]
+    halo = REACH * 64
     pairs = ((order_hbm, order_ref), (vec_hbm, vec_ref), (basis_hbm, basis_ref))
     copies = [pltpu.make_async_copy(src, dst, sems.at[i]) for i, (src, dst) in enumerate(pairs)]
     for copy in copies:
@@ -69,23 +70,19 @@
 
     copies[2].wait()
     mine = (iota((256, 512), 0) & 7) == (iota((256, 512), 1) >> 6)
-    writes = []
     for g in range(points // 512):
         one = basis_ref[:, g * 512 : (g + 1) * 512].astype(F32)
         eight = jnp.broadcast_to(one[:, None, :], (rank, 8, 512)).reshape(256, 512)
         masked = jnp.where(mine, eight, 0.0).astype(BF)
         masked_ref[g] = masked
-        writes.append(pltpu.make_async_copy(masked_ref.at[g], masked_hbm.at[g], out_sems.at[g]))
-        writes[-1].start()
         coeffs = dot(ordered_ref[:, g * 512 : (g + 1) * 512], masked, NT).astype(BF)
-        zero_ref[:, g * 256 : (g + 1) * 256] = coeffs
-    for write in writes:
-        write.wait()
+        message_ref[:, halo + g * 256 : halo + (g + 1) * 256] = coeffs
+    odd = lax.axis_index("leaf") % 2 == 1
+    message_ref[:, :halo] = jnp.where(odd, ordered_ref[:, :halo], ordered_ref[:, points - halo :])
 
 
 def lift_kernel(
-    zero_ref, ordered_ref, transfer_ref, first_ref, second_ref, copies_ref, weights_hbm,
-    rows32, weights_ref, sem,
+    message_ref, ordered_ref, transfer_ref, lifted_ref, second_ref, copies_ref, weights_ref, rows32,
 ):
     rank = 32
     base = REACH * 64
@@ -103,9 +100,7 @@
             rows32[m * 4 + q] = jnp.where(family, dot(turned, spread[q], NN), 0.0)
     for k in range(16):
         weights_ref[k] = rows32[:, k * 8 : k * 8 + 8, :].reshape(256, 256).astype(BF)
-    write = pltpu.make_async_copy(weights_ref, weights_hbm, sem)
-    write.start()
-    coeffs = [zero_ref[:, g * 256 : (g + 1) * 256] for g in range(8)] + [None] * 8
+    coeffs = [message_ref[:, base + g * 256 : base + (g + 1) * 256] for g in range(8)] + [None] * 8
     for n in range(7):
         lifted = dot(coeffs[2 * n], weights_ref[2 * n], NN) + dot(coeffs[2 * n + 1], weights_ref[2 * n + 1], NN)
         coeffs[8 + n] = lifted.astype(BF)
@@ -118,13 +113,11 @@
     for q in range(copies_ref.shape[0]):
         copies_ref[q] = tile
     odd = lax.axis_index("leaf") % 2 == 1
-    low, high = ordered_ref[:, :base], ordered_ref[:, points - base :]
-    first_ref[:, :base] = jnp.where(odd, low, high)
-    second_ref[:, :base] = jnp.where(odd, high, low)
+    second_ref[:, :base] = jnp.where(odd, ordered_ref[:, points - base :], ordered_ref[:, :base])
     for g in range(16):
-        first_ref[:, base + g * 256 : base + (g + 1) * 256] = coeffs[g]
         second_ref[:, base + g * 256 : base + (g + 1) * 256] = coeffs[g]
-    write.wait()
+    for g in range(8):
+        lifted_ref[:, g * 256 : (g + 1) * 256] = coeffs[8 + g]
 
 
 def lane_numbers(rows):
@@ -259,10 +252,10 @@
 
 
 def outer_kernel(
-    ordered_ref, own_ref, first_ref, second_ref, near_in, blocks_ref,
-    near_ref, matrices_ref, spots_ref, inverse_ref, weights_hbm, masked_hbm, hot_ref, six_ref,
+    ordered_ref, own_ref, first0_ref, first1_ref, second_ref, near_in, blocks_ref,
+    near_ref, matrices_ref, spots_ref, inverse_ref, weights_ref, masked_ref, hot_ref, six_ref,
     applied_hbm,
-    applied_ref, leaves, nodes, far, stacked, stacked_nodes, edges, weights_ref, masked_ref, sems, out_sems,
+    applied_ref, leaves, nodes, far, stacked, stacked_nodes, edges, sems, out_sems,
 ):
     columns, points = ordered_ref.shape
     halo = REACH * 64
@@ -272,13 +265,11 @@
         pltpu.make_async_copy(blocks_ref.at[pl.ds(at, REACH)], edges.at[i], sems.at[i])
         for i, at in enumerate((0, count - REACH))
     ]
-    copies.append(pltpu.make_async_copy(weights_hbm, weights_ref, sems.at[2]))
-    copies.append(pltpu.make_async_copy(masked_hbm, masked_ref, sems.at[3]))
     for copy in copies:
         copy.start()
 
     odd = device % 2
-    for ref, right in ((first_ref, 1 - odd), (second_ref, odd)):
+    for ref, right in ((first0_ref, 1 - odd), (second_ref, odd)):
         for c in range(halo // 128):
             place_leaves(leaves, right * (REACH + count) + c * 2, ref[:, c * 128 : (c + 1) * 128])
     near_ends = REACH * 64 * 2 // 128
@@ -288,9 +279,15 @@
     nodes[3 * 128] = jnp.zeros((columns, 128), BF)
     lane, row = iota((256, 1024), 1), iota((256, 1024), 0)
     spread = jnp.where(row == (lane & 31) * 8 + (lane >> 7), 1.0, 0.0).astype(BF)
-    for side, ref in ((1, own_ref), (2 - 2 * odd, first_ref), (2 * odd, second_ref)):
+    for side, ref in ((1, own_ref), (2 - 2 * odd, None), (2 * odd, second_ref)):
         for n in range(16):
-            stacked_nodes[n * columns : (n + 1) * columns, :] = ref[:, halo + n * 256 : halo + (n + 1) * 256]
+            if ref is not None:
+                chunk = ref[:, halo + n * 256 : halo + (n + 1) * 256]
+            elif n < 8:
+                chunk = first0_ref[:, halo + n * 256 : halo + (n + 1) * 256]
+            else:
+                chunk = first1_ref[:, (n - 8) * 256 : (n - 7) * 256]
+            stacked_nodes[n * columns : (n + 1) * columns, :] = chunk
         for c in range(0, 8, 2):
             out = dot(stacked_nodes[...], spread[:, c * 128 : (c + 2) * 128], NN)
             for n in range(16):
@@ -395,36 +392,30 @@
     matrices = couplings.reshape(6, rank * rank, -1)
 
     any_spec = pl.BlockSpec(memory_space=pl.ANY)
-    ordered, zero, masked = call(
+    ordered, own0, masked = call(
         leaf_kernel,
-        [((columns, points), BF), ((columns, 2048), BF), pltpu.HBM((points // 512, 256, 512), BF)],
+        [((columns, points), BF), ((columns, halo + 2048), BF), ((points // 512, 256, 512), BF)],
         [
             pltpu.VMEM(vectors.shape, BF), pltpu.VMEM(order.shape, jnp.int32),
             pltpu.VMEM(leaf_basis.shape, BF), pltpu.VMEM((points // 256 * columns, 256), BF),
-            pltpu.VMEM((points // 512, 256, 512), BF), pltpu.SemaphoreType.DMA((3,)),
-            pltpu.SemaphoreType.DMA((points // 512,)),
+            pltpu.SemaphoreType.DMA((3,)),
         ],
         [any_spec] * 3, 10**9, "leaf", tuple(in_hbm(x) for x in (vectors, order, leaf_basis)),
-        out_specs=[VMEM, VMEM, any_spec],
     )
     pairs = [(i, i ^ 1) for i in range(devices)]
     odds = [(i, i + 1) for i in range(1, devices - 1, 2)]
-    to_first, to_second, copies, weights = call(
+    first0 = lax.ppermute(own0, "leaf", pairs)
+    own1, own, copies, weights = call(
         lift_kernel,
         [
-            ((columns, halo + 4096), BF), ((columns, halo + 4096), BF), ((devices, columns, 128), BF),
-            pltpu.HBM((16, 256, 256), BF),
+            ((columns, 2048), BF), ((columns, halo + 4096), BF), ((devices, columns, 128), BF),
+            ((16, 256, 256), BF),
         ],
-        [
-            pltpu.VMEM((rank, 128, 256), F32), pltpu.VMEM((16, 256, 256), BF),
-            pltpu.SemaphoreType.DMA(()),
-        ],
-        [VMEM] * 3, 10**6, "lift", (zero, ordered, moves), out_specs=[VMEM] * 3 + [any_spec],
-    )
-    first = lax.ppermute(to_first, "leaf", pairs)
-    second = lax.ppermute(to_second, "leaf", odds + [(j, i) for i, j in odds])
-    gathered = lax.all_to_all(copies, "leaf", 0, 0)
-    gathered, order, ordered_late = lax.optimization_barrier((gathered, order, ordered))
+        [pltpu.VMEM((rank, 128, 256), F32)], [VMEM] * 3, 2 * 10**9, "lift", (own0, ordered, moves),
+    )
+    first1 = lax.ppermute(own1, "leaf", pairs)
+    second = lax.ppermute(own, "leaf", odds + [(j, i) for i, j in odds])
+    first0, order, ordered = lax.optimization_barrier((first0, order, ordered))
     coupling_rows, spots, hot, blocks = call(
         matrices_kernel,
         [
@@ -432,16 +423,18 @@
             ((points // 256, 256), jnp.int32),
         ],
         [pltpu.VMEM((rank, 128, 256), F32)],
-        [VMEM] * 3, 10**6, "matrices", (matrices, lists_t, order),
+        [VMEM] * 3, 4 * 10**9, "matrices", (matrices, lists_t, order),
     )
     (near_part,) = call(
         near_kernel, [((columns, points), F32)],
         [pltpu.VMEM((points // 64, columns, 128), BF)],
-        [VMEM, VMEM, SMEM], 10**6, "near", (ordered_late, near_blocks, near_t),
-    )
+        [VMEM, VMEM, SMEM], 4 * 10**9, "near", (ordered, near_blocks, near_t),
+    )
+    copies, near_part, blocks = lax.optimization_barrier((copies, near_part, blocks))
+    gathered = lax.all_to_all(copies, "leaf", 0, 0)
     (six,) = call(
         root_kernel, [((columns, 256), F32)], [pltpu.VMEM((2 * devices, columns, 32), F32)],
-        [VMEM] * 3 + [SMEM], 10**6, "root",
+        [VMEM] * 3 + [SMEM], 2 * 10**9, "root",
         (
             gathered, jnp.transpose(top_transfers, (2, 0, 1)), jnp.transpose(top_couplings, (0, 3, 1, 2)),
             jnp.transpose(top_lists),
@@ -454,15 +447,14 @@
             pltpu.VMEM((columns, points), F32), pltpu.VMEM((points // 64 + 2 * REACH, columns, 128), BF),
             pltpu.VMEM((385, columns, 128), BF), pltpu.VMEM((columns, 4096), F32),
             pltpu.VMEM((points // 256 * columns, 256), BF), pltpu.VMEM((16 * columns, 256), BF),
-            pltpu.VMEM((2, REACH) + near_blocks.shape[1:], BF), pltpu.VMEM((16, 256, 256), BF),
-            pltpu.VMEM((points // 512, 256, 512), BF), pltpu.SemaphoreType.DMA((4,)),
+            pltpu.VMEM((2, REACH) + near_blocks.shape[1:], BF), pltpu.SemaphoreType.DMA((2,)),
             pltpu.SemaphoreType.DMA((points // 1024,)),
         ],
-        [VMEM] * 5 + [any_spec, SMEM, VMEM, SMEM, VMEM, any_spec, any_spec, VMEM, VMEM],
+        [VMEM] * 6 + [any_spec, SMEM, VMEM, SMEM] + [VMEM] * 5,
         4 * 10**9, "outer",
         (
-            ordered_late, to_first, first, second, near_part, in_hbm(near_blocks),
-            near_t, coupling_rows, spots, blocks, in_hbm(weights), in_hbm(masked), hot, six,
+            ordered, own, first0, first1, second, near_part, in_hbm(near_blocks),
+            near_t, coupling_rows, spots, blocks, weights, masked, hot, six,
         ),
         out_specs=[any_spec],
     )

time: 38.7 us -> 44.8 us (1.16)
  blocking collectives: 12.6 us -> 0 us
  starting transfers between devices: 6.46 us -> 14.5 us
  local copies, waits for them, and re-layouts: 0.04 us -> 6.98 us
  waiting for transfers between devices: 0.03 us -> 5.93 us
  Pallas kernels: 19.3 us -> 16.9 us
    all_to_all x1 -> x0, blocking collectives: 12.6 us -> none  [local(): gathered = lax.all_to_all(copies, 'leaf', 0, 0)]
    unnamed x18 -> x34, local copies, waits for them, and re-layouts: 0.04 us -> 6.98 us
    all_to_all x0 -> x1, starting transfers between devices: none -> 6.06 us  [local(): gathered = lax.all_to_all(copies, 'leaf', 0, 0)]
    ppermute x2 -> x3, waiting for transfers between devices: 0.03 us -> 4.48 us  [the longest x1 4.01 us: local(): first1 = lax.ppermute(own1, 'leaf', pairs)]
    pallas_call x6, Pallas kernels: 19.3 us -> 16.9 us  [call(): pl.pallas_call(kernel, out_shape=[jax.ShapeDtypeStruct(*o) if isinstance(...]
    ppermute x2 -> x3, starting transfers between devices: 6.46 us -> 8.41 us  [the longest x1 4.78 us: local(): first1 = lax.ppermute(own1, 'leaf', pairs)]
    all_to_all x0 -> x1, waiting for transfers between devices: none -> 1.45 us  [local(): gathered = lax.all_to_all(copies, 'leaf', 0, 0)]
  transfers between devices with their start and end apart: 2 -> 4, of which waited for: 0 -> 3; matrix products, arithmetic and copies ran while one was open for 0% -> 0% of each run, Pallas kernels for 11% -> 9%
where the time goes in v9:
time: 44.8 us; the launch traced here: 44.5 us
  Pallas kernels  16.9 us (38%)
  starting transfers between devices  14.5 us (32%)
  local copies, waits for them, and re-layouts  6.98 us (16%)
  waiting for transfers between devices  5.93 us (13%)
    pallas_call x6, Pallas kernels, call(): pl.pallas_call(kernel, out_shape=[jax.ShapeDtypeStruct(*o) if isinstance(...  16.9 us
    unnamed x34, local copies, waits for them, and re-layouts  6.98 us
    all_to_all x1, starting transfers between devices, local(): gathered = lax.all_to_all(copies, 'leaf', 0, 0)  6.06 us
    ppermute x1, starting transfers between devices, local(): first1 = lax.ppermute(own1, 'leaf', pairs)  4.78 us
    ppermute x1, waiting for transfers between devices, local(): first1 = lax.ppermute(own1, 'leaf', pairs)  4.01 us
    ppermute x1, starting transfers between devices, local(): first0 = lax.ppermute(own0, 'leaf', pairs)  2.97 us
    all_to_all x1, waiting for transfers between devices, local(): gathered = lax.all_to_all(copies, 'leaf', 0, 0)  1.45 us
  transfers between devices with their start and end apart: 4, of which 3 were waited for; matrix products, arithmetic and copies ran while one was open for 0% of the time, Pallas kernels for 9%

profile of v9, /device:TPU:0, one launch (start us, length us, event | category | flops | bytes accessed | tf_op | source)
XLA Modules:
  0.0 44.5 jit_solution(15697849129310643597)
XLA Ops:
  0.0 0.0 copy-start.3
  0.0 3.2 %leaf.1 = (bf16[32,4096]{1,0:T(8,128)(2,1)S(1)}, bf16[32,2560]{1,0:T(8,128)(2,1)S(1)}, bf16[8,256,512]{2,1,0:T(8,128)(2,1)S(1)}) custom-call(bf16[32,4096]{1,0:T(8,128)(2,1)} %vec_hbm.1, s32[32,128]{1,0:T(8,128)} %bitcast.12, bf16[32,4096]{1,0:T(8,128)(2,1)} %basis_hbm.1), custom_call_target="tpu_custom_call" | custom-call | flops 1000000000 | tf_op jit(solution)/shard_map/leaf/pallas_call | solution.py:368
  3.2 0.0 copy-start.9
  3.2 1.3 %copy-done.9 = bf16[8,256,512]{2,1,0:T(8,128)(2,1)} copy-done((bf16[8,256,512]{2,1,0:T(8,128)(2,1)}, bf16[8,256,512]{2,1,0:T(8,128)(2,1)S(1)}, u32[]{:S(2)}) %copy-start.9) | copy-done | bytes 2097176
  4.5 3.0 %collective-permute-start = (bf16[32,2560]{1,0:T(8,128)(2,1)S(1)}, bf16[32,2560]{1,0:T(8,128)(2,1)S(1)}, u32[]{:S(2)}, u32[]{:S(2)}) collective-permute-start(bf16[32,2560]{1,0:T(8,128)(2,1)S(1)} %get-tuple-element.22.message_ref), channel_id=1, source_target_pairs={{0,2},{2,0},{4,6},{6,4},{8,10},{10,8},{12,14},{14,12},{1,3},{3,1},... | collective-permute-start | bytes 491528 | tf_op jit(solution)/shard_map/ppermute | solution.py:407
  7.5 0.0 copy-done.3
  7.5 0.0 copy-start
  7.5 0.0 copy-start.8
  7.5 2.4 %lift.1 = (bf16[32,2048]{1,0:T(8,128)(2,1)S(1)}, bf16[32,4608]{1,0:T(8,128)(2,1)S(1)}, bf16[8,32,128]{2,1,0:T(8,128)(2,1)}, bf16[16,256,256]{2,1,0:T(8,128)(2,1)S(1)}) custom-call(bf16[32,2560]{1,0:T(8,128)(2,1)S(1)} %get-tuple-element.22.message_ref, bf16[32,4096]{1,0:T(8,128)(2,1)S(1)} %get-tuple-element.24.ordered_ref, bf16[1024,126]{1,0:T(8,128)(2,1)S(1)} %bitcast.10), custom_call_target="tpu_custom_call" | custom-call | flops 2000000000 | tf_op jit(solution)/shard_map/lift/pallas_call | solution.py:368
  9.9 0.0 copy-start.11
  9.9 1.3 %copy-done.11 = bf16[16,256,256]{2,1,0:T(8,128)(2,1)} copy-done((bf16[16,256,256]{2,1,0:T(8,128)(2,1)}, bf16[16,256,256]{2,1,0:T(8,128)(2,1)S(1)}, u32[]{:S(2)}) %copy-start.11) | copy-done | bytes 2097176
  11.2 0.5 %collective-permute-done.first0_ref = bf16[32,2560]{1,0:T(8,128)(2,1)S(1)} collective-permute-done((bf16[32,2560]{1,0:T(8,128)(2,1)S(1)}, bf16[32,2560]{1,0:T(8,128)(2,1)S(1)}, u32[]{:S(2)}, u32[]{:S(2)}) %collective-permute-start) | collective-permute-done | bytes 163872 | tf_op jit(solution)/shard_map/ppermute | solution.py:407
  11.7 0.0 copy-done
  11.7 0.0 copy-done.8
  11.7 0.0 copy-start.1
  11.7 0.0 copy-start.5
  11.7 0.0 copy-start.6
  11.7 1.7 %near.1.near_in = f32[32,4096]{1,0:T(8,128)S(1)} custom-call(bf16[32,4096]{1,0:T(8,128)(2,1)S(1)} %get-tuple-element.24.ordered_ref, bf16[64,64,256]{2,1,0:T(8,128)(2,1)S(1)} %copy-done, s32[4,64]{1,0:T(4,128)S(1)} %bitcast.16), custom_call_target="tpu_custom_call" | custom-call | flops 4000000000 | tf_op jit(solution)/shard_map/near/pallas_call | solution.py:368
  13.4 0.0 copy-done.1
  13.4 0.0 copy-done.5
  13.4 0.0 copy-done.6
  13.4 0.0 copy-start.2
  13.5 0.0 copy-start.4
  13.5 0.0 copy-start.7
  13.5 1.1 %matrices.1 = (bf16[16,256,256]{2,1,0:T(8,128)(2,1)S(1)}, s32[8,128]{1,0:T(8,128)S(1)}, bf16[16,256,256]{2,1,0:T(8,128)(2,1)S(1)}, s32[16,256]{1,0:T(8,128)S(1)}) custom-call(bf16[6,1024,126]{2,1,0:T(8,128)(2,1)S(1)} %bitcast.8, s32[6,126]{1,0:T(8,128)S(1)} %bitcast.14, s32[32,128]{1,0:T(8,128)S(1)} %bitcast.13), custom_call_target="tpu_custom_call" | custom-call | flops 4000000000 | tf_op jit(solution)/shard_map/matrices/pallas_call | solution.py:368
  14.6 0.0 copy-start.13
  14.6 1.3 %copy-done.13 = bf16[16,256,256]{2,1,0:T(8,128)(2,1)} copy-done((bf16[16,256,256]{2,1,0:T(8,128)(2,1)}, bf16[16,256,256]{2,1,0:T(8,128)(2,1)S(1)}, u32[]{:S(2)}) %copy-start.13) | copy-done | bytes 2097176
  15.9 0.0 copy-start.15
  15.9 1.4 %copy-done.15 = bf16[16,256,256]{2,1,0:T(8,128)(2,1)} copy-done((bf16[16,256,256]{2,1,0:T(8,128)(2,1)}, bf16[16,256,256]{2,1,0:T(8,128)(2,1)S(1)}, u32[]{:S(2)}) %copy-start.15) | copy-done | bytes 2097176
  17.3 6.1 %all-to-all-start = ((bf16[8,32,128]{2,1,0:T(8,128)(2,1)}), bf16[8,32,128]{2,1,0:T(8,128)(2,1)S(1)}, u32[]{:S(2)}, u32[]{:S(2)}) async-start(bf16[8,32,128]{2,1,0:T(8,128)(2,1)} %get-tuple-element.38), calls=%async_computation | async-start | bytes 131072 | tf_op jit(solution)/shard_map/all_to_all | solution.py:434
  23.4 0.7 %collective-permute-start.2 = (bf16[32,4608]{1,0:T(8,128)(2,1)S(1)}, bf16[32,4608]{1,0:T(8,128)(2,1)S(1)}, u32[]{:S(2)}, u32[]{:S(2)}) collective-permute-start(bf16[32,4608]{1,0:T(8,128)(2,1)S(1)} %get-tuple-element.25.own_ref), channel_id=1, source_target_pairs={{2,4},{6,8},{10,12},{4,2},{8,6},{12,10},{3,5},{7,9},{11,13},{5,3},... | collective-permute-start | bytes 884744 | tf_op jit(solution)/shard_map/ppermute | solution.py:417
  24.0 4.8 %collective-permute-start.1 = (bf16[32,2048]{1,0:T(8,128)(2,1)S(1)}, bf16[32,2048]{1,0:T(8,128)(2,1)S(1)}, u32[]{:S(2)}, u32[]{:S(2)}) collective-permute-start(bf16[32,2048]{1,0:T(8,128)(2,1)S(1)} %get-tuple-element.27), channel_id=1, source_target_pairs={{0,2},{2,0},{4,6},{6,4},{8,10},{10,8},{12,14},{14,12},{1,3},{3,1},... | collective-permute-start | bytes 393224 | tf_op jit(solution)/shard_map/ppermute | solution.py:416
  28.8 1.5 %all-to-all-done.gathered_ref = bf16[8,32,128]{2,1,0:T(8,128)(2,1)S(1)} async-done(((bf16[8,32,128]{2,1,0:T(8,128)(2,1)}), bf16[8,32,128]{2,1,0:T(8,128)(2,1)S(1)}, u32[]{:S(2)}, u32[]{:S(2)}) %all-to-all-start) | async-done | bytes 65568 | tf_op jit(solution)/shard_map/all_to_all | solution.py:434
  30.3 0.0 copy-done.2
  30.3 0.0 copy-done.4
  30.3 0.0 copy-done.7
  30.3 0.0 copy-start.10
  30.3 0.0 copy-start.12
  30.3 0.0 copy-start.14
  30.3 1.7 %root.1.six_ref = f32[32,256]{1,0:T(8,128)S(1)} custom-call(bf16[8,32,128]{2,1,0:T(8,128)(2,1)S(1)} %all-to-all-done.gathered_ref, bf16[14,32,32]{2,1,0:T(8,128)(2,1)S(1)} %bitcast.11, bf16[6,15,32,32]{3,2,1,0:T(8,128)(2,1)S(1)} %bitcast.9, s32[6,15]{1,0:T(8,128)S(1)} %bitcast.15), custom_call_target="tpu_custom_call" | custom-call | flops 2000000000 | tf_op jit(solution)/shard_map/root/pallas_call | solution.py:368
  32.0 4.0 %collective-permute-done.1.first1_ref = bf16[32,2048]{1,0:T(8,128)(2,1)S(1)} collective-permute-done((bf16[32,2048]{1,0:T(8,128)(2,1)S(1)}, bf16[32,2048]{1,0:T(8,128)(2,1)S(1)}, u32[]{:S(2)}, u32[]{:S(2)}) %collective-permute-start.1) | collective-permute-done | bytes 131104 | tf_op jit(solution)/shard_map/ppermute | solution.py:416
  36.0 0.0 collective-permute-done.2.second_ref
  36.0 0.0 copy-done.10
  36.0 0.0 copy-done.12
  36.0 0.0 copy-done.14
  36.0 0.0 copy-start.16
  36.0 1.6 %copy-done.16 = bf16[16,256,256]{2,1,0:T(8,128)(2,1)S(1)} copy-done((bf16[16,256,256]{2,1,0:T(8,128)(2,1)S(1)}, bf16[16,256,256]{2,1,0:T(8,128)(2,1)}, u32[]{:S(2)}) %copy-start.16) | copy-done | bytes 2097176
  37.6 6.9 %outer.1 = f32[32,4096]{1,0:T(8,128)} custom-call(bf16[32,4096]{1,0:T(8,128)(2,1)S(1)} %get-tuple-element.24.ordered_ref, bf16[32,4608]{1,0:T(8,128)(2,1)S(1)} %get-tuple-element.25.own_ref, bf16[32,2560]{1,0:T(8,128)(2,1)S(1)} %collective-permute-done.first0_ref, bf16[32,2048]{1,0:T(8,128)(2,1)S(1)} %collective-permute-done.1.first1_ref, ...), custom_call_target="tpu_custom_call" | custom-call | flops 4000000000 | tf_op jit(solution)/shard_map/outer/pallas_call | solution.py:368
Async XLA Ops:
  0.0 7.5 %copy-start.3 = (bf16[32,32,126]{2,1,0:T(8,128)(2,1)S(1)}, bf16[32,32,126]{2,1,0:T(8,128)(2,1)}, u32[]{:S(2)}) copy-start(bf16[32,32,126]{2,1,0:T(8,128)(2,1)} %param.16) | copy-start | bytes 774148
  3.2 1.3 %copy-start.9 = (bf16[8,256,512]{2,1,0:T(8,128)(2,1)}, bf16[8,256,512]{2,1,0:T(8,128)(2,1)S(1)}, u32[]{:S(2)}) copy-start(bf16[8,256,512]{2,1,0:T(8,128)(2,1)S(1)} %get-tuple-element.36.masked_ref) | copy-start | bytes 6291460
  4.5 7.2 %collective-permute-start = (bf16[32,2560]{1,0:T(8,128)(2,1)S(1)}, bf16[32,2560]{1,0:T(8,128)(2,1)S(1)}, u32[]{:S(2)}, u32[]{:S(2)}) collective-permute-start(bf16[32,2560]{1,0:T(8,128)(2,1)S(1)} %get-tuple-element.22.message_ref), channel_id=1, source_target_pairs={{0,2},{2,0},{4,6},{6,4},{8,10},{10,8},{12,14},{14,12},{1,3},{3,1},... | collective-permute-start | bytes 491528 | tf_op jit(solution)/shard_map/ppermute | solution.py:407
  7.5 4.2 %copy-start = (bf16[64,64,256]{2,1,0:T(8,128)(2,1)S(1)}, bf16[64,64,256]{2,1,0:T(8,128)(2,1)}, u32[]{:S(2)}) copy-start(bf16[64,64,256]{2,1,0:T(8,128)(2,1)} %blocks_ref.3) | copy-start | bytes 6291460
  7.5 4.2 %copy-start.8 = (s32[64,4]{0,1:T(4,128)S(1)}, s32[64,4]{0,1:T(4,128)}, u32[]{:S(2)}) copy-start(s32[64,4]{0,1:T(4,128)} %param.15) | copy-start | bytes 3076
  9.9 1.3 %copy-start.11 = (bf16[16,256,256]{2,1,0:T(8,128)(2,1)}, bf16[16,256,256]{2,1,0:T(8,128)(2,1)S(1)}, u32[]{:S(2)}) copy-start(bf16[16,256,256]{2,1,0:T(8,128)(2,1)S(1)} %get-tuple-element.35.weights_ref) | copy-start | bytes 6291460
  11.7 1.7 %copy-start.1 = (bf16[6,32,32,126]{3,2,1,0:T(8,128)(2,1)S(1)}, bf16[6,32,32,126]{3,2,1,0:T(8,128)(2,1)}, u32[]{:S(2)}) copy-start(bf16[6,32,32,126]{3,2,1,0:T(8,128)(2,1)} %param.17) | copy-start | bytes 4644868
  11.7 1.7 %copy-start.5 = (s32[4096]{0:T(1024)S(1)}, s32[4096]{0:T(1024)}, u32[]{:S(2)}) copy-start(s32[4096]{0:T(1024)} %param.12) | copy-start | bytes 49156
  11.7 1.7 %copy-start.6 = (s32[126,6]{0,1:T(8,128)S(1)}, s32[126,6]{0,1:T(8,128)}, u32[]{:S(2)}) copy-start(s32[126,6]{0,1:T(8,128)} %param.18) | copy-start | bytes 9076
  13.4 16.8 %copy-start.2 = (bf16[6,32,32,15]{2,1,3,0:T(8,128)(2,1)S(1)}, bf16[6,32,32,15]{2,1,3,0:T(8,128)(2,1)}, u32[]{:S(2)}) copy-start(bf16[6,32,32,15]{2,1,3,0:T(8,128)(2,1)} %param.20) | copy-start | bytes 552964
  13.5 16.8 %copy-start.4 = (bf16[32,32,14]{1,0,2:T(8,128)(2,1)S(1)}, bf16[32,32,14]{1,0,2:T(8,128)(2,1)}, u32[]{:S(2)}) copy-start(bf16[32,32,14]{1,0,2:T(8,128)(2,1)} %param.19) | copy-start | bytes 86020
  13.5 16.8 %copy-start.7 = (s32[15,6]{0,1:T(8,128)S(1)}, s32[15,6]{0,1:T(8,128)}, u32[]{:S(2)}) copy-start(s32[15,6]{0,1:T(8,128)} %param.21) | copy-start | bytes 1084
  14.6 1.3 %copy-start.13 = (bf16[16,256,256]{2,1,0:T(8,128)(2,1)}, bf16[16,256,256]{2,1,0:T(8,128)(2,1)S(1)}, u32[]{:S(2)}) copy-start(bf16[16,256,256]{2,1,0:T(8,128)(2,1)S(1)} %get-tuple-element.32.matrices_ref) | copy-start | bytes 6291460
  15.9 1.4 %copy-start.15 = (bf16[16,256,256]{2,1,0:T(8,128)(2,1)}, bf16[16,256,256]{2,1,0:T(8,128)(2,1)S(1)}, u32[]{:S(2)}) copy-start(bf16[16,256,256]{2,1,0:T(8,128)(2,1)S(1)} %get-tuple-element.37.hot_ref) | copy-start | bytes 6291460
  17.3 13.0 %all-to-all-start = ((bf16[8,32,128]{2,1,0:T(8,128)(2,1)}), bf16[8,32,128]{2,1,0:T(8,128)(2,1)S(1)}, u32[]{:S(2)}, u32[]{:S(2)}) async-start(bf16[8,32,128]{2,1,0:T(8,128)(2,1)} %get-tuple-element.38), calls=%async_computation | async-start | bytes 131072 | tf_op jit(solution)/shard_map/all_to_all | solution.py:434
  23.4 12.6 %collective-permute-start.2 = (bf16[32,4608]{1,0:T(8,128)(2,1)S(1)}, bf16[32,4608]{1,0:T(8,128)(2,1)S(1)}, u32[]{:S(2)}, u32[]{:S(2)}) collective-permute-start(bf16[32,4608]{1,0:T(8,128)(2,1)S(1)} %get-tuple-element.25.own_ref), channel_id=1, source_target_pairs={{2,4},{6,8},{10,12},{4,2},{8,6},{12,10},{3,5},{7,9},{11,13},{5,3},... | collective-permute-start | bytes 884744 | tf_op jit(solution)/shard_map/ppermute | solution.py:417
  24.0 11.9 %collective-permute-start.1 = (bf16[32,2048]{1,0:T(8,128)(2,1)S(1)}, bf16[32,2048]{1,0:T(8,128)(2,1)S(1)}, u32[]{:S(2)}, u32[]{:S(2)}) collective-permute-start(bf16[32,2048]{1,0:T(8,128)(2,1)S(1)} %get-tuple-element.27), channel_id=1, source_target_pairs={{0,2},{2,0},{4,6},{6,4},{8,10},{10,8},{12,14},{14,12},{1,3},{3,1},... | collective-permute-start | bytes 393224 | tf_op jit(solution)/shard_map/ppermute | solution.py:416
  30.3 5.7 %copy-start.10 = (bf16[8,256,512]{2,1,0:T(8,128)(2,1)S(1)}, bf16[8,256,512]{2,1,0:T(8,128)(2,1)}, u32[]{:S(2)}) copy-start(bf16[8,256,512]{2,1,0:T(8,128)(2,1)} %copy-done.9) | copy-start | bytes 6291460
  30.3 5.7 %copy-start.12 = (bf16[16,256,256]{2,1,0:T(8,128)(2,1)S(1)}, bf16[16,256,256]{2,1,0:T(8,128)(2,1)}, u32[]{:S(2)}) copy-start(bf16[16,256,256]{2,1,0:T(8,128)(2,1)} %copy-done.11) | copy-start | bytes 6291460
  30.3 5.7 %copy-start.14 = (bf16[16,256,256]{2,1,0:T(8,128)(2,1)S(1)}, bf16[16,256,256]{2,1,0:T(8,128)(2,1)}, u32[]{:S(2)}) copy-start(bf16[16,256,256]{2,1,0:T(8,128)(2,1)} %copy-done.13) | copy-start | bytes 6291460
  36.0 1.6 %copy-start.16 = (bf16[16,256,256]{2,1,0:T(8,128)(2,1)S(1)}, bf16[16,256,256]{2,1,0:T(8,128)(2,1)}, u32[]{:S(2)}) copy-start(bf16[16,256,256]{2,1,0:T(8,128)(2,1)} %copy-done.15) | copy-start | bytes 6291460

commit v10 on v7

--- a/solution.py
+++ b/solution.py
@@ -76,14 +76,17 @@
         masked = jnp.where(mine, eight, 0.0).astype(BF)
         masked_ref[g] = masked
         coeffs = dot(ordered_ref[:, g * 512 : (g + 1) * 512], masked, NT).astype(BF)
-        message_ref[:, 2 * halo + g * 256 : 2 * halo + (g + 1) * 256] = coeffs
-    message_ref[:, :halo] = ordered_ref[:, :halo]
-    message_ref[:, halo : 2 * halo] = ordered_ref[:, points - halo :]
-
-
-def lift_kernel(message_ref, transfer_ref, lifted_ref, top_ref, weights_ref, rows32):
+        message_ref[:, halo + g * 256 : halo + (g + 1) * 256] = coeffs
+    odd = lax.axis_index("leaf") % 2 == 1
+    message_ref[:, :halo] = jnp.where(odd, ordered_ref[:, :halo], ordered_ref[:, points - halo :])
+
+
+def lift_kernel(message_ref, ordered_ref, transfer_ref, lifted_ref, top_ref, weights_ref, rows32):
     rank = 32
-    base = 2 * REACH * 64
+    base = REACH * 64
+    points = ordered_ref.shape[1]
+    odd = lax.axis_index("leaf") % 2 == 1
+    lifted_ref[:, 2048:] = jnp.where(odd, ordered_ref[:, points - base :], ordered_ref[:, :base])
 
     lane, row = iota((128, 256), 1), iota((128, 256), 0)
     family = (lane & 7) == ((row >> 1) & 7)
@@ -266,10 +269,10 @@
         copy.start()
 
     odd = device % 2
-    for ref, right in ((first0_ref, 1 - odd), (second0_ref, odd)):
+    for ref, start, right in ((first0_ref, 0, 1 - odd), (second1_ref, 2048, odd)):
         for c in range(halo // 128):
-            at = pl.multiple_of((1 - right) * halo + c * 128, 128)
-            place_leaves(leaves, right * (REACH + count) + c * 2, ref[:, pl.ds(at, 128)])
+            at = start + c * 128
+            place_leaves(leaves, right * (REACH + count) + c * 2, ref[:, at : at + 128])
     near_ends = REACH * 64 * 2 // 128
     for c in list(range(near_ends)) + list(range(count // 2 - near_ends, count // 2)):
         place_leaves(leaves, REACH + c * 2, ordered_ref[:, c * 128 : (c + 1) * 128])
@@ -282,7 +285,7 @@
     )
     for side, ref0, ref1 in sources:
         for n in range(8):
-            at = 2 * halo + n * 256
+            at = halo + n * 256
             stacked_nodes[n * columns : (n + 1) * columns, :] = ref0[:, at : at + 256]
             stacked_nodes[(8 + n) * columns : (9 + n) * columns, :] = ref1[:, n * 256 : (n + 1) * 256]
         for c in range(0, 8, 2):
@@ -392,7 +395,7 @@
     tile = max(devices // 2 * rank, 128)
     ordered, own0, masked = call(
         leaf_kernel,
-        [((columns, points), BF), ((columns, 2 * halo + 2048), BF), ((points // 512, 256, 512), BF)],
+        [((columns, points), BF), ((columns, halo + 2048), BF), ((points // 512, 256, 512), BF)],
         [
             pltpu.VMEM(vectors.shape, BF), pltpu.VMEM(order.shape, jnp.int32),
             pltpu.VMEM(leaf_basis.shape, BF), pltpu.VMEM((points // 256 * columns, 256), BF),
@@ -405,10 +408,9 @@
     first0 = lax.ppermute(own0, "leaf", pairs)
     own1, top, weights = call(
         lift_kernel,
-        [((columns, 2048), BF), ((columns, tile), BF), ((16, 256, 256), BF)],
-        [pltpu.VMEM((rank, 128, 256), F32)], [VMEM, VMEM], 10**9, "lift", (own0, moves),
-    )
-    first1 = lax.ppermute(own1, "leaf", pairs)
+        [((columns, halo + 2048), BF), ((columns, tile), BF), ((16, 256, 256), BF)],
+        [pltpu.VMEM((rank, 128, 256), F32)], [VMEM] * 3, 10**9, "lift", (own0, ordered, moves),
+    )
 
     def step(tile_sum, reached):
         return lax.ppermute(tile_sum, "leaf", [(i, i ^ reached) for i in range(devices)])
@@ -426,21 +428,19 @@
         [pltpu.VMEM((rank, 128, 256), F32)],
         [VMEM] * 3, 10**6, "matrices", (matrices, lists_t, order),
     )
-    first0, blocks, other = lax.optimization_barrier((first0, blocks, other))
+    first1 = lax.ppermute(own1, "leaf", pairs)
+    first0, top, blocks = lax.optimization_barrier((first0, top + other, blocks))
+    other = step(top, steps[-1])
     second0 = lax.ppermute(first0, "leaf", onward)
-    top = top + other
-    other = step(top, steps[-1])
-    first1, other = lax.optimization_barrier((first1, other))
-    top = top + other
+    first1, top = lax.optimization_barrier((first1, top + other))
+    other = step(top, 1)
     second1 = lax.ppermute(first1, "leaf", onward)
-    other = step(top, 1)
-    first1, ordered_late = lax.optimization_barrier((first1, ordered))
+    first1, ordered = lax.optimization_barrier((first1, ordered))
     (near_part,) = call(
         near_kernel, [((columns, points), F32)],
         [pltpu.VMEM((points // 64, columns, 128), BF)],
-        [VMEM, VMEM, SMEM], 10**6, "near", (ordered_late, near_blocks, near_t),
-    )
-    other, near_part = lax.optimization_barrier((other, near_part))
+        [VMEM, VMEM, SMEM], 10**6, "near", (ordered, near_blocks, near_t),
+    )
     (six,) = call(
         root_kernel, [((columns, 256), F32)], [pltpu.VMEM((2 * devices, columns, 32), F32)],
         [VMEM] * 4 + [SMEM], 10**6, "root",

time: 36.9 us -> 34.4 us (0.932)
  waiting for transfers between devices: 4.53 us -> 2.45 us
  starting transfers between devices: 15.6 us -> 15.1 us
    ppermute x3, waiting for transfers between devices: 4.5 us -> 2.42 us  [step(): lax.ppermute(tile_sum, 'leaf', [(i, i ^ reached) for i in range(devices)])]
    ppermute x1, starting transfers between devices: 3.82 us -> 2.02 us  [local(): second0 = lax.ppermute(first0, 'leaf', onward)]
    ppermute x1, starting transfers between devices: 3.9 us -> 4.94 us  [local(): second1 = lax.ppermute(first1, 'leaf', onward)]
  transfers between devices with their start and end apart: 7 -> 7, of which waited for: 3 -> 2; matrix products, arithmetic and copies ran while one was open for 0% -> 0% of each run, Pallas kernels for 17% -> 18%
where the time goes in v10:
time: 34.4 us; the launch traced here: 34.2 us
  Pallas kernels  16.4 us (48%)
  starting transfers between devices  15.1 us (44%)
  waiting for transfers between devices  2.45 us (7%)
    pallas_call x6, Pallas kernels, call(): pl.pallas_call(kernel, out_shape=[jax.ShapeDtypeStruct(s, t) for s, t in...  16.4 us
    ppermute x3, starting transfers between devices, step(): lax.ppermute(tile_sum, 'leaf', [(i, i ^ reached) for i in range(devices)])  5.1 us
    ppermute x1, starting transfers between devices, local(): second1 = lax.ppermute(first1, 'leaf', onward)  4.94 us
    ppermute x1, starting transfers between devices, local(): first0 = lax.ppermute(own0, 'leaf', pairs)  3.03 us
    ppermute x3, waiting for transfers between devices, step(): lax.ppermute(tile_sum, 'leaf', [(i, i ^ reached) for i in range(devices)])  2.42 us
    ppermute x1, starting transfers between devices, local(): second0 = lax.ppermute(first0, 'leaf', onward)  2.02 us
  transfers between devices with their start and end apart: 7, of which 2 were waited for; matrix products, arithmetic and copies ran while one was open for 0% of the time, Pallas kernels for 18%

profile of v10, /device:TPU:0, one launch (start us, length us, event | category | flops | bytes accessed | tf_op | source)
XLA Modules:
  0.0 34.2 jit_solution(3669301105529776054)
XLA Ops:
  0.0 0.0 copy-start.8
  0.0 3.2 %leaf.1 = (bf16[32,4096]{1,0:T(8,128)(2,1)S(1)}, bf16[32,2560]{1,0:T(8,128)(2,1)S(1)}, bf16[8,256,512]{2,1,0:T(8,128)(2,1)S(1)}) custom-call(bf16[32,4096]{1,0:T(8,128)(2,1)} %vec_hbm.1, s32[32,128]{1,0:T(8,128)} %bitcast.11, bf16[32,4096]{1,0:T(8,128)(2,1)} %basis_hbm.1), custom_call_target="tpu_custom_call" | custom-call | flops 1000000000 | tf_op jit(solution)/shard_map/leaf/pallas_call | solution.py:368
  3.2 0.0 copy-start.1
  3.2 0.0 copy-start.4
  3.2 0.0 copy-start.5
  3.2 3.0 %collective-permute-start.1 = (bf16[32,2560]{1,0:T(8,128)(2,1)S(1)}, bf16[32,2560]{1,0:T(8,128)(2,1)S(1)}, u32[]{:S(2)}, u32[]{:S(2)}) collective-permute-start(bf16[32,2560]{1,0:T(8,128)(2,1)S(1)} %get-tuple-element.22.message_ref.own0_ref), channel_id=1, source_target_pairs={{0,2},{2,0},{4,6},{6,4},{8,10},{10,8},{12,14},{14,12},{1,3},{3,1},... | collective-permute-start | bytes 491528 | tf_op jit(solution)/shard_map/ppermute | solution.py:408
  6.3 0.0 copy-done.8
  6.3 0.0 copy-start
  6.3 0.0 copy-start.7
  6.3 1.8 %lift.1 = (bf16[32,2560]{1,0:T(8,128)(2,1)S(1)}, bf16[32,128]{1,0:T(8,128)(2,1)S(1)}, bf16[16,256,256]{2,1,0:T(8,128)(2,1)S(1)}) custom-call(bf16[32,2560]{1,0:T(8,128)(2,1)S(1)} %get-tuple-element.22.message_ref.own0_ref, bf16[32,4096]{1,0:T(8,128)(2,1)S(1)} %get-tuple-element.29.ordered_ref, bf16[1024,126]{1,0:T(8,128)(2,1)S(1)} %bitcast.17), custom_call_target="tpu_custom_call" | custom-call | flops 1000000000 | tf_op jit(solution)/shard_map/lift/pallas_call | solution.py:368
  8.0 0.0 collective-permute-start
  8.1 3.1 %collective-permute-start.2 = (bf16[32,128]{1,0:T(8,128)(2,1)S(1)}, bf16[32,128]{1,0:T(8,128)(2,1)S(1)}, u32[]{:S(2)}, u32[]{:S(2)}) collective-permute-start(bf16[32,128]{1,0:T(8,128)(2,1)S(1)} %get-tuple-element.25), channel_id=1, source_target_pairs={{0,8},{2,10},{4,12},{6,14},{8,0},{10,2},{12,4},{14,6},{1,9},{3,11}... | collective-permute-start | bytes 24584 | tf_op jit(solution)/shard_map/ppermute | solution.py:416
  11.2 0.0 copy-done.1
  11.2 0.0 copy-done.4
  11.2 0.0 copy-done.5
  11.2 0.0 copy-start.2
  11.2 0.0 copy-start.3
  11.2 0.0 copy-start.6
  11.2 1.1 %matrices.1 = (bf16[16,256,256]{2,1,0:T(8,128)(2,1)S(1)}, s32[8,128]{1,0:T(8,128)S(1)}, bf16[16,256,256]{2,1,0:T(8,128)(2,1)S(1)}, s32[16,256]{1,0:T(8,128)S(1)}) custom-call(bf16[6,1024,126]{2,1,0:T(8,128)(2,1)S(1)} %bitcast.8, s32[6,126]{1,0:T(8,128)S(1)} %bitcast.13, s32[32,128]{1,0:T(8,128)S(1)} %bitcast.12), custom_call_target="tpu_custom_call" | custom-call | flops 1000000 | tf_op jit(solution)/shard_map/matrices/pallas_call | solution.py:368
  12.3 0.5 %collective-permute-done.2 = bf16[32,128]{1,0:T(8,128)(2,1)S(1)} collective-permute-done((bf16[32,128]{1,0:T(8,128)(2,1)S(1)}, bf16[32,128]{1,0:T(8,128)(2,1)S(1)}, u32[]{:S(2)}, u32[]{:S(2)}) %collective-permute-start.2) | collective-permute-done | bytes 8224 | tf_op jit(solution)/shard_map/ppermute | solution.py:416
  12.8 0.0 collective-permute-done.1.first0_ref
  12.8 2.0 %collective-permute-start.3 = (bf16[32,128]{1,0:T(8,128)(2,1)S(1)}, bf16[32,128]{1,0:T(8,128)(2,1)S(1)}, u32[]{:S(2)}, u32[]{:S(2)}) collective-permute-start(bf16[32,128]{1,0:T(8,128)(2,1)S(1)} %add.6), channel_id=1, source_target_pairs={{0,4},{2,6},{4,0},{6,2},{8,12},{10,14},{12,8},{14,10},{1,5},{3,7},... | collective-permute-start | bytes 24584 | tf_op jit(solution)/shard_map/ppermute | solution.py:416
  14.8 2.0 %collective-permute-start.4 = (bf16[32,2560]{1,0:T(8,128)(2,1)S(1)}, bf16[32,2560]{1,0:T(8,128)(2,1)S(1)}, u32[]{:S(2)}, u32[]{:S(2)}) collective-permute-start(bf16[32,2560]{1,0:T(8,128)(2,1)S(1)} %collective-permute-done.1.first0_ref), channel_id=1, source_target_pairs={{0,4},{4,8},{8,12},{6,2},{10,6},{14,10},{1,5},{5,9},{9,13},{7,3},{... | collective-permute-start | bytes 491528 | tf_op jit(solution)/shard_map/ppermute | solution.py:434
  16.8 0.0 collective-permute-done.3
  16.8 0.0 collective-permute-done.first1_ref
  16.8 4.9 %collective-permute-start.5 = (bf16[32,2560]{1,0:T(8,128)(2,1)S(1)}, bf16[32,2560]{1,0:T(8,128)(2,1)S(1)}, u32[]{:S(2)}, u32[]{:S(2)}) collective-permute-start(bf16[32,2560]{1,0:T(8,128)(2,1)S(1)} %collective-permute-done.first1_ref), channel_id=1, source_target_pairs={{0,4},{4,8},{8,12},{6,2},{10,6},{14,10},{1,5},{5,9},{9,13},{7,3},{... | collective-permute-start | bytes 491528 | tf_op jit(solution)/shard_map/ppermute | solution.py:437
  21.8 0.1 collective-permute-start.6
  21.9 0.0 copy-done
  21.9 0.0 copy-done.7
  21.9 1.7 %near.1.near_in = f32[32,4096]{1,0:T(8,128)S(1)} custom-call(bf16[32,4096]{1,0:T(8,128)(2,1)S(1)} %get-tuple-element.29.ordered_ref, bf16[64,64,256]{2,1,0:T(8,128)(2,1)S(1)} %copy-done, s32[4,64]{1,0:T(4,128)S(1)} %bitcast.15), custom_call_target="tpu_custom_call" | custom-call | flops 1000000 | tf_op jit(solution)/shard_map/near/pallas_call | solution.py:368
  23.6 1.9 %collective-permute-done.6.other_ref = bf16[32,128]{1,0:T(8,128)(2,1)S(1)} collective-permute-done((bf16[32,128]{1,0:T(8,128)(2,1)S(1)}, bf16[32,128]{1,0:T(8,128)(2,1)S(1)}, u32[]{:S(2)}, u32[]{:S(2)}) %collective-permute-start.6) | collective-permute-done | bytes 8224 | tf_op jit(solution)/shard_map/ppermute | solution.py:416
  25.5 0.0 copy-done.2
  25.5 0.0 copy-done.3
  25.5 0.0 copy-done.6
  25.5 1.7 %root.1.six_ref = f32[32,256]{1,0:T(8,128)S(1)} custom-call(bf16[32,128]{1,0:T(8,128)(2,1)S(1)} %add.7.own_ref, bf16[32,128]{1,0:T(8,128)(2,1)S(1)} %collective-permute-done.6.other_ref, bf16[14,32,32]{2,1,0:T(8,128)(2,1)S(1)} %bitcast.10, bf16[6,15,32,32]{3,2,1,0:T(8,128)(2,1)S(1)} %bitcast.9, s32[6,15]{1,0:T(8,128)S(1)} %bitcast.14), custom_call_target="tpu_custom_call" | custom-call | flops 1000000 | tf_op jit(solution)/shard_map/root/pallas_call | solution.py:368
  27.2 0.0 collective-permute-done.4.second0_ref
  27.3 0.0 collective-permute-done.5.second1_ref
  27.3 6.9 %outer.1 = f32[32,4096]{1,0:T(8,128)} custom-call(bf16[32,4096]{1,0:T(8,128)(2,1)S(1)} %get-tuple-element.29.ordered_ref, bf16[32,2560]{1,0:T(8,128)(2,1)S(1)} %get-tuple-element.22.message_ref.own0_ref, bf16[32,2560]{1,0:T(8,128)(2,1)S(1)} %get-tuple-element.24.own1_ref, bf16[32,2560]{1,0:T(8,128)(2,1)S(1)} %collective-permute-done.1.first0_ref, ...), custom_call_target="tpu_custom_call" | custom-call | flops 4000000000 | tf_op jit(solution)/shard_map/outer/pallas_call | solution.py:368
  (2 shorter events, 0.0 us)
Async XLA Ops:
  0.0 6.3 %copy-start.8 = (bf16[32,32,126]{2,1,0:T(8,128)(2,1)S(1)}, bf16[32,32,126]{2,1,0:T(8,128)(2,1)}, u32[]{:S(2)}) copy-start(bf16[32,32,126]{2,1,0:T(8,128)(2,1)} %param.16) | copy-start | bytes 774148
  3.2 7.9 %copy-start.1 = (bf16[6,32,32,126]{3,2,1,0:T(8,128)(2,1)S(1)}, bf16[6,32,32,126]{3,2,1,0:T(8,128)(2,1)}, u32[]{:S(2)}) copy-start(bf16[6,32,32,126]{3,2,1,0:T(8,128)(2,1)} %param.17) | copy-start | bytes 4644868
  3.2 7.9 %copy-start.4 = (s32[4096]{0:T(1024)S(1)}, s32[4096]{0:T(1024)}, u32[]{:S(2)}) copy-start(s32[4096]{0:T(1024)} %param.12) | copy-start | bytes 49156
  3.2 7.9 %copy-start.5 = (s32[126,6]{0,1:T(8,128)S(1)}, s32[126,6]{0,1:T(8,128)}, u32[]{:S(2)}) copy-start(s32[126,6]{0,1:T(8,128)} %param.18) | copy-start | bytes 9076
  3.2 9.5 %collective-permute-start.1 = (bf16[32,2560]{1,0:T(8,128)(2,1)S(1)}, bf16[32,2560]{1,0:T(8,128)(2,1)S(1)}, u32[]{:S(2)}, u32[]{:S(2)}) collective-permute-start(bf16[32,2560]{1,0:T(8,128)(2,1)S(1)} %get-tuple-element.22.message_ref.own0_ref), channel_id=1, source_target_pairs={{0,2},{2,0},{4,6},{6,4},{8,10},{10,8},{12,14},{14,12},{1,3},{3,1},... | collective-permute-start | bytes 491528 | tf_op jit(solution)/shard_map/ppermute | solution.py:408
  6.3 15.6 %copy-start = (bf16[64,64,256]{2,1,0:T(8,128)(2,1)S(1)}, bf16[64,64,256]{2,1,0:T(8,128)(2,1)}, u32[]{:S(2)}) copy-start(bf16[64,64,256]{2,1,0:T(8,128)(2,1)} %blocks_ref.3) | copy-start | bytes 6291460
  6.3 15.6 %copy-start.7 = (s32[64,4]{0,1:T(4,128)S(1)}, s32[64,4]{0,1:T(4,128)}, u32[]{:S(2)}) copy-start(s32[64,4]{0,1:T(4,128)} %param.15) | copy-start | bytes 3076
  8.0 8.8 %collective-permute-start = (bf16[32,2560]{1,0:T(8,128)(2,1)S(1)}, bf16[32,2560]{1,0:T(8,128)(2,1)S(1)}, u32[]{:S(2)}, u32[]{:S(2)}) collective-permute-start(bf16[32,2560]{1,0:T(8,128)(2,1)S(1)} %get-tuple-element.24.own1_ref), channel_id=1, source_target_pairs={{0,2},{2,0},{4,6},{6,4},{8,10},{10,8},{12,14},{14,12},{1,3},{3,1},... | collective-permute-start | bytes 491528 | tf_op jit(solution)/shard_map/ppermute | solution.py:431
  8.1 4.7 %collective-permute-start.2 = (bf16[32,128]{1,0:T(8,128)(2,1)S(1)}, bf16[32,128]{1,0:T(8,128)(2,1)S(1)}, u32[]{:S(2)}, u32[]{:S(2)}) collective-permute-start(bf16[32,128]{1,0:T(8,128)(2,1)S(1)} %get-tuple-element.25), channel_id=1, source_target_pairs={{0,8},{2,10},{4,12},{6,14},{8,0},{10,2},{12,4},{14,6},{1,9},{3,11}... | collective-permute-start | bytes 24584 | tf_op jit(solution)/shard_map/ppermute | solution.py:416
  11.2 14.3 %copy-start.2 = (bf16[6,32,32,15]{2,1,3,0:T(8,128)(2,1)S(1)}, bf16[6,32,32,15]{2,1,3,0:T(8,128)(2,1)}, u32[]{:S(2)}) copy-start(bf16[6,32,32,15]{2,1,3,0:T(8,128)(2,1)} %param.20) | copy-start | bytes 552964
  11.2 14.3 %copy-start.3 = (bf16[32,32,14]{1,0,2:T(8,128)(2,1)S(1)}, bf16[32,32,14]{1,0,2:T(8,128)(2,1)}, u32[]{:S(2)}) copy-start(bf16[32,32,14]{1,0,2:T(8,128)(2,1)} %param.19) | copy-start | bytes 86020
  11.2 14.3 %copy-start.6 = (s32[15,6]{0,1:T(8,128)S(1)}, s32[15,6]{0,1:T(8,128)}, u32[]{:S(2)}) copy-start(s32[15,6]{0,1:T(8,128)} %param.21) | copy-start | bytes 1084
  12.8 4.0 %collective-permute-start.3 = (bf16[32,128]{1,0:T(8,128)(2,1)S(1)}, bf16[32,128]{1,0:T(8,128)(2,1)S(1)}, u32[]{:S(2)}, u32[]{:S(2)}) collective-permute-start(bf16[32,128]{1,0:T(8,128)(2,1)S(1)} %add.6), channel_id=1, source_target_pairs={{0,4},{2,6},{4,0},{6,2},{8,12},{10,14},{12,8},{14,10},{1,5},{3,7},... | collective-permute-start | bytes 24584 | tf_op jit(solution)/shard_map/ppermute | solution.py:416
  14.8 12.5 %collective-permute-start.4 = (bf16[32,2560]{1,0:T(8,128)(2,1)S(1)}, bf16[32,2560]{1,0:T(8,128)(2,1)S(1)}, u32[]{:S(2)}, u32[]{:S(2)}) collective-permute-start(bf16[32,2560]{1,0:T(8,128)(2,1)S(1)} %collective-permute-done.1.first0_ref), channel_id=1, source_target_pairs={{0,4},{4,8},{8,12},{6,2},{10,6},{14,10},{1,5},{5,9},{9,13},{7,3},{... | collective-permute-start | bytes 491528 | tf_op jit(solution)/shard_map/ppermute | solution.py:434
  16.8 10.4 %collective-permute-start.5 = (bf16[32,2560]{1,0:T(8,128)(2,1)S(1)}, bf16[32,2560]{1,0:T(8,128)(2,1)S(1)}, u32[]{:S(2)}, u32[]{:S(2)}) collective-permute-start(bf16[32,2560]{1,0:T(8,128)(2,1)S(1)} %collective-permute-done.first1_ref), channel_id=1, source_target_pairs={{0,4},{4,8},{8,12},{6,2},{10,6},{14,10},{1,5},{5,9},{9,13},{7,3},{... | collective-permute-start | bytes 491528 | tf_op jit(solution)/shard_map/ppermute | solution.py:437
  21.8 3.7 %collective-permute-start.6 = (bf16[32,128]{1,0:T(8,128)(2,1)S(1)}, bf16[32,128]{1,0:T(8,128)(2,1)S(1)}, u32[]{:S(2)}, u32[]{:S(2)}) collective-permute-start(bf16[32,128]{1,0:T(8,128)(2,1)S(1)} %add.7.own_ref), channel_id=1, source_target_pairs={{0,2},{2,0},{4,6},{6,4},{8,10},{10,8},{12,14},{14,12},{1,3},{3,1},... | collective-permute-start | bytes 24584 | tf_op jit(solution)/shard_map/ppermute | solution.py:416

commit v11 on v10

--- a/solution.py
+++ b/solution.py
@@ -41,12 +41,12 @@
 
 
 def pick(stacked, hot, high, rows):
-    out = dot(stacked, hot, NN)
-    high = jnp.broadcast_to(high, (rows, 256))
-    total = out[:rows]
-    for block in range(1, stacked.shape[0] // rows):
-        total = jnp.where(high == block, out[block * rows : (block + 1) * rows], total)
-    return total
+    out = dot(stacked, hot, NN).reshape(-1, rows // 8, 8, 256)
+    high = jnp.broadcast_to(high, (8, 256))
+    total = out[0]
+    for block in range(1, out.shape[0]):
+        total = jnp.where((high == block)[None], out[block], total)
+    return total.reshape(rows, 256)
 
 
 def leaf_kernel(
@@ -255,7 +255,7 @@
     ordered_ref, own0_ref, own1_ref, first0_ref, first1_ref, second0_ref, second1_ref, near_in, blocks_ref,
     near_ref, matrices_ref, spots_ref, inverse_ref, weights_ref, masked_ref, hot_ref, six_ref,
     applied_hbm,
-    applied_ref, leaves, nodes, far, stacked, stacked_nodes, edges, sems, out_sems,
+    applied_ref, leaves, nodes, stacked, stacked_nodes, edges, sems, out_sems,
 ):
     columns, points = ordered_ref.shape
     halo = REACH * 64
@@ -298,7 +298,7 @@
     lane = lane_numbers(columns)
     lane_node = iota((columns, 256), 1) & 7
 
-    for g in range(16):
+    def couple(g):
         picked = []
         for i in range(8):
             parts = [nodes[spots_ref[s, g * 8 + i]] for s in range(6)]
@@ -311,18 +311,24 @@
         total = out[:columns]
         for i in range(1, 8):
             total = jnp.where(lane_node == i, out[i * columns : (i + 1) * columns], total)
-        far[:, g * 256 : (g + 1) * 256] = total
+        return total
+
+    six = six_ref[...]
+    down, at_points = [None] * 16, [None] * 8
+    for k in reversed(range(16)):
+        far = couple(k)
+        if k == 15:
+            five = far + dot(six.astype(BF), weights_ref[15], NT)
+            five = jnp.where(lane_node >= 4, five, 0.0) + six
+            parent = five.astype(BF)
+        else:
+            parent = down[8 + k // 2]
+        down[k] = (far + dot(parent, weights_ref[k], NT)).astype(BF)
+        if k < 8:
+            at_points[k] = dot(down[k], masked_ref[k], NN)
 
     for copy in copies:
         copy.wait()
-    six = six_ref[...]
-    down = [None] * 16
-    last = far[:, 15 * 256 :]
-    five = last + dot(six.astype(BF), weights_ref[15], NT)
-    five = jnp.where(lane_node >= 4, five, 0.0) + six
-    down[15] = (last + dot(five.astype(BF), weights_ref[15], NT)).astype(BF)
-    for k in reversed(range(15)):
-        down[k] = (far[:, k * 256 : (k + 1) * 256] + dot(down[8 + k // 2], weights_ref[k], NT)).astype(BF)
     groups = count // 4
     edge = REACH // 4
     for g in range(groups):
@@ -337,9 +343,7 @@
             near = near_in[:, g * 256 : (g + 1) * 256]
         else:
             near = near_group(leaves, near_ref, blocks, g * 4, device * count - REACH, columns)
-        if g % 2 == 0:
-            at_points = dot(down[g // 2], masked_ref[g // 2], NN)
-        half = at_points[:, g % 2 * 256 : (g % 2 + 1) * 256]
+        half = at_points[g // 2][:, g % 2 * 256 : (g % 2 + 1) * 256]
         stacked[g * columns : (g + 1) * columns, :] = (near + half).astype(BF)
 
     writes = []
@@ -454,7 +458,7 @@
         [((columns, points), F32)],
         [
             pltpu.VMEM((columns, points), F32), pltpu.VMEM((points // 64 + 2 * REACH, columns, 128), BF),
-            pltpu.VMEM((385, columns, 128), BF), pltpu.VMEM((columns, 4096), F32),
+            pltpu.VMEM((385, columns, 128), BF),
             pltpu.VMEM((points // 256 * columns, 256), BF), pltpu.VMEM((16 * columns, 256), BF),
             pltpu.VMEM((2, REACH) + near_blocks.shape[1:], BF), pltpu.SemaphoreType.DMA((2,)),
             pltpu.SemaphoreType.DMA((points // 1024,)),

time: 34.4 us -> 35.2 us (1.023)
  Pallas kernels: 16.4 us -> 17.2 us
    pallas_call x6, Pallas kernels: 16.4 us -> 17.2 us  [call(): pl.pallas_call(kernel, out_shape=[jax.ShapeDtypeStruct(s, t) for s, t in...]
where the time goes in v11:
time: 35.2 us; the launch traced here: 35 us
  Pallas kernels  17.2 us (49%)
  starting transfers between devices  15.1 us (43%)
  waiting for transfers between devices  2.46 us (7%)
    pallas_call x6, Pallas kernels, call(): pl.pallas_call(kernel, out_shape=[jax.ShapeDtypeStruct(s, t) for s, t in...  17.2 us
    ppermute x3, starting transfers between devices, step(): lax.ppermute(tile_sum, 'leaf', [(i, i ^ reached) for i in range(devices)])  5.1 us
    ppermute x1, starting transfers between devices, local(): second1 = lax.ppermute(first1, 'leaf', onward)  4.94 us
    ppermute x1, starting transfers between devices, local(): first0 = lax.ppermute(own0, 'leaf', pairs)  3.03 us
    ppermute x3, waiting for transfers between devices, step(): lax.ppermute(tile_sum, 'leaf', [(i, i ^ reached) for i in range(devices)])  2.42 us
    ppermute x1, starting transfers between devices, local(): second0 = lax.ppermute(first0, 'leaf', onward)  2.02 us
  transfers between devices with their start and end apart: 7, of which 2 were waited for; matrix products, arithmetic and copies ran while one was open for 0% of the time, Pallas kernels for 18%

profile of v11, /device:TPU:0, one launch (start us, length us, event | category | flops | bytes accessed | tf_op | source)
XLA Modules:
  0.0 35.0 jit_solution(4114927898000860722)
XLA Ops:
  0.0 0.0 copy-start.8
  0.0 3.2 %leaf.1 = (bf16[32,4096]{1,0:T(8,128)(2,1)S(1)}, bf16[32,2560]{1,0:T(8,128)(2,1)S(1)}, bf16[8,256,512]{2,1,0:T(8,128)(2,1)S(1)}) custom-call(bf16[32,4096]{1,0:T(8,128)(2,1)} %vec_hbm.1, s32[32,128]{1,0:T(8,128)} %bitcast.11, bf16[32,4096]{1,0:T(8,128)(2,1)} %basis_hbm.1), custom_call_target="tpu_custom_call" | custom-call | flops 1000000000 | tf_op jit(solution)/shard_map/leaf/pallas_call | solution.py:372
  3.2 0.0 copy-start.1
  3.2 0.0 copy-start.4
  3.2 0.0 copy-start.5
  3.2 3.0 %collective-permute-start.1 = (bf16[32,2560]{1,0:T(8,128)(2,1)S(1)}, bf16[32,2560]{1,0:T(8,128)(2,1)S(1)}, u32[]{:S(2)}, u32[]{:S(2)}) collective-permute-start(bf16[32,2560]{1,0:T(8,128)(2,1)S(1)} %get-tuple-element.22.message_ref.own0_ref), channel_id=1, source_target_pairs={{0,2},{2,0},{4,6},{6,4},{8,10},{10,8},{12,14},{14,12},{1,3},{3,1},... | collective-permute-start | bytes 491528 | tf_op jit(solution)/shard_map/ppermute | solution.py:412
  6.3 0.0 copy-done.8
  6.3 0.0 copy-start
  6.3 0.0 copy-start.7
  6.3 1.8 %lift.1 = (bf16[32,2560]{1,0:T(8,128)(2,1)S(1)}, bf16[32,128]{1,0:T(8,128)(2,1)S(1)}, bf16[16,256,256]{2,1,0:T(8,128)(2,1)S(1)}) custom-call(bf16[32,2560]{1,0:T(8,128)(2,1)S(1)} %get-tuple-element.22.message_ref.own0_ref, bf16[32,4096]{1,0:T(8,128)(2,1)S(1)} %get-tuple-element.29.ordered_ref, bf16[1024,126]{1,0:T(8,128)(2,1)S(1)} %bitcast.17), custom_call_target="tpu_custom_call" | custom-call | flops 1000000000 | tf_op jit(solution)/shard_map/lift/pallas_call | solution.py:372
  8.0 0.0 collective-permute-start
  8.1 3.1 %collective-permute-start.2 = (bf16[32,128]{1,0:T(8,128)(2,1)S(1)}, bf16[32,128]{1,0:T(8,128)(2,1)S(1)}, u32[]{:S(2)}, u32[]{:S(2)}) collective-permute-start(bf16[32,128]{1,0:T(8,128)(2,1)S(1)} %get-tuple-element.25), channel_id=1, source_target_pairs={{0,8},{2,10},{4,12},{6,14},{8,0},{10,2},{12,4},{14,6},{1,9},{3,11}... | collective-permute-start | bytes 24584 | tf_op jit(solution)/shard_map/ppermute | solution.py:420
  11.2 0.0 copy-done.1
  11.2 0.0 copy-done.4
  11.2 0.0 copy-done.5
  11.2 0.0 copy-start.2
  11.2 0.0 copy-start.3
  11.2 0.0 copy-start.6
  11.2 1.1 %matrices.1 = (bf16[16,256,256]{2,1,0:T(8,128)(2,1)S(1)}, s32[8,128]{1,0:T(8,128)S(1)}, bf16[16,256,256]{2,1,0:T(8,128)(2,1)S(1)}, s32[16,256]{1,0:T(8,128)S(1)}) custom-call(bf16[6,1024,126]{2,1,0:T(8,128)(2,1)S(1)} %bitcast.8, s32[6,126]{1,0:T(8,128)S(1)} %bitcast.13, s32[32,128]{1,0:T(8,128)S(1)} %bitcast.12), custom_call_target="tpu_custom_call" | custom-call | flops 1000000 | tf_op jit(solution)/shard_map/matrices/pallas_call | solution.py:372
  12.3 0.5 %collective-permute-done.2 = bf16[32,128]{1,0:T(8,128)(2,1)S(1)} collective-permute-done((bf16[32,128]{1,0:T(8,128)(2,1)S(1)}, bf16[32,128]{1,0:T(8,128)(2,1)S(1)}, u32[]{:S(2)}, u32[]{:S(2)}) %collective-permute-start.2) | collective-permute-done | bytes 8224 | tf_op jit(solution)/shard_map/ppermute | solution.py:420
  12.8 0.0 collective-permute-done.1.first0_ref
  12.8 2.0 %collective-permute-start.3 = (bf16[32,128]{1,0:T(8,128)(2,1)S(1)}, bf16[32,128]{1,0:T(8,128)(2,1)S(1)}, u32[]{:S(2)}, u32[]{:S(2)}) collective-permute-start(bf16[32,128]{1,0:T(8,128)(2,1)S(1)} %add.6), channel_id=1, source_target_pairs={{0,4},{2,6},{4,0},{6,2},{8,12},{10,14},{12,8},{14,10},{1,5},{3,7},... | collective-permute-start | bytes 24584 | tf_op jit(solution)/shard_map/ppermute | solution.py:420
  14.8 2.0 %collective-permute-start.4 = (bf16[32,2560]{1,0:T(8,128)(2,1)S(1)}, bf16[32,2560]{1,0:T(8,128)(2,1)S(1)}, u32[]{:S(2)}, u32[]{:S(2)}) collective-permute-start(bf16[32,2560]{1,0:T(8,128)(2,1)S(1)} %collective-permute-done.1.first0_ref), channel_id=1, source_target_pairs={{0,4},{4,8},{8,12},{6,2},{10,6},{14,10},{1,5},{5,9},{9,13},{7,3},{... | collective-permute-start | bytes 491528 | tf_op jit(solution)/shard_map/ppermute | solution.py:438
  16.8 0.0 collective-permute-done.3
  16.8 0.0 collective-permute-done.first1_ref
  16.8 4.9 %collective-permute-start.5 = (bf16[32,2560]{1,0:T(8,128)(2,1)S(1)}, bf16[32,2560]{1,0:T(8,128)(2,1)S(1)}, u32[]{:S(2)}, u32[]{:S(2)}) collective-permute-start(bf16[32,2560]{1,0:T(8,128)(2,1)S(1)} %collective-permute-done.first1_ref), channel_id=1, source_target_pairs={{0,4},{4,8},{8,12},{6,2},{10,6},{14,10},{1,5},{5,9},{9,13},{7,3},{... | collective-permute-start | bytes 491528 | tf_op jit(solution)/shard_map/ppermute | solution.py:441
  21.8 0.1 collective-permute-start.6
  21.9 0.0 copy-done
  21.9 0.0 copy-done.7
  21.9 1.7 %near.1.near_in = f32[32,4096]{1,0:T(8,128)S(1)} custom-call(bf16[32,4096]{1,0:T(8,128)(2,1)S(1)} %get-tuple-element.29.ordered_ref, bf16[64,64,256]{2,1,0:T(8,128)(2,1)S(1)} %copy-done, s32[4,64]{1,0:T(4,128)S(1)} %bitcast.15), custom_call_target="tpu_custom_call" | custom-call | flops 1000000 | tf_op jit(solution)/shard_map/near/pallas_call | solution.py:372
  23.6 1.9 %collective-permute-done.6.other_ref = bf16[32,128]{1,0:T(8,128)(2,1)S(1)} collective-permute-done((bf16[32,128]{1,0:T(8,128)(2,1)S(1)}, bf16[32,128]{1,0:T(8,128)(2,1)S(1)}, u32[]{:S(2)}, u32[]{:S(2)}) %collective-permute-start.6) | collective-permute-done | bytes 8224 | tf_op jit(solution)/shard_map/ppermute | solution.py:420
  25.5 0.0 copy-done.2
  25.5 0.0 copy-done.3
  25.5 0.0 copy-done.6
  25.5 1.7 %root.1.six_ref = f32[32,256]{1,0:T(8,128)S(1)} custom-call(bf16[32,128]{1,0:T(8,128)(2,1)S(1)} %add.7.own_ref, bf16[32,128]{1,0:T(8,128)(2,1)S(1)} %collective-permute-done.6.other_ref, bf16[14,32,32]{2,1,0:T(8,128)(2,1)S(1)} %bitcast.10, bf16[6,15,32,32]{3,2,1,0:T(8,128)(2,1)S(1)} %bitcast.9, s32[6,15]{1,0:T(8,128)S(1)} %bitcast.14), custom_call_target="tpu_custom_call" | custom-call | flops 1000000 | tf_op jit(solution)/shard_map/root/pallas_call | solution.py:372
  27.2 0.0 collective-permute-done.4.second0_ref
  27.3 0.0 collective-permute-done.5.second1_ref
  27.3 7.8 %outer.1 = f32[32,4096]{1,0:T(8,128)} custom-call(bf16[32,4096]{1,0:T(8,128)(2,1)S(1)} %get-tuple-element.29.ordered_ref, bf16[32,2560]{1,0:T(8,128)(2,1)S(1)} %get-tuple-element.22.message_ref.own0_ref, bf16[32,2560]{1,0:T(8,128)(2,1)S(1)} %get-tuple-element.24.own1_ref, bf16[32,2560]{1,0:T(8,128)(2,1)S(1)} %collective-permute-done.1.first0_ref, ...), custom_call_target="tpu_custom_call" | custom-call | flops 4000000000 | tf_op jit(solution)/shard_map/outer/pallas_call | solution.py:372
  (2 shorter events, 0.0 us)
Async XLA Ops:
  0.0 6.3 %copy-start.8 = (bf16[32,32,126]{2,1,0:T(8,128)(2,1)S(1)}, bf16[32,32,126]{2,1,0:T(8,128)(2,1)}, u32[]{:S(2)}) copy-start(bf16[32,32,126]{2,1,0:T(8,128)(2,1)} %param.16) | copy-start | bytes 774148
  3.2 7.9 %copy-start.1 = (bf16[6,32,32,126]{3,2,1,0:T(8,128)(2,1)S(1)}, bf16[6,32,32,126]{3,2,1,0:T(8,128)(2,1)}, u32[]{:S(2)}) copy-start(bf16[6,32,32,126]{3,2,1,0:T(8,128)(2,1)} %param.17) | copy-start | bytes 4644868
  3.2 7.9 %copy-start.4 = (s32[4096]{0:T(1024)S(1)}, s32[4096]{0:T(1024)}, u32[]{:S(2)}) copy-start(s32[4096]{0:T(1024)} %param.12) | copy-start | bytes 49156
  3.2 7.9 %copy-start.5 = (s32[126,6]{0,1:T(8,128)S(1)}, s32[126,6]{0,1:T(8,128)}, u32[]{:S(2)}) copy-start(s32[126,6]{0,1:T(8,128)} %param.18) | copy-start | bytes 9076
  3.2 9.5 %collective-permute-start.1 = (bf16[32,2560]{1,0:T(8,128)(2,1)S(1)}, bf16[32,2560]{1,0:T(8,128)(2,1)S(1)}, u32[]{:S(2)}, u32[]{:S(2)}) collective-permute-start(bf16[32,2560]{1,0:T(8,128)(2,1)S(1)} %get-tuple-element.22.message_ref.own0_ref), channel_id=1, source_target_pairs={{0,2},{2,0},{4,6},{6,4},{8,10},{10,8},{12,14},{14,12},{1,3},{3,1},... | collective-permute-start | bytes 491528 | tf_op jit(solution)/shard_map/ppermute | solution.py:412
  6.3 15.6 %copy-start = (bf16[64,64,256]{2,1,0:T(8,128)(2,1)S(1)}, bf16[64,64,256]{2,1,0:T(8,128)(2,1)}, u32[]{:S(2)}) copy-start(bf16[64,64,256]{2,1,0:T(8,128)(2,1)} %blocks_ref.3) | copy-start | bytes 6291460
  6.3 15.6 %copy-start.7 = (s32[64,4]{0,1:T(4,128)S(1)}, s32[64,4]{0,1:T(4,128)}, u32[]{:S(2)}) copy-start(s32[64,4]{0,1:T(4,128)} %param.15) | copy-start | bytes 3076
  8.0 8.8 %collective-permute-start = (bf16[32,2560]{1,0:T(8,128)(2,1)S(1)}, bf16[32,2560]{1,0:T(8,128)(2,1)S(1)}, u32[]{:S(2)}, u32[]{:S(2)}) collective-permute-start(bf16[32,2560]{1,0:T(8,128)(2,1)S(1)} %get-tuple-element.24.own1_ref), channel_id=1, source_target_pairs={{0,2},{2,0},{4,6},{6,4},{8,10},{10,8},{12,14},{14,12},{1,3},{3,1},... | collective-permute-start | bytes 491528 | tf_op jit(solution)/shard_map/ppermute | solution.py:435
  8.1 4.7 %collective-permute-start.2 = (bf16[32,128]{1,0:T(8,128)(2,1)S(1)}, bf16[32,128]{1,0:T(8,128)(2,1)S(1)}, u32[]{:S(2)}, u32[]{:S(2)}) collective-permute-start(bf16[32,128]{1,0:T(8,128)(2,1)S(1)} %get-tuple-element.25), channel_id=1, source_target_pairs={{0,8},{2,10},{4,12},{6,14},{8,0},{10,2},{12,4},{14,6},{1,9},{3,11}... | collective-permute-start | bytes 24584 | tf_op jit(solution)/shard_map/ppermute | solution.py:420
  11.2 14.3 %copy-start.2 = (bf16[6,32,32,15]{2,1,3,0:T(8,128)(2,1)S(1)}, bf16[6,32,32,15]{2,1,3,0:T(8,128)(2,1)}, u32[]{:S(2)}) copy-start(bf16[6,32,32,15]{2,1,3,0:T(8,128)(2,1)} %param.20) | copy-start | bytes 552964
  11.2 14.3 %copy-start.3 = (bf16[32,32,14]{1,0,2:T(8,128)(2,1)S(1)}, bf16[32,32,14]{1,0,2:T(8,128)(2,1)}, u32[]{:S(2)}) copy-start(bf16[32,32,14]{1,0,2:T(8,128)(2,1)} %param.19) | copy-start | bytes 86020
  11.2 14.3 %copy-start.6 = (s32[15,6]{0,1:T(8,128)S(1)}, s32[15,6]{0,1:T(8,128)}, u32[]{:S(2)}) copy-start(s32[15,6]{0,1:T(8,128)} %param.21) | copy-start | bytes 1084
  12.8 4.0 %collective-permute-start.3 = (bf16[32,128]{1,0:T(8,128)(2,1)S(1)}, bf16[32,128]{1,0:T(8,128)(2,1)S(1)}, u32[]{:S(2)}, u32[]{:S(2)}) collective-permute-start(bf16[32,128]{1,0:T(8,128)(2,1)S(1)} %add.6), channel_id=1, source_target_pairs={{0,4},{2,6},{4,0},{6,2},{8,12},{10,14},{12,8},{14,10},{1,5},{3,7},... | collective-permute-start | bytes 24584 | tf_op jit(solution)/shard_map/ppermute | solution.py:420
  14.8 12.5 %collective-permute-start.4 = (bf16[32,2560]{1,0:T(8,128)(2,1)S(1)}, bf16[32,2560]{1,0:T(8,128)(2,1)S(1)}, u32[]{:S(2)}, u32[]{:S(2)}) collective-permute-start(bf16[32,2560]{1,0:T(8,128)(2,1)S(1)} %collective-permute-done.1.first0_ref), channel_id=1, source_target_pairs={{0,4},{4,8},{8,12},{6,2},{10,6},{14,10},{1,5},{5,9},{9,13},{7,3},{... | collective-permute-start | bytes 491528 | tf_op jit(solution)/shard_map/ppermute | solution.py:438
  16.8 10.4 %collective-permute-start.5 = (bf16[32,2560]{1,0:T(8,128)(2,1)S(1)}, bf16[32,2560]{1,0:T(8,128)(2,1)S(1)}, u32[]{:S(2)}, u32[]{:S(2)}) collective-permute-start(bf16[32,2560]{1,0:T(8,128)(2,1)S(1)} %collective-permute-done.first1_ref), channel_id=1, source_target_pairs={{0,4},{4,8},{8,12},{6,2},{10,6},{14,10},{1,5},{5,9},{9,13},{7,3},{... | collective-permute-start | bytes 491528 | tf_op jit(solution)/shard_map/ppermute | solution.py:441
  21.8 3.7 %collective-permute-start.6 = (bf16[32,128]{1,0:T(8,128)(2,1)S(1)}, bf16[32,128]{1,0:T(8,128)(2,1)S(1)}, u32[]{:S(2)}, u32[]{:S(2)}) collective-permute-start(bf16[32,128]{1,0:T(8,128)(2,1)S(1)} %add.7.own_ref), channel_id=1, source_target_pairs={{0,2},{2,0},{4,6},{6,4},{8,10},{10,8},{12,14},{14,12},{1,3},{3,1},... | collective-permute-start | bytes 24584 | tf_op jit(solution)/shard_map/ppermute | solution.py:420

commit v12 on v10

--- a/solution.py
+++ b/solution.py
@@ -41,12 +41,12 @@
 
 
 def pick(stacked, hot, high, rows):
-    out = dot(stacked, hot, NN)
-    high = jnp.broadcast_to(high, (rows, 256))
-    total = out[:rows]
-    for block in range(1, stacked.shape[0] // rows):
-        total = jnp.where(high == block, out[block * rows : (block + 1) * rows], total)
-    return total
+    out = dot(stacked, hot, NN).reshape(-1, rows // 8, 8, 256)
+    high = jnp.broadcast_to(high, (8, 256))
+    total = out[0]
+    for block in range(1, out.shape[0]):
+        total = jnp.where((high == block)[None], out[block], total)
+    return total.reshape(rows, 256)
 
 
 def leaf_kernel(
@@ -251,11 +251,11 @@
     six_ref[...] = dot(down, sixth, NN)
 
 
-def outer_kernel(
-    ordered_ref, own0_ref, own1_ref, first0_ref, first1_ref, second0_ref, second1_ref, near_in, blocks_ref,
-    near_ref, matrices_ref, spots_ref, inverse_ref, weights_ref, masked_ref, hot_ref, six_ref,
-    applied_hbm,
-    applied_ref, leaves, nodes, far, stacked, stacked_nodes, edges, sems, out_sems,
+def far_kernel(
+    ordered_ref, own0_ref, own1_ref, first0_ref, first1_ref, second0_ref, second1_ref, blocks_ref,
+    near_ref, matrices_ref, spots_ref,
+    far, edge_out,
+    leaves, nodes, stacked_nodes, edges, sems,
 ):
     columns, points = ordered_ref.shape
     halo = REACH * 64
@@ -315,6 +315,24 @@
 
     for copy in copies:
         copy.wait()
+    groups = count // 4
+    edge = REACH // 4
+    for e in range(2 * edge):
+        g = e if e < edge else groups - 2 * edge + e
+        at = e % edge * 4
+        blocks = edges[e // edge, at : at + 4].reshape(256, 256)
+        edge_out[:, e * 256 : (e + 1) * 256] = near_group(
+            leaves, near_ref, blocks, g * 4, device * count - REACH, columns
+        )
+
+
+def down_kernel(
+    far, near_in, edge_in, six_ref, inverse_ref, weights_ref, masked_ref, hot_ref,
+    applied_hbm,
+    applied_ref, stacked, out_sems,
+):
+    columns, points = near_in.shape
+    lane_node = iota((columns, 256), 1) & 7
     six = six_ref[...]
     down = [None] * 16
     last = far[:, 15 * 256 :]
@@ -323,20 +341,16 @@
     down[15] = (last + dot(five.astype(BF), weights_ref[15], NT)).astype(BF)
     for k in reversed(range(15)):
         down[k] = (far[:, k * 256 : (k + 1) * 256] + dot(down[8 + k // 2], weights_ref[k], NT)).astype(BF)
-    groups = count // 4
+    groups = points // 256
     edge = REACH // 4
     for g in range(groups):
         if g < edge:
-            blocks = edges[0, g * 4 : g * 4 + 4].reshape(256, 256)
+            near = edge_in[:, g * 256 : (g + 1) * 256]
         elif g >= groups - edge:
-            at = (g - groups + edge) * 4
-            blocks = edges[1, at : at + 4].reshape(256, 256)
+            at = (g - groups + 2 * edge) * 256
+            near = edge_in[:, at : at + 256]
         else:
-            blocks = None
-        if blocks is None:
             near = near_in[:, g * 256 : (g + 1) * 256]
-        else:
-            near = near_group(leaves, near_ref, blocks, g * 4, device * count - REACH, columns)
         if g % 2 == 0:
             at_points = dot(down[g // 2], masked_ref[g // 2], NN)
         half = at_points[:, g % 2 * 256 : (g % 2 + 1) * 256]
@@ -441,6 +455,20 @@
         [pltpu.VMEM((points // 64, columns, 128), BF)],
         [VMEM, VMEM, SMEM], 10**6, "near", (ordered, near_blocks, near_t),
     )
+    far, edge_part = call(
+        far_kernel, [((columns, 4096), F32), ((columns, 2 * halo), F32)],
+        [
+            pltpu.VMEM((points // 64 + 2 * REACH, columns, 128), BF),
+            pltpu.VMEM((385, columns, 128), BF), pltpu.VMEM((16 * columns, 256), BF),
+            pltpu.VMEM((2, REACH) + near_blocks.shape[1:], BF), pltpu.SemaphoreType.DMA((2,)),
+        ],
+        [VMEM] * 7 + [any_spec, SMEM, VMEM, SMEM], 4 * 10**9, "far",
+        (
+            ordered, own0, own1, first0, first1, second0, second1, in_hbm(near_blocks),
+            near_t, coupling_rows, spots,
+        ),
+    )
+    other, far = lax.optimization_barrier((other, far))
     (six,) = call(
         root_kernel, [((columns, 256), F32)], [pltpu.VMEM((2 * devices, columns, 32), F32)],
         [VMEM] * 4 + [SMEM], 10**6, "root",
@@ -450,21 +478,12 @@
         ),
     )
     (applied,) = call(
-        outer_kernel,
-        [((columns, points), F32)],
+        down_kernel, [((columns, points), F32)],
         [
-            pltpu.VMEM((columns, points), F32), pltpu.VMEM((points // 64 + 2 * REACH, columns, 128), BF),
-            pltpu.VMEM((385, columns, 128), BF), pltpu.VMEM((columns, 4096), F32),
-            pltpu.VMEM((points // 256 * columns, 256), BF), pltpu.VMEM((16 * columns, 256), BF),
-            pltpu.VMEM((2, REACH) + near_blocks.shape[1:], BF), pltpu.SemaphoreType.DMA((2,)),
+            pltpu.VMEM((columns, points), F32), pltpu.VMEM((points // 256 * columns, 256), BF),
             pltpu.SemaphoreType.DMA((points // 1024,)),
         ],
-        [VMEM] * 8 + [any_spec, SMEM, VMEM, SMEM] + [VMEM] * 5,
-        4 * 10**9, "outer",
-        (
-            ordered, own0, own1, first0, first1, second0, second1, near_part, in_hbm(near_blocks),
-            near_t, coupling_rows, spots, blocks, weights, masked, hot, six,
-        ),
+        [VMEM] * 8, 4 * 10**9, "down", (far, near_part, edge_part, six, blocks, weights, masked, hot),
         out_specs=[any_spec],
     )
     return applied

time: 34.4 us -> 33.7 us (0.980)
  waiting for transfers between devices: 2.45 us -> 1.55 us
    ppermute x3, waiting for transfers between devices: 2.42 us -> 0.53 us  [step(): lax.ppermute(tile_sum, 'leaf', [(i, i ^ reached) for i in range(devices)])]
    ppermute x1, waiting for transfers between devices: 0.03 us -> 1.01 us  [local(): second1 = lax.ppermute(first1, 'leaf', onward)]
    pallas_call x6 -> x7, Pallas kernels: 16.4 us -> 16.6 us  [call(): pl.pallas_call(kernel, out_shape=[jax.ShapeDtypeStruct(s, t) for s, t in...]
  transfers between devices with their start and end apart: 7 -> 7, of which waited for: 2 -> 2; matrix products, arithmetic and copies ran while one was open for 0% -> 0% of each run, Pallas kernels for 18% -> 25%
where the time goes in v12:
time: 33.7 us; the launch traced here: 33.5 us
  Pallas kernels  16.6 us (49%)
  starting transfers between devices  15.1 us (45%)
  waiting for transfers between devices  1.55 us (5%)
    pallas_call x7, Pallas kernels, call(): pl.pallas_call(kernel, out_shape=[jax.ShapeDtypeStruct(s, t) for s, t in...  16.6 us
    ppermute x3, starting transfers between devices, step(): lax.ppermute(tile_sum, 'leaf', [(i, i ^ reached) for i in range(devices)])  5.1 us
    ppermute x1, starting transfers between devices, local(): second1 = lax.ppermute(first1, 'leaf', onward)  4.94 us
    ppermute x1, starting transfers between devices, local(): first0 = lax.ppermute(own0, 'leaf', pairs)  3.03 us
    ppermute x1, starting transfers between devices, local(): second0 = lax.ppermute(first0, 'leaf', onward)  2.02 us
    ppermute x1, waiting for transfers between devices, local(): second1 = lax.ppermute(first1, 'leaf', onward)  1.01 us
  transfers between devices with their start and end apart: 7, of which 2 were waited for; matrix products, arithmetic and copies ran while one was open for 0% of the time, Pallas kernels for 25%

profile of v12, /device:TPU:0, one launch (start us, length us, event | category | flops | bytes accessed | tf_op | source)
XLA Modules:
  0.0 33.5 jit_solution(7595335844985525217)
XLA Ops:
  0.0 0.0 copy-start.8
  0.0 3.2 %leaf.1 = (bf16[32,4096]{1,0:T(8,128)(2,1)S(1)}, bf16[32,2560]{1,0:T(8,128)(2,1)S(1)}, bf16[8,256,512]{2,1,0:T(8,128)(2,1)S(1)}) custom-call(bf16[32,4096]{1,0:T(8,128)(2,1)} %vec_hbm.1, s32[32,128]{1,0:T(8,128)} %bitcast.11, bf16[32,4096]{1,0:T(8,128)(2,1)} %basis_hbm.1), custom_call_target="tpu_custom_call" | custom-call | flops 1000000000 | tf_op jit(solution)/shard_map/leaf/pallas_call | solution.py:382
  3.2 0.0 copy-start.1
  3.2 0.0 copy-start.4
  3.2 0.0 copy-start.5
  3.2 3.0 %collective-permute-start.1 = (bf16[32,2560]{1,0:T(8,128)(2,1)S(1)}, bf16[32,2560]{1,0:T(8,128)(2,1)S(1)}, u32[]{:S(2)}, u32[]{:S(2)}) collective-permute-start(bf16[32,2560]{1,0:T(8,128)(2,1)S(1)} %get-tuple-element.26.message_ref.own0_ref), channel_id=1, source_target_pairs={{0,2},{2,0},{4,6},{6,4},{8,10},{10,8},{12,14},{14,12},{1,3},{3,1},... | collective-permute-start | bytes 491528 | tf_op jit(solution)/shard_map/ppermute | solution.py:422
  6.3 0.0 copy-done.8
  6.3 0.0 copy-start
  6.3 0.0 copy-start.7
  6.3 1.8 %lift.1 = (bf16[32,2560]{1,0:T(8,128)(2,1)S(1)}, bf16[32,128]{1,0:T(8,128)(2,1)S(1)}, bf16[16,256,256]{2,1,0:T(8,128)(2,1)S(1)}) custom-call(bf16[32,2560]{1,0:T(8,128)(2,1)S(1)} %get-tuple-element.26.message_ref.own0_ref, bf16[32,4096]{1,0:T(8,128)(2,1)S(1)} %get-tuple-element.34.ordered_ref, bf16[1024,126]{1,0:T(8,128)(2,1)S(1)} %bitcast.17), custom_call_target="tpu_custom_call" | custom-call | flops 1000000000 | tf_op jit(solution)/shard_map/lift/pallas_call | solution.py:382
  8.0 0.0 collective-permute-start
  8.1 3.1 %collective-permute-start.2 = (bf16[32,128]{1,0:T(8,128)(2,1)S(1)}, bf16[32,128]{1,0:T(8,128)(2,1)S(1)}, u32[]{:S(2)}, u32[]{:S(2)}) collective-permute-start(bf16[32,128]{1,0:T(8,128)(2,1)S(1)} %get-tuple-element.29), channel_id=1, source_target_pairs={{0,8},{2,10},{4,12},{6,14},{8,0},{10,2},{12,4},{14,6},{1,9},{3,11}... | collective-permute-start | bytes 24584 | tf_op jit(solution)/shard_map/ppermute | solution.py:430
  11.2 0.0 copy-done.1
  11.2 0.0 copy-done.4
  11.2 0.0 copy-done.5
  11.2 1.1 %matrices.1 = (bf16[16,256,256]{2,1,0:T(8,128)(2,1)S(1)}, s32[8,128]{1,0:T(8,128)S(1)}, bf16[16,256,256]{2,1,0:T(8,128)(2,1)S(1)}, s32[16,256]{1,0:T(8,128)S(1)}) custom-call(bf16[6,1024,126]{2,1,0:T(8,128)(2,1)S(1)} %bitcast.8, s32[6,126]{1,0:T(8,128)S(1)} %bitcast.13, s32[32,128]{1,0:T(8,128)S(1)} %bitcast.12), custom_call_target="tpu_custom_call" | custom-call | flops 1000000 | tf_op jit(solution)/shard_map/matrices/pallas_call | solution.py:382
  12.3 0.5 %collective-permute-done.2 = bf16[32,128]{1,0:T(8,128)(2,1)S(1)} collective-permute-done((bf16[32,128]{1,0:T(8,128)(2,1)S(1)}, bf16[32,128]{1,0:T(8,128)(2,1)S(1)}, u32[]{:S(2)}, u32[]{:S(2)}) %collective-permute-start.2) | collective-permute-done | bytes 8224 | tf_op jit(solution)/shard_map/ppermute | solution.py:430
  12.8 0.0 collective-permute-done.1.first0_ref
  12.8 2.0 %collective-permute-start.3 = (bf16[32,128]{1,0:T(8,128)(2,1)S(1)}, bf16[32,128]{1,0:T(8,128)(2,1)S(1)}, u32[]{:S(2)}, u32[]{:S(2)}) collective-permute-start(bf16[32,128]{1,0:T(8,128)(2,1)S(1)} %add.6), channel_id=1, source_target_pairs={{0,4},{2,6},{4,0},{6,2},{8,12},{10,14},{12,8},{14,10},{1,5},{3,7},... | collective-permute-start | bytes 24584 | tf_op jit(solution)/shard_map/ppermute | solution.py:430
  14.8 2.0 %collective-permute-start.5 = (bf16[32,2560]{1,0:T(8,128)(2,1)S(1)}, bf16[32,2560]{1,0:T(8,128)(2,1)S(1)}, u32[]{:S(2)}, u32[]{:S(2)}) collective-permute-start(bf16[32,2560]{1,0:T(8,128)(2,1)S(1)} %collective-permute-done.1.first0_ref), channel_id=1, source_target_pairs={{0,4},{4,8},{8,12},{6,2},{10,6},{14,10},{1,5},{5,9},{9,13},{7,3},{... | collective-permute-start | bytes 491528 | tf_op jit(solution)/shard_map/ppermute | solution.py:448
  16.8 0.0 collective-permute-done.3
  16.8 0.0 collective-permute-done.first1_ref
  16.8 4.9 %collective-permute-start.6 = (bf16[32,2560]{1,0:T(8,128)(2,1)S(1)}, bf16[32,2560]{1,0:T(8,128)(2,1)S(1)}, u32[]{:S(2)}, u32[]{:S(2)}) collective-permute-start(bf16[32,2560]{1,0:T(8,128)(2,1)S(1)} %collective-permute-done.first1_ref), channel_id=1, source_target_pairs={{0,4},{4,8},{8,12},{6,2},{10,6},{14,10},{1,5},{5,9},{9,13},{7,3},{... | collective-permute-start | bytes 491528 | tf_op jit(solution)/shard_map/ppermute | solution.py:451
  21.8 0.1 collective-permute-start.4
  21.9 0.0 copy-done
  21.9 0.0 copy-done.7
  21.9 1.7 %near.1.near_in = f32[32,4096]{1,0:T(8,128)S(1)} custom-call(bf16[32,4096]{1,0:T(8,128)(2,1)S(1)} %get-tuple-element.34.ordered_ref, bf16[64,64,256]{2,1,0:T(8,128)(2,1)S(1)} %copy-done, s32[4,64]{1,0:T(4,128)S(1)} %bitcast.15), custom_call_target="tpu_custom_call" | custom-call | flops 1000000 | tf_op jit(solution)/shard_map/near/pallas_call | solution.py:382
  23.6 0.0 collective-permute-done.5.second0_ref
  23.6 1.0 %collective-permute-done.6.second1_ref = bf16[32,2560]{1,0:T(8,128)(2,1)S(1)} collective-permute-done((bf16[32,2560]{1,0:T(8,128)(2,1)S(1)}, bf16[32,2560]{1,0:T(8,128)(2,1)S(1)}, u32[]{:S(2)}, u32[]{:S(2)}) %collective-permute-start.6) | collective-permute-done | bytes 163872 | tf_op jit(solution)/shard_map/ppermute | solution.py:451
  24.6 0.0 copy-start.2
  24.6 0.0 copy-start.3
  24.6 0.0 copy-start.6
  24.6 3.7 %far.1 = (f32[32,4096]{1,0:T(8,128)S(1)}, f32[32,1024]{1,0:T(8,128)S(1)}) custom-call(bf16[32,4096]{1,0:T(8,128)(2,1)S(1)} %get-tuple-element.34.ordered_ref, bf16[32,2560]{1,0:T(8,128)(2,1)S(1)} %get-tuple-element.26.message_ref.own0_ref, bf16[32,2560]{1,0:T(8,128)(2,1)S(1)} %get-tuple-element.28.own1_ref, ...), custom_call_target="tpu_custom_call" | custom-call | flops 4000000000 | tf_op jit(solution)/shard_map/far/pallas_call | solution.py:382
  28.3 0.0 collective-permute-done.4.other_ref
  28.3 0.0 copy-done.2
  28.4 0.0 copy-done.3
  28.4 0.0 copy-done.6
  28.4 1.7 %root.1.six_ref = f32[32,256]{1,0:T(8,128)S(1)} custom-call(bf16[32,128]{1,0:T(8,128)(2,1)S(1)} %add.7.own_ref, bf16[32,128]{1,0:T(8,128)(2,1)S(1)} %collective-permute-done.4.other_ref, bf16[14,32,32]{2,1,0:T(8,128)(2,1)S(1)} %bitcast.10, bf16[6,15,32,32]{3,2,1,0:T(8,128)(2,1)S(1)} %bitcast.9, s32[6,15]{1,0:T(8,128)S(1)} %bitcast.14), custom_call_target="tpu_custom_call" | custom-call | flops 1000000 | tf_op jit(solution)/shard_map/root/pallas_call | solution.py:382
  30.1 3.4 %down.1 = f32[32,4096]{1,0:T(8,128)} custom-call(f32[32,4096]{1,0:T(8,128)S(1)} %get-tuple-element.40.far, f32[32,4096]{1,0:T(8,128)S(1)} %near.1.near_in, f32[32,1024]{1,0:T(8,128)S(1)} %get-tuple-element.41.edge_in, f32[32,256]{1,0:T(8,128)S(1)} %root.1.six_ref, s32[16,256]{1,0:T(8,128)S(1)} %get-tuple-element.43.inverse_ref, ...), custom_call_target="tpu_custom_call" | custom-call | flops 4000000000 | tf_op jit(solution)/shard_map/down/pallas_call | solution.py:382
  (2 shorter events, 0.0 us)
Async XLA Ops:
  0.0 6.3 %copy-start.8 = (bf16[32,32,126]{2,1,0:T(8,128)(2,1)S(1)}, bf16[32,32,126]{2,1,0:T(8,128)(2,1)}, u32[]{:S(2)}) copy-start(bf16[32,32,126]{2,1,0:T(8,128)(2,1)} %param.16) | copy-start | bytes 774148
  3.2 8.0 %copy-start.1 = (bf16[6,32,32,126]{3,2,1,0:T(8,128)(2,1)S(1)}, bf16[6,32,32,126]{3,2,1,0:T(8,128)(2,1)}, u32[]{:S(2)}) copy-start(bf16[6,32,32,126]{3,2,1,0:T(8,128)(2,1)} %param.17) | copy-start | bytes 4644868
  3.2 7.9 %copy-start.4 = (s32[4096]{0:T(1024)S(1)}, s32[4096]{0:T(1024)}, u32[]{:S(2)}) copy-start(s32[4096]{0:T(1024)} %param.12) | copy-start | bytes 49156
  3.2 7.9 %copy-start.5 = (s32[126,6]{0,1:T(8,128)S(1)}, s32[126,6]{0,1:T(8,128)}, u32[]{:S(2)}) copy-start(s32[126,6]{0,1:T(8,128)} %param.18) | copy-start | bytes 9076
  3.2 9.5 %collective-permute-start.1 = (bf16[32,2560]{1,0:T(8,128)(2,1)S(1)}, bf16[32,2560]{1,0:T(8,128)(2,1)S(1)}, u32[]{:S(2)}, u32[]{:S(2)}) collective-permute-start(bf16[32,2560]{1,0:T(8,128)(2,1)S(1)} %get-tuple-element.26.message_ref.own0_ref), channel_id=1, source_target_pairs={{0,2},{2,0},{4,6},{6,4},{8,10},{10,8},{12,14},{14,12},{1,3},{3,1},... | collective-permute-start | bytes 491528 | tf_op jit(solution)/shard_map/ppermute | solution.py:422
  6.3 15.6 %copy-start = (bf16[64,64,256]{2,1,0:T(8,128)(2,1)S(1)}, bf16[64,64,256]{2,1,0:T(8,128)(2,1)}, u32[]{:S(2)}) copy-start(bf16[64,64,256]{2,1,0:T(8,128)(2,1)} %blocks_ref.3) | copy-start | bytes 6291460
  6.3 15.6 %copy-start.7 = (s32[64,4]{0,1:T(4,128)S(1)}, s32[64,4]{0,1:T(4,128)}, u32[]{:S(2)}) copy-start(s32[64,4]{0,1:T(4,128)} %param.15) | copy-start | bytes 3076
  8.0 8.8 %collective-permute-start = (bf16[32,2560]{1,0:T(8,128)(2,1)S(1)}, bf16[32,2560]{1,0:T(8,128)(2,1)S(1)}, u32[]{:S(2)}, u32[]{:S(2)}) collective-permute-start(bf16[32,2560]{1,0:T(8,128)(2,1)S(1)} %get-tuple-element.28.own1_ref), channel_id=1, source_target_pairs={{0,2},{2,0},{4,6},{6,4},{8,10},{10,8},{12,14},{14,12},{1,3},{3,1},... | collective-permute-start | bytes 491528 | tf_op jit(solution)/shard_map/ppermute | solution.py:445
  8.1 4.7 %collective-permute-start.2 = (bf16[32,128]{1,0:T(8,128)(2,1)S(1)}, bf16[32,128]{1,0:T(8,128)(2,1)S(1)}, u32[]{:S(2)}, u32[]{:S(2)}) collective-permute-start(bf16[32,128]{1,0:T(8,128)(2,1)S(1)} %get-tuple-element.29), channel_id=1, source_target_pairs={{0,8},{2,10},{4,12},{6,14},{8,0},{10,2},{12,4},{14,6},{1,9},{3,11}... | collective-permute-start | bytes 24584 | tf_op jit(solution)/shard_map/ppermute | solution.py:430
  12.8 4.0 %collective-permute-start.3 = (bf16[32,128]{1,0:T(8,128)(2,1)S(1)}, bf16[32,128]{1,0:T(8,128)(2,1)S(1)}, u32[]{:S(2)}, u32[]{:S(2)}) collective-permute-start(bf16[32,128]{1,0:T(8,128)(2,1)S(1)} %add.6), channel_id=1, source_target_pairs={{0,4},{2,6},{4,0},{6,2},{8,12},{10,14},{12,8},{14,10},{1,5},{3,7},... | collective-permute-start | bytes 24584 | tf_op jit(solution)/shard_map/ppermute | solution.py:430
  14.8 8.8 %collective-permute-start.5 = (bf16[32,2560]{1,0:T(8,128)(2,1)S(1)}, bf16[32,2560]{1,0:T(8,128)(2,1)S(1)}, u32[]{:S(2)}, u32[]{:S(2)}) collective-permute-start(bf16[32,2560]{1,0:T(8,128)(2,1)S(1)} %collective-permute-done.1.first0_ref), channel_id=1, source_target_pairs={{0,4},{4,8},{8,12},{6,2},{10,6},{14,10},{1,5},{5,9},{9,13},{7,3},{... | collective-permute-start | bytes 491528 | tf_op jit(solution)/shard_map/ppermute | solution.py:448
  16.8 7.8 %collective-permute-start.6 = (bf16[32,2560]{1,0:T(8,128)(2,1)S(1)}, bf16[32,2560]{1,0:T(8,128)(2,1)S(1)}, u32[]{:S(2)}, u32[]{:S(2)}) collective-permute-start(bf16[32,2560]{1,0:T(8,128)(2,1)S(1)} %collective-permute-done.first1_ref), channel_id=1, source_target_pairs={{0,4},{4,8},{8,12},{6,2},{10,6},{14,10},{1,5},{5,9},{9,13},{7,3},{... | collective-permute-start | bytes 491528 | tf_op jit(solution)/shard_map/ppermute | solution.py:451
  21.8 6.6 %collective-permute-start.4 = (bf16[32,128]{1,0:T(8,128)(2,1)S(1)}, bf16[32,128]{1,0:T(8,128)(2,1)S(1)}, u32[]{:S(2)}, u32[]{:S(2)}) collective-permute-start(bf16[32,128]{1,0:T(8,128)(2,1)S(1)} %add.7.own_ref), channel_id=1, source_target_pairs={{0,2},{2,0},{4,6},{6,4},{8,10},{10,8},{12,14},{14,12},{1,3},{3,1},... | collective-permute-start | bytes 24584 | tf_op jit(solution)/shard_map/ppermute | solution.py:430
  24.6 3.8 %copy-start.2 = (bf16[6,32,32,15]{2,1,3,0:T(8,128)(2,1)S(1)}, bf16[6,32,32,15]{2,1,3,0:T(8,128)(2,1)}, u32[]{:S(2)}) copy-start(bf16[6,32,32,15]{2,1,3,0:T(8,128)(2,1)} %param.20) | copy-start | bytes 552964
  24.6 3.8 %copy-start.3 = (bf16[32,32,14]{1,0,2:T(8,128)(2,1)S(1)}, bf16[32,32,14]{1,0,2:T(8,128)(2,1)}, u32[]{:S(2)}) copy-start(bf16[32,32,14]{1,0,2:T(8,128)(2,1)} %param.19) | copy-start | bytes 86020
  24.6 3.8 %copy-start.6 = (s32[15,6]{0,1:T(8,128)S(1)}, s32[15,6]{0,1:T(8,128)}, u32[]{:S(2)}) copy-start(s32[15,6]{0,1:T(8,128)} %param.21) | copy-start | bytes 1084

commit v13 on v12

--- a/solution.py
+++ b/solution.py
@@ -50,25 +50,23 @@
 
 
 def leaf_kernel(
-    vec_hbm, order_hbm, basis_hbm, ordered_ref, message_ref, masked_ref,
+    vec_hbm, order_hbm, basis_hbm, ordered_ref, zero_ref, masked_ref,
     vec_ref, order_ref, basis_ref, stacked, sems,
 ):
     columns, points = vec_ref.shape
     rank = basis_ref.shape[0]
-    halo = REACH * 64
     pairs = ((order_hbm, order_ref), (vec_hbm, vec_ref), (basis_hbm, basis_ref))
     copies = [pltpu.make_async_copy(src, dst, sems.at[i]) for i, (src, dst) in enumerate(pairs)]
     for copy in copies:
         copy.start()
-    copies[0].wait()
-    copies[1].wait()
+    for copy in copies:
+        copy.wait()
     for block in range(points // 256):
         stacked[block * columns : (block + 1) * columns, :] = vec_ref[:, block * 256 : (block + 1) * 256]
     for c in range(points // 256):
         high, low = split_ids(order_ref, c, points)
         ordered_ref[:, c * 256 : (c + 1) * 256] = pick(stacked[...], one_hot(low), high, columns).astype(BF)
 
-    copies[2].wait()
     mine = (iota((256, 512), 0) & 7) == (iota((256, 512), 1) >> 6)
     for g in range(points // 512):
         one = basis_ref[:, g * 512 : (g + 1) * 512].astype(F32)
@@ -76,17 +74,20 @@
         masked = jnp.where(mine, eight, 0.0).astype(BF)
         masked_ref[g] = masked
         coeffs = dot(ordered_ref[:, g * 512 : (g + 1) * 512], masked, NT).astype(BF)
-        message_ref[:, halo + g * 256 : halo + (g + 1) * 256] = coeffs
+        zero_ref[:, g * 256 : (g + 1) * 256] = coeffs
+    halo = zero_ref.shape[1] - 2048
     odd = lax.axis_index("leaf") % 2 == 1
-    message_ref[:, :halo] = jnp.where(odd, ordered_ref[:, :halo], ordered_ref[:, points - halo :])
-
-
-def lift_kernel(message_ref, ordered_ref, transfer_ref, lifted_ref, top_ref, weights_ref, rows32):
+    zero_ref[:, 2048:] = jnp.where(odd, ordered_ref[:, points - halo :], ordered_ref[:, :halo])
+
+
+def lift_kernel(zero_ref, ordered_ref, transfer_ref, lifted_ref, top_ref, last_ref, weights_ref, rows32):
     rank = 32
     base = REACH * 64
     points = ordered_ref.shape[1]
     odd = lax.axis_index("leaf") % 2 == 1
-    lifted_ref[:, 2048:] = jnp.where(odd, ordered_ref[:, points - base :], ordered_ref[:, :base])
+    low, high = ordered_ref[:, :base], ordered_ref[:, points - base :]
+    last_ref[:, top_ref.shape[1] :] = jnp.where(odd, low, high)
+    last_ref[:, : top_ref.shape[1]] = jnp.zeros(top_ref.shape, BF)
 
     lane, row = iota((128, 256), 1), iota((128, 256), 0)
     family = (lane & 7) == ((row >> 1) & 7)
@@ -100,7 +101,7 @@
             rows32[m * 4 + q] = jnp.where(family, dot(turned, spread[q], NN), 0.0)
     for k in range(16):
         weights_ref[k] = rows32[:, k * 8 : k * 8 + 8, :].reshape(256, 256).astype(BF)
-    coeffs = [message_ref[:, base + g * 256 : base + (g + 1) * 256] for g in range(8)] + [None] * 8
+    coeffs = [zero_ref[:, g * 256 : (g + 1) * 256] for g in range(8)] + [None] * 8
     for n in range(7):
         lifted = dot(coeffs[2 * n], weights_ref[2 * n], NN) + dot(coeffs[2 * n + 1], weights_ref[2 * n + 1], NN)
         coeffs[8 + n] = lifted.astype(BF)
@@ -252,30 +253,11 @@
 
 
 def far_kernel(
-    ordered_ref, own0_ref, own1_ref, first0_ref, first1_ref, second0_ref, second1_ref, blocks_ref,
-    near_ref, matrices_ref, spots_ref,
-    far, edge_out,
-    leaves, nodes, stacked_nodes, edges, sems,
+    own0_ref, own1_ref, first0_ref, first1_ref, second0_ref, second1_ref, matrices_ref, spots_ref,
+    far, nodes, stacked_nodes,
 ):
-    columns, points = ordered_ref.shape
-    halo = REACH * 64
-    device = lax.axis_index("leaf")
-    count = points // 64
-    copies = [
-        pltpu.make_async_copy(blocks_ref.at[pl.ds(at, REACH)], edges.at[i], sems.at[i])
-        for i, at in enumerate((0, count - REACH))
-    ]
-    for copy in copies:
-        copy.start()
-
-    odd = device % 2
-    for ref, start, right in ((first0_ref, 0, 1 - odd), (second1_ref, 2048, odd)):
-        for c in range(halo // 128):
-            at = start + c * 128
-            place_leaves(leaves, right * (REACH + count) + c * 2, ref[:, at : at + 128])
-    near_ends = REACH * 64 * 2 // 128
-    for c in list(range(near_ends)) + list(range(count // 2 - near_ends, count // 2)):
-        place_leaves(leaves, REACH + c * 2, ordered_ref[:, c * 128 : (c + 1) * 128])
+    columns = far.shape[0]
+    odd = lax.axis_index("leaf") % 2
 
     nodes[3 * 128] = jnp.zeros((columns, 128), BF)
     lane, row = iota((256, 1024), 1), iota((256, 1024), 0)
@@ -285,8 +267,7 @@
     )
     for side, ref0, ref1 in sources:
         for n in range(8):
-            at = halo + n * 256
-            stacked_nodes[n * columns : (n + 1) * columns, :] = ref0[:, at : at + 256]
+            stacked_nodes[n * columns : (n + 1) * columns, :] = ref0[:, n * 256 : (n + 1) * 256]
             stacked_nodes[(8 + n) * columns : (9 + n) * columns, :] = ref1[:, n * 256 : (n + 1) * 256]
         for c in range(0, 8, 2):
             out = dot(stacked_nodes[...], spread[:, c * 128 : (c + 2) * 128], NN)
@@ -313,25 +294,33 @@
             total = jnp.where(lane_node == i, out[i * columns : (i + 1) * columns], total)
         far[:, g * 256 : (g + 1) * 256] = total
 
-    for copy in copies:
-        copy.wait()
-    groups = count // 4
-    edge = REACH // 4
-    for e in range(2 * edge):
-        g = e if e < edge else groups - 2 * edge + e
-        at = e % edge * 4
-        blocks = edges[e // edge, at : at + 4].reshape(256, 256)
-        edge_out[:, e * 256 : (e + 1) * 256] = near_group(
-            leaves, near_ref, blocks, g * 4, device * count - REACH, columns
-        )
-
 
 def down_kernel(
-    far, near_in, edge_in, six_ref, inverse_ref, weights_ref, masked_ref, hot_ref,
+    far, near_in, ordered_ref, last_ref, second0_ref, blocks_ref, near_ref,
+    six_ref, inverse_ref, weights_ref, masked_ref, hot_ref,
     applied_hbm,
-    applied_ref, stacked, out_sems,
+    applied_ref, leaves, stacked, edges, sems, out_sems,
 ):
     columns, points = near_in.shape
+    halo = REACH * 64
+    device = lax.axis_index("leaf")
+    count = points // 64
+    copies = [
+        pltpu.make_async_copy(blocks_ref.at[pl.ds(at, REACH)], edges.at[i], sems.at[i])
+        for i, at in enumerate((0, count - REACH))
+    ]
+    for copy in copies:
+        copy.start()
+
+    odd = device % 2
+    for ref, start, right in ((last_ref, last_ref.shape[1] - halo, 1 - odd), (second0_ref, 2048, odd)):
+        for c in range(halo // 128):
+            at = start + c * 128
+            place_leaves(leaves, right * (REACH + count) + c * 2, ref[:, at : at + 128])
+    near_ends = REACH * 64 * 2 // 128
+    for c in list(range(near_ends)) + list(range(count // 2 - near_ends, count // 2)):
+        place_leaves(leaves, REACH + c * 2, ordered_ref[:, c * 128 : (c + 1) * 128])
+
     lane_node = iota((columns, 256), 1) & 7
     six = six_ref[...]
     down = [None] * 16
@@ -341,16 +330,17 @@
     down[15] = (last + dot(five.astype(BF), weights_ref[15], NT)).astype(BF)
     for k in reversed(range(15)):
         down[k] = (far[:, k * 256 : (k + 1) * 256] + dot(down[8 + k // 2], weights_ref[k], NT)).astype(BF)
+    for copy in copies:
+        copy.wait()
     groups = points // 256
     edge = REACH // 4
     for g in range(groups):
-        if g < edge:
-            near = edge_in[:, g * 256 : (g + 1) * 256]
-        elif g >= groups - edge:
-            at = (g - groups + 2 * edge) * 256
-            near = edge_in[:, at : at + 256]
+        if edge <= g < groups - edge:
+            near = near_in[:, g * 256 : (g + 1) * 256]
         else:
-            near = near_in[:, g * 256 : (g + 1) * 256]
+            at = g if g < edge else g - groups + edge
+            blocks = edges[0 if g < edge else 1, at * 4 : at * 4 + 4].reshape(256, 256)
+            near = near_group(leaves, near_ref, blocks, g * 4, device * count - REACH, columns)
         if g % 2 == 0:
             at_points = dot(down[g // 2], masked_ref[g // 2], NN)
         half = at_points[:, g % 2 * 256 : (g % 2 + 1) * 256]
@@ -409,7 +399,7 @@
     tile = max(devices // 2 * rank, 128)
     ordered, own0, masked = call(
         leaf_kernel,
-        [((columns, points), BF), ((columns, halo + 2048), BF), ((points // 512, 256, 512), BF)],
+        [((columns, points), BF), ((columns, 2048 + halo), BF), ((points // 512, 256, 512), BF)],
         [
             pltpu.VMEM(vectors.shape, BF), pltpu.VMEM(order.shape, jnp.int32),
             pltpu.VMEM(leaf_basis.shape, BF), pltpu.VMEM((points // 256 * columns, 256), BF),
@@ -420,9 +410,12 @@
     pairs = [(i, i ^ 1) for i in range(devices)]
     onward = [(i, i + 2) for i in range(0, devices - 2, 2)] + [(i, i - 2) for i in range(3, devices, 2)]
     first0 = lax.ppermute(own0, "leaf", pairs)
-    own1, top, weights = call(
+    own1, top, last, weights = call(
         lift_kernel,
-        [((columns, halo + 2048), BF), ((columns, tile), BF), ((16, 256, 256), BF)],
+        [
+            ((columns, 2048), BF), ((columns, tile), BF), ((columns, tile + halo), BF),
+            ((16, 256, 256), BF),
+        ],
         [pltpu.VMEM((rank, 128, 256), F32)], [VMEM] * 3, 10**9, "lift", (own0, ordered, moves),
     )
 
@@ -443,11 +436,12 @@
         [VMEM] * 3, 10**6, "matrices", (matrices, lists_t, order),
     )
     first1 = lax.ppermute(own1, "leaf", pairs)
-    first0, top, blocks = lax.optimization_barrier((first0, top + other, blocks))
+    first0, first1, top, blocks = lax.optimization_barrier((first0, first1, top + other, blocks))
     other = step(top, steps[-1])
     second0 = lax.ppermute(first0, "leaf", onward)
-    first1, top = lax.optimization_barrier((first1, top + other))
-    other = step(top, 1)
+    last = lax.dynamic_update_slice(last, top + other, (0, 0))
+    first1, last = lax.optimization_barrier((first1, last))
+    other = step(last, 1)
     second1 = lax.ppermute(first1, "leaf", onward)
     first1, ordered = lax.optimization_barrier((first1, ordered))
     (near_part,) = call(
@@ -455,35 +449,33 @@
         [pltpu.VMEM((points // 64, columns, 128), BF)],
         [VMEM, VMEM, SMEM], 10**6, "near", (ordered, near_blocks, near_t),
     )
-    far, edge_part = call(
-        far_kernel, [((columns, 4096), F32), ((columns, 2 * halo), F32)],
-        [
-            pltpu.VMEM((points // 64 + 2 * REACH, columns, 128), BF),
-            pltpu.VMEM((385, columns, 128), BF), pltpu.VMEM((16 * columns, 256), BF),
-            pltpu.VMEM((2, REACH) + near_blocks.shape[1:], BF), pltpu.SemaphoreType.DMA((2,)),
-        ],
-        [VMEM] * 7 + [any_spec, SMEM, VMEM, SMEM], 4 * 10**9, "far",
-        (
-            ordered, own0, own1, first0, first1, second0, second1, in_hbm(near_blocks),
-            near_t, coupling_rows, spots,
-        ),
+    (far,) = call(
+        far_kernel, [((columns, 4096), F32)],
+        [pltpu.VMEM((385, columns, 128), BF), pltpu.VMEM((16 * columns, 256), BF)],
+        [VMEM] * 7 + [SMEM], 4 * 10**9, "far",
+        (own0, own1, first0, first1, second0, second1, coupling_rows, spots),
     )
     other, far = lax.optimization_barrier((other, far))
     (six,) = call(
         root_kernel, [((columns, 256), F32)], [pltpu.VMEM((2 * devices, columns, 32), F32)],
         [VMEM] * 4 + [SMEM], 10**6, "root",
         (
-            top, other, jnp.transpose(top_transfers, (2, 0, 1)), jnp.transpose(top_couplings, (0, 3, 1, 2)),
+            last, other, jnp.transpose(top_transfers, (2, 0, 1)), jnp.transpose(top_couplings, (0, 3, 1, 2)),
             jnp.transpose(top_lists),
         ),
     )
     (applied,) = call(
         down_kernel, [((columns, points), F32)],
         [
-            pltpu.VMEM((columns, points), F32), pltpu.VMEM((points // 256 * columns, 256), BF),
-            pltpu.SemaphoreType.DMA((points // 1024,)),
+            pltpu.VMEM((columns, points), F32), pltpu.VMEM((points // 64 + 2 * REACH, columns, 128), BF),
+            pltpu.VMEM((points // 256 * columns, 256), BF), pltpu.VMEM((2, REACH) + near_blocks.shape[1:], BF),
+            pltpu.SemaphoreType.DMA((2,)), pltpu.SemaphoreType.DMA((points // 1024,)),
         ],
-        [VMEM] * 8, 4 * 10**9, "down", (far, near_part, edge_part, six, blocks, weights, masked, hot),
+        [VMEM] * 5 + [any_spec, SMEM] + [VMEM] * 5, 4 * 10**9, "down",
+        (
+            far, near_part, ordered, other, second0, in_hbm(near_blocks), near_t,
+            six, blocks, weights, masked, hot,
+        ),
         out_specs=[any_spec],
     )
     return applied

time: 33.7 us -> 34 us (level)
    ppermute x1, waiting for transfers between devices: 0.01 us -> 0.5 us  [local(): first1 = lax.ppermute(own1, 'leaf', pairs)]
  transfers between devices with their start and end apart: 7 -> 7, of which waited for: 2 -> 3; matrix products, arithmetic and copies ran while one was open for 0% -> 0% of each run, Pallas kernels for 25% -> 21%
where the time goes in v13:
time: 34 us; the launch traced here: 33.8 us
  Pallas kernels  16.9 us (50%)
  starting transfers between devices  15 us (44%)
  waiting for transfers between devices  1.74 us (5%)
    pallas_call x7, Pallas kernels, call(): pl.pallas_call(kernel, out_shape=[jax.ShapeDtypeStruct(s, t) for s, t in...  16.9 us
    ppermute x3, starting transfers between devices, step(): lax.ppermute(tile_sum, 'leaf', [(i, i ^ reached) for i in range(devices)])  4.92 us
    ppermute x1, starting transfers between devices, local(): second1 = lax.ppermute(first1, 'leaf', onward)  4.83 us
    ppermute x1, starting transfers between devices, local(): first0 = lax.ppermute(own0, 'leaf', pairs)  3.03 us
    ppermute x1, starting transfers between devices, local(): second0 = lax.ppermute(first0, 'leaf', onward)  2.13 us
    ppermute x1, waiting for transfers between devices, local(): second1 = lax.ppermute(first1, 'leaf', onward)  0.7 us
  transfers between devices with their start and end apart: 7, of which 3 were waited for; matrix products, arithmetic and copies ran while one was open for 0% of the time, Pallas kernels for 21%

profile of v13, /device:TPU:0, one launch (start us, length us, event | category | flops | bytes accessed | tf_op | source)
XLA Modules:
  0.0 33.8 jit_solution(1032145720496817824)
XLA Ops:
  0.0 0.0 copy-start.8
  0.0 3.2 %leaf.1 = (bf16[32,4096]{1,0:T(8,128)(2,1)S(1)}, bf16[32,2560]{1,0:T(8,128)(2,1)S(1)}, bf16[8,256,512]{2,1,0:T(8,128)(2,1)S(1)}) custom-call(bf16[32,4096]{1,0:T(8,128)(2,1)} %vec_hbm.1, s32[32,128]{1,0:T(8,128)} %bitcast.11, bf16[32,4096]{1,0:T(8,128)(2,1)} %basis_hbm.1), custom_call_target="tpu_custom_call" | custom-call | flops 1000000000 | tf_op jit(solution)/shard_map/leaf/pallas_call | solution.py:372
  3.2 0.0 copy-start.1
  3.2 0.0 copy-start.4
  3.2 0.0 copy-start.5
  3.2 3.0 %collective-permute-start = (bf16[32,2560]{1,0:T(8,128)(2,1)S(1)}, bf16[32,2560]{1,0:T(8,128)(2,1)S(1)}, u32[]{:S(2)}, u32[]{:S(2)}) collective-permute-start(bf16[32,2560]{1,0:T(8,128)(2,1)S(1)} %get-tuple-element.26.zero_ref.own0_ref), channel_id=1, source_target_pairs={{0,2},{2,0},{4,6},{6,4},{8,10},{10,8},{12,14},{14,12},{1,3},{3,1},... | collective-permute-start | bytes 491528 | tf_op jit(solution)/shard_map/ppermute | solution.py:412
  6.3 0.0 copy-done.8
  6.3 0.0 copy-start
  6.3 0.0 copy-start.7
  6.3 1.8 %lift.1 = (bf16[32,2048]{1,0:T(8,128)(2,1)S(1)}, bf16[32,128]{1,0:T(8,128)(2,1)S(1)}, bf16[32,640]{1,0:T(8,128)(2,1)S(1)}, bf16[16,256,256]{2,1,0:T(8,128)(2,1)S(1)}) custom-call(bf16[32,2560]{1,0:T(8,128)(2,1)S(1)} %get-tuple-element.26.zero_ref.own0_ref, bf16[32,4096]{1,0:T(8,128)(2,1)S(1)} %get-tuple-element.41.ordered_ref, bf16[1024,126]{1,0:T(8,128)(2,1)S(1)} %bitcast.17), custom_call_target="tpu_custom_call" | custom-call | flops 1000000000 | tf_op jit(solution)/shard_map/lift/pallas_call | solution.py:372
  8.0 0.1 collective-permute-start.1
  8.1 3.0 %collective-permute-start.2 = (bf16[32,128]{1,0:T(8,128)(2,1)S(1)}, bf16[32,128]{1,0:T(8,128)(2,1)S(1)}, u32[]{:S(2)}, u32[]{:S(2)}) collective-permute-start(bf16[32,128]{1,0:T(8,128)(2,1)S(1)} %get-tuple-element.29), channel_id=1, source_target_pairs={{0,8},{2,10},{4,12},{6,14},{8,0},{10,2},{12,4},{14,6},{1,9},{3,11}... | collective-permute-start | bytes 24584 | tf_op jit(solution)/shard_map/ppermute | solution.py:423
  11.1 0.0 copy-done.1
  11.1 0.0 copy-done.4
  11.2 0.0 copy-done.5
  11.2 1.1 %matrices.1 = (bf16[16,256,256]{2,1,0:T(8,128)(2,1)S(1)}, s32[8,128]{1,0:T(8,128)S(1)}, bf16[16,256,256]{2,1,0:T(8,128)(2,1)S(1)}, s32[16,256]{1,0:T(8,128)S(1)}) custom-call(bf16[6,1024,126]{2,1,0:T(8,128)(2,1)S(1)} %bitcast.8, s32[6,126]{1,0:T(8,128)S(1)} %bitcast.13, s32[32,128]{1,0:T(8,128)S(1)} %bitcast.12), custom_call_target="tpu_custom_call" | custom-call | flops 1000000 | tf_op jit(solution)/shard_map/matrices/pallas_call | solution.py:372
  12.2 0.5 %collective-permute-done.2 = bf16[32,128]{1,0:T(8,128)(2,1)S(1)} collective-permute-done((bf16[32,128]{1,0:T(8,128)(2,1)S(1)}, bf16[32,128]{1,0:T(8,128)(2,1)S(1)}, u32[]{:S(2)}, u32[]{:S(2)}) %collective-permute-start.2) | collective-permute-done | bytes 8224 | tf_op jit(solution)/shard_map/ppermute | solution.py:423
  12.8 0.5 %collective-permute-done.1.first1_ref = bf16[32,2048]{1,0:T(8,128)(2,1)S(1)} collective-permute-done((bf16[32,2048]{1,0:T(8,128)(2,1)S(1)}, bf16[32,2048]{1,0:T(8,128)(2,1)S(1)}, u32[]{:S(2)}, u32[]{:S(2)}) %collective-permute-start.1) | collective-permute-done | bytes 131104 | tf_op jit(solution)/shard_map/ppermute | solution.py:438
  13.3 0.0 collective-permute-done.first0_ref
  13.3 1.8 %collective-permute-start.3 = (bf16[32,128]{1,0:T(8,128)(2,1)S(1)}, bf16[32,128]{1,0:T(8,128)(2,1)S(1)}, u32[]{:S(2)}, u32[]{:S(2)}) collective-permute-start(bf16[32,128]{1,0:T(8,128)(2,1)S(1)} %add.6), channel_id=1, source_target_pairs={{0,4},{2,6},{4,0},{6,2},{8,12},{10,14},{12,8},{14,10},{1,5},{3,7},... | collective-permute-start | bytes 24584 | tf_op jit(solution)/shard_map/ppermute | solution.py:423
  15.1 2.1 %collective-permute-start.5 = (bf16[32,2560]{1,0:T(8,128)(2,1)S(1)}, bf16[32,2560]{1,0:T(8,128)(2,1)S(1)}, u32[]{:S(2)}, u32[]{:S(2)}) collective-permute-start(bf16[32,2560]{1,0:T(8,128)(2,1)S(1)} %collective-permute-done.first0_ref), channel_id=1, source_target_pairs={{0,4},{4,8},{8,12},{6,2},{10,6},{14,10},{1,5},{5,9},{9,13},{7,3},{... | collective-permute-start | bytes 491528 | tf_op jit(solution)/shard_map/ppermute | solution.py:441
  17.2 0.0 collective-permute-done.3
  17.2 4.8 %collective-permute-start.6 = (bf16[32,2048]{1,0:T(8,128)(2,1)S(1)}, bf16[32,2048]{1,0:T(8,128)(2,1)S(1)}, u32[]{:S(2)}, u32[]{:S(2)}) collective-permute-start(bf16[32,2048]{1,0:T(8,128)(2,1)S(1)} %collective-permute-done.1.first1_ref), channel_id=1, source_target_pairs={{0,4},{4,8},{8,12},{6,2},{10,6},{14,10},{1,5},{5,9},{9,13},{7,3},{... | collective-permute-start | bytes 393224 | tf_op jit(solution)/shard_map/ppermute | solution.py:445
  22.1 0.1 collective-permute-start.4
  22.2 0.0 copy-done
  22.2 0.0 copy-done.7
  22.2 1.7 %near.1.near_in = f32[32,4096]{1,0:T(8,128)S(1)} custom-call(bf16[32,4096]{1,0:T(8,128)(2,1)S(1)} %get-tuple-element.41.ordered_ref, bf16[64,64,256]{2,1,0:T(8,128)(2,1)S(1)} %copy-done, s32[4,64]{1,0:T(4,128)S(1)} %bitcast.15), custom_call_target="tpu_custom_call" | custom-call | flops 1000000 | tf_op jit(solution)/shard_map/near/pallas_call | solution.py:372
  23.9 0.7 %collective-permute-done.6.second1_ref = bf16[32,2048]{1,0:T(8,128)(2,1)S(1)} collective-permute-done((bf16[32,2048]{1,0:T(8,128)(2,1)S(1)}, bf16[32,2048]{1,0:T(8,128)(2,1)S(1)}, u32[]{:S(2)}, u32[]{:S(2)}) %collective-permute-start.6) | collective-permute-done | bytes 131104 | tf_op jit(solution)/shard_map/ppermute | solution.py:445
  24.6 0.0 collective-permute-done.5.second0_ref
  24.6 0.0 copy-start.2
  24.6 0.0 copy-start.3
  24.6 0.0 copy-start.6
  24.6 2.4 %far.1 = f32[32,4096]{1,0:T(8,128)S(1)} custom-call(bf16[32,2560]{1,0:T(8,128)(2,1)S(1)} %get-tuple-element.26.zero_ref.own0_ref, bf16[32,2048]{1,0:T(8,128)(2,1)S(1)} %get-tuple-element.28.own1_ref, bf16[32,2560]{1,0:T(8,128)(2,1)S(1)} %collective-permute-done.first0_ref, bf16[32,2048]{1,0:T(8,128)(2,1)S(1)} %collective-permute-done.1.first1_ref, ...), custom_call_target="tpu_custom_call" | custom-call | flops 4000000000 | tf_op jit(solution)/shard_map/far/pallas_call | solution.py:372
  27.0 0.0 collective-permute-done.4.other_ref.last_ref
  27.0 0.0 copy-done.2
  27.0 0.0 copy-done.3
  27.0 0.0 copy-done.6
  27.0 1.7 %root.1.six_ref = f32[32,256]{1,0:T(8,128)S(1)} custom-call(bf16[32,640]{1,0:T(8,128)(2,1)S(1)} %add_dynamic-update-slice_fusion.own_ref, bf16[32,640]{1,0:T(8,128)(2,1)S(1)} %collective-permute-done.4.other_ref.last_ref, bf16[14,32,32]{2,1,0:T(8,128)(2,1)S(1)} %bitcast.10, bf16[6,15,32,32]{3,2,1,0:T(8,128)(2,1)S(1)} %bitcast.9, s32[6,15]{1,0:T(8,128)S(1)} %bitcast.14), custom_call_target="tpu_custom_call" | custom-call | flops 1000000 | tf_op jit(solution)/shard_map/root/pallas_call | solution.py:372
  28.8 5.0 %down.1 = f32[32,4096]{1,0:T(8,128)} custom-call(f32[32,4096]{1,0:T(8,128)S(1)} %far.1, f32[32,4096]{1,0:T(8,128)S(1)} %near.1.near_in, bf16[32,4096]{1,0:T(8,128)(2,1)S(1)} %get-tuple-element.41.ordered_ref, bf16[32,640]{1,0:T(8,128)(2,1)S(1)} %collective-permute-done.4.other_ref.last_ref, bf16[32,2560]{1,0:T(8,128)(2,1)S(1)} %collective-permute-done.5.second0_ref, ...), custom_call_target="tpu_custom_call" | custom-call | flops 4000000000 | tf_op jit(solution)/shard_map/down/pallas_call | solution.py:372
  (2 shorter events, 0.0 us)
Async XLA Ops:
  0.0 6.3 %copy-start.8 = (bf16[32,32,126]{2,1,0:T(8,128)(2,1)S(1)}, bf16[32,32,126]{2,1,0:T(8,128)(2,1)}, u32[]{:S(2)}) copy-start(bf16[32,32,126]{2,1,0:T(8,128)(2,1)} %param.16) | copy-start | bytes 774148
  3.2 7.9 %copy-start.1 = (bf16[6,32,32,126]{3,2,1,0:T(8,128)(2,1)S(1)}, bf16[6,32,32,126]{3,2,1,0:T(8,128)(2,1)}, u32[]{:S(2)}) copy-start(bf16[6,32,32,126]{3,2,1,0:T(8,128)(2,1)} %param.17) | copy-start | bytes 4644868
  3.2 7.9 %copy-start.4 = (s32[4096]{0:T(1024)S(1)}, s32[4096]{0:T(1024)}, u32[]{:S(2)}) copy-start(s32[4096]{0:T(1024)} %param.12) | copy-start | bytes 49156
  3.2 7.9 %copy-start.5 = (s32[126,6]{0,1:T(8,128)S(1)}, s32[126,6]{0,1:T(8,128)}, u32[]{:S(2)}) copy-start(s32[126,6]{0,1:T(8,128)} %param.18) | copy-start | bytes 9076
  3.2 10.0 %collective-permute-start = (bf16[32,2560]{1,0:T(8,128)(2,1)S(1)}, bf16[32,2560]{1,0:T(8,128)(2,1)S(1)}, u32[]{:S(2)}, u32[]{:S(2)}) collective-permute-start(bf16[32,2560]{1,0:T(8,128)(2,1)S(1)} %get-tuple-element.26.zero_ref.own0_ref), channel_id=1, source_target_pairs={{0,2},{2,0},{4,6},{6,4},{8,10},{10,8},{12,14},{14,12},{1,3},{3,1},... | collective-permute-start | bytes 491528 | tf_op jit(solution)/shard_map/ppermute | solution.py:412
  6.3 15.9 %copy-start = (bf16[64,64,256]{2,1,0:T(8,128)(2,1)S(1)}, bf16[64,64,256]{2,1,0:T(8,128)(2,1)}, u32[]{:S(2)}) copy-start(bf16[64,64,256]{2,1,0:T(8,128)(2,1)} %blocks_ref.3) | copy-start | bytes 6291460
  6.3 15.9 %copy-start.7 = (s32[64,4]{0,1:T(4,128)S(1)}, s32[64,4]{0,1:T(4,128)}, u32[]{:S(2)}) copy-start(s32[64,4]{0,1:T(4,128)} %param.15) | copy-start | bytes 3076
  8.0 5.2 %collective-permute-start.1 = (bf16[32,2048]{1,0:T(8,128)(2,1)S(1)}, bf16[32,2048]{1,0:T(8,128)(2,1)S(1)}, u32[]{:S(2)}, u32[]{:S(2)}) collective-permute-start(bf16[32,2048]{1,0:T(8,128)(2,1)S(1)} %get-tuple-element.28.own1_ref), channel_id=1, source_target_pairs={{0,2},{2,0},{4,6},{6,4},{8,10},{10,8},{12,14},{14,12},{1,3},{3,1},... | collective-permute-start | bytes 393224 | tf_op jit(solution)/shard_map/ppermute | solution.py:438
  8.1 4.7 %collective-permute-start.2 = (bf16[32,128]{1,0:T(8,128)(2,1)S(1)}, bf16[32,128]{1,0:T(8,128)(2,1)S(1)}, u32[]{:S(2)}, u32[]{:S(2)}) collective-permute-start(bf16[32,128]{1,0:T(8,128)(2,1)S(1)} %get-tuple-element.29), channel_id=1, source_target_pairs={{0,8},{2,10},{4,12},{6,14},{8,0},{10,2},{12,4},{14,6},{1,9},{3,11}... | collective-permute-start | bytes 24584 | tf_op jit(solution)/shard_map/ppermute | solution.py:423
  13.3 3.9 %collective-permute-start.3 = (bf16[32,128]{1,0:T(8,128)(2,1)S(1)}, bf16[32,128]{1,0:T(8,128)(2,1)S(1)}, u32[]{:S(2)}, u32[]{:S(2)}) collective-permute-start(bf16[32,128]{1,0:T(8,128)(2,1)S(1)} %add.6), channel_id=1, source_target_pairs={{0,4},{2,6},{4,0},{6,2},{8,12},{10,14},{12,8},{14,10},{1,5},{3,7},... | collective-permute-start | bytes 24584 | tf_op jit(solution)/shard_map/ppermute | solution.py:423
  15.1 9.5 %collective-permute-start.5 = (bf16[32,2560]{1,0:T(8,128)(2,1)S(1)}, bf16[32,2560]{1,0:T(8,128)(2,1)S(1)}, u32[]{:S(2)}, u32[]{:S(2)}) collective-permute-start(bf16[32,2560]{1,0:T(8,128)(2,1)S(1)} %collective-permute-done.first0_ref), channel_id=1, source_target_pairs={{0,4},{4,8},{8,12},{6,2},{10,6},{14,10},{1,5},{5,9},{9,13},{7,3},{... | collective-permute-start | bytes 491528 | tf_op jit(solution)/shard_map/ppermute | solution.py:441
  17.2 7.3 %collective-permute-start.6 = (bf16[32,2048]{1,0:T(8,128)(2,1)S(1)}, bf16[32,2048]{1,0:T(8,128)(2,1)S(1)}, u32[]{:S(2)}, u32[]{:S(2)}) collective-permute-start(bf16[32,2048]{1,0:T(8,128)(2,1)S(1)} %collective-permute-done.1.first1_ref), channel_id=1, source_target_pairs={{0,4},{4,8},{8,12},{6,2},{10,6},{14,10},{1,5},{5,9},{9,13},{7,3},{... | collective-permute-start | bytes 393224 | tf_op jit(solution)/shard_map/ppermute | solution.py:445
  22.1 4.9 %collective-permute-start.4 = (bf16[32,640]{1,0:T(8,128)(2,1)S(1)}, bf16[32,640]{1,0:T(8,128)(2,1)S(1)}, u32[]{:S(2)}, u32[]{:S(2)}) collective-permute-start(bf16[32,640]{1,0:T(8,128)(2,1)S(1)} %add_dynamic-update-slice_fusion.own_ref), channel_id=1, source_target_pairs={{0,2},{2,0},{4,6},{6,4},{8,10},{10,8},{12,14},{14,12},{1,3},{3,1},... | collective-permute-start | bytes 122888 | tf_op jit(solution)/shard_map/ppermute | solution.py:423
  24.6 2.4 %copy-start.2 = (bf16[6,32,32,15]{2,1,3,0:T(8,128)(2,1)S(1)}, bf16[6,32,32,15]{2,1,3,0:T(8,128)(2,1)}, u32[]{:S(2)}) copy-start(bf16[6,32,32,15]{2,1,3,0:T(8,128)(2,1)} %param.20) | copy-start | bytes 552964
  24.6 2.4 %copy-start.3 = (bf16[32,32,14]{1,0,2:T(8,128)(2,1)S(1)}, bf16[32,32,14]{1,0,2:T(8,128)(2,1)}, u32[]{:S(2)}) copy-start(bf16[32,32,14]{1,0,2:T(8,128)(2,1)} %param.19) | copy-start | bytes 86020
  24.6 2.4 %copy-start.6 = (s32[15,6]{0,1:T(8,128)S(1)}, s32[15,6]{0,1:T(8,128)}, u32[]{:S(2)}) copy-start(s32[15,6]{0,1:T(8,128)} %param.21) | copy-start | bytes 1084
